TPU v7x, 32 devices: a whole 2x2x4 slice. The times are simulated.
32 devices in a mesh: expert: 4 (over y, x), etp: 8 (over z, core).
Axes of the slice: x: 2, y: 2, z: 4, core: 2. Of those that a mesh axis runs over, the one named last changes fastest.
Arguments:
- tokens: bfloat16 [512, 3072], P('expert', 'etp'), may hold values from -6 to 6
- expert_ids: int32 [512, 2], P('expert'), may hold values from 0 to 3, all different within a row
- live_tokens: int32 [4], replicated, may hold values from 32 to 128, as said below
- replicated: int32 [4], replicated, may hold values from 0 to 1, as said below
- w_router: bfloat16 [3072, 4], P('etp'), may hold values from -0.109375 to 0.109375
- w_gate: bfloat16 [4, 3072, 8192], P('expert', None, 'etp'), may hold values from -0.109375 to 0.109375
- w_up: bfloat16 [4, 3072, 8192], P('expert', None, 'etp'), may hold values from -0.109375 to 0.109375
- w_down: bfloat16 [4, 8192, 3072], P('expert', 'etp'), may hold values from -0.0625 to 0.0625
- cotangent: bfloat16 [512, 3072], P('expert', 'etp'), may hold values from -6 to 6
Outputs:
- mixed: bfloat16 [512, 3072], P('expert', 'etp')
- grad_gate: bfloat16 [4, 3072, 8192], P('expert', None, 'etp')
- grad_up: bfloat16 [4, 3072, 8192], P('expert', None, 'etp')
- grad_down: bfloat16 [4, 8192, 3072], P('expert', 'etp')
- grad_router: bfloat16 [3072, 4], P('etp')
Inputs may be any that keep to these rules, and one draw needn't show every extreme that they name: `replicated`: for every expert e below half of 4, exactly one of e and e plus half of 4 has the entry 1. `live_tokens`: some group has 128 live tokens and some other group has 32.
All inputs are finite; a program needn't handle non-finite values.
Results may differ from a plain program's by a relative error of at most 0.0065.
Values may be sent and summed in bfloat16 or wider, within the bound.
No kernel may reach another device: no remote copies, remote signals or barrier semaphores. Data moves between devices by JAX's collectives and lax.ppermute only.
A program may use at most 192 MiB of HBM per device.

v0:
```python
import jax
import jax.numpy as jnp
from jax import lax
from jax.sharding import PartitionSpec as P

CAPG = 32
RCAP = 8


def partner(block, axis, bit):
    count = lax.axis_size(axis)
    route = []
    for low in range(count):
        high = low | 1 << bit
        if high != low and high < count:
            route += [(low, high), (high, low)]
    return lax.ppermute(block, axis, route)


def silu_parts(pre):
    sigma = jax.nn.sigmoid(pre)
    return (pre * sigma, sigma * (1.0 + pre * (1.0 - sigma)))


def project_in(rows, gate_w, up_w):
    gate_pre = jnp.dot(rows, gate_w, preferred_element_type=jnp.float32)
    up_pre = jnp.dot(rows, up_w, preferred_element_type=jnp.float32)
    active, slope = silu_parts(gate_pre)
    hidden = (active * up_pre).astype(jnp.bfloat16)
    return (up_pre, active, slope, hidden)


def project_out(down_w, hidden):
    return lax.dot_general(
        down_w, hidden, (((0,), (2,)), ((), ())), preferred_element_type=jnp.float32
    )


def project_back(rows_x, rows_d, down_w, parts):
    up_pre, active, slope, hidden = parts
    d_hidden = lax.dot_general(
        rows_d, down_w, (((2,), (1,)), ((), ())), preferred_element_type=jnp.float32
    )
    d_gate = (d_hidden * up_pre * slope).astype(jnp.bfloat16)
    d_up = (d_hidden * active).astype(jnp.bfloat16)
    paired = (((0, 1), (0, 1)), ((), ()))
    grad_g = lax.dot_general(rows_x, d_gate, paired, preferred_element_type=jnp.float32)
    grad_u = lax.dot_general(rows_x, d_up, paired, preferred_element_type=jnp.float32)
    grad_d = lax.dot_general(hidden, rows_d, paired, preferred_element_type=jnp.float32)
    return (grad_g, grad_u, grad_d)


def shards(tokens, expert_ids, live_tokens, replicated, w_router, w_gate, w_up, w_down, cotangent):
    groups = lax.axis_size("expert")
    group = lax.axis_index("expert")
    count_tok = tokens.shape[0]
    experts = w_router.shape[1]
    capacity = CAPG + RCAP
    partner_bit = lax.axis_size("expert").bit_length() - 2
    logits = lax.psum(jnp.dot(tokens, w_router, preferred_element_type=jnp.float32), "etp")
    lanes = jnp.arange(experts, dtype=jnp.int32)
    order = jnp.concatenate([expert_ids[:, 0], expert_ids[:, 1]])
    choose = order[:, None] == lanes[None, :]
    chosen = jnp.sum(jnp.where(choose, jnp.concatenate([logits, logits]), 0.0), axis=1)
    first_logit = chosen[:count_tok]
    second_logit = chosen[count_tok:]
    gate_one = jax.nn.sigmoid(first_logit - second_logit)
    gate_two = jax.nn.sigmoid(second_logit - first_logit)
    gates = jnp.concatenate([gate_one, gate_two])
    live = jnp.arange(count_tok, dtype=jnp.int32) < live_tokens[group]
    alive = jnp.concatenate([live, live])
    onehot = choose & alive[:, None]
    ones = onehot.astype(jnp.int32)
    before = jnp.cumsum(ones, axis=0, dtype=jnp.int32) - ones
    slot = jnp.sum(jnp.where(onehot, before, 0), axis=1, dtype=jnp.int32)
    flagged = jnp.sum(jnp.where(choose, replicated[None, :], 0), axis=1, dtype=jnp.int32)
    kept = alive & ((slot < CAPG) | (flagged == 1) & (slot < capacity))
    target = jnp.where(slot < CAPG, order, (order + groups // 2) % groups)
    position = target * capacity + slot
    slot_lanes = jnp.arange(groups * capacity, dtype=jnp.int32)
    select = ((slot_lanes[:, None] == position[None, :]) & kept[None, :]).astype(jnp.bfloat16)
    doubled_dy = jnp.concatenate([cotangent, cotangent])
    scaled = (gates[:, None] * doubled_dy.astype(jnp.float32)).astype(jnp.bfloat16)
    doubled_x = jnp.concatenate([tokens, tokens])
    send_x = (
        jnp.dot(select, doubled_x, preferred_element_type=jnp.float32)
        .astype(jnp.bfloat16)
        .reshape(groups, capacity, -1)
    )
    send_d = (
        jnp.dot(select, scaled, preferred_element_type=jnp.float32)
        .astype(jnp.bfloat16)
        .reshape(groups, capacity, -1)
    )
    recv_x, recv_d = (
        lax.all_to_all(send_x, "expert", split_axis=0, concat_axis=0, tiled=True),
        lax.all_to_all(send_d, "expert", split_axis=0, concat_axis=0, tiled=True),
    )
    rows_x, rows_d = (
        lax.all_gather(recv_x, "etp", axis=2, tiled=True),
        lax.all_gather(recv_d, "etp", axis=2, tiled=True),
    )
    own_gate = w_gate[0]
    own_up = w_up[0]
    own_down = w_down[0]
    far_gate, far_up, far_down = partner((own_gate, own_up, own_down), "expert", partner_bit)
    near_x = rows_x[:, :CAPG]
    extra_x = rows_x[:, CAPG:]
    near_d = rows_d[:, :CAPG]
    extra_d = rows_d[:, CAPG:]
    near_parts = project_in(near_x, own_gate, own_up)
    extra_parts = project_in(extra_x, far_gate, far_up)
    summed = lax.psum_scatter(
        jnp.concatenate(
            [project_out(own_down, near_parts[3]), project_out(far_down, extra_parts[3])], axis=2
        ),
        "etp",
        scatter_dimension=0,
        tiled=True,
    )
    expert_out = summed.astype(jnp.bfloat16)
    back = lax.all_to_all(expert_out, "expert", split_axis=1, concat_axis=1, tiled=True)
    assigned = jnp.dot(back.reshape(back.shape[0], -1), select, preferred_element_type=jnp.float32)
    mixed_cols = (
        gate_one[None, :] * assigned[:, :count_tok] + gate_two[None, :] * assigned[:, count_tok:]
    )
    mixed = mixed_cols.T.astype(jnp.bfloat16)
    partial_dots = jnp.sum(assigned.T * doubled_dy.astype(jnp.float32), axis=1)
    dots = lax.psum(partial_dots, "etp")
    d_logit = (dots[:count_tok] - dots[count_tok:]) * gate_one * gate_two
    d_logits = jnp.where(choose[:count_tok], d_logit[:, None], 0.0) - jnp.where(
        choose[count_tok:], d_logit[:, None], 0.0
    )
    router_part = jnp.dot(tokens.astype(jnp.float32).T, d_logits, precision=lax.Precision.HIGHEST)
    grad_router = lax.psum(router_part, "expert").astype(jnp.bfloat16)
    near_grads = project_back(near_x, near_d, own_down, near_parts)
    extra_grads = project_back(extra_x, extra_d, far_down, extra_parts)
    came_back = partner((extra_grads[0], extra_grads[1], extra_grads[2]), "expert", partner_bit)
    grads = (
        near_grads[0] + came_back[0],
        near_grads[1] + came_back[1],
        near_grads[2] + came_back[2],
    )
    grad_gate = grads[0].astype(jnp.bfloat16)[None]
    grad_up = grads[1].astype(jnp.bfloat16)[None]
    grad_down = grads[2].astype(jnp.bfloat16)[None]
    return (mixed, grad_gate, grad_up, grad_down, grad_router)


def solution(mesh):
    in_specs = (
        P("expert", "etp"),
        P("expert", None),
        P(),
        P(),
        P("etp", None),
        P("expert", None, "etp"),
        P("expert", None, "etp"),
        P("expert", "etp", None),
        P("expert", "etp"),
    )
    out_specs = (
        P("expert", "etp"),
        P("expert", None, "etp"),
        P("expert", None, "etp"),
        P("expert", "etp", None),
        P("etp", None),
    )
    return jax.shard_map(shards, mesh=mesh, in_specs=in_specs, out_specs=out_specs, check_vma=False)
```

profile of v0, /device:TPU:0, one launch (start us, length us, event | category | flops | bytes accessed | tf_op | source)
XLA Modules:
  0.0 1374.8 jit_solution(8738871236114827697)
XLA Ops:
  7.2 0.0 copy-start
  7.2 0.0 reduce-scatter.2.cloned.1.call-start
  7.2 3.0 collective-permute-start
  10.3 0.1 collective-permute-start.1
  10.3 1.9 collective-permute-start.2
  12.3 1.2 dynamic_slice.3
  13.5 0.6 iota_compare_fusion.2
  14.2 0.8 slice_bitcast_fusion.1
  15.0 1.2 reduce-window.6
  16.2 0.1 slice.64
  16.3 0.1 copy.14
  16.4 0.1 copy.15
  16.5 0.1 add_bitcast_fusion
  16.6 0.9 select_reduce_fusion
  17.5 1.4 convolution_convert_fusion.1
  18.9 398.1 %all_to_all.15 = bf16[4,40,384]{2,1,0:T(8,128)(2,1)S(1)} all-to-all(bf16[4,40,384]{2,1,0:T(8,128)(2,1)S(1)} %bitcast.118), channel_id=1, replica_groups=mesh['expert'=4,'etp'=8] {'expert'}, dimensions={0} | all-to-all | bytes 245760 | tf_op jit(solution)/shard_map/all_to_all | solution.py:96
  417.0 17.0 %all_gather.6 = bf16[4,40,3072]{2,1,0:T(8,128)(2,1)S(1)} all-gather(bf16[4,40,384]{2,1,0:T(8,128)(2,1)S(1)} %all_to_all.15), channel_id=1, replica_groups=mesh['expert'=4,'etp'=8] {'etp'}, dimensions={2}, use_global_device_ids=true | all-gather | bytes 1105920 | tf_op jit(solution)/shard_map/all_gather | solution.py:100
  434.0 4.0 fusion.17
  437.9 0.0 copy-done.5
  437.9 0.0 slice-start.1
  438.0 1.9 multiply_convert_fusion.2
  439.8 0.0 slice-done
  439.8 0.0 slice-done.1
  439.8 1.0 fusion.22
  440.8 0.0 collective-permute-done
  440.9 3.9 fusion.9
  444.8 0.0 collective-permute-done.1
  444.8 4.6 multiply_convert_fusion.7
  449.4 0.0 collective-permute-done.2
  449.4 4.0 fusion.25
  453.4 1.4 pad_maximum_fusion
  454.8 0.0 reduce-scatter.2.cloned.1.call-update
  454.8 36.7 %reduce-scatter.2.cloned.1.call-done = f32[384,4,40]{0,2,1:T(8,128)} async-done(((f32[3072,4,40]{0,2,1:T(8,128)}), f32[384,4,40]{0,2,1:T(8,128)}) %reduce-scatter.2.cloned.1.call-update) | async-done | bytes 245776 | tf_op jit(solution)/shard_map/reduce_scatter | solution.py:113
  491.5 1.6 convert_element_type.66
  493.1 3.6 all-to-all-start.1
  496.7 0.0 copy-done
  496.7 0.0 copy-done.2
  496.7 0.1 fusion.89
  496.9 0.1 copy.16
  497.0 4.7 all-to-all-done.1
  501.7 0.3 fusion.36
  502.0 13.6 all-reduce
  515.6 0.2 convolution_convert_fusion
  515.9 7.4 all_to_all.16
  523.3 16.5 %all_gather.7 = bf16[4,40,3072]{2,1,0:T(8,128)(2,1)S(1)} all-gather(bf16[4,40,384]{2,1,0:T(8,128)(2,1)S(1)} %all_to_all.16), channel_id=1, replica_groups=mesh['expert'=4,'etp'=8] {'etp'}, dimensions={2}, use_global_device_ids=true | all-gather | bytes 1105920 | tf_op jit(solution)/shard_map/all_gather | solution.py:101
  539.8 6.4 convolution_bitcast_fusion
  546.2 1.0 collective-permute-start.5
  547.2 4.7 fusion.3
  551.9 0.0 copy-start.3
  551.9 6.3 convolution_bitcast_fusion.1
  558.2 1.0 collective-permute-start.4
  559.2 6.4 convolution_bitcast_fusion.2
  565.6 1.0 collective-permute-start.3
  566.7 0.8 copy.18
  567.5 0.2 convolution_bitcast_fusion.3
  567.6 10.1 psum.23
  577.7 5.0 fusion.11
  582.7 237.3 %collective-permute-done.5 = f32[1024,3072]{1,0:T(8,128)} collective-permute-done((f32[1024,3072]{1,0:T(8,128)}, f32[1024,3072]{1,0:T(8,128)}, u32[]{:S(2)}, u32[]{:S(2)}) %collective-permute-start.5) | collective-permute-done | bytes 12582944 | tf_op jit(solution)/shard_map/ppermute | solution.py:17
  820.0 9.1 fusion.21
  829.1 260.5 %collective-permute-done.4 = f32[3072,1024]{1,0:T(8,128)} collective-permute-done((f32[3072,1024]{1,0:T(8,128)}, f32[3072,1024]{1,0:T(8,128)}, u32[]{:S(2)}, u32[]{:S(2)}) %collective-permute-start.4) | collective-permute-done | bytes 12582944 | tf_op jit(solution)/shard_map/ppermute | solution.py:17
  1089.6 9.2 fusion.20
  1098.8 259.9 %collective-permute-done.3 = f32[3072,1024]{1,0:T(8,128)} collective-permute-done((f32[3072,1024]{1,0:T(8,128)}, f32[3072,1024]{1,0:T(8,128)}, u32[]{:S(2)}, u32[]{:S(2)}) %collective-permute-start.3) | collective-permute-done | bytes 12582944 | tf_op jit(solution)/shard_map/ppermute | solution.py:17
  1358.7 9.2 fusion.19
  1368.0 0.0 copy-done.1
  (22 shorter events, 0.2 us)
Async XLA Ops:
  7.2 489.6 %copy-start = (bf16[384,4]{0,1:T(4,128)(2,1)S(1)}, bf16[384,4]{0,1:T(4,128)(2,1)}, u32[]{:S(2)}) copy-start(bf16[384,4]{0,1:T(4,128)(2,1)} %param.13) | copy-start | bytes 9220
  7.2 484.3 %reduce-scatter.2.cloned.1.call-start = ((), (), s32[]{:S(2)}) async-start(), calls=%async_computation.4 | async-start | bytes 2211840 | tf_op jit(solution)/shard_map/reduce_scatter | solution.py:113
  7.2 433.6 %collective-permute-start = (bf16[3072,1024]{1,0:T(8,128)(2,1)}, bf16[3072,1024]{1,0:T(8,128)(2,1)}, u32[]{:S(2)}, u32[]{:S(2)}) collective-permute-start(bf16[3072,1024]{1,0:T(8,128)(2,1)} %bitcast.115), channel_id=1, source_target_pairs={{0,16},{16,0},{8,24},{24,8},{1,17},{17,1},{9,25},{25,9},{2,18},{18... | collective-permute-start | bytes 18874376 | tf_op jit(solution)/shard_map/ppermute | solution.py:17
  10.3 434.5 %collective-permute-start.1 = (bf16[3072,1024]{1,0:T(8,128)(2,1)}, bf16[3072,1024]{1,0:T(8,128)(2,1)}, u32[]{:S(2)}, u32[]{:S(2)}) collective-permute-start(bf16[3072,1024]{1,0:T(8,128)(2,1)} %bitcast.120), channel_id=1, source_target_pairs={{0,16},{16,0},{8,24},{24,8},{1,17},{17,1},{9,25},{25,9},{2,18},{18... | collective-permute-start | bytes 18874376 | tf_op jit(solution)/shard_map/ppermute | solution.py:17
  10.3 439.1 %collective-permute-start.2 = (bf16[1024,3072]{1,0:T(8,128)(2,1)}, bf16[1024,3072]{1,0:T(8,128)(2,1)}, u32[]{:S(2)}, u32[]{:S(2)}) collective-permute-start(bf16[1024,3072]{1,0:T(8,128)(2,1)} %bitcast.112), channel_id=1, source_target_pairs={{0,16},{16,0},{8,24},{24,8},{1,17},{17,1},{9,25},{25,9},{2,18},{18... | collective-permute-start | bytes 18874376 | tf_op jit(solution)/shard_map/ppermute | solution.py:17
  16.5 421.4 %copy-start.5 = (bf16[1,3072,1024]{2,1,0:T(8,128)(2,1)S(1)}, bf16[1,3072,1024]{2,1,0:T(8,128)(2,1)}, u32[]{:S(2)}) copy-start(bf16[1,3072,1024]{2,1,0:T(8,128)(2,1)} %param.15) | copy-start | bytes 18874372
  434.0 5.9 slice-start
  437.9 1.9 slice-start.1
  449.4 47.3 %copy-start.2 = (bf16[128,384]{1,0:T(8,128)(2,1)S(1)}, bf16[128,384]{1,0:T(8,128)(2,1)}, u32[]{:S(2)}) copy-start(bf16[128,384]{1,0:T(8,128)(2,1)} %param.9) | copy-start | bytes 294916
  449.4 47.5 %copy-start.4 = (bf16[128,384]{1,0:T(8,128)(2,1)S(1)}, bf16[128,384]{1,0:T(8,128)(2,1)}, u32[]{:S(2)}) copy-start(bf16[128,384]{1,0:T(8,128)(2,1)} %param.17) | copy-start | bytes 294916
  493.1 8.6 all-to-all-start.1
  546.2 273.8 %collective-permute-start.5 = (f32[1024,3072]{1,0:T(8,128)}, f32[1024,3072]{1,0:T(8,128)}, u32[]{:S(2)}, u32[]{:S(2)}) collective-permute-start(f32[1024,3072]{1,0:T(8,128)} %convolution_bitcast_fusion), channel_id=1, source_target_pairs={{0,16},{16,0},{8,24},{24,8},{1,17},{17,1},{9,25},{25,9},{2,18},{18... | collective-permute-start | bytes 37748744 | tf_op jit(solution)/shard_map/ppermute | solution.py:17
  551.9 7.3 copy-start.3
  558.2 531.4 %collective-permute-start.4 = (f32[3072,1024]{1,0:T(8,128)}, f32[3072,1024]{1,0:T(8,128)}, u32[]{:S(2)}, u32[]{:S(2)}) collective-permute-start(f32[3072,1024]{1,0:T(8,128)} %convolution_bitcast_fusion.1), channel_id=1, source_target_pairs={{0,16},{16,0},{8,24},{24,8},{1,17},{17,1},{9,25},{25,9},{2,18},{18... | collective-permute-start | bytes 37748744 | tf_op jit(solution)/shard_map/ppermute | solution.py:17
  565.6 793.1 %collective-permute-start.3 = (f32[3072,1024]{1,0:T(8,128)}, f32[3072,1024]{1,0:T(8,128)}, u32[]{:S(2)}, u32[]{:S(2)}) collective-permute-start(f32[3072,1024]{1,0:T(8,128)} %convolution_bitcast_fusion.2), channel_id=1, source_target_pairs={{0,16},{16,0},{8,24},{24,8},{1,17},{17,1},{9,25},{25,9},{2,18},{18... | collective-permute-start | bytes 37748744 | tf_op jit(solution)/shard_map/ppermute | solution.py:17
  829.1 529.6 %copy-start.6 = (f32[4,32,1024]{2,1,0:T(8,128)S(1)}, f32[4,32,1024]{2,1,0:T(8,128)}, u32[]{:S(2)}) copy-start(f32[4,32,1024]{2,1,0:T(8,128)} %get-tuple-element.26) | copy-start | bytes 1572868
  1358.7 9.2 copy-start.1
Sparse Core Ops, SparseCore 0:
  454.9 36.5 reduce-scatter.1
where the time goes:
time: 1380 us; the launch traced here: 1370 us
  waiting for transfers between devices  799 us (58%)
  blocking collectives  463 us (34%)
  matrix products  77.8 us (6%)
  between operations  14.2 us (1%)
    ppermute x6, waiting for transfers between devices, partner(): return lax.ppermute(block, axis, route)  758 us
    all_to_all x1, blocking collectives, shards(): lax.all_to_all(send_x, 'expert', split_axis=0, concat_axis=0, tiled=True)  398 us
    reduce_scatter x1, waiting for transfers between devices, shards(): lax.psum_scatter(jnp.concatenate([project_out(own_down, near_parts[3]), p...  36.7 us
  transfers between devices with their start and end apart: 8, of which 5 were waited for; matrix products, arithmetic and copies ran while one was open for 5% of the time, Pallas kernels for 0%

commit v1 on v0

v1 whole, which is shorter than its diff:
```python
import functools

import jax
import jax.numpy as jnp
from jax import lax
from jax.experimental import pallas as pl
from jax.experimental.pallas import tpu as pltpu
from jax.sharding import Mesh, PartitionSpec as P

CAPG = 32
RCAP = 8
CAP = CAPG + RCAP
META = 8
ROWS = CAP + META
MIB = 1024 * 1024
LANES = 128

F32 = jnp.float32
BF16 = jnp.bfloat16


def dot(a, b, dims):
    return lax.dot_general(a, b, (dims, ((), ())), preferred_element_type=F32)


def split3(value):
    hi = value.astype(BF16).astype(F32)
    rest = value - hi
    mid = rest.astype(BF16).astype(F32)
    return hi, mid, rest - mid


def pack_kernel(experts, *refs):
    sources, pos_ref, send_refs = refs[:6], refs[6], refs[7 : 7 + experts]
    held, sems = refs[7 + experts : 13 + experts], refs[13 + experts]
    copies = [pltpu.make_async_copy(a, b, sems.at[i]) for i, (a, b) in enumerate(zip(sources, held))]
    for copy in copies:
        copy.start()
    for copy in copies:
        copy.wait()
    live_ref, flags_ref, ids_ref, router_ref, tok_ref, cot_ref = held
    count, width = tok_ref.shape
    both = 2 * count
    lanes = max(experts, 8)
    group = lax.axis_index("expert")
    live = live_ref[group]
    ids = ids_ref[...]
    first, second = ids[0:1, :], ids[1:2, :]
    order = jnp.concatenate([first, second], axis=1)
    other = jnp.concatenate([second, first], axis=1)
    lane = lax.broadcasted_iota(jnp.int32, (1, both), 1)
    token = jnp.where(lane < count, lane, lane - count)
    alive = token < live
    expert_rows = lax.broadcasted_iota(jnp.int32, (lanes, both), 0)
    onehot = ((expert_rows == order) & alive).astype(F32)
    earlier = lax.broadcasted_iota(jnp.int32, (both, both), 0)
    later = lax.broadcasted_iota(jnp.int32, (both, both), 1)
    before = dot(onehot.astype(BF16), (earlier < later).astype(BF16), ((1,), (0,)))
    slot = jnp.sum(onehot * before, axis=0, keepdims=True).astype(jnp.int32)
    limit = jnp.full((1, both), CAPG, jnp.int32)
    for e in range(experts):
        limit = jnp.where(order == e, CAPG + RCAP * flags_ref[e], limit)
    kept = alive & (slot < limit)
    position = jnp.where(kept, (order ^ group) * ROWS + slot, -1)
    pos_ref[...] = position

    slots = lax.broadcasted_iota(jnp.int32, (experts * ROWS, both), 0)
    select = (slots == position).astype(F32)
    merged = (select[:, :count] + select[:, count:]).astype(BF16)
    rows_x = dot(merged, tok_ref[...], ((1,), (0,)))
    rows_d = dot(merged, cot_ref[...], ((1,), (0,)))

    logits = dot(router_ref[...], tok_ref[...], ((1,), (1,)))
    pick = lax.broadcasted_iota(jnp.int32, (experts, count), 0)
    gap = jnp.sum(
        jnp.where(pick == first, logits, 0.0) - jnp.where(pick == second, logits, 0.0),
        axis=0,
        keepdims=True,
    )
    hi, mid, low = split3(jnp.concatenate([gap, -gap], axis=1))
    meta_row = lax.broadcasted_iota(jnp.int32, (META, both), 0)
    meta = jnp.where(
        meta_row == 0,
        hi,
        jnp.where(
            meta_row == 1,
            mid,
            jnp.where(meta_row == 2, low, jnp.where(meta_row == 3, other.astype(F32), 0.0)),
        ),
    ).astype(BF16)
    span = min(width, LANES)
    near = lax.broadcasted_iota(jnp.int32, (span, both), 0)
    for e in range(experts):
        mine = ((near + e * ROWS == position) & (near < CAP)).astype(F32).astype(BF16)
        block = dot(meta, mine, ((1,), (1,)))
        if width > span:
            block = jnp.concatenate([block, jnp.zeros((META, width - span), F32)], axis=1)
        base = e * ROWS
        send_refs[e][:ROWS] = jnp.concatenate([rows_x[base : base + CAP], block], axis=0).astype(BF16)
        send_refs[e][ROWS:] = rows_d[base : base + CAP].astype(BF16)


def stack_kernel(count, lo, hi, *refs):
    for q in range(count):
        refs[-1][q] = refs[q][lo:hi]


def column(row):
    size = row.shape[1]
    down = lax.broadcasted_iota(jnp.int32, (size, size), 0)
    across = lax.broadcasted_iota(jnp.int32, (size, size), 1)
    return jnp.sum(jnp.where(down == across, row, 0.0), axis=1, keepdims=True)


def visit(groups, hops, width, relative, body):
    core = lax.axis_index("core")
    z = lax.axis_index("z")
    if width % LANES == 0:
        for side in range(2):
            for k in range(hops):
                at = ((z ^ k if relative else k) * 2 + (core ^ side)) * width
                body(side, k, pl.ds(pl.multiple_of(at, LANES), width))
        return
    for here in range(2):

        @pl.when(core == here)
        def _():
            for side in range(2):
                for k in range(hops):
                    at = (k * 2 + (here ^ side)) * width
                    body(side, k, pl.ds(at, width))


def load_kernel(source, out, mark, sem):
    mark[...] = jnp.zeros(mark.shape, F32)
    copy = pltpu.make_async_copy(source, out, sem)
    copy.start()
    copy.wait()


def reader(relative, hops, refs):
    if relative:
        return lambda side, q, k: refs[side * hops + k][q]
    return lambda side, q, k: refs[side][k, q]


def forward_kernel(relative, groups, hops, *refs):
    inputs = 2 * hops if relative else 2
    take = reader(relative, hops, refs[:inputs])
    gate_ref, up_ref, down_ref = refs[inputs : inputs + 3]
    x_ref, hid_ref, active_ref, slope_ref, gates_ref, rival_ref, other_ref, keep_ref, give_ref, total = refs[
        inputs + 3 :
    ]
    width = keep_ref.shape[-1]
    model = x_ref.shape[1]
    units = hid_ref.shape[1]
    tile = min(units, 256)

    def place(side, k, features):
        for q in range(groups):
            x_ref[q * ROWS : (q + 1) * ROWS, features] = take(side, q, k)[:ROWS]

    visit(groups, hops, width, relative, place)
    for q in range(groups):
        logit = jnp.zeros((META, ROWS), F32)
        for k in range(hops):
            for side in range(2):
                meta = take(side, q, k)[:ROWS].astype(F32)[CAP:, :ROWS]
                logit = logit + meta
        gap = column(logit[0:1] + logit[1:2] + logit[2:3])
        here = slice(q * ROWS, (q + 1) * ROWS)
        gates_ref[here, :] = jax.nn.sigmoid(gap)
        rival_ref[here, :] = jax.nn.sigmoid(-gap)
        other_ref[here, :] = column(meta[3:4])

    rows_x = x_ref[...]
    for f in range(0, units, tile):
        now = slice(f, f + tile)
        gate_pre = dot(rows_x, gate_ref[0, :, now], ((1,), (0,)))
        up_pre = dot(rows_x, up_ref[0, :, now], ((1,), (0,)))
        sigma = jax.nn.sigmoid(gate_pre)
        active = gate_pre * sigma
        active_ref[:, now] = active
        slope_ref[:, now] = sigma * (1.0 + gate_pre * (1.0 - sigma)) * up_pre
        hid_ref[:, now] = (active * up_pre).astype(BF16)
    hidden = hid_ref[...]
    for f in range(0, model, 512):
        now = slice(f, f + 512)
        total[:, now] = gates_ref[...] * dot(hidden, down_ref[0, :, now], ((1,), (0,)))

    def emit(side, k, features):
        for q in range(groups):
            rows = total[q * ROWS : (q + 1) * ROWS, features]
            if side == 0:
                keep_ref[k, q] = rows
            else:
                give_ref[k, q] = rows.astype(BF16)

    visit(groups, hops, width, relative, emit)


def backward_kernel(relative, groups, hops, *refs):
    inputs = 2 * hops if relative else 2
    take = reader(relative, hops, refs[:inputs])
    x_ref, active_ref, slope_ref, hid_ref, gates_ref, rival_ref, other_ref, down_ref = refs[inputs : inputs + 8]
    d_ref, dgate_ref, dup_ref, keep_ref, give_ref, scratch = refs[inputs + 8 :]
    experts, width = keep_ref.shape[1:]
    units = hid_ref.shape[1]
    tile = min(units, 256)

    def place(side, k, features):
        for q in range(groups):
            rows = gates_ref[q * ROWS : q * ROWS + CAP, :] * take(side, q, k)[ROWS:].astype(F32)
            rows = jnp.concatenate([rows, jnp.zeros((META, width), F32)], axis=0)
            d_ref[q * ROWS : (q + 1) * ROWS, features] = rows.astype(BF16)

    visit(groups, hops, width, relative, place)
    rows_d = d_ref[...]
    dots = jnp.zeros((rows_d.shape[0], 1), F32)
    for f in range(0, units, tile):
        now = slice(f, f + tile)
        d_hidden = dot(rows_d, down_ref[0, now, :], ((1,), (1,)))
        dgate_ref[:, now] = (d_hidden * slope_ref[:, now]).astype(BF16)
        dup_ref[:, now] = (d_hidden * active_ref[:, now]).astype(BF16)
        dots += jnp.sum(hid_ref[:, now].astype(F32) * d_hidden, axis=1, keepdims=True)
    weight = dots * rival_ref[...]
    lane = lax.broadcasted_iota(jnp.int32, (weight.shape[0], experts), 1)
    signed = jnp.where(lane == lax.axis_index("expert"), weight, 0.0) - jnp.where(
        lane == other_ref[...].astype(jnp.int32), weight, 0.0
    )
    router = jnp.zeros((experts, x_ref.shape[1]), F32)
    for piece in split3(signed):
        router = router + dot(piece.astype(BF16), x_ref[...], ((0,), (0,)))
    scratch[...] = router

    def emit(side, k, features):
        rows = scratch[:, features]
        if side == 0:
            keep_ref[k] = rows
        else:
            give_ref[k] = halves(rows).astype(BF16)

    visit(groups, hops, width, relative, emit)


def halves(rows):
    top = rows.astype(BF16).astype(F32)
    return jnp.concatenate([top, rows - top], axis=0)


def merge_kernel(keep_ref, got_ref, rkeep_ref, rgot_ref, *out_refs):
    experts = rkeep_ref.shape[1]
    hops = keep_ref.shape[0]
    for k in range(hops):
        got = rgot_ref[k].astype(F32)
        router = halves(rkeep_ref[k] + got[:experts] + got[experts:])
        put(out_refs[k], keep_ref[k] + got_ref[k].astype(F32), router)


def pass_kernel(block_ref, _, out_ref):
    out_ref[...] = block_ref[...]


def put(out_ref, blocks, router):
    groups, height, width = out_ref.shape
    spare = height - CAP - router.shape[0]
    for q in range(groups):
        rows = [blocks[q][:CAP], router]
        if spare:
            rows.append(jnp.zeros((spare, width), F32))
        out_ref[q] = jnp.concatenate(rows, axis=0).astype(BF16)


def grads_kernel(x_ref, d_ref, dgate_ref, dup_ref, hid_ref, _, gate_ref, up_ref, down_ref, mark_ref):
    rows_x = x_ref[...]
    first = ((0,), (0,))
    gate_ref[0] = dot(rows_x, dgate_ref[...], first).astype(BF16)
    up_ref[0] = dot(rows_x, dup_ref[...], first).astype(BF16)
    down_ref[0] = dot(hid_ref[...], d_ref[...], first).astype(BF16)
    mark_ref[...] = jnp.zeros(mark_ref.shape, F32)


def add_blocks(experts, parts, sends):
    router = None
    for q, send in enumerate(sends):
        block = parts[0][q].astype(F32)
        for ref in parts[1:]:
            block = block + ref[q].astype(F32)
        if router is None:
            router = halves(block[CAP : CAP + experts] + block[CAP + experts : CAP + 2 * experts])
        height, width = send.shape
        rows = [block[:CAP], router]
        if height > CAP + 2 * experts:
            rows.append(jnp.zeros((height - CAP - 2 * experts, width), F32))
        send[...] = jnp.concatenate(rows, axis=0).astype(BF16)


def sum_kernel(experts, groups, *refs):
    add_blocks(experts, refs[: len(refs) - groups - 1], refs[len(refs) - groups :])


def combine_kernel(groups, pos_ref, *refs):
    backs, mixed_ref, router_ref = refs[:groups], refs[groups], refs[groups + 1]
    experts, width = router_ref.shape
    count = mixed_ref.shape[0]
    blocks = []
    router = jnp.zeros((2 * experts, width), F32)
    for ref in backs:
        block = ref[...].astype(F32)
        router = router + block[CAP : CAP + 2 * experts]
        blocks.append(block[:CAP])
        blocks.append(jnp.zeros((ROWS - CAP, width), F32))
    rows = jnp.concatenate(blocks, axis=0).astype(BF16)
    slots = lax.broadcasted_iota(jnp.int32, (experts * ROWS, 2 * count), 0)
    select = (slots == pos_ref[...]).astype(F32)
    merged = (select[:, :count] + select[:, count:]).astype(BF16)
    mixed_ref[...] = dot(merged, rows, ((0,), (0,))).astype(BF16)
    router_ref[...] = (router[:experts] + router[experts:]).astype(BF16)


def swap(block, axis, bits):
    size = lax.axis_size(axis)
    return lax.ppermute(block, axis, [(i, i ^ bits) for i in range(size)])


def shards(tokens, expert_ids, live_tokens, replicated, w_router, w_gate, w_up, w_down, cotangent):
    groups = lax.axis_size("expert")
    hops = lax.axis_size("z")
    experts = w_router.shape[1]
    count, width = tokens.shape
    _, model, units = w_gate.shape
    rows = groups * ROWS
    height = -(-(CAP + 2 * experts) // 16) * 16
    relative = width % LANES == 0 and hops <= 4
    whole = pl.BlockSpec(memory_space=pltpu.VMEM)
    anywhere = pl.BlockSpec(memory_space=pl.ANY)
    fixed = pl.BlockSpec(memory_space=pltpu.HBM)
    shape = jax.ShapeDtypeStruct

    def call(kernel, args, outs, name, scratch=(), loose=(), cost=None, limit=4 * MIB):
        args = [pltpu.with_memory_space_constraint(a, pltpu.HBM) if i in loose else a for i, a in enumerate(args)]
        return pl.pallas_call(
            kernel,
            out_shape=tuple(outs),
            in_specs=[fixed if i in loose else whole for i in range(len(args))],
            out_specs=(whole,) * len(outs),
            scratch_shapes=list(scratch),
            compiler_params=pltpu.CompilerParams(vmem_limit_bytes=limit),
            cost_estimate=cost,
            name=name,
        )(*args)

    position, *sends = call(
        functools.partial(pack_kernel, experts),
        (live_tokens, replicated, expert_ids.T, w_router.T, tokens, cotangent),
        [shape((1, 2 * count), jnp.int32)] + [shape((ROWS + CAP, width), BF16)] * experts,
        "pack",
        scratch=[
            pltpu.SMEM(live_tokens.shape, jnp.int32),
            pltpu.SMEM(replicated.shape, jnp.int32),
            pltpu.VMEM((2, count), jnp.int32),
            pltpu.VMEM((experts, width), BF16),
            pltpu.VMEM((count, width), BF16),
            pltpu.VMEM((count, width), BF16),
            pltpu.SemaphoreType.DMA((6,)),
        ],
        loose=range(6),
    )
    arrived = [sends[0]] + [swap(sends[q], "expert", q) for q in range(1, groups)]
    def load(weight, name):
        return call(
            load_kernel,
            (weight,),
            [pltpu.VMEM(weight.shape, BF16), shape((8, LANES), F32)],
            name,
            scratch=[pltpu.SemaphoreType.DMA],
            loose=(0,),
            cost=pl.CostEstimate(flops=0, bytes_accessed=2 * 2 * model * units, transcendentals=0),
            limit=8 * MIB,
        )

    gate_w, gate_mark = load(w_gate, "load_gate")
    up_w, up_mark = load(w_up, "load_up")
    down_w, down_mark = load(w_down, "load_down")
    (stacked,) = call(
        functools.partial(stack_kernel, groups, 0, ROWS + CAP),
        (*arrived, gate_mark, up_mark),
        [shape((groups, ROWS + CAP, width), BF16)],
        "stack",
    )
    if relative:
        blocks = [stacked]
        if hops > 2:
            second = swap(stacked, "z", 2)
        if hops > 1:
            blocks.append(swap(stacked, "z", 1))
        if hops > 2:
            (relay,) = call(pass_kernel, (second, down_mark), [shape(second.shape, BF16)], "relay")
            blocks += [second, swap(relay, "z", 1)]
    else:
        blocks = [lax.all_gather(stacked, "z", axis=0, tiled=False)]
    blocks = blocks + [swap(block, "core", 1) for block in blocks]

    cost = 2 * rows * model * units
    rows_x, hidden, active, slope, gates, rival, others, keep, give = call(
        functools.partial(forward_kernel, relative, groups, hops),
        (*blocks, gate_w, up_w, down_w),
        [
            shape((rows, model), BF16),
            shape((rows, units), BF16),
            shape((rows, units), F32),
            shape((rows, units), F32),
            shape((rows, 1), F32),
            shape((rows, 1), F32),
            shape((rows, 1), F32),
            shape((hops, groups, ROWS, width), F32),
            shape((hops, groups, ROWS, width), BF16),
        ],
        "forward",
        scratch=[pltpu.VMEM((rows, model), F32)],
        cost=pl.CostEstimate(flops=3 * cost, bytes_accessed=6 * model * units, transcendentals=rows * units),
        limit=16 * MIB,
    )
    got = swap(give, "core", 1)
    rows_d, d_gate, d_up, router_keep, router_give = call(
        functools.partial(backward_kernel, relative, groups, hops),
        (*blocks, rows_x, active, slope, hidden, gates, rival, others, down_w),
        [
            shape((rows, model), BF16),
            shape((rows, units), BF16),
            shape((rows, units), BF16),
            shape((hops, experts, width), F32),
            shape((hops, 2 * experts, width), BF16),
        ],
        "backward",
        scratch=[pltpu.VMEM((experts, model), F32)],
        cost=pl.CostEstimate(flops=cost, bytes_accessed=2 * model * units, transcendentals=0),
        limit=14 * MIB,
    )
    router_got = swap(router_give, "core", 1)
    merged = call(
        merge_kernel,
        (keep, got, router_keep, router_got),
        [shape((groups, height, width), BF16)] * hops,
        "merge",
    )
    if relative:
        outs = [merged[0]] + [swap(merged[k], "z", k) for k in range(1, hops)]
    else:
        outs = lax.all_to_all(jnp.stack(merged), "z", split_axis=0, concat_axis=0, tiled=True)
        outs = [outs[k] for k in range(hops)]

    parts = 8
    once = lambda *shape: pl.BlockSpec(shape, lambda i: (0,) * len(shape))
    strip = max(units // parts, LANES)
    at = lambda i: i if units >= LANES * parts else 0
    grad_gate, grad_up, grad_down, mark = pl.pallas_call(
        grads_kernel,
        grid=(parts,),
        out_shape=(
            shape(w_gate.shape, BF16),
            shape(w_up.shape, BF16),
            shape(w_down.shape, BF16),
            shape((8, LANES), F32),
        ),
        in_specs=[
            pl.BlockSpec((rows, model // parts), lambda i: (0, i)),
            once(rows, model),
            once(rows, units),
            once(rows, units),
            pl.BlockSpec((rows, strip), lambda i: (0, at(i))),
            anywhere,
        ],
        out_specs=(
            pl.BlockSpec((1, model // parts, units), lambda i: (0, i, 0)),
            pl.BlockSpec((1, model // parts, units), lambda i: (0, i, 0)),
            pl.BlockSpec((1, strip, model), lambda i: (0, at(i), 0)),
            once(8, LANES),
        ),
        compiler_params=pltpu.CompilerParams(vmem_limit_bytes=24 * MIB),
        cost_estimate=pl.CostEstimate(flops=3 * cost, bytes_accessed=6 * model * units, transcendentals=0),
        name="grads",
    )(rows_x, rows_d, d_gate, d_up, hidden, merged[0])

    backs = call(
        functools.partial(sum_kernel, experts, groups),
        (*outs, mark),
        [shape((height, width), BF16)] * groups,
        "total",
    )
    backs = [backs[0]] + [swap(backs[q], "expert", q) for q in range(1, groups)]
    mixed, grad_router = call(
        functools.partial(combine_kernel, groups),
        (position, *backs),
        [shape((count, width), BF16), shape((experts, width), BF16)],
        "combine",
    )
    return (mixed, grad_gate, grad_up, grad_down, grad_router.T)


def solution(mesh):
    groups, etp = mesh.devices.shape
    inner = Mesh(mesh.devices.reshape(groups, etp // 2, 2), ("expert", "z", "core"))
    etp = ("z", "core")
    in_specs = (
        P("expert", etp),
        P("expert", None),
        P(),
        P(),
        P(etp, None),
        P("expert", None, etp),
        P("expert", None, etp),
        P("expert", etp, None),
        P("expert", etp),
    )
    out_specs = (
        P("expert", etp),
        P("expert", None, etp),
        P("expert", None, etp),
        P("expert", etp, None),
        P(etp, None),
    )
    return jax.shard_map(shards, mesh=inner, in_specs=in_specs, out_specs=out_specs, check_vma=False)
```

time: 1380 us -> 70.6 us (0.05)
  waiting for transfers between devices: 799 us -> 22.9 us
  blocking collectives: 463 us -> 0 us
  matrix products: 77.8 us -> 0 us
  Pallas kernels: 0 us -> 27.4 us
    ppermute x6 -> x18, waiting for transfers between devices: 758 us -> 22.9 us  [swap(): return lax.ppermute(block, axis, [(i, i ^ bits) for i in range(size)])]
    all_to_all x2 -> x0, blocking collectives: 405 us -> none  [the longest x1 398 us: shards(): lax.all_to_all(send_x, 'expert', split_axis=0, concat_axis=0, tiled=True)]
    dot_general x19 -> x0, matrix products: 77.8 us -> none  [the longest x2 15.7 us: project_back(): lax.dot_general(rows_x, d_gate, paired, preferred_element_type=jnp.float32)]
    reduce_scatter x1 -> x0, waiting for transfers between devices: 36.7 us -> none  [shards(): lax.psum_scatter(jnp.concatenate([project_out(own_down, near_parts[3]), p...]
    all_gather x2 -> x0, blocking collectives: 33.5 us -> none  [the longest x1 17 us: shards(): lax.all_gather(recv_x, 'etp', axis=2, tiled=True)]
    pallas_call x0 -> x12, Pallas kernels: none -> 27.4 us  [the longest x11 18.5 us: call(): pl.pallas_call(kernel, out_shape=tuple(outs), in_specs=[fixed if i in loo...]
    psum x2 -> x0, blocking collectives: 23.7 us -> none  [the longest x1 13.6 us: shards(): lax.psum(jnp.dot(tokens, w_router, preferred_element_type=jnp.float32), '...]
  transfers between devices with their start and end apart: 8 -> 18, of which waited for: 5 -> 9; matrix products, arithmetic and copies ran while one was open for 5% -> 0% of each run, Pallas kernels for 0% -> 29%
where the time goes in v1:
time: 70.6 us; the launch traced here: 70.2 us
  Pallas kernels  27.4 us (39%)
  waiting for transfers between devices  22.9 us (32%)
  starting transfers between devices  19.2 us (27%)
  between operations  0.75 us (1%)
    ppermute x18, waiting for transfers between devices, swap(): return lax.ppermute(block, axis, [(i, i ^ bits) for i in range(size)])  22.9 us
    ppermute x18, starting transfers between devices, swap(): return lax.ppermute(block, axis, [(i, i ^ bits) for i in range(size)])  19.2 us
    pallas_call x11, Pallas kernels, call(): pl.pallas_call(kernel, out_shape=tuple(outs), in_specs=[fixed if i in loo...  18.5 us
    pallas_call x1, Pallas kernels, shards(): pl.pallas_call(grads_kernel, grid=(parts,), out_shape=(shape(w_gate.shape...  8.84 us
  transfers between devices with their start and end apart: 18, of which 9 were waited for; matrix products, arithmetic and copies ran while one was open for 0% of the time, Pallas kernels for 29%

profile of v1, /device:TPU:0, one launch (start us, length us, event | category | flops | bytes accessed | tf_op | source)
XLA Modules:
  0.0 70.2 jit_solution(5199212541126785468)
XLA Ops:
  0.6 1.6 %pack.1 = (s32[1,256]{1,0:T(1,128)S(1)}, bf16[88,384]{1,0:T(8,128)(2,1)S(1)}, bf16[88,384]{1,0:T(8,128)(2,1)S(1)}, bf16[88,384]{1,0:T(8,128)(2,1)S(1)}, bf16[88,384]{1,0:T(8,128)(2,1)S(1)}) custom-call(s32[4]{0:T(128)} %refs_0_.1, s32[4]{0:T(128)} %refs_1_.1, s32[2,128]{1,0:T(2,128)} %bitcast.4, bf16[4,384]{1,0:T(4,128)(2,1)} %bitcast.3, ...), custom_call_target="tpu_custom_call" | custom-call | tf_op jit(solution)/shard_map/pack/pallas_call | solution.py:342
  2.2 3.0 %collective-permute-start = (bf16[88,384]{1,0:T(8,128)(2,1)S(1)}, bf16[88,384]{1,0:T(8,128)(2,1)S(1)}, u32[]{:S(2)}, u32[]{:S(2)}) collective-permute-start(bf16[88,384]{1,0:T(8,128)(2,1)S(1)} %get-tuple-element.46), channel_id=1, source_target_pairs={{0,8},{8,0},{16,24},{24,16},{1,9},{9,1},{17,25},{25,17},{2,10},{10... | collective-permute-start | bytes 202760 | tf_op jit(solution)/shard_map/ppermute | solution.py:323
  5.2 1.5 %collective-permute-start.1 = (bf16[88,384]{1,0:T(8,128)(2,1)S(1)}, bf16[88,384]{1,0:T(8,128)(2,1)S(1)}, u32[]{:S(2)}, u32[]{:S(2)}) collective-permute-start(bf16[88,384]{1,0:T(8,128)(2,1)S(1)} %get-tuple-element.47), channel_id=1, source_target_pairs={{0,16},{8,24},{16,0},{24,8},{1,17},{9,25},{17,1},{25,9},{2,18},{10... | collective-permute-start | bytes 202760 | tf_op jit(solution)/shard_map/ppermute | solution.py:323
  6.7 0.0 collective-permute-start.2
  6.8 2.8 %load_gate.1 = (bf16[1,3072,1024]{2,1,0:T(8,128)(2,1)S(1)}, f32[8,128]{1,0:T(8,128)S(1)}) custom-call(bf16[1,3072,1024]{2,1,0:T(8,128)(2,1)} %source.3), custom_call_target="tpu_custom_call" | custom-call | bytes 12582912 | tf_op jit(solution)/shard_map/load_gate/pallas_call | solution.py:342
  9.6 2.8 %load_up.1 = (bf16[1,3072,1024]{2,1,0:T(8,128)(2,1)S(1)}, f32[8,128]{1,0:T(8,128)S(1)}) custom-call(bf16[1,3072,1024]{2,1,0:T(8,128)(2,1)} %source.4), custom_call_target="tpu_custom_call" | custom-call | bytes 12582912 | tf_op jit(solution)/shard_map/load_up/pallas_call | solution.py:342
  12.4 0.0 collective-permute-done.refs_1_
  12.4 0.0 collective-permute-done.1.refs_2_
  12.4 0.0 collective-permute-done.2.refs_3_
  12.4 3.1 %collective-permute-start.4 = (bf16[4,88,384]{2,1,0:T(8,128)(2,1)S(1)}, bf16[4,88,384]{2,1,0:T(8,128)(2,1)S(1)}, u32[]{:S(2)}, u32[]{:S(2)}) collective-permute-start(bf16[4,88,384]{2,1,0:T(8,128)(2,1)S(1)} %stack.1.refs_0_), channel_id=1, source_target_pairs={{0,4},{2,6},{4,0},{6,2},{1,5},{3,7},{5,1},{7,3},{8,12},{10,14},{12... | collective-permute-start | bytes 811016 | tf_op jit(solution)/shard_map/ppermute | solution.py:323
  15.6 2.8 %load_down.1 = (bf16[1,1024,3072]{2,1,0:T(8,128)(2,1)S(1)}, f32[8,128]{1,0:T(8,128)S(1)}) custom-call(bf16[1,1024,3072]{2,1,0:T(8,128)(2,1)} %source.5), custom_call_target="tpu_custom_call" | custom-call | bytes 12582912 | tf_op jit(solution)/shard_map/load_down/pallas_call | solution.py:342
  18.4 1.6 %collective-permute-start.3 = (bf16[4,88,384]{2,1,0:T(8,128)(2,1)S(1)}, bf16[4,88,384]{2,1,0:T(8,128)(2,1)S(1)}, u32[]{:S(2)}, u32[]{:S(2)}) collective-permute-start(bf16[4,88,384]{2,1,0:T(8,128)(2,1)S(1)} %stack.1.refs_0_), channel_id=1, source_target_pairs={{0,2},{2,0},{4,6},{6,4},{1,3},{3,1},{5,7},{7,5},{8,10},{10,8},{12,... | collective-permute-start | bytes 811016 | tf_op jit(solution)/shard_map/ppermute | solution.py:323
  20.0 7.1 %collective-permute-done.4.block_ref.refs_2_ = bf16[4,88,384]{2,1,0:T(8,128)(2,1)S(1)} collective-permute-done((bf16[4,88,384]{2,1,0:T(8,128)(2,1)S(1)}, bf16[4,88,384]{2,1,0:T(8,128)(2,1)S(1)}, u32[]{:S(2)}, u32[]{:S(2)}) %collective-permute-start.4) | collective-permute-done | bytes 270368 | tf_op jit(solution)/shard_map/ppermute | solution.py:323
  27.1 0.7 %collective-permute-start.5 = (bf16[4,88,384]{2,1,0:T(8,128)(2,1)S(1)}, bf16[4,88,384]{2,1,0:T(8,128)(2,1)S(1)}, u32[]{:S(2)}, u32[]{:S(2)}) collective-permute-start(bf16[4,88,384]{2,1,0:T(8,128)(2,1)S(1)} %relay.1), channel_id=1, source_target_pairs={{0,2},{2,0},{4,6},{6,4},{1,3},{3,1},{5,7},{7,5},{8,10},{10,8},{12,... | collective-permute-start | bytes 811016 | tf_op jit(solution)/shard_map/ppermute | solution.py:323
  27.8 0.0 collective-permute-start.6
  27.8 0.5 collective-permute-start.8
  28.4 3.2 %collective-permute-done.3.refs_1_ = bf16[4,88,384]{2,1,0:T(8,128)(2,1)S(1)} collective-permute-done((bf16[4,88,384]{2,1,0:T(8,128)(2,1)S(1)}, bf16[4,88,384]{2,1,0:T(8,128)(2,1)S(1)}, u32[]{:S(2)}, u32[]{:S(2)}) %collective-permute-start.3) | collective-permute-done | bytes 270368 | tf_op jit(solution)/shard_map/ppermute | solution.py:323
  31.5 0.0 collective-permute-start.7
  31.5 4.4 %collective-permute-done.5.refs_3_ = bf16[4,88,384]{2,1,0:T(8,128)(2,1)S(1)} collective-permute-done((bf16[4,88,384]{2,1,0:T(8,128)(2,1)S(1)}, bf16[4,88,384]{2,1,0:T(8,128)(2,1)S(1)}, u32[]{:S(2)}, u32[]{:S(2)}) %collective-permute-start.5) | collective-permute-done | bytes 270368 | tf_op jit(solution)/shard_map/ppermute | solution.py:323
  35.9 0.0 collective-permute-start.9
  35.9 0.0 collective-permute-done.6.refs_4_
  35.9 0.0 collective-permute-done.8.refs_6_
  36.0 0.0 collective-permute-done.7.refs_5_
  36.0 1.5 %collective-permute-done.9.refs_7_ = bf16[4,88,384]{2,1,0:T(8,128)(2,1)S(1)} collective-permute-done((bf16[4,88,384]{2,1,0:T(8,128)(2,1)S(1)}, bf16[4,88,384]{2,1,0:T(8,128)(2,1)S(1)}, u32[]{:S(2)}, u32[]{:S(2)}) %collective-permute-start.9) | collective-permute-done | bytes 270368 | tf_op jit(solution)/shard_map/ppermute | solution.py:323
  37.5 4.2 %forward.1 = (bf16[192,3072]{1,0:T(8,128)(2,1)S(1)}, bf16[192,1024]{1,0:T(8,128)(2,1)S(1)}, f32[192,1024]{1,0:T(8,128)S(1)}, f32[192,1024]{1,0:T(8,128)S(1)}, f3...) custom-call(bf16[4,88,384]{2,1,0:T(8,128)(2,1)S(1)} %stack.1.refs_0_, ...), custom_call_target="tpu_custom_call" | custom-call | flops 3623878656 | bytes 18874368 | tf_op jit(solution)/shard_map/forward/pallas_call | solution.py:342
  41.7 0.2 collective-permute-start.10
  41.9 3.3 %backward.1 = (bf16[192,3072]{1,0:T(8,128)(2,1)S(1)}, bf16[192,1024]{1,0:T(8,128)(2,1)S(1)}, bf16[192,1024]{1,0:T(8,128)(2,1)S(1)}, f32[4,4,384]{2,1,0:T(4,128)S(1)}, bf16[4,8,384]{2,1,0:T(8,128)(2,1)S(1)}) custom-call(bf16[4,88,384]{2,1,0:T(8,128)(2,1)S(1)} %stack.1.refs_0_, bf16[4,88,384]{2,1,0:T(8,128)(2,1)S(1)} %collective-permute-done.3.refs_1_, ...), custom_call_target="tpu_custom_call" | custom-call | flops 1207959552 | bytes 6291456 | tf_op jit(solution)/shard_map/backward/pallas_call | solution.py:342
  45.2 0.4 collective-permute-start.11
  45.6 0.8 %collective-permute-done.11.rgot_ref = bf16[4,8,384]{2,1,0:T(8,128)(2,1)S(1)} collective-permute-done((bf16[4,8,384]{2,1,0:T(8,128)(2,1)S(1)}, bf16[4,8,384]{2,1,0:T(8,128)(2,1)S(1)}, u32[]{:S(2)}, u32[]{:S(2)}) %collective-permute-start.11) | collective-permute-done | bytes 24608 | tf_op jit(solution)/shard_map/ppermute | solution.py:323
  46.5 0.0 collective-permute-done.10.got_ref
  46.5 0.1 merge.1
  46.6 0.4 collective-permute-start.12
  47.0 3.4 %collective-permute-start.13 = (bf16[4,48,384]{2,1,0:T(8,128)(2,1)S(1)}, bf16[4,48,384]{2,1,0:T(8,128)(2,1)S(1)}, u32[]{:S(2)}, u32[]{:S(2)}) collective-permute-start(bf16[4,48,384]{2,1,0:T(8,128)(2,1)S(1)} %get-tuple-element.68), channel_id=1, source_target_pairs={{0,4},{2,6},{4,0},{6,2},{1,5},{3,7},{5,1},{7,3},{8,12},{10,14},{12... | collective-permute-start | bytes 442376 | tf_op jit(solution)/shard_map/ppermute | solution.py:323
  50.4 0.7 collective-permute-start.14
  51.1 8.8 %grads.1 = (bf16[1,3072,1024]{2,1,0:T(8,128)(2,1)}, bf16[1,3072,1024]{2,1,0:T(8,128)(2,1)}, bf16[1,1024,3072]{2,1,0:T(8,128)(2,1)}, f32[8,128]{1,0:T(8,128)S(1)}) custom-call(bf16[192,3072]{1,0:T(8,128)(2,1)S(1)} %get-tuple-element.57.refs_8_.x_ref, bf16[192,3072]{1,0:T(8,128)(2,1)S(1)} %get-tuple-element.70.d_ref, ...), custom_call_target="tpu_custom_call" | custom-call | flops 3623878656 | bytes 18874368 | tf_op jit(solution)/shard_map/grads/pallas_call | solution.py:457
  59.9 0.0 collective-permute-done.12.refs_1_
  59.9 1.5 %collective-permute-done.13.refs_2_ = bf16[4,48,384]{2,1,0:T(8,128)(2,1)S(1)} collective-permute-done((bf16[4,48,384]{2,1,0:T(8,128)(2,1)S(1)}, bf16[4,48,384]{2,1,0:T(8,128)(2,1)S(1)}, u32[]{:S(2)}, u32[]{:S(2)}) %collective-permute-start.13) | collective-permute-done | bytes 147488 | tf_op jit(solution)/shard_map/ppermute | solution.py:323
  61.4 0.0 collective-permute-done.14.refs_3_
  61.4 0.1 total.1
  61.4 1.5 %collective-permute-start.15 = (bf16[48,384]{1,0:T(8,128)(2,1)S(1)}, bf16[48,384]{1,0:T(8,128)(2,1)S(1)}, u32[]{:S(2)}, u32[]{:S(2)}) collective-permute-start(bf16[48,384]{1,0:T(8,128)(2,1)S(1)} %get-tuple-element.75), channel_id=1, source_target_pairs={{0,8},{8,0},{16,24},{24,16},{1,9},{9,1},{17,25},{25,17},{2,10},{10... | collective-permute-start | bytes 110600 | tf_op jit(solution)/shard_map/ppermute | solution.py:323
  63.0 1.5 %collective-permute-start.16 = (bf16[48,384]{1,0:T(8,128)(2,1)S(1)}, bf16[48,384]{1,0:T(8,128)(2,1)S(1)}, u32[]{:S(2)}, u32[]{:S(2)}) collective-permute-start(bf16[48,384]{1,0:T(8,128)(2,1)S(1)} %get-tuple-element.76), channel_id=1, source_target_pairs={{0,16},{8,24},{16,0},{24,8},{1,17},{9,25},{17,1},{25,9},{2,18},{10... | collective-permute-start | bytes 110600 | tf_op jit(solution)/shard_map/ppermute | solution.py:323
  64.5 0.5 collective-permute-start.17
  65.0 0.7 %collective-permute-done.15.refs_1_ = bf16[48,384]{1,0:T(8,128)(2,1)S(1)} collective-permute-done((bf16[48,384]{1,0:T(8,128)(2,1)S(1)}, bf16[48,384]{1,0:T(8,128)(2,1)S(1)}, u32[]{:S(2)}, u32[]{:S(2)}) %collective-permute-start.15) | collective-permute-done | bytes 36896 | tf_op jit(solution)/shard_map/ppermute | solution.py:323
  65.7 1.4 %collective-permute-done.16.refs_2_ = bf16[48,384]{1,0:T(8,128)(2,1)S(1)} collective-permute-done((bf16[48,384]{1,0:T(8,128)(2,1)S(1)}, bf16[48,384]{1,0:T(8,128)(2,1)S(1)}, u32[]{:S(2)}, u32[]{:S(2)}) %collective-permute-start.16) | collective-permute-done | bytes 36896 | tf_op jit(solution)/shard_map/ppermute | solution.py:323
  67.1 2.2 %collective-permute-done.17.refs_3_ = bf16[48,384]{1,0:T(8,128)(2,1)S(1)} collective-permute-done((bf16[48,384]{1,0:T(8,128)(2,1)S(1)}, bf16[48,384]{1,0:T(8,128)(2,1)S(1)}, u32[]{:S(2)}, u32[]{:S(2)}) %collective-permute-start.17) | collective-permute-done | bytes 36896 | tf_op jit(solution)/shard_map/ppermute | solution.py:323
  69.4 0.9 %combine.1 = (bf16[128,384]{1,0:T(8,128)(2,1)}, bf16[4,384]{1,0:T(4,128)(2,1)}) custom-call(s32[1,256]{1,0:T(1,128)S(1)} %get-tuple-element.44.pos_ref, bf16[48,384]{1,0:T(8,128)(2,1)S(1)} %get-tuple-element.74.refs_0_, bf16[48,384]{1,0:T(8,128)(2,1)S(1)} %collective-permute-done.15.refs_1_, bf16[48,384]{1,0:T(8,128)(2,1)S(1)} %collective-permute-done.16.refs_2_, ...), custom_call_target="tpu_custom_call" | custom-call | tf_op jit(solution)/shard_map/combine/pallas_call | solution.py:342
  (2 shorter events, 0.1 us)
Async XLA Ops:
  2.2 10.2 %collective-permute-start = (bf16[88,384]{1,0:T(8,128)(2,1)S(1)}, bf16[88,384]{1,0:T(8,128)(2,1)S(1)}, u32[]{:S(2)}, u32[]{:S(2)}) collective-permute-start(bf16[88,384]{1,0:T(8,128)(2,1)S(1)} %get-tuple-element.46), channel_id=1, source_target_pairs={{0,8},{8,0},{16,24},{24,16},{1,9},{9,1},{17,25},{25,17},{2,10},{10... | collective-permute-start | bytes 202760 | tf_op jit(solution)/shard_map/ppermute | solution.py:323
  5.2 7.2 %collective-permute-start.1 = (bf16[88,384]{1,0:T(8,128)(2,1)S(1)}, bf16[88,384]{1,0:T(8,128)(2,1)S(1)}, u32[]{:S(2)}, u32[]{:S(2)}) collective-permute-start(bf16[88,384]{1,0:T(8,128)(2,1)S(1)} %get-tuple-element.47), channel_id=1, source_target_pairs={{0,16},{8,24},{16,0},{24,8},{1,17},{9,25},{17,1},{25,9},{2,18},{10... | collective-permute-start | bytes 202760 | tf_op jit(solution)/shard_map/ppermute | solution.py:323
  6.7 5.6 %collective-permute-start.2 = (bf16[88,384]{1,0:T(8,128)(2,1)S(1)}, bf16[88,384]{1,0:T(8,128)(2,1)S(1)}, u32[]{:S(2)}, u32[]{:S(2)}) collective-permute-start(bf16[88,384]{1,0:T(8,128)(2,1)S(1)} %get-tuple-element.48), channel_id=1, source_target_pairs={{0,24},{8,16},{16,8},{24,0},{1,25},{9,17},{17,9},{25,1},{2,26},{10... | collective-permute-start | bytes 202760 | tf_op jit(solution)/shard_map/ppermute | solution.py:323
  12.4 14.7 %collective-permute-start.4 = (bf16[4,88,384]{2,1,0:T(8,128)(2,1)S(1)}, bf16[4,88,384]{2,1,0:T(8,128)(2,1)S(1)}, u32[]{:S(2)}, u32[]{:S(2)}) collective-permute-start(bf16[4,88,384]{2,1,0:T(8,128)(2,1)S(1)} %stack.1.refs_0_), channel_id=1, source_target_pairs={{0,4},{2,6},{4,0},{6,2},{1,5},{3,7},{5,1},{7,3},{8,12},{10,14},{12... | collective-permute-start | bytes 811016 | tf_op jit(solution)/shard_map/ppermute | solution.py:323
  18.4 13.2 %collective-permute-start.3 = (bf16[4,88,384]{2,1,0:T(8,128)(2,1)S(1)}, bf16[4,88,384]{2,1,0:T(8,128)(2,1)S(1)}, u32[]{:S(2)}, u32[]{:S(2)}) collective-permute-start(bf16[4,88,384]{2,1,0:T(8,128)(2,1)S(1)} %stack.1.refs_0_), channel_id=1, source_target_pairs={{0,2},{2,0},{4,6},{6,4},{1,3},{3,1},{5,7},{7,5},{8,10},{10,8},{12,... | collective-permute-start | bytes 811016 | tf_op jit(solution)/shard_map/ppermute | solution.py:323
  27.1 8.8 %collective-permute-start.5 = (bf16[4,88,384]{2,1,0:T(8,128)(2,1)S(1)}, bf16[4,88,384]{2,1,0:T(8,128)(2,1)S(1)}, u32[]{:S(2)}, u32[]{:S(2)}) collective-permute-start(bf16[4,88,384]{2,1,0:T(8,128)(2,1)S(1)} %relay.1), channel_id=1, source_target_pairs={{0,2},{2,0},{4,6},{6,4},{1,3},{3,1},{5,7},{7,5},{8,10},{10,8},{12,... | collective-permute-start | bytes 811016 | tf_op jit(solution)/shard_map/ppermute | solution.py:323
  27.8 8.1 %collective-permute-start.6 = (bf16[4,88,384]{2,1,0:T(8,128)(2,1)S(1)}, bf16[4,88,384]{2,1,0:T(8,128)(2,1)S(1)}, u32[]{:S(2)}, u32[]{:S(2)}) collective-permute-start(bf16[4,88,384]{2,1,0:T(8,128)(2,1)S(1)} %stack.1.refs_0_), channel_id=1, source_target_pairs={{0,1},{1,0},{2,3},{3,2},{4,5},{5,4},{6,7},{7,6},{8,9},{9,8},{10,11... | collective-permute-start | bytes 811016 | tf_op jit(solution)/shard_map/ppermute | solution.py:323
  27.8 8.1 %collective-permute-start.8 = (bf16[4,88,384]{2,1,0:T(8,128)(2,1)S(1)}, bf16[4,88,384]{2,1,0:T(8,128)(2,1)S(1)}, u32[]{:S(2)}, u32[]{:S(2)}) collective-permute-start(bf16[4,88,384]{2,1,0:T(8,128)(2,1)S(1)} %collective-permute-done.4.block_ref.refs_2_), channel_id=1, source_target_pairs={{0,1},{1,0},{2,3},{3,2},{4,5},{5,4},{6,7},{7,6},{8,9},{9,8},{10,11... | collective-permute-start | bytes 811016 | tf_op jit(solution)/shard_map/ppermute | solution.py:323
  31.5 4.4 %collective-permute-start.7 = (bf16[4,88,384]{2,1,0:T(8,128)(2,1)S(1)}, bf16[4,88,384]{2,1,0:T(8,128)(2,1)S(1)}, u32[]{:S(2)}, u32[]{:S(2)}) collective-permute-start(bf16[4,88,384]{2,1,0:T(8,128)(2,1)S(1)} %collective-permute-done.3.refs_1_), channel_id=1, source_target_pairs={{0,1},{1,0},{2,3},{3,2},{4,5},{5,4},{6,7},{7,6},{8,9},{9,8},{10,11... | collective-permute-start | bytes 811016 | tf_op jit(solution)/shard_map/ppermute | solution.py:323
  35.9 1.5 %collective-permute-start.9 = (bf16[4,88,384]{2,1,0:T(8,128)(2,1)S(1)}, bf16[4,88,384]{2,1,0:T(8,128)(2,1)S(1)}, u32[]{:S(2)}, u32[]{:S(2)}) collective-permute-start(bf16[4,88,384]{2,1,0:T(8,128)(2,1)S(1)} %collective-permute-done.5.refs_3_), channel_id=1, source_target_pairs={{0,1},{1,0},{2,3},{3,2},{4,5},{5,4},{6,7},{7,6},{8,9},{9,8},{10,11... | collective-permute-start | bytes 811016 | tf_op jit(solution)/shard_map/ppermute | solution.py:323
  41.7 4.8 %collective-permute-start.10 = (bf16[4,4,48,384]{3,2,1,0:T(8,128)(2,1)S(1)}, bf16[4,4,48,384]{3,2,1,0:T(8,128)(2,1)S(1)}, u32[]{:S(2)}, u32[]{:S(2)}) collective-permute-start(bf16[4,4,48,384]{3,2,1,0:T(8,128)(2,1)S(1)} %get-tuple-element.56), channel_id=1, source_target_pairs={{0,1},{1,0},{2,3},{3,2},{4,5},{5,4},{6,7},{7,6},{8,9},{9,8},{10,11... | collective-permute-start | bytes 1769480 | tf_op jit(solution)/shard_map/ppermute | solution.py:323
  45.2 1.3 %collective-permute-start.11 = (bf16[4,8,384]{2,1,0:T(8,128)(2,1)S(1)}, bf16[4,8,384]{2,1,0:T(8,128)(2,1)S(1)}, u32[]{:S(2)}, u32[]{:S(2)}) collective-permute-start(bf16[4,8,384]{2,1,0:T(8,128)(2,1)S(1)} %get-tuple-element.65), channel_id=1, source_target_pairs={{0,1},{1,0},{2,3},{3,2},{4,5},{5,4},{6,7},{7,6},{8,9},{9,8},{10,11... | collective-permute-start | bytes 73736 | tf_op jit(solution)/shard_map/ppermute | solution.py:323
  46.6 13.3 %collective-permute-start.12 = (bf16[4,48,384]{2,1,0:T(8,128)(2,1)S(1)}, bf16[4,48,384]{2,1,0:T(8,128)(2,1)S(1)}, u32[]{:S(2)}, u32[]{:S(2)}) collective-permute-start(bf16[4,48,384]{2,1,0:T(8,128)(2,1)S(1)} %get-tuple-element.67), channel_id=1, source_target_pairs={{0,2},{2,0},{4,6},{6,4},{1,3},{3,1},{5,7},{7,5},{8,10},{10,8},{12,... | collective-permute-start | bytes 442376 | tf_op jit(solution)/shard_map/ppermute | solution.py:323
  47.0 14.4 %collective-permute-start.13 = (bf16[4,48,384]{2,1,0:T(8,128)(2,1)S(1)}, bf16[4,48,384]{2,1,0:T(8,128)(2,1)S(1)}, u32[]{:S(2)}, u32[]{:S(2)}) collective-permute-start(bf16[4,48,384]{2,1,0:T(8,128)(2,1)S(1)} %get-tuple-element.68), channel_id=1, source_target_pairs={{0,4},{2,6},{4,0},{6,2},{1,5},{3,7},{5,1},{7,3},{8,12},{10,14},{12... | collective-permute-start | bytes 442376 | tf_op jit(solution)/shard_map/ppermute | solution.py:323
  50.4 11.0 %collective-permute-start.14 = (bf16[4,48,384]{2,1,0:T(8,128)(2,1)S(1)}, bf16[4,48,384]{2,1,0:T(8,128)(2,1)S(1)}, u32[]{:S(2)}, u32[]{:S(2)}) collective-permute-start(bf16[4,48,384]{2,1,0:T(8,128)(2,1)S(1)} %get-tuple-element.69), channel_id=1, source_target_pairs={{0,6},{2,4},{4,2},{6,0},{1,7},{3,5},{5,3},{7,1},{8,14},{10,12},{12... | collective-permute-start | bytes 442376 | tf_op jit(solution)/shard_map/ppermute | solution.py:323
  61.4 4.3 %collective-permute-start.15 = (bf16[48,384]{1,0:T(8,128)(2,1)S(1)}, bf16[48,384]{1,0:T(8,128)(2,1)S(1)}, u32[]{:S(2)}, u32[]{:S(2)}) collective-permute-start(bf16[48,384]{1,0:T(8,128)(2,1)S(1)} %get-tuple-element.75), channel_id=1, source_target_pairs={{0,8},{8,0},{16,24},{24,16},{1,9},{9,1},{17,25},{25,17},{2,10},{10... | collective-permute-start | bytes 110600 | tf_op jit(solution)/shard_map/ppermute | solution.py:323
  63.0 4.2 %collective-permute-start.16 = (bf16[48,384]{1,0:T(8,128)(2,1)S(1)}, bf16[48,384]{1,0:T(8,128)(2,1)S(1)}, u32[]{:S(2)}, u32[]{:S(2)}) collective-permute-start(bf16[48,384]{1,0:T(8,128)(2,1)S(1)} %get-tuple-element.76), channel_id=1, source_target_pairs={{0,16},{8,24},{16,0},{24,8},{1,17},{9,25},{17,1},{25,9},{2,18},{10... | collective-permute-start | bytes 110600 | tf_op jit(solution)/shard_map/ppermute | solution.py:323
  64.5 4.9 %collective-permute-start.17 = (bf16[48,384]{1,0:T(8,128)(2,1)S(1)}, bf16[48,384]{1,0:T(8,128)(2,1)S(1)}, u32[]{:S(2)}, u32[]{:S(2)}) collective-permute-start(bf16[48,384]{1,0:T(8,128)(2,1)S(1)} %get-tuple-element.77), channel_id=1, source_target_pairs={{0,24},{8,16},{16,8},{24,0},{1,25},{9,17},{17,9},{25,1},{2,26},{10... | collective-permute-start | bytes 110600 | tf_op jit(solution)/shard_map/ppermute | solution.py:323

commit v2 on v1

--- a/solution.py
+++ b/solution.py
@@ -30,15 +30,22 @@
     return hi, mid, rest - mid
 
 
+def chosen(position, experts):
+    count = position.shape[1] // 2
+    slots = lax.broadcasted_iota(jnp.int32, (experts * ROWS, 2 * count), 0)
+    select = (slots == position).astype(F32)
+    return (select[:, :count] + select[:, count:]).astype(BF16)
+
+
 def pack_kernel(experts, *refs):
-    sources, pos_ref, send_refs = refs[:6], refs[6], refs[7 : 7 + experts]
-    held, sems = refs[7 + experts : 13 + experts], refs[13 + experts]
+    sources, pos_ref, pass_ref, send_refs = refs[:6], refs[6], refs[7], refs[8 : 8 + experts]
+    held, sems = [*refs[8 + experts : 13 + experts], pass_ref], refs[13 + experts]
     copies = [pltpu.make_async_copy(a, b, sems.at[i]) for i, (a, b) in enumerate(zip(sources, held))]
     for copy in copies:
         copy.start()
     for copy in copies:
         copy.wait()
-    live_ref, flags_ref, ids_ref, router_ref, tok_ref, cot_ref = held
+    live_ref, flags_ref, ids_ref, router_ref, tok_ref, _ = held
     count, width = tok_ref.shape
     both = 2 * count
     lanes = max(experts, 8)
@@ -64,11 +71,8 @@
     position = jnp.where(kept, (order ^ group) * ROWS + slot, -1)
     pos_ref[...] = position
 
-    slots = lax.broadcasted_iota(jnp.int32, (experts * ROWS, both), 0)
-    select = (slots == position).astype(F32)
-    merged = (select[:, :count] + select[:, count:]).astype(BF16)
+    merged = chosen(position, experts)
     rows_x = dot(merged, tok_ref[...], ((1,), (0,)))
-    rows_d = dot(merged, cot_ref[...], ((1,), (0,)))
 
     logits = dot(router_ref[...], tok_ref[...], ((1,), (1,)))
     pick = lax.broadcasted_iota(jnp.int32, (experts, count), 0)
@@ -96,13 +100,21 @@
         if width > span:
             block = jnp.concatenate([block, jnp.zeros((META, width - span), F32)], axis=1)
         base = e * ROWS
-        send_refs[e][:ROWS] = jnp.concatenate([rows_x[base : base + CAP], block], axis=0).astype(BF16)
-        send_refs[e][ROWS:] = rows_d[base : base + CAP].astype(BF16)
-
-
-def stack_kernel(count, lo, hi, *refs):
+        send_refs[e][...] = jnp.concatenate([rows_x[base : base + CAP], block], axis=0).astype(BF16)
+
+
+def stack_kernel(count, *refs):
     for q in range(count):
-        refs[-1][q] = refs[q][lo:hi]
+        refs[-1][q] = refs[q][...]
+
+
+def pick_kernel(relative, experts, hops, pos_ref, *refs):
+    sources, sends = refs[: len(refs) - experts], refs[len(refs) - experts :]
+    merged = chosen(pos_ref[...], experts)
+    for k in range(hops):
+        rows = dot(merged, sources[k][...] if relative else sources[0][k], ((1,), (0,)))
+        for q in range(experts):
+            sends[q][k] = rows[q * ROWS : q * ROWS + CAP].astype(BF16)
 
 
 def column(row):
@@ -147,10 +159,13 @@
 def forward_kernel(relative, groups, hops, *refs):
     inputs = 2 * hops if relative else 2
     take = reader(relative, hops, refs[:inputs])
-    gate_ref, up_ref, down_ref = refs[inputs : inputs + 3]
-    x_ref, hid_ref, active_ref, slope_ref, gates_ref, rival_ref, other_ref, keep_ref, give_ref, total = refs[
-        inputs + 3 :
+    gate_ref, up_ref, _, down_hbm = refs[inputs : inputs + 4]
+    x_ref, hid_ref, active_ref, slope_ref, gates_ref, rival_ref, other_ref, keep_ref, give_ref, down_ref = refs[
+        inputs + 4 : inputs + 14
     ]
+    total, sem = refs[inputs + 14 :]
+    fetch = pltpu.make_async_copy(down_hbm, down_ref, sem)
+    fetch.start()
     width = keep_ref.shape[-1]
     model = x_ref.shape[1]
     units = hid_ref.shape[1]
@@ -158,14 +173,14 @@
 
     def place(side, k, features):
         for q in range(groups):
-            x_ref[q * ROWS : (q + 1) * ROWS, features] = take(side, q, k)[:ROWS]
+            x_ref[q * ROWS : (q + 1) * ROWS, features] = take(side, q, k)
 
     visit(groups, hops, width, relative, place)
     for q in range(groups):
         logit = jnp.zeros((META, ROWS), F32)
         for k in range(hops):
             for side in range(2):
-                meta = take(side, q, k)[:ROWS].astype(F32)[CAP:, :ROWS]
+                meta = take(side, q, k).astype(F32)[CAP:, :ROWS]
                 logit = logit + meta
         gap = column(logit[0:1] + logit[1:2] + logit[2:3])
         here = slice(q * ROWS, (q + 1) * ROWS)
@@ -184,6 +199,7 @@
         slope_ref[:, now] = sigma * (1.0 + gate_pre * (1.0 - sigma)) * up_pre
         hid_ref[:, now] = (active * up_pre).astype(BF16)
     hidden = hid_ref[...]
+    fetch.wait()
     for f in range(0, model, 512):
         now = slice(f, f + 512)
         total[:, now] = gates_ref[...] * dot(hidden, down_ref[0, :, now], ((1,), (0,)))
@@ -200,8 +216,7 @@
 
 
 def backward_kernel(relative, groups, hops, *refs):
-    inputs = 2 * hops if relative else 2
-    take = reader(relative, hops, refs[:inputs])
+    inputs = 2
     x_ref, active_ref, slope_ref, hid_ref, gates_ref, rival_ref, other_ref, down_ref = refs[inputs : inputs + 8]
     d_ref, dgate_ref, dup_ref, keep_ref, give_ref, scratch = refs[inputs + 8 :]
     experts, width = keep_ref.shape[1:]
@@ -210,7 +225,7 @@
 
     def place(side, k, features):
         for q in range(groups):
-            rows = gates_ref[q * ROWS : q * ROWS + CAP, :] * take(side, q, k)[ROWS:].astype(F32)
+            rows = gates_ref[q * ROWS : q * ROWS + CAP, :] * refs[side][q, k].astype(F32)
             rows = jnp.concatenate([rows, jnp.zeros((META, width), F32)], axis=0)
             d_ref[q * ROWS : (q + 1) * ROWS, features] = rows.astype(BF16)
 
@@ -257,8 +272,8 @@
         put(out_refs[k], keep_ref[k] + got_ref[k].astype(F32), router)
 
 
-def pass_kernel(block_ref, _, out_ref):
-    out_ref[...] = block_ref[...]
+def pass_kernel(block_ref, *refs):
+    refs[-1][...] = block_ref[...]
 
 
 def put(out_ref, blocks, router):
@@ -302,7 +317,6 @@
 def combine_kernel(groups, pos_ref, *refs):
     backs, mixed_ref, router_ref = refs[:groups], refs[groups], refs[groups + 1]
     experts, width = router_ref.shape
-    count = mixed_ref.shape[0]
     blocks = []
     router = jnp.zeros((2 * experts, width), F32)
     for ref in backs:
@@ -311,9 +325,7 @@
         blocks.append(block[:CAP])
         blocks.append(jnp.zeros((ROWS - CAP, width), F32))
     rows = jnp.concatenate(blocks, axis=0).astype(BF16)
-    slots = lax.broadcasted_iota(jnp.int32, (experts * ROWS, 2 * count), 0)
-    select = (slots == pos_ref[...]).astype(F32)
-    merged = (select[:, :count] + select[:, count:]).astype(BF16)
+    merged = chosen(pos_ref[...], experts)
     mixed_ref[...] = dot(merged, rows, ((0,), (0,))).astype(BF16)
     router_ref[...] = (router[:experts] + router[experts:]).astype(BF16)
 
@@ -350,10 +362,10 @@
             name=name,
         )(*args)
 
-    position, *sends = call(
+    position, handed, *sends = call(
         functools.partial(pack_kernel, experts),
         (live_tokens, replicated, expert_ids.T, w_router.T, tokens, cotangent),
-        [shape((1, 2 * count), jnp.int32)] + [shape((ROWS + CAP, width), BF16)] * experts,
+        [shape((1, 2 * count), jnp.int32), shape(cotangent.shape, BF16)] + [shape((ROWS, width), BF16)] * experts,
         "pack",
         scratch=[
             pltpu.SMEM(live_tokens.shape, jnp.int32),
@@ -361,12 +373,10 @@
             pltpu.VMEM((2, count), jnp.int32),
             pltpu.VMEM((experts, width), BF16),
             pltpu.VMEM((count, width), BF16),
-            pltpu.VMEM((count, width), BF16),
             pltpu.SemaphoreType.DMA((6,)),
         ],
         loose=range(6),
     )
-    arrived = [sends[0]] + [swap(sends[q], "expert", q) for q in range(1, groups)]
     def load(weight, name):
         return call(
             load_kernel,
@@ -381,30 +391,44 @@
 
     gate_w, gate_mark = load(w_gate, "load_gate")
     up_w, up_mark = load(w_up, "load_up")
-    down_w, down_mark = load(w_down, "load_down")
+    def gather(block, forward):
+        if not relative:
+            return [lax.all_gather(block, "z", axis=0, tiled=False)]
+        blocks = [block]
+        if hops > 2:
+            second = swap(block, "z", 2)
+        if hops > 1:
+            blocks.append(swap(block, "z", 1))
+        if hops > 2:
+            blocks += [second, swap(forward(second, blocks[1]), "z", 1)]
+        return blocks
+
+    arrived = [sends[0]] + [swap(sends[q], "expert", q) for q in range(1, groups)]
+    slices = gather(handed, lambda second, near: second)
+    picked = call(
+        functools.partial(pick_kernel, relative, experts, hops),
+        (position, *slices),
+        [shape((hops, CAP, width), BF16)] * experts,
+        "pick",
+    )
     (stacked,) = call(
-        functools.partial(stack_kernel, groups, 0, ROWS + CAP),
+        functools.partial(stack_kernel, groups),
         (*arrived, gate_mark, up_mark),
-        [shape((groups, ROWS + CAP, width), BF16)],
+        [shape((groups, ROWS, width), BF16)],
         "stack",
     )
-    if relative:
-        blocks = [stacked]
-        if hops > 2:
-            second = swap(stacked, "z", 2)
-        if hops > 1:
-            blocks.append(swap(stacked, "z", 1))
-        if hops > 2:
-            (relay,) = call(pass_kernel, (second, down_mark), [shape(second.shape, BF16)], "relay")
-            blocks += [second, swap(relay, "z", 1)]
-    else:
-        blocks = [lax.all_gather(stacked, "z", axis=0, tiled=False)]
+
+    def relay(second, near):
+        return call(pass_kernel, (second, near), [shape(second.shape, BF16)], "relay")[0]
+
+    blocks = gather(stacked, relay)
     blocks = blocks + [swap(block, "core", 1) for block in blocks]
+    blocks_d = [picked[0]] + [swap(picked[q], "expert", q) for q in range(1, groups)]
 
     cost = 2 * rows * model * units
-    rows_x, hidden, active, slope, gates, rival, others, keep, give = call(
+    rows_x, hidden, active, slope, gates, rival, others, keep, give, down_w = call(
         functools.partial(forward_kernel, relative, groups, hops),
-        (*blocks, gate_w, up_w, down_w),
+        (*blocks, gate_w, up_w, blocks_d[1 if groups > 1 else 0], w_down),
         [
             shape((rows, model), BF16),
             shape((rows, units), BF16),
@@ -415,16 +439,25 @@
             shape((rows, 1), F32),
             shape((hops, groups, ROWS, width), F32),
             shape((hops, groups, ROWS, width), BF16),
+            pltpu.VMEM(w_down.shape, BF16),
         ],
         "forward",
-        scratch=[pltpu.VMEM((rows, model), F32)],
+        scratch=[pltpu.VMEM((rows, model), F32), pltpu.SemaphoreType.DMA],
+        loose=(len(blocks) + 3,),
         cost=pl.CostEstimate(flops=3 * cost, bytes_accessed=6 * model * units, transcendentals=rows * units),
         limit=16 * MIB,
     )
     got = swap(give, "core", 1)
+    (own_d,) = call(
+        functools.partial(stack_kernel, groups),
+        (*blocks_d, gates),
+        [shape((groups, hops, CAP, width), BF16)],
+        "stack_d",
+    )
+    far_d = swap(own_d, "core", 1)
     rows_d, d_gate, d_up, router_keep, router_give = call(
         functools.partial(backward_kernel, relative, groups, hops),
-        (*blocks, rows_x, active, slope, hidden, gates, rival, others, down_w),
+        (own_d, far_d, rows_x, active, slope, hidden, gates, rival, others, down_w),
         [
             shape((rows, model), BF16),
             shape((rows, units), BF16),

time: 70.6 us -> 77 us (1.091)
  starting transfers between devices: 19.2 us -> 28.9 us
  waiting for transfers between devices: 22.9 us -> 19.4 us
    ppermute x18 -> x25, starting transfers between devices: 19.2 us -> 28.9 us  [swap(): return lax.ppermute(block, axis, [(i, i ^ bits) for i in range(size)])]
    ppermute x18 -> x25, waiting for transfers between devices: 22.9 us -> 19.4 us  [swap(): return lax.ppermute(block, axis, [(i, i ^ bits) for i in range(size)])]
    pallas_call x11 -> x12, Pallas kernels: 18.5 us -> 18.9 us  [call(): pl.pallas_call(kernel, out_shape=tuple(outs), in_specs=[fixed if i in loo...]
  transfers between devices with their start and end apart: 18 -> 25, of which waited for: 9 -> 11; matrix products, arithmetic and copies ran while one was open for 0% -> 0% of each run, Pallas kernels for 29% -> 33%
where the time goes in v2:
time: 77 us; the launch traced here: 76.7 us
  starting transfers between devices  28.9 us (38%)
  Pallas kernels  27.7 us (36%)
  waiting for transfers between devices  19.4 us (25%)
  between operations  0.78 us (1%)
    ppermute x25, starting transfers between devices, swap(): return lax.ppermute(block, axis, [(i, i ^ bits) for i in range(size)])  28.9 us
    ppermute x25, waiting for transfers between devices, swap(): return lax.ppermute(block, axis, [(i, i ^ bits) for i in range(size)])  19.4 us
    pallas_call x12, Pallas kernels, call(): pl.pallas_call(kernel, out_shape=tuple(outs), in_specs=[fixed if i in loo...  18.9 us
    pallas_call x1, Pallas kernels, shards(): pl.pallas_call(grads_kernel, grid=(parts,), out_shape=(shape(w_gate.shape...  8.85 us
  transfers between devices with their start and end apart: 25, of which 11 were waited for; matrix products, arithmetic and copies ran while one was open for 0% of the time, Pallas kernels for 33%

profile of v2, /device:TPU:0, one launch (start us, length us, event | category | flops | bytes accessed | tf_op | source)
XLA Modules:
  0.0 76.7 jit_solution(1990821743786259559)
XLA Ops:
  0.6 1.6 %pack.1 = (s32[1,256]{1,0:T(1,128)S(1)}, bf16[128,384]{1,0:T(8,128)(2,1)S(1)}, bf16[48,384]{1,0:T(8,128)(2,1)S(1)}, bf16[48,384]{1,0:T(8,128)(2,1)S(1)}, bf16[48...) custom-call(s32[4]{0:T(128)} %refs_0_.1, s32[4]{0:T(128)} %refs_1_.1, s32[2,128]{1,0:T(2,128)} %bitcast.4, ...), custom_call_target="tpu_custom_call" | custom-call | tf_op jit(solution)/shard_map/pack/pallas_call | solution.py:354
  2.2 3.0 %collective-permute-start = (bf16[48,384]{1,0:T(8,128)(2,1)S(1)}, bf16[48,384]{1,0:T(8,128)(2,1)S(1)}, u32[]{:S(2)}, u32[]{:S(2)}) collective-permute-start(bf16[48,384]{1,0:T(8,128)(2,1)S(1)} %get-tuple-element.50), channel_id=1, source_target_pairs={{0,8},{8,0},{16,24},{24,16},{1,9},{9,1},{17,25},{25,17},{2,10},{10... | collective-permute-start | bytes 110600 | tf_op jit(solution)/shard_map/ppermute | solution.py:335
  5.2 1.5 %collective-permute-start.1 = (bf16[48,384]{1,0:T(8,128)(2,1)S(1)}, bf16[48,384]{1,0:T(8,128)(2,1)S(1)}, u32[]{:S(2)}, u32[]{:S(2)}) collective-permute-start(bf16[48,384]{1,0:T(8,128)(2,1)S(1)} %get-tuple-element.51), channel_id=1, source_target_pairs={{0,16},{8,24},{16,0},{24,8},{1,17},{9,25},{17,1},{25,9},{2,18},{10... | collective-permute-start | bytes 110600 | tf_op jit(solution)/shard_map/ppermute | solution.py:335
  6.7 0.0 collective-permute-start.2
  6.8 2.8 %load_gate.1 = (bf16[1,3072,1024]{2,1,0:T(8,128)(2,1)S(1)}, f32[8,128]{1,0:T(8,128)S(1)}) custom-call(bf16[1,3072,1024]{2,1,0:T(8,128)(2,1)} %source.2), custom_call_target="tpu_custom_call" | custom-call | bytes 12582912 | tf_op jit(solution)/shard_map/load_gate/pallas_call | solution.py:354
  9.6 2.8 %load_up.1 = (bf16[1,3072,1024]{2,1,0:T(8,128)(2,1)S(1)}, f32[8,128]{1,0:T(8,128)S(1)}) custom-call(bf16[1,3072,1024]{2,1,0:T(8,128)(2,1)} %source.3), custom_call_target="tpu_custom_call" | custom-call | bytes 12582912 | tf_op jit(solution)/shard_map/load_up/pallas_call | solution.py:354
  12.4 0.0 collective-permute-done.refs_1_
  12.4 0.0 collective-permute-done.1.refs_2_
  12.4 0.0 collective-permute-done.2.refs_3_
  12.4 3.1 %collective-permute-start.4 = (bf16[4,48,384]{2,1,0:T(8,128)(2,1)S(1)}, bf16[4,48,384]{2,1,0:T(8,128)(2,1)S(1)}, u32[]{:S(2)}, u32[]{:S(2)}) collective-permute-start(bf16[4,48,384]{2,1,0:T(8,128)(2,1)S(1)} %stack.1.refs_0_), channel_id=1, source_target_pairs={{0,4},{2,6},{4,0},{6,2},{1,5},{3,7},{5,1},{7,3},{8,12},{10,14},{12... | collective-permute-start | bytes 442376 | tf_op jit(solution)/shard_map/ppermute | solution.py:335
  15.5 1.6 %collective-permute-start.3 = (bf16[4,48,384]{2,1,0:T(8,128)(2,1)S(1)}, bf16[4,48,384]{2,1,0:T(8,128)(2,1)S(1)}, u32[]{:S(2)}, u32[]{:S(2)}) collective-permute-start(bf16[4,48,384]{2,1,0:T(8,128)(2,1)S(1)} %stack.1.refs_0_), channel_id=1, source_target_pairs={{0,2},{2,0},{4,6},{6,4},{1,3},{3,1},{5,7},{7,5},{8,10},{10,8},{12,... | collective-permute-start | bytes 442376 | tf_op jit(solution)/shard_map/ppermute | solution.py:335
  17.1 0.3 collective-permute-start.11
  17.4 6.4 %collective-permute-done.4.block_ref.refs_2_ = bf16[4,48,384]{2,1,0:T(8,128)(2,1)S(1)} collective-permute-done((bf16[4,48,384]{2,1,0:T(8,128)(2,1)S(1)}, bf16[4,48,384]{2,1,0:T(8,128)(2,1)S(1)}, u32[]{:S(2)}, u32[]{:S(2)}) %collective-permute-start.4) | collective-permute-done | bytes 147488 | tf_op jit(solution)/shard_map/ppermute | solution.py:335
  23.8 0.0 collective-permute-done.3.refs_0_.refs_1_
  23.8 1.2 %collective-permute-start.5 = (bf16[4,48,384]{2,1,0:T(8,128)(2,1)S(1)}, bf16[4,48,384]{2,1,0:T(8,128)(2,1)S(1)}, u32[]{:S(2)}, u32[]{:S(2)}) collective-permute-start(bf16[4,48,384]{2,1,0:T(8,128)(2,1)S(1)} %relay.1), channel_id=1, source_target_pairs={{0,2},{2,0},{4,6},{6,4},{1,3},{3,1},{5,7},{7,5},{8,10},{10,8},{12,... | collective-permute-start | bytes 442376 | tf_op jit(solution)/shard_map/ppermute | solution.py:335
  25.0 0.9 %collective-permute-start.10 = (bf16[128,384]{1,0:T(8,128)(2,1)S(1)}, bf16[128,384]{1,0:T(8,128)(2,1)S(1)}, u32[]{:S(2)}, u32[]{:S(2)}) collective-permute-start(bf16[128,384]{1,0:T(8,128)(2,1)S(1)} %get-tuple-element.57.refs_0_), channel_id=1, source_target_pairs={{0,2},{2,0},{4,6},{6,4},{1,3},{3,1},{5,7},{7,5},{8,10},{10,8},{12,... | collective-permute-start | bytes 294920 | tf_op jit(solution)/shard_map/ppermute | solution.py:335
  25.9 0.1 collective-permute-done.11.refs_2_
  26.0 1.0 %collective-permute-start.12 = (bf16[128,384]{1,0:T(8,128)(2,1)S(1)}, bf16[128,384]{1,0:T(8,128)(2,1)S(1)}, u32[]{:S(2)}, u32[]{:S(2)}) collective-permute-start(bf16[128,384]{1,0:T(8,128)(2,1)S(1)} %collective-permute-done.11.refs_2_), channel_id=1, source_target_pairs={{0,2},{2,0},{4,6},{6,4},{1,3},{3,1},{5,7},{7,5},{8,10},{10,8},{12,... | collective-permute-start | bytes 294920 | tf_op jit(solution)/shard_map/ppermute | solution.py:335
  27.1 0.0 collective-permute-start.6
  27.1 0.5 collective-permute-start.8
  27.6 3.6 %collective-permute-done.10.refs_1_ = bf16[128,384]{1,0:T(8,128)(2,1)S(1)} collective-permute-done((bf16[128,384]{1,0:T(8,128)(2,1)S(1)}, bf16[128,384]{1,0:T(8,128)(2,1)S(1)}, u32[]{:S(2)}, u32[]{:S(2)}) %collective-permute-start.10) | collective-permute-done | bytes 98336 | tf_op jit(solution)/shard_map/ppermute | solution.py:335
  31.2 0.0 collective-permute-start.7
  31.2 0.0 collective-permute-done.5.refs_3_
  31.2 0.5 collective-permute-start.9
  31.7 0.5 collective-permute-done.12.refs_3_
  32.2 0.3 pick.1
  32.5 1.6 %collective-permute-start.13 = (bf16[4,40,384]{2,1,0:T(8,128)(2,1)S(1)}, bf16[4,40,384]{2,1,0:T(8,128)(2,1)S(1)}, u32[]{:S(2)}, u32[]{:S(2)}) collective-permute-start(bf16[4,40,384]{2,1,0:T(8,128)(2,1)S(1)} %get-tuple-element.58), channel_id=1, source_target_pairs={{0,8},{8,0},{16,24},{24,16},{1,9},{9,1},{17,25},{25,17},{2,10},{10... | collective-permute-start | bytes 368648 | tf_op jit(solution)/shard_map/ppermute | solution.py:335
  34.2 0.0 collective-permute-done.6.refs_4_
  34.2 1.5 %collective-permute-start.15 = (bf16[4,40,384]{2,1,0:T(8,128)(2,1)S(1)}, bf16[4,40,384]{2,1,0:T(8,128)(2,1)S(1)}, u32[]{:S(2)}, u32[]{:S(2)}) collective-permute-start(bf16[4,40,384]{2,1,0:T(8,128)(2,1)S(1)} %get-tuple-element.62), channel_id=1, source_target_pairs={{0,16},{8,24},{16,0},{24,8},{1,17},{9,25},{17,1},{25,9},{2,18},{10... | collective-permute-start | bytes 368648 | tf_op jit(solution)/shard_map/ppermute | solution.py:335
  35.7 1.8 %collective-permute-done.13.refs_10_.refs_1_ = bf16[4,40,384]{2,1,0:T(8,128)(2,1)S(1)} collective-permute-done((bf16[4,40,384]{2,1,0:T(8,128)(2,1)S(1)}, bf16[4,40,384]{2,1,0:T(8,128)(2,1)S(1)}, u32[]{:S(2)}, u32[]{:S(2)}) %collective-permute-start.13) | collective-permute-done | bytes 122912 | tf_op jit(solution)/shard_map/ppermute | solution.py:335
  37.5 2.5 %collective-permute-start.16 = (bf16[4,40,384]{2,1,0:T(8,128)(2,1)S(1)}, bf16[4,40,384]{2,1,0:T(8,128)(2,1)S(1)}, u32[]{:S(2)}, u32[]{:S(2)}) collective-permute-start(bf16[4,40,384]{2,1,0:T(8,128)(2,1)S(1)} %get-tuple-element.63), channel_id=1, source_target_pairs={{0,24},{8,16},{16,8},{24,0},{1,25},{9,17},{17,9},{25,1},{2,26},{10... | collective-permute-start | bytes 368648 | tf_op jit(solution)/shard_map/ppermute | solution.py:335
  40.0 0.0 collective-permute-done.8.refs_6_
  40.0 0.0 collective-permute-done.7.refs_5_
  40.0 0.0 collective-permute-done.9.refs_7_
  40.0 7.0 %forward.1 = (bf16[192,3072]{1,0:T(8,128)(2,1)S(1)}, bf16[192,1024]{1,0:T(8,128)(2,1)S(1)}, f32[192,1024]{1,0:T(8,128)S(1)}, f32[192,1024]{1,0:T(8,128)S(1)}, f3...) custom-call(bf16[4,48,384]{2,1,0:T(8,128)(2,1)S(1)} %stack.1.refs_0_, ...), custom_call_target="tpu_custom_call" | custom-call | flops 3623878656 | bytes 18874368 | tf_op jit(solution)/shard_map/forward/pallas_call | solution.py:354
  47.0 0.0 collective-permute-done.15.refs_2_
  47.0 0.0 collective-permute-done.16.refs_3_
  47.1 0.1 collective-permute-start.17
  47.2 0.5 collective-permute-start.14
  47.7 1.4 %collective-permute-done.17.refs_1_ = bf16[4,4,40,384]{3,2,1,0:T(8,128)(2,1)S(1)} collective-permute-done((bf16[4,4,40,384]{3,2,1,0:T(8,128)(2,1)S(1)}, bf16[4,4,40,384]{3,2,1,0:T(8,128)(2,1)S(1)}, u32[]{:S(2)}, u32[]{:S(2)}) %collective-permute-start.17) | collective-permute-done | bytes 491552 | tf_op jit(solution)/shard_map/ppermute | solution.py:335
  49.0 3.3 %backward.1 = (bf16[192,3072]{1,0:T(8,128)(2,1)S(1)}, bf16[192,1024]{1,0:T(8,128)(2,1)S(1)}, bf16[192,1024]{1,0:T(8,128)(2,1)S(1)}, f32[4,4,384]{2,1,0:T(4,128)S(1)}, bf16[4,8,384]{2,1,0:T(8,128)(2,1)S(1)}) custom-call(bf16[4,4,40,384]{3,2,1,0:T(8,128)(2,1)S(1)} %stack_d.1.refs_0_, bf16[4,4,40,384]{3,2,1,0:T(8,128)(2,1)S(1)} %collective-permute-done.17.refs_1_, ...), custom_call_target="tpu_custom_call" | custom-call | flops 1207959552 | bytes 6291456 | tf_op jit(solution)/shard_map/backward/pallas_call | solution.py:354
  52.3 0.2 collective-permute-start.18
  52.5 1.1 %collective-permute-done.18.rgot_ref = bf16[4,8,384]{2,1,0:T(8,128)(2,1)S(1)} collective-permute-done((bf16[4,8,384]{2,1,0:T(8,128)(2,1)S(1)}, bf16[4,8,384]{2,1,0:T(8,128)(2,1)S(1)}, u32[]{:S(2)}, u32[]{:S(2)}) %collective-permute-start.18) | collective-permute-done | bytes 24608 | tf_op jit(solution)/shard_map/ppermute | solution.py:335
  53.5 0.0 collective-permute-done.14.got_ref
  53.6 0.1 merge.1
  53.7 1.1 %collective-permute-start.19 = (bf16[4,48,384]{2,1,0:T(8,128)(2,1)S(1)}, bf16[4,48,384]{2,1,0:T(8,128)(2,1)S(1)}, u32[]{:S(2)}, u32[]{:S(2)}) collective-permute-start(bf16[4,48,384]{2,1,0:T(8,128)(2,1)S(1)} %get-tuple-element.75), channel_id=1, source_target_pairs={{0,2},{2,0},{4,6},{6,4},{1,3},{3,1},{5,7},{7,5},{8,10},{10,8},{12,... | collective-permute-start | bytes 442376 | tf_op jit(solution)/shard_map/ppermute | solution.py:335
  54.8 4.1 %collective-permute-start.20 = (bf16[4,48,384]{2,1,0:T(8,128)(2,1)S(1)}, bf16[4,48,384]{2,1,0:T(8,128)(2,1)S(1)}, u32[]{:S(2)}, u32[]{:S(2)}) collective-permute-start(bf16[4,48,384]{2,1,0:T(8,128)(2,1)S(1)} %get-tuple-element.76), channel_id=1, source_target_pairs={{0,4},{2,6},{4,0},{6,2},{1,5},{3,7},{5,1},{7,3},{8,12},{10,14},{12... | collective-permute-start | bytes 442376 | tf_op jit(solution)/shard_map/ppermute | solution.py:335
  58.9 0.0 collective-permute-start.21
  58.9 8.8 %grads.1 = (bf16[1,3072,1024]{2,1,0:T(8,128)(2,1)}, bf16[1,3072,1024]{2,1,0:T(8,128)(2,1)}, bf16[1,1024,3072]{2,1,0:T(8,128)(2,1)}, f32[8,128]{1,0:T(8,128)S(1)}) custom-call(bf16[192,3072]{1,0:T(8,128)(2,1)S(1)} %get-tuple-element.65.refs_2_.x_ref, bf16[192,3072]{1,0:T(8,128)(2,1)S(1)} %get-tuple-element.78.d_ref, ...), custom_call_target="tpu_custom_call" | custom-call | flops 3623878656 | bytes 18874368 | tf_op jit(solution)/shard_map/grads/pallas_call | solution.py:490
  67.7 0.0 collective-permute-done.19.refs_1_
  67.7 2.1 %collective-permute-done.20.refs_2_ = bf16[4,48,384]{2,1,0:T(8,128)(2,1)S(1)} collective-permute-done((bf16[4,48,384]{2,1,0:T(8,128)(2,1)S(1)}, bf16[4,48,384]{2,1,0:T(8,128)(2,1)S(1)}, u32[]{:S(2)}, u32[]{:S(2)}) %collective-permute-start.20) | collective-permute-done | bytes 147488 | tf_op jit(solution)/shard_map/ppermute | solution.py:335
  69.8 0.0 collective-permute-done.21.refs_3_
  69.8 0.1 total.1
  69.9 0.6 collective-permute-start.22
  70.5 0.5 collective-permute-start.23
  71.0 2.5 %collective-permute-start.24 = (bf16[48,384]{1,0:T(8,128)(2,1)S(1)}, bf16[48,384]{1,0:T(8,128)(2,1)S(1)}, u32[]{:S(2)}, u32[]{:S(2)}) collective-permute-start(bf16[48,384]{1,0:T(8,128)(2,1)S(1)} %get-tuple-element.85), channel_id=1, source_target_pairs={{0,24},{8,16},{16,8},{24,0},{1,25},{9,17},{17,9},{25,1},{2,26},{10... | collective-permute-start | bytes 110600 | tf_op jit(solution)/shard_map/ppermute | solution.py:335
  73.5 0.5 collective-permute-done.22.refs_1_
  73.9 0.5 collective-permute-done.23.refs_2_
  74.5 1.4 %collective-permute-done.24.refs_3_ = bf16[48,384]{1,0:T(8,128)(2,1)S(1)} collective-permute-done((bf16[48,384]{1,0:T(8,128)(2,1)S(1)}, bf16[48,384]{1,0:T(8,128)(2,1)S(1)}, u32[]{:S(2)}, u32[]{:S(2)}) %collective-permute-start.24) | collective-permute-done | bytes 36896 | tf_op jit(solution)/shard_map/ppermute | solution.py:335
  75.9 0.9 %combine.1 = (bf16[128,384]{1,0:T(8,128)(2,1)}, bf16[4,384]{1,0:T(4,128)(2,1)}) custom-call(s32[1,256]{1,0:T(1,128)S(1)} %get-tuple-element.48.pos_ref, bf16[48,384]{1,0:T(8,128)(2,1)S(1)} %get-tuple-element.82.refs_0_, bf16[48,384]{1,0:T(8,128)(2,1)S(1)} %collective-permute-done.22.refs_1_, bf16[48,384]{1,0:T(8,128)(2,1)S(1)} %collective-permute-done.23.refs_2_, ...), custom_call_target="tpu_custom_call" | custom-call | tf_op jit(solution)/shard_map/combine/pallas_call | solution.py:354
  (3 shorter events, 0.1 us)
Async XLA Ops:
  2.2 10.2 %collective-permute-start = (bf16[48,384]{1,0:T(8,128)(2,1)S(1)}, bf16[48,384]{1,0:T(8,128)(2,1)S(1)}, u32[]{:S(2)}, u32[]{:S(2)}) collective-permute-start(bf16[48,384]{1,0:T(8,128)(2,1)S(1)} %get-tuple-element.50), channel_id=1, source_target_pairs={{0,8},{8,0},{16,24},{24,16},{1,9},{9,1},{17,25},{25,17},{2,10},{10... | collective-permute-start | bytes 110600 | tf_op jit(solution)/shard_map/ppermute | solution.py:335
  5.2 7.2 %collective-permute-start.1 = (bf16[48,384]{1,0:T(8,128)(2,1)S(1)}, bf16[48,384]{1,0:T(8,128)(2,1)S(1)}, u32[]{:S(2)}, u32[]{:S(2)}) collective-permute-start(bf16[48,384]{1,0:T(8,128)(2,1)S(1)} %get-tuple-element.51), channel_id=1, source_target_pairs={{0,16},{8,24},{16,0},{24,8},{1,17},{9,25},{17,1},{25,9},{2,18},{10... | collective-permute-start | bytes 110600 | tf_op jit(solution)/shard_map/ppermute | solution.py:335
  6.7 5.7 %collective-permute-start.2 = (bf16[48,384]{1,0:T(8,128)(2,1)S(1)}, bf16[48,384]{1,0:T(8,128)(2,1)S(1)}, u32[]{:S(2)}, u32[]{:S(2)}) collective-permute-start(bf16[48,384]{1,0:T(8,128)(2,1)S(1)} %get-tuple-element.52), channel_id=1, source_target_pairs={{0,24},{8,16},{16,8},{24,0},{1,25},{9,17},{17,9},{25,1},{2,26},{10... | collective-permute-start | bytes 110600 | tf_op jit(solution)/shard_map/ppermute | solution.py:335
  12.4 11.4 %collective-permute-start.4 = (bf16[4,48,384]{2,1,0:T(8,128)(2,1)S(1)}, bf16[4,48,384]{2,1,0:T(8,128)(2,1)S(1)}, u32[]{:S(2)}, u32[]{:S(2)}) collective-permute-start(bf16[4,48,384]{2,1,0:T(8,128)(2,1)S(1)} %stack.1.refs_0_), channel_id=1, source_target_pairs={{0,4},{2,6},{4,0},{6,2},{1,5},{3,7},{5,1},{7,3},{8,12},{10,14},{12... | collective-permute-start | bytes 442376 | tf_op jit(solution)/shard_map/ppermute | solution.py:335
  15.5 8.3 %collective-permute-start.3 = (bf16[4,48,384]{2,1,0:T(8,128)(2,1)S(1)}, bf16[4,48,384]{2,1,0:T(8,128)(2,1)S(1)}, u32[]{:S(2)}, u32[]{:S(2)}) collective-permute-start(bf16[4,48,384]{2,1,0:T(8,128)(2,1)S(1)} %stack.1.refs_0_), channel_id=1, source_target_pairs={{0,2},{2,0},{4,6},{6,4},{1,3},{3,1},{5,7},{7,5},{8,10},{10,8},{12,... | collective-permute-start | bytes 442376 | tf_op jit(solution)/shard_map/ppermute | solution.py:335
  17.1 8.9 %collective-permute-start.11 = (bf16[128,384]{1,0:T(8,128)(2,1)S(1)}, bf16[128,384]{1,0:T(8,128)(2,1)S(1)}, u32[]{:S(2)}, u32[]{:S(2)}) collective-permute-start(bf16[128,384]{1,0:T(8,128)(2,1)S(1)} %get-tuple-element.57.refs_0_), channel_id=1, source_target_pairs={{0,4},{2,6},{4,0},{6,2},{1,5},{3,7},{5,1},{7,3},{8,12},{10,14},{12... | collective-permute-start | bytes 294920 | tf_op jit(solution)/shard_map/ppermute | solution.py:335
  23.8 7.4 %collective-permute-start.5 = (bf16[4,48,384]{2,1,0:T(8,128)(2,1)S(1)}, bf16[4,48,384]{2,1,0:T(8,128)(2,1)S(1)}, u32[]{:S(2)}, u32[]{:S(2)}) collective-permute-start(bf16[4,48,384]{2,1,0:T(8,128)(2,1)S(1)} %relay.1), channel_id=1, source_target_pairs={{0,2},{2,0},{4,6},{6,4},{1,3},{3,1},{5,7},{7,5},{8,10},{10,8},{12,... | collective-permute-start | bytes 442376 | tf_op jit(solution)/shard_map/ppermute | solution.py:335
  25.0 6.2 %collective-permute-start.10 = (bf16[128,384]{1,0:T(8,128)(2,1)S(1)}, bf16[128,384]{1,0:T(8,128)(2,1)S(1)}, u32[]{:S(2)}, u32[]{:S(2)}) collective-permute-start(bf16[128,384]{1,0:T(8,128)(2,1)S(1)} %get-tuple-element.57.refs_0_), channel_id=1, source_target_pairs={{0,2},{2,0},{4,6},{6,4},{1,3},{3,1},{5,7},{7,5},{8,10},{10,8},{12,... | collective-permute-start | bytes 294920 | tf_op jit(solution)/shard_map/ppermute | solution.py:335
  26.0 6.2 %collective-permute-start.12 = (bf16[128,384]{1,0:T(8,128)(2,1)S(1)}, bf16[128,384]{1,0:T(8,128)(2,1)S(1)}, u32[]{:S(2)}, u32[]{:S(2)}) collective-permute-start(bf16[128,384]{1,0:T(8,128)(2,1)S(1)} %collective-permute-done.11.refs_2_), channel_id=1, source_target_pairs={{0,2},{2,0},{4,6},{6,4},{1,3},{3,1},{5,7},{7,5},{8,10},{10,8},{12,... | collective-permute-start | bytes 294920 | tf_op jit(solution)/shard_map/ppermute | solution.py:335
  27.1 7.1 %collective-permute-start.6 = (bf16[4,48,384]{2,1,0:T(8,128)(2,1)S(1)}, bf16[4,48,384]{2,1,0:T(8,128)(2,1)S(1)}, u32[]{:S(2)}, u32[]{:S(2)}) collective-permute-start(bf16[4,48,384]{2,1,0:T(8,128)(2,1)S(1)} %stack.1.refs_0_), channel_id=1, source_target_pairs={{0,1},{1,0},{2,3},{3,2},{4,5},{5,4},{6,7},{7,6},{8,9},{9,8},{10,11... | collective-permute-start | bytes 442376 | tf_op jit(solution)/shard_map/ppermute | solution.py:335
  27.1 12.9 %collective-permute-start.8 = (bf16[4,48,384]{2,1,0:T(8,128)(2,1)S(1)}, bf16[4,48,384]{2,1,0:T(8,128)(2,1)S(1)}, u32[]{:S(2)}, u32[]{:S(2)}) collective-permute-start(bf16[4,48,384]{2,1,0:T(8,128)(2,1)S(1)} %collective-permute-done.4.block_ref.refs_2_), channel_id=1, source_target_pairs={{0,1},{1,0},{2,3},{3,2},{4,5},{5,4},{6,7},{7,6},{8,9},{9,8},{10,11... | collective-permute-start | bytes 442376 | tf_op jit(solution)/shard_map/ppermute | solution.py:335
  31.2 8.8 %collective-permute-start.7 = (bf16[4,48,384]{2,1,0:T(8,128)(2,1)S(1)}, bf16[4,48,384]{2,1,0:T(8,128)(2,1)S(1)}, u32[]{:S(2)}, u32[]{:S(2)}) collective-permute-start(bf16[4,48,384]{2,1,0:T(8,128)(2,1)S(1)} %collective-permute-done.3.refs_0_.refs_1_), channel_id=1, source_target_pairs={{0,1},{1,0},{2,3},{3,2},{4,5},{5,4},{6,7},{7,6},{8,9},{9,8},{10,11... | collective-permute-start | bytes 442376 | tf_op jit(solution)/shard_map/ppermute | solution.py:335
  31.2 8.8 %collective-permute-start.9 = (bf16[4,48,384]{2,1,0:T(8,128)(2,1)S(1)}, bf16[4,48,384]{2,1,0:T(8,128)(2,1)S(1)}, u32[]{:S(2)}, u32[]{:S(2)}) collective-permute-start(bf16[4,48,384]{2,1,0:T(8,128)(2,1)S(1)} %collective-permute-done.5.refs_3_), channel_id=1, source_target_pairs={{0,1},{1,0},{2,3},{3,2},{4,5},{5,4},{6,7},{7,6},{8,9},{9,8},{10,11... | collective-permute-start | bytes 442376 | tf_op jit(solution)/shard_map/ppermute | solution.py:335
  32.5 4.9 %collective-permute-start.13 = (bf16[4,40,384]{2,1,0:T(8,128)(2,1)S(1)}, bf16[4,40,384]{2,1,0:T(8,128)(2,1)S(1)}, u32[]{:S(2)}, u32[]{:S(2)}) collective-permute-start(bf16[4,40,384]{2,1,0:T(8,128)(2,1)S(1)} %get-tuple-element.58), channel_id=1, source_target_pairs={{0,8},{8,0},{16,24},{24,16},{1,9},{9,1},{17,25},{25,17},{2,10},{10... | collective-permute-start | bytes 368648 | tf_op jit(solution)/shard_map/ppermute | solution.py:335
  34.2 12.9 %collective-permute-start.15 = (bf16[4,40,384]{2,1,0:T(8,128)(2,1)S(1)}, bf16[4,40,384]{2,1,0:T(8,128)(2,1)S(1)}, u32[]{:S(2)}, u32[]{:S(2)}) collective-permute-start(bf16[4,40,384]{2,1,0:T(8,128)(2,1)S(1)} %get-tuple-element.62), channel_id=1, source_target_pairs={{0,16},{8,24},{16,0},{24,8},{1,17},{9,25},{17,1},{25,9},{2,18},{10... | collective-permute-start | bytes 368648 | tf_op jit(solution)/shard_map/ppermute | solution.py:335
  37.5 9.5 %collective-permute-start.16 = (bf16[4,40,384]{2,1,0:T(8,128)(2,1)S(1)}, bf16[4,40,384]{2,1,0:T(8,128)(2,1)S(1)}, u32[]{:S(2)}, u32[]{:S(2)}) collective-permute-start(bf16[4,40,384]{2,1,0:T(8,128)(2,1)S(1)} %get-tuple-element.63), channel_id=1, source_target_pairs={{0,24},{8,16},{16,8},{24,0},{1,25},{9,17},{17,9},{25,1},{2,26},{10... | collective-permute-start | bytes 368648 | tf_op jit(solution)/shard_map/ppermute | solution.py:335
  47.1 1.9 %collective-permute-start.17 = (bf16[4,4,40,384]{3,2,1,0:T(8,128)(2,1)S(1)}, bf16[4,4,40,384]{3,2,1,0:T(8,128)(2,1)S(1)}, u32[]{:S(2)}, u32[]{:S(2)}) collective-permute-start(bf16[4,4,40,384]{3,2,1,0:T(8,128)(2,1)S(1)} %stack_d.1.refs_0_), channel_id=1, source_target_pairs={{0,1},{1,0},{2,3},{3,2},{4,5},{5,4},{6,7},{7,6},{8,9},{9,8},{10,11... | collective-permute-start | bytes 1474568 | tf_op jit(solution)/shard_map/ppermute | solution.py:335
  47.2 6.4 %collective-permute-start.14 = (bf16[4,4,48,384]{3,2,1,0:T(8,128)(2,1)S(1)}, bf16[4,4,48,384]{3,2,1,0:T(8,128)(2,1)S(1)}, u32[]{:S(2)}, u32[]{:S(2)}) collective-permute-start(bf16[4,4,48,384]{3,2,1,0:T(8,128)(2,1)S(1)} %get-tuple-element.60), channel_id=1, source_target_pairs={{0,1},{1,0},{2,3},{3,2},{4,5},{5,4},{6,7},{7,6},{8,9},{9,8},{10,11... | collective-permute-start | bytes 1769480 | tf_op jit(solution)/shard_map/ppermute | solution.py:335
  52.3 1.3 %collective-permute-start.18 = (bf16[4,8,384]{2,1,0:T(8,128)(2,1)S(1)}, bf16[4,8,384]{2,1,0:T(8,128)(2,1)S(1)}, u32[]{:S(2)}, u32[]{:S(2)}) collective-permute-start(bf16[4,8,384]{2,1,0:T(8,128)(2,1)S(1)} %get-tuple-element.73), channel_id=1, source_target_pairs={{0,1},{1,0},{2,3},{3,2},{4,5},{5,4},{6,7},{7,6},{8,9},{9,8},{10,11... | collective-permute-start | bytes 73736 | tf_op jit(solution)/shard_map/ppermute | solution.py:335
  53.7 14.0 %collective-permute-start.19 = (bf16[4,48,384]{2,1,0:T(8,128)(2,1)S(1)}, bf16[4,48,384]{2,1,0:T(8,128)(2,1)S(1)}, u32[]{:S(2)}, u32[]{:S(2)}) collective-permute-start(bf16[4,48,384]{2,1,0:T(8,128)(2,1)S(1)} %get-tuple-element.75), channel_id=1, source_target_pairs={{0,2},{2,0},{4,6},{6,4},{1,3},{3,1},{5,7},{7,5},{8,10},{10,8},{12,... | collective-permute-start | bytes 442376 | tf_op jit(solution)/shard_map/ppermute | solution.py:335
  54.8 15.1 %collective-permute-start.20 = (bf16[4,48,384]{2,1,0:T(8,128)(2,1)S(1)}, bf16[4,48,384]{2,1,0:T(8,128)(2,1)S(1)}, u32[]{:S(2)}, u32[]{:S(2)}) collective-permute-start(bf16[4,48,384]{2,1,0:T(8,128)(2,1)S(1)} %get-tuple-element.76), channel_id=1, source_target_pairs={{0,4},{2,6},{4,0},{6,2},{1,5},{3,7},{5,1},{7,3},{8,12},{10,14},{12... | collective-permute-start | bytes 442376 | tf_op jit(solution)/shard_map/ppermute | solution.py:335
  58.9 11.0 %collective-permute-start.21 = (bf16[4,48,384]{2,1,0:T(8,128)(2,1)S(1)}, bf16[4,48,384]{2,1,0:T(8,128)(2,1)S(1)}, u32[]{:S(2)}, u32[]{:S(2)}) collective-permute-start(bf16[4,48,384]{2,1,0:T(8,128)(2,1)S(1)} %get-tuple-element.77), channel_id=1, source_target_pairs={{0,6},{2,4},{4,2},{6,0},{1,7},{3,5},{5,3},{7,1},{8,14},{10,12},{12... | collective-permute-start | bytes 442376 | tf_op jit(solution)/shard_map/ppermute | solution.py:335
  69.9 4.0 %collective-permute-start.22 = (bf16[48,384]{1,0:T(8,128)(2,1)S(1)}, bf16[48,384]{1,0:T(8,128)(2,1)S(1)}, u32[]{:S(2)}, u32[]{:S(2)}) collective-permute-start(bf16[48,384]{1,0:T(8,128)(2,1)S(1)} %get-tuple-element.83), channel_id=1, source_target_pairs={{0,8},{8,0},{16,24},{24,16},{1,9},{9,1},{17,25},{25,17},{2,10},{10... | collective-permute-start | bytes 110600 | tf_op jit(solution)/shard_map/ppermute | solution.py:335
  70.5 4.0 %collective-permute-start.23 = (bf16[48,384]{1,0:T(8,128)(2,1)S(1)}, bf16[48,384]{1,0:T(8,128)(2,1)S(1)}, u32[]{:S(2)}, u32[]{:S(2)}) collective-permute-start(bf16[48,384]{1,0:T(8,128)(2,1)S(1)} %get-tuple-element.84), channel_id=1, source_target_pairs={{0,16},{8,24},{16,0},{24,8},{1,17},{9,25},{17,1},{25,9},{2,18},{10... | collective-permute-start | bytes 110600 | tf_op jit(solution)/shard_map/ppermute | solution.py:335
  71.0 4.9 %collective-permute-start.24 = (bf16[48,384]{1,0:T(8,128)(2,1)S(1)}, bf16[48,384]{1,0:T(8,128)(2,1)S(1)}, u32[]{:S(2)}, u32[]{:S(2)}) collective-permute-start(bf16[48,384]{1,0:T(8,128)(2,1)S(1)} %get-tuple-element.85), channel_id=1, source_target_pairs={{0,24},{8,16},{16,8},{24,0},{1,25},{9,17},{17,9},{25,1},{2,26},{10... | collective-permute-start | bytes 110600 | tf_op jit(solution)/shard_map/ppermute | solution.py:335

commit v3 on v2

--- a/solution.py
+++ b/solution.py
@@ -152,20 +152,17 @@
 
 def reader(relative, hops, refs):
     if relative:
-        return lambda side, q, k: refs[side * hops + k][q]
+        return lambda side, q, k: refs[2 * side + k // 3][k % 3, q]
     return lambda side, q, k: refs[side][k, q]
 
 
 def forward_kernel(relative, groups, hops, *refs):
-    inputs = 2 * hops if relative else 2
+    inputs = 4 if relative else 2
     take = reader(relative, hops, refs[:inputs])
-    gate_ref, up_ref, _, down_hbm = refs[inputs : inputs + 4]
-    x_ref, hid_ref, active_ref, slope_ref, gates_ref, rival_ref, other_ref, keep_ref, give_ref, down_ref = refs[
-        inputs + 4 : inputs + 14
+    gate_ref, up_ref, down_ref, _ = refs[inputs : inputs + 4]
+    x_ref, hid_ref, active_ref, slope_ref, gates_ref, rival_ref, other_ref, keep_ref, give_ref, total = refs[
+        inputs + 4 :
     ]
-    total, sem = refs[inputs + 14 :]
-    fetch = pltpu.make_async_copy(down_hbm, down_ref, sem)
-    fetch.start()
     width = keep_ref.shape[-1]
     model = x_ref.shape[1]
     units = hid_ref.shape[1]
@@ -199,7 +196,6 @@
         slope_ref[:, now] = sigma * (1.0 + gate_pre * (1.0 - sigma)) * up_pre
         hid_ref[:, now] = (active * up_pre).astype(BF16)
     hidden = hid_ref[...]
-    fetch.wait()
     for f in range(0, model, 512):
         now = slice(f, f + 512)
         total[:, now] = gates_ref[...] * dot(hidden, down_ref[0, :, now], ((1,), (0,)))
@@ -272,8 +268,11 @@
         put(out_refs[k], keep_ref[k] + got_ref[k].astype(F32), router)
 
 
-def pass_kernel(block_ref, *refs):
-    refs[-1][...] = block_ref[...]
+def relay_kernel(own_ref, near_ref, second_ref, _, __, ___, three_ref, relay_ref):
+    three_ref[0] = own_ref[...]
+    three_ref[1] = near_ref[...]
+    three_ref[2] = second_ref[...]
+    relay_ref[...] = second_ref[...]
 
 
 def put(out_ref, blocks, router):
@@ -343,7 +342,7 @@
     _, model, units = w_gate.shape
     rows = groups * ROWS
     height = -(-(CAP + 2 * experts) // 16) * 16
-    relative = width % LANES == 0 and hops <= 4
+    relative = width % LANES == 0 and hops == 4
     whole = pl.BlockSpec(memory_space=pltpu.VMEM)
     anywhere = pl.BlockSpec(memory_space=pl.ANY)
     fixed = pl.BlockSpec(memory_space=pltpu.HBM)
@@ -391,20 +390,15 @@
 
     gate_w, gate_mark = load(w_gate, "load_gate")
     up_w, up_mark = load(w_up, "load_up")
-    def gather(block, forward):
-        if not relative:
-            return [lax.all_gather(block, "z", axis=0, tiled=False)]
-        blocks = [block]
-        if hops > 2:
+    down_w, down_mark = load(w_down, "load_down")
+    def gather(block):
+        if relative:
             second = swap(block, "z", 2)
-        if hops > 1:
-            blocks.append(swap(block, "z", 1))
-        if hops > 2:
-            blocks += [second, swap(forward(second, blocks[1]), "z", 1)]
-        return blocks
+            return [block, swap(block, "z", 1), second, swap(second, "z", 1)]
+        return [lax.all_gather(block, "z", axis=0, tiled=False)]
 
     arrived = [sends[0]] + [swap(sends[q], "expert", q) for q in range(1, groups)]
-    slices = gather(handed, lambda second, near: second)
+    slices = gather(handed)
     picked = call(
         functools.partial(pick_kernel, relative, experts, hops),
         (position, *slices),
@@ -413,22 +407,28 @@
     )
     (stacked,) = call(
         functools.partial(stack_kernel, groups),
-        (*arrived, gate_mark, up_mark),
+        (*arrived, gate_mark, *slices[1:3]),
         [shape((groups, ROWS, width), BF16)],
         "stack",
     )
-
-    def relay(second, near):
-        return call(pass_kernel, (second, near), [shape(second.shape, BF16)], "relay")[0]
-
-    blocks = gather(stacked, relay)
+    if relative:
+        near, second = swap(stacked, "z", 1), swap(stacked, "z", 2)
+        three, relay = call(
+            relay_kernel,
+            (stacked, near, second, up_mark, down_mark, picked[0]),
+            [shape((3, *stacked.shape), BF16), shape(stacked.shape, BF16)],
+            "relay",
+        )
+        blocks = [three, swap(relay, "z", 1)[None]]
+    else:
+        blocks = gather(stacked)
     blocks = blocks + [swap(block, "core", 1) for block in blocks]
     blocks_d = [picked[0]] + [swap(picked[q], "expert", q) for q in range(1, groups)]
 
     cost = 2 * rows * model * units
-    rows_x, hidden, active, slope, gates, rival, others, keep, give, down_w = call(
+    rows_x, hidden, active, slope, gates, rival, others, keep, give = call(
         functools.partial(forward_kernel, relative, groups, hops),
-        (*blocks, gate_w, up_w, blocks_d[1 if groups > 1 else 0], w_down),
+        (*blocks, gate_w, up_w, down_w, picked[0]),
         [
             shape((rows, model), BF16),
             shape((rows, units), BF16),
@@ -439,11 +439,9 @@
             shape((rows, 1), F32),
             shape((hops, groups, ROWS, width), F32),
             shape((hops, groups, ROWS, width), BF16),
-            pltpu.VMEM(w_down.shape, BF16),
         ],
         "forward",
-        scratch=[pltpu.VMEM((rows, model), F32), pltpu.SemaphoreType.DMA],
-        loose=(len(blocks) + 3,),
+        scratch=[pltpu.VMEM((rows, model), F32)],
         cost=pl.CostEstimate(flops=3 * cost, bytes_accessed=6 * model * units, transcendentals=rows * units),
         limit=16 * MIB,
     )

time: 77 us -> 69.9 us (0.908)
  starting transfers between devices: 28.9 us -> 24.3 us
  waiting for transfers between devices: 19.4 us -> 16.7 us
    ppermute x25 -> x23, starting transfers between devices: 28.9 us -> 24.3 us  [swap(): return lax.ppermute(block, axis, [(i, i ^ bits) for i in range(size)])]
    ppermute x25 -> x23, waiting for transfers between devices: 19.4 us -> 16.7 us  [swap(): return lax.ppermute(block, axis, [(i, i ^ bits) for i in range(size)])]
    pallas_call x12 -> x13, Pallas kernels: 18.9 us -> 19 us  [call(): pl.pallas_call(kernel, out_shape=tuple(outs), in_specs=[fixed if i in loo...]
  transfers between devices with their start and end apart: 25 -> 23, of which waited for: 11 -> 10; matrix products, arithmetic and copies ran while one was open for 0% -> 0% of each run, Pallas kernels for 33% -> 36%
where the time goes in v3:
time: 69.9 us; the launch traced here: 69.6 us
  Pallas kernels  27.8 us (40%)
  starting transfers between devices  24.3 us (35%)
  waiting for transfers between devices  16.7 us (24%)
  between operations  0.79 us (1%)
    ppermute x23, starting transfers between devices, swap(): return lax.ppermute(block, axis, [(i, i ^ bits) for i in range(size)])  24.3 us
    pallas_call x13, Pallas kernels, call(): pl.pallas_call(kernel, out_shape=tuple(outs), in_specs=[fixed if i in loo...  19 us
    ppermute x23, waiting for transfers between devices, swap(): return lax.ppermute(block, axis, [(i, i ^ bits) for i in range(size)])  16.7 us
    pallas_call x1, Pallas kernels, shards(): pl.pallas_call(grads_kernel, grid=(parts,), out_shape=(shape(w_gate.shape...  8.84 us
  transfers between devices with their start and end apart: 23, of which 10 were waited for; matrix products, arithmetic and copies ran while one was open for 0% of the time, Pallas kernels for 36%

profile of v3, /device:TPU:0, one launch (start us, length us, event | category | flops | bytes accessed | tf_op | source)
XLA Modules:
  0.0 69.6 jit_solution(11715030675519720078)
XLA Ops:
  0.6 1.6 %pack.1 = (s32[1,256]{1,0:T(1,128)S(1)}, bf16[128,384]{1,0:T(8,128)(2,1)S(1)}, bf16[48,384]{1,0:T(8,128)(2,1)S(1)}, bf16[48,384]{1,0:T(8,128)(2,1)S(1)}, bf16[48...) custom-call(s32[4]{0:T(128)} %refs_0_.1, s32[4]{0:T(128)} %refs_1_.1, s32[2,128]{1,0:T(2,128)} %bitcast.7, ...), custom_call_target="tpu_custom_call" | custom-call | tf_op jit(solution)/shard_map/pack/pallas_call | solution.py:353
  2.2 4.1 %collective-permute-start.4 = (bf16[128,384]{1,0:T(8,128)(2,1)S(1)}, bf16[128,384]{1,0:T(8,128)(2,1)S(1)}, u32[]{:S(2)}, u32[]{:S(2)}) collective-permute-start(bf16[128,384]{1,0:T(8,128)(2,1)S(1)} %get-tuple-element.57.refs_0_), channel_id=1, source_target_pairs={{0,4},{2,6},{4,0},{6,2},{1,5},{3,7},{5,1},{7,3},{8,12},{10,14},{12... | collective-permute-start | bytes 294920 | tf_op jit(solution)/shard_map/ppermute | solution.py:334
  6.3 1.6 %collective-permute-start.3 = (bf16[128,384]{1,0:T(8,128)(2,1)S(1)}, bf16[128,384]{1,0:T(8,128)(2,1)S(1)}, u32[]{:S(2)}, u32[]{:S(2)}) collective-permute-start(bf16[128,384]{1,0:T(8,128)(2,1)S(1)} %get-tuple-element.57.refs_0_), channel_id=1, source_target_pairs={{0,2},{2,0},{4,6},{6,4},{1,3},{3,1},{5,7},{7,5},{8,10},{10,8},{12,... | collective-permute-start | bytes 294920 | tf_op jit(solution)/shard_map/ppermute | solution.py:334
  7.9 1.5 %collective-permute-start = (bf16[48,384]{1,0:T(8,128)(2,1)S(1)}, bf16[48,384]{1,0:T(8,128)(2,1)S(1)}, u32[]{:S(2)}, u32[]{:S(2)}) collective-permute-start(bf16[48,384]{1,0:T(8,128)(2,1)S(1)} %get-tuple-element.53), channel_id=1, source_target_pairs={{0,8},{8,0},{16,24},{24,16},{1,9},{9,1},{17,25},{25,17},{2,10},{10... | collective-permute-start | bytes 110600 | tf_op jit(solution)/shard_map/ppermute | solution.py:334
  9.4 1.5 %collective-permute-start.1 = (bf16[48,384]{1,0:T(8,128)(2,1)S(1)}, bf16[48,384]{1,0:T(8,128)(2,1)S(1)}, u32[]{:S(2)}, u32[]{:S(2)}) collective-permute-start(bf16[48,384]{1,0:T(8,128)(2,1)S(1)} %get-tuple-element.54), channel_id=1, source_target_pairs={{0,16},{8,24},{16,0},{24,8},{1,17},{9,25},{17,1},{25,9},{2,18},{10... | collective-permute-start | bytes 110600 | tf_op jit(solution)/shard_map/ppermute | solution.py:334
  10.9 0.5 collective-permute-start.2
  11.4 2.8 %load_gate.1 = (bf16[1,3072,1024]{2,1,0:T(8,128)(2,1)S(1)}, f32[8,128]{1,0:T(8,128)S(1)}) custom-call(bf16[1,3072,1024]{2,1,0:T(8,128)(2,1)} %source.3), custom_call_target="tpu_custom_call" | custom-call | bytes 12582912 | tf_op jit(solution)/shard_map/load_gate/pallas_call | solution.py:353
  14.2 0.0 collective-permute-done.refs_1_
  14.2 0.0 collective-permute-done.1.refs_2_
  14.2 1.6 %collective-permute-done.2.refs_3_ = bf16[48,384]{1,0:T(8,128)(2,1)S(1)} collective-permute-done((bf16[48,384]{1,0:T(8,128)(2,1)S(1)}, bf16[48,384]{1,0:T(8,128)(2,1)S(1)}, u32[]{:S(2)}, u32[]{:S(2)}) %collective-permute-start.2) | collective-permute-done | bytes 36896 | tf_op jit(solution)/shard_map/ppermute | solution.py:334
  15.8 0.0 collective-permute-done.4.refs_6_.refs_2_
  15.8 0.0 collective-permute-done.3.refs_5_.refs_1_
  15.8 0.4 collective-permute-start.6
  16.2 0.5 collective-permute-start.5
  16.6 1.6 %collective-permute-start.7 = (bf16[128,384]{1,0:T(8,128)(2,1)S(1)}, bf16[128,384]{1,0:T(8,128)(2,1)S(1)}, u32[]{:S(2)}, u32[]{:S(2)}) collective-permute-start(bf16[128,384]{1,0:T(8,128)(2,1)S(1)} %collective-permute-done.4.refs_6_.refs_2_), channel_id=1, source_target_pairs={{0,2},{2,0},{4,6},{6,4},{1,3},{3,1},{5,7},{7,5},{8,10},{10,8},{12,... | collective-permute-start | bytes 294920 | tf_op jit(solution)/shard_map/ppermute | solution.py:334
  18.2 2.8 %load_up.1 = (bf16[1,3072,1024]{2,1,0:T(8,128)(2,1)S(1)}, f32[8,128]{1,0:T(8,128)S(1)}) custom-call(bf16[1,3072,1024]{2,1,0:T(8,128)(2,1)} %source.4), custom_call_target="tpu_custom_call" | custom-call | bytes 12582912 | tf_op jit(solution)/shard_map/load_up/pallas_call | solution.py:353
  21.0 2.8 %load_down.1 = (bf16[1,1024,3072]{2,1,0:T(8,128)(2,1)S(1)}, f32[8,128]{1,0:T(8,128)S(1)}) custom-call(bf16[1,1024,3072]{2,1,0:T(8,128)(2,1)} %source.5), custom_call_target="tpu_custom_call" | custom-call | bytes 12582912 | tf_op jit(solution)/shard_map/load_down/pallas_call | solution.py:353
  23.8 0.8 %collective-permute-done.7.refs_3_ = bf16[128,384]{1,0:T(8,128)(2,1)S(1)} collective-permute-done((bf16[128,384]{1,0:T(8,128)(2,1)S(1)}, bf16[128,384]{1,0:T(8,128)(2,1)S(1)}, u32[]{:S(2)}, u32[]{:S(2)}) %collective-permute-start.7) | collective-permute-done | bytes 98336 | tf_op jit(solution)/shard_map/ppermute | solution.py:334
  24.6 0.3 pick.1
  24.9 0.0 collective-permute-done.6.second_ref
  24.9 0.0 collective-permute-done.5.near_ref
  25.0 0.1 relay.1
  25.0 0.1 collective-permute-start.9
  25.1 0.3 collective-permute-start.8
  25.4 5.9 %collective-permute-done.8 = bf16[4,48,384]{2,1,0:T(8,128)(2,1)S(1)} collective-permute-done((bf16[4,48,384]{2,1,0:T(8,128)(2,1)S(1)}, bf16[4,48,384]{2,1,0:T(8,128)(2,1)S(1)}, u32[]{:S(2)}, u32[]{:S(2)}) %collective-permute-start.8) | collective-permute-done | bytes 147488 | tf_op jit(solution)/shard_map/ppermute | solution.py:334
  31.4 0.0 collective-permute-start.10
  31.4 1.3 %collective-permute-start.12 = (bf16[4,40,384]{2,1,0:T(8,128)(2,1)S(1)}, bf16[4,40,384]{2,1,0:T(8,128)(2,1)S(1)}, u32[]{:S(2)}, u32[]{:S(2)}) collective-permute-start(bf16[4,40,384]{2,1,0:T(8,128)(2,1)S(1)} %get-tuple-element.68), channel_id=1, source_target_pairs={{0,8},{8,0},{16,24},{24,16},{1,9},{9,1},{17,25},{25,17},{2,10},{10... | collective-permute-start | bytes 368648 | tf_op jit(solution)/shard_map/ppermute | solution.py:334
  32.7 1.5 %collective-permute-start.13 = (bf16[4,40,384]{2,1,0:T(8,128)(2,1)S(1)}, bf16[4,40,384]{2,1,0:T(8,128)(2,1)S(1)}, u32[]{:S(2)}, u32[]{:S(2)}) collective-permute-start(bf16[4,40,384]{2,1,0:T(8,128)(2,1)S(1)} %get-tuple-element.69), channel_id=1, source_target_pairs={{0,16},{8,24},{16,0},{24,8},{1,17},{9,25},{17,1},{25,9},{2,18},{10... | collective-permute-start | bytes 368648 | tf_op jit(solution)/shard_map/ppermute | solution.py:334
  34.2 0.7 collective-permute-start.14
  34.9 0.0 collective-permute-done.10.refs_3_
  34.9 0.0 collective-permute-done.9.refs_2_
  34.9 4.3 %forward.1 = (bf16[192,3072]{1,0:T(8,128)(2,1)S(1)}, bf16[192,1024]{1,0:T(8,128)(2,1)S(1)}, f32[192,1024]{1,0:T(8,128)S(1)}, f32[192,1024]{1,0:T(8,128)S(1)}, f3...) custom-call(bf16[3,4,48,384]{3,2,1,0:T(8,128)(2,1)S(1)} %get-tuple-e, ...), custom_call_target="tpu_custom_call" | custom-call | flops 3623878656 | bytes 18874368 | tf_op jit(solution)/shard_map/forward/pallas_call | solution.py:353
  39.1 0.0 collective-permute-done.12.refs_1_
  39.1 1.6 %collective-permute-done.13.refs_2_ = bf16[4,40,384]{2,1,0:T(8,128)(2,1)S(1)} collective-permute-done((bf16[4,40,384]{2,1,0:T(8,128)(2,1)S(1)}, bf16[4,40,384]{2,1,0:T(8,128)(2,1)S(1)}, u32[]{:S(2)}, u32[]{:S(2)}) %collective-permute-start.13) | collective-permute-done | bytes 122912 | tf_op jit(solution)/shard_map/ppermute | solution.py:334
  40.7 0.0 collective-permute-done.14.refs_3_
  40.8 0.1 collective-permute-start.15
  40.9 0.5 collective-permute-start.11
  41.4 1.4 %collective-permute-done.15.refs_1_ = bf16[4,4,40,384]{3,2,1,0:T(8,128)(2,1)S(1)} collective-permute-done((bf16[4,4,40,384]{3,2,1,0:T(8,128)(2,1)S(1)}, bf16[4,4,40,384]{3,2,1,0:T(8,128)(2,1)S(1)}, u32[]{:S(2)}, u32[]{:S(2)}) %collective-permute-start.15) | collective-permute-done | bytes 491552 | tf_op jit(solution)/shard_map/ppermute | solution.py:334
  42.7 3.3 %backward.1 = (bf16[192,3072]{1,0:T(8,128)(2,1)S(1)}, bf16[192,1024]{1,0:T(8,128)(2,1)S(1)}, bf16[192,1024]{1,0:T(8,128)(2,1)S(1)}, f32[4,4,384]{2,1,0:T(4,128)S(1)}, bf16[4,8,384]{2,1,0:T(8,128)(2,1)S(1)}) custom-call(bf16[4,4,40,384]{3,2,1,0:T(8,128)(2,1)S(1)} %stack_d.1.refs_0_, bf16[4,4,40,384]{3,2,1,0:T(8,128)(2,1)S(1)} %collective-permute-done.15.refs_1_, ...), custom_call_target="tpu_custom_call" | custom-call | flops 1207959552 | bytes 6291456 | tf_op jit(solution)/shard_map/backward/pallas_call | solution.py:353
  46.0 0.2 collective-permute-start.16
  46.2 1.1 %collective-permute-done.16.rgot_ref = bf16[4,8,384]{2,1,0:T(8,128)(2,1)S(1)} collective-permute-done((bf16[4,8,384]{2,1,0:T(8,128)(2,1)S(1)}, bf16[4,8,384]{2,1,0:T(8,128)(2,1)S(1)}, u32[]{:S(2)}, u32[]{:S(2)}) %collective-permute-start.16) | collective-permute-done | bytes 24608 | tf_op jit(solution)/shard_map/ppermute | solution.py:334
  47.3 0.0 collective-permute-done.11.got_ref
  47.3 0.1 merge.1
  47.4 0.3 collective-permute-start.17
  47.7 2.2 %collective-permute-start.18 = (bf16[4,48,384]{2,1,0:T(8,128)(2,1)S(1)}, bf16[4,48,384]{2,1,0:T(8,128)(2,1)S(1)}, u32[]{:S(2)}, u32[]{:S(2)}) collective-permute-start(bf16[4,48,384]{2,1,0:T(8,128)(2,1)S(1)} %get-tuple-element.82), channel_id=1, source_target_pairs={{0,4},{2,6},{4,0},{6,2},{1,5},{3,7},{5,1},{7,3},{8,12},{10,14},{12... | collective-permute-start | bytes 442376 | tf_op jit(solution)/shard_map/ppermute | solution.py:334
  49.9 1.9 %collective-permute-start.19 = (bf16[4,48,384]{2,1,0:T(8,128)(2,1)S(1)}, bf16[4,48,384]{2,1,0:T(8,128)(2,1)S(1)}, u32[]{:S(2)}, u32[]{:S(2)}) collective-permute-start(bf16[4,48,384]{2,1,0:T(8,128)(2,1)S(1)} %get-tuple-element.83), channel_id=1, source_target_pairs={{0,6},{2,4},{4,2},{6,0},{1,7},{3,5},{5,3},{7,1},{8,14},{10,12},{12... | collective-permute-start | bytes 442376 | tf_op jit(solution)/shard_map/ppermute | solution.py:334
  51.8 8.8 %grads.1 = (bf16[1,3072,1024]{2,1,0:T(8,128)(2,1)}, bf16[1,3072,1024]{2,1,0:T(8,128)(2,1)}, bf16[1,1024,3072]{2,1,0:T(8,128)(2,1)}, f32[8,128]{1,0:T(8,128)S(1)}) custom-call(bf16[192,3072]{1,0:T(8,128)(2,1)S(1)} %get-tuple-element.72.refs_2_.x_ref, bf16[192,3072]{1,0:T(8,128)(2,1)S(1)} %get-tuple-element.84.d_ref, ...), custom_call_target="tpu_custom_call" | custom-call | flops 3623878656 | bytes 18874368 | tf_op jit(solution)/shard_map/grads/pallas_call | solution.py:488
  60.7 0.0 collective-permute-done.17.refs_1_
  60.7 1.0 %collective-permute-done.18.refs_2_ = bf16[4,48,384]{2,1,0:T(8,128)(2,1)S(1)} collective-permute-done((bf16[4,48,384]{2,1,0:T(8,128)(2,1)S(1)}, bf16[4,48,384]{2,1,0:T(8,128)(2,1)S(1)}, u32[]{:S(2)}, u32[]{:S(2)}) %collective-permute-start.18) | collective-permute-done | bytes 147488 | tf_op jit(solution)/shard_map/ppermute | solution.py:334
  61.7 0.0 collective-permute-done.19.refs_3_
  61.7 0.1 total.1
  61.8 1.3 %collective-permute-start.20 = (bf16[48,384]{1,0:T(8,128)(2,1)S(1)}, bf16[48,384]{1,0:T(8,128)(2,1)S(1)}, u32[]{:S(2)}, u32[]{:S(2)}) collective-permute-start(bf16[48,384]{1,0:T(8,128)(2,1)S(1)} %get-tuple-element.89), channel_id=1, source_target_pairs={{0,8},{8,0},{16,24},{24,16},{1,9},{9,1},{17,25},{25,17},{2,10},{10... | collective-permute-start | bytes 110600 | tf_op jit(solution)/shard_map/ppermute | solution.py:334
  63.1 0.8 %collective-permute-start.21 = (bf16[48,384]{1,0:T(8,128)(2,1)S(1)}, bf16[48,384]{1,0:T(8,128)(2,1)S(1)}, u32[]{:S(2)}, u32[]{:S(2)}) collective-permute-start(bf16[48,384]{1,0:T(8,128)(2,1)S(1)} %get-tuple-element.90), channel_id=1, source_target_pairs={{0,16},{8,24},{16,0},{24,8},{1,17},{9,25},{17,1},{25,9},{2,18},{10... | collective-permute-start | bytes 110600 | tf_op jit(solution)/shard_map/ppermute | solution.py:334
  63.9 1.4 %collective-permute-start.22 = (bf16[48,384]{1,0:T(8,128)(2,1)S(1)}, bf16[48,384]{1,0:T(8,128)(2,1)S(1)}, u32[]{:S(2)}, u32[]{:S(2)}) collective-permute-start(bf16[48,384]{1,0:T(8,128)(2,1)S(1)} %get-tuple-element.91), channel_id=1, source_target_pairs={{0,24},{8,16},{16,8},{24,0},{1,25},{9,17},{17,9},{25,1},{2,26},{10... | collective-permute-start | bytes 110600 | tf_op jit(solution)/shard_map/ppermute | solution.py:334
  65.3 0.5 collective-permute-done.20.refs_1_
  65.8 1.2 %collective-permute-done.21.refs_2_ = bf16[48,384]{1,0:T(8,128)(2,1)S(1)} collective-permute-done((bf16[48,384]{1,0:T(8,128)(2,1)S(1)}, bf16[48,384]{1,0:T(8,128)(2,1)S(1)}, u32[]{:S(2)}, u32[]{:S(2)}) %collective-permute-start.21) | collective-permute-done | bytes 36896 | tf_op jit(solution)/shard_map/ppermute | solution.py:334
  67.0 1.7 %collective-permute-done.22.refs_3_ = bf16[48,384]{1,0:T(8,128)(2,1)S(1)} collective-permute-done((bf16[48,384]{1,0:T(8,128)(2,1)S(1)}, bf16[48,384]{1,0:T(8,128)(2,1)S(1)}, u32[]{:S(2)}, u32[]{:S(2)}) %collective-permute-start.22) | collective-permute-done | bytes 36896 | tf_op jit(solution)/shard_map/ppermute | solution.py:334
  68.7 0.9 %combine.1 = (bf16[128,384]{1,0:T(8,128)(2,1)}, bf16[4,384]{1,0:T(4,128)(2,1)}) custom-call(s32[1,256]{1,0:T(1,128)S(1)} %get-tuple-element.51.pos_ref, bf16[48,384]{1,0:T(8,128)(2,1)S(1)} %get-tuple-element.88.refs_0_, bf16[48,384]{1,0:T(8,128)(2,1)S(1)} %collective-permute-done.20.refs_1_, bf16[48,384]{1,0:T(8,128)(2,1)S(1)} %collective-permute-done.21.refs_2_, ...), custom_call_target="tpu_custom_call" | custom-call | tf_op jit(solution)/shard_map/combine/pallas_call | solution.py:353
  (2 shorter events, 0.1 us)
Async XLA Ops:
  2.2 13.6 %collective-permute-start.4 = (bf16[128,384]{1,0:T(8,128)(2,1)S(1)}, bf16[128,384]{1,0:T(8,128)(2,1)S(1)}, u32[]{:S(2)}, u32[]{:S(2)}) collective-permute-start(bf16[128,384]{1,0:T(8,128)(2,1)S(1)} %get-tuple-element.57.refs_0_), channel_id=1, source_target_pairs={{0,4},{2,6},{4,0},{6,2},{1,5},{3,7},{5,1},{7,3},{8,12},{10,14},{12... | collective-permute-start | bytes 294920 | tf_op jit(solution)/shard_map/ppermute | solution.py:334
  6.3 9.5 %collective-permute-start.3 = (bf16[128,384]{1,0:T(8,128)(2,1)S(1)}, bf16[128,384]{1,0:T(8,128)(2,1)S(1)}, u32[]{:S(2)}, u32[]{:S(2)}) collective-permute-start(bf16[128,384]{1,0:T(8,128)(2,1)S(1)} %get-tuple-element.57.refs_0_), channel_id=1, source_target_pairs={{0,2},{2,0},{4,6},{6,4},{1,3},{3,1},{5,7},{7,5},{8,10},{10,8},{12,... | collective-permute-start | bytes 294920 | tf_op jit(solution)/shard_map/ppermute | solution.py:334
  7.9 6.3 %collective-permute-start = (bf16[48,384]{1,0:T(8,128)(2,1)S(1)}, bf16[48,384]{1,0:T(8,128)(2,1)S(1)}, u32[]{:S(2)}, u32[]{:S(2)}) collective-permute-start(bf16[48,384]{1,0:T(8,128)(2,1)S(1)} %get-tuple-element.53), channel_id=1, source_target_pairs={{0,8},{8,0},{16,24},{24,16},{1,9},{9,1},{17,25},{25,17},{2,10},{10... | collective-permute-start | bytes 110600 | tf_op jit(solution)/shard_map/ppermute | solution.py:334
  9.4 4.8 %collective-permute-start.1 = (bf16[48,384]{1,0:T(8,128)(2,1)S(1)}, bf16[48,384]{1,0:T(8,128)(2,1)S(1)}, u32[]{:S(2)}, u32[]{:S(2)}) collective-permute-start(bf16[48,384]{1,0:T(8,128)(2,1)S(1)} %get-tuple-element.54), channel_id=1, source_target_pairs={{0,16},{8,24},{16,0},{24,8},{1,17},{9,25},{17,1},{25,9},{2,18},{10... | collective-permute-start | bytes 110600 | tf_op jit(solution)/shard_map/ppermute | solution.py:334
  10.9 4.9 %collective-permute-start.2 = (bf16[48,384]{1,0:T(8,128)(2,1)S(1)}, bf16[48,384]{1,0:T(8,128)(2,1)S(1)}, u32[]{:S(2)}, u32[]{:S(2)}) collective-permute-start(bf16[48,384]{1,0:T(8,128)(2,1)S(1)} %get-tuple-element.55), channel_id=1, source_target_pairs={{0,24},{8,16},{16,8},{24,0},{1,25},{9,17},{17,9},{25,1},{2,26},{10... | collective-permute-start | bytes 110600 | tf_op jit(solution)/shard_map/ppermute | solution.py:334
  15.8 9.1 %collective-permute-start.6 = (bf16[4,48,384]{2,1,0:T(8,128)(2,1)S(1)}, bf16[4,48,384]{2,1,0:T(8,128)(2,1)S(1)}, u32[]{:S(2)}, u32[]{:S(2)}) collective-permute-start(bf16[4,48,384]{2,1,0:T(8,128)(2,1)S(1)} %stack.1.own_ref), channel_id=1, source_target_pairs={{0,4},{2,6},{4,0},{6,2},{1,5},{3,7},{5,1},{7,3},{8,12},{10,14},{12... | collective-permute-start | bytes 442376 | tf_op jit(solution)/shard_map/ppermute | solution.py:334
  16.2 8.8 %collective-permute-start.5 = (bf16[4,48,384]{2,1,0:T(8,128)(2,1)S(1)}, bf16[4,48,384]{2,1,0:T(8,128)(2,1)S(1)}, u32[]{:S(2)}, u32[]{:S(2)}) collective-permute-start(bf16[4,48,384]{2,1,0:T(8,128)(2,1)S(1)} %stack.1.own_ref), channel_id=1, source_target_pairs={{0,2},{2,0},{4,6},{6,4},{1,3},{3,1},{5,7},{7,5},{8,10},{10,8},{12,... | collective-permute-start | bytes 442376 | tf_op jit(solution)/shard_map/ppermute | solution.py:334
  16.6 8.0 %collective-permute-start.7 = (bf16[128,384]{1,0:T(8,128)(2,1)S(1)}, bf16[128,384]{1,0:T(8,128)(2,1)S(1)}, u32[]{:S(2)}, u32[]{:S(2)}) collective-permute-start(bf16[128,384]{1,0:T(8,128)(2,1)S(1)} %collective-permute-done.4.refs_6_.refs_2_), channel_id=1, source_target_pairs={{0,2},{2,0},{4,6},{6,4},{1,3},{3,1},{5,7},{7,5},{8,10},{10,8},{12,... | collective-permute-start | bytes 294920 | tf_op jit(solution)/shard_map/ppermute | solution.py:334
  25.0 9.8 %collective-permute-start.9 = (bf16[3,4,48,384]{3,2,1,0:T(8,128)(2,1)S(1)}, bf16[3,4,48,384]{3,2,1,0:T(8,128)(2,1)S(1)}, u32[]{:S(2)}, u32[]{:S(2)}) collective-permute-start(bf16[3,4,48,384]{3,2,1,0:T(8,128)(2,1)S(1)} %get-tuple-element.61.refs_0_), channel_id=1, source_target_pairs={{0,1},{1,0},{2,3},{3,2},{4,5},{5,4},{6,7},{7,6},{8,9},{9,8},{10,11... | collective-permute-start | bytes 1327112 | tf_op jit(solution)/shard_map/ppermute | solution.py:334
  25.1 6.3 %collective-permute-start.8 = (bf16[4,48,384]{2,1,0:T(8,128)(2,1)S(1)}, bf16[4,48,384]{2,1,0:T(8,128)(2,1)S(1)}, u32[]{:S(2)}, u32[]{:S(2)}) collective-permute-start(bf16[4,48,384]{2,1,0:T(8,128)(2,1)S(1)} %get-tuple-element.62), channel_id=1, source_target_pairs={{0,2},{2,0},{4,6},{6,4},{1,3},{3,1},{5,7},{7,5},{8,10},{10,8},{12,... | collective-permute-start | bytes 442376 | tf_op jit(solution)/shard_map/ppermute | solution.py:334
  31.4 3.5 %collective-permute-start.10 = (bf16[1,4,48,384]{3,2,1,0:T(8,128)(2,1)S(1)}, bf16[1,4,48,384]{3,2,1,0:T(8,128)(2,1)S(1)}, u32[]{:S(2)}, u32[]{:S(2)}) collective-permute-start(bf16[1,4,48,384]{3,2,1,0:T(8,128)(2,1)S(1)} %bitcast.4), channel_id=1, source_target_pairs={{0,1},{1,0},{2,3},{3,2},{4,5},{5,4},{6,7},{7,6},{8,9},{9,8},{10,11... | collective-permute-start | bytes 442376 | tf_op jit(solution)/shard_map/ppermute | solution.py:334
  31.4 7.8 %collective-permute-start.12 = (bf16[4,40,384]{2,1,0:T(8,128)(2,1)S(1)}, bf16[4,40,384]{2,1,0:T(8,128)(2,1)S(1)}, u32[]{:S(2)}, u32[]{:S(2)}) collective-permute-start(bf16[4,40,384]{2,1,0:T(8,128)(2,1)S(1)} %get-tuple-element.68), channel_id=1, source_target_pairs={{0,8},{8,0},{16,24},{24,16},{1,9},{9,1},{17,25},{25,17},{2,10},{10... | collective-permute-start | bytes 368648 | tf_op jit(solution)/shard_map/ppermute | solution.py:334
  32.7 8.1 %collective-permute-start.13 = (bf16[4,40,384]{2,1,0:T(8,128)(2,1)S(1)}, bf16[4,40,384]{2,1,0:T(8,128)(2,1)S(1)}, u32[]{:S(2)}, u32[]{:S(2)}) collective-permute-start(bf16[4,40,384]{2,1,0:T(8,128)(2,1)S(1)} %get-tuple-element.69), channel_id=1, source_target_pairs={{0,16},{8,24},{16,0},{24,8},{1,17},{9,25},{17,1},{25,9},{2,18},{10... | collective-permute-start | bytes 368648 | tf_op jit(solution)/shard_map/ppermute | solution.py:334
  34.2 6.6 %collective-permute-start.14 = (bf16[4,40,384]{2,1,0:T(8,128)(2,1)S(1)}, bf16[4,40,384]{2,1,0:T(8,128)(2,1)S(1)}, u32[]{:S(2)}, u32[]{:S(2)}) collective-permute-start(bf16[4,40,384]{2,1,0:T(8,128)(2,1)S(1)} %get-tuple-element.70), channel_id=1, source_target_pairs={{0,24},{8,16},{16,8},{24,0},{1,25},{9,17},{17,9},{25,1},{2,26},{10... | collective-permute-start | bytes 368648 | tf_op jit(solution)/shard_map/ppermute | solution.py:334
  40.8 1.9 %collective-permute-start.15 = (bf16[4,4,40,384]{3,2,1,0:T(8,128)(2,1)S(1)}, bf16[4,4,40,384]{3,2,1,0:T(8,128)(2,1)S(1)}, u32[]{:S(2)}, u32[]{:S(2)}) collective-permute-start(bf16[4,4,40,384]{3,2,1,0:T(8,128)(2,1)S(1)} %stack_d.1.refs_0_), channel_id=1, source_target_pairs={{0,1},{1,0},{2,3},{3,2},{4,5},{5,4},{6,7},{7,6},{8,9},{9,8},{10,11... | collective-permute-start | bytes 1474568 | tf_op jit(solution)/shard_map/ppermute | solution.py:334
  40.9 6.4 %collective-permute-start.11 = (bf16[4,4,48,384]{3,2,1,0:T(8,128)(2,1)S(1)}, bf16[4,4,48,384]{3,2,1,0:T(8,128)(2,1)S(1)}, u32[]{:S(2)}, u32[]{:S(2)}) collective-permute-start(bf16[4,4,48,384]{3,2,1,0:T(8,128)(2,1)S(1)} %get-tuple-element.67), channel_id=1, source_target_pairs={{0,1},{1,0},{2,3},{3,2},{4,5},{5,4},{6,7},{7,6},{8,9},{9,8},{10,11... | collective-permute-start | bytes 1769480 | tf_op jit(solution)/shard_map/ppermute | solution.py:334
  46.0 1.3 %collective-permute-start.16 = (bf16[4,8,384]{2,1,0:T(8,128)(2,1)S(1)}, bf16[4,8,384]{2,1,0:T(8,128)(2,1)S(1)}, u32[]{:S(2)}, u32[]{:S(2)}) collective-permute-start(bf16[4,8,384]{2,1,0:T(8,128)(2,1)S(1)} %get-tuple-element.79), channel_id=1, source_target_pairs={{0,1},{1,0},{2,3},{3,2},{4,5},{5,4},{6,7},{7,6},{8,9},{9,8},{10,11... | collective-permute-start | bytes 73736 | tf_op jit(solution)/shard_map/ppermute | solution.py:334
  47.4 13.3 %collective-permute-start.17 = (bf16[4,48,384]{2,1,0:T(8,128)(2,1)S(1)}, bf16[4,48,384]{2,1,0:T(8,128)(2,1)S(1)}, u32[]{:S(2)}, u32[]{:S(2)}) collective-permute-start(bf16[4,48,384]{2,1,0:T(8,128)(2,1)S(1)} %get-tuple-element.81), channel_id=1, source_target_pairs={{0,2},{2,0},{4,6},{6,4},{1,3},{3,1},{5,7},{7,5},{8,10},{10,8},{12,... | collective-permute-start | bytes 442376 | tf_op jit(solution)/shard_map/ppermute | solution.py:334
  47.7 13.9 %collective-permute-start.18 = (bf16[4,48,384]{2,1,0:T(8,128)(2,1)S(1)}, bf16[4,48,384]{2,1,0:T(8,128)(2,1)S(1)}, u32[]{:S(2)}, u32[]{:S(2)}) collective-permute-start(bf16[4,48,384]{2,1,0:T(8,128)(2,1)S(1)} %get-tuple-element.82), channel_id=1, source_target_pairs={{0,4},{2,6},{4,0},{6,2},{1,5},{3,7},{5,1},{7,3},{8,12},{10,14},{12... | collective-permute-start | bytes 442376 | tf_op jit(solution)/shard_map/ppermute | solution.py:334
  49.9 11.8 %collective-permute-start.19 = (bf16[4,48,384]{2,1,0:T(8,128)(2,1)S(1)}, bf16[4,48,384]{2,1,0:T(8,128)(2,1)S(1)}, u32[]{:S(2)}, u32[]{:S(2)}) collective-permute-start(bf16[4,48,384]{2,1,0:T(8,128)(2,1)S(1)} %get-tuple-element.83), channel_id=1, source_target_pairs={{0,6},{2,4},{4,2},{6,0},{1,7},{3,5},{5,3},{7,1},{8,14},{10,12},{12... | collective-permute-start | bytes 442376 | tf_op jit(solution)/shard_map/ppermute | solution.py:334
  61.8 4.0 %collective-permute-start.20 = (bf16[48,384]{1,0:T(8,128)(2,1)S(1)}, bf16[48,384]{1,0:T(8,128)(2,1)S(1)}, u32[]{:S(2)}, u32[]{:S(2)}) collective-permute-start(bf16[48,384]{1,0:T(8,128)(2,1)S(1)} %get-tuple-element.89), channel_id=1, source_target_pairs={{0,8},{8,0},{16,24},{24,16},{1,9},{9,1},{17,25},{25,17},{2,10},{10... | collective-permute-start | bytes 110600 | tf_op jit(solution)/shard_map/ppermute | solution.py:334
  63.1 4.0 %collective-permute-start.21 = (bf16[48,384]{1,0:T(8,128)(2,1)S(1)}, bf16[48,384]{1,0:T(8,128)(2,1)S(1)}, u32[]{:S(2)}, u32[]{:S(2)}) collective-permute-start(bf16[48,384]{1,0:T(8,128)(2,1)S(1)} %get-tuple-element.90), channel_id=1, source_target_pairs={{0,16},{8,24},{16,0},{24,8},{1,17},{9,25},{17,1},{25,9},{2,18},{10... | collective-permute-start | bytes 110600 | tf_op jit(solution)/shard_map/ppermute | solution.py:334
  63.9 4.9 %collective-permute-start.22 = (bf16[48,384]{1,0:T(8,128)(2,1)S(1)}, bf16[48,384]{1,0:T(8,128)(2,1)S(1)}, u32[]{:S(2)}, u32[]{:S(2)}) collective-permute-start(bf16[48,384]{1,0:T(8,128)(2,1)S(1)} %get-tuple-element.91), channel_id=1, source_target_pairs={{0,24},{8,16},{16,8},{24,0},{1,25},{9,17},{17,9},{25,1},{2,26},{10... | collective-permute-start | bytes 110600 | tf_op jit(solution)/shard_map/ppermute | solution.py:334

commit v4 on v3

--- a/solution.py
+++ b/solution.py
@@ -108,6 +108,17 @@
         refs[-1][q] = refs[q][...]
 
 
+def join_kernel(groups, _, __, *refs):
+    blocks_d, blocks_x, own_x, own_d = refs[:groups], refs[groups:-2], refs[-2], refs[-1]
+    for q in range(groups):
+        own_d[q] = blocks_d[q][...]
+    if len(blocks_x) == 1:
+        own_x[...] = blocks_x[0][...]
+    else:
+        for k in range(len(blocks_x)):
+            own_x[k] = blocks_x[k][...]
+
+
 def pick_kernel(relative, experts, hops, pos_ref, *refs):
     sources, sends = refs[: len(refs) - experts], refs[len(refs) - experts :]
     merged = chosen(pos_ref[...], experts)
@@ -150,18 +161,10 @@
     copy.wait()
 
 
-def reader(relative, hops, refs):
-    if relative:
-        return lambda side, q, k: refs[2 * side + k // 3][k % 3, q]
-    return lambda side, q, k: refs[side][k, q]
-
-
 def forward_kernel(relative, groups, hops, *refs):
-    inputs = 4 if relative else 2
-    take = reader(relative, hops, refs[:inputs])
-    gate_ref, up_ref, down_ref, _ = refs[inputs : inputs + 4]
+    sides, (gate_ref, up_ref, down_ref) = refs[:2], refs[2:5]
     x_ref, hid_ref, active_ref, slope_ref, gates_ref, rival_ref, other_ref, keep_ref, give_ref, total = refs[
-        inputs + 4 :
+        5:
     ]
     width = keep_ref.shape[-1]
     model = x_ref.shape[1]
@@ -170,14 +173,14 @@
 
     def place(side, k, features):
         for q in range(groups):
-            x_ref[q * ROWS : (q + 1) * ROWS, features] = take(side, q, k)
+            x_ref[q * ROWS : (q + 1) * ROWS, features] = sides[side][k, q]
 
     visit(groups, hops, width, relative, place)
     for q in range(groups):
         logit = jnp.zeros((META, ROWS), F32)
         for k in range(hops):
             for side in range(2):
-                meta = take(side, q, k).astype(F32)[CAP:, :ROWS]
+                meta = sides[side][k, q].astype(F32)[CAP:, :ROWS]
                 logit = logit + meta
         gap = column(logit[0:1] + logit[1:2] + logit[2:3])
         here = slice(q * ROWS, (q + 1) * ROWS)
@@ -268,13 +271,6 @@
         put(out_refs[k], keep_ref[k] + got_ref[k].astype(F32), router)
 
 
-def relay_kernel(own_ref, near_ref, second_ref, _, __, ___, three_ref, relay_ref):
-    three_ref[0] = own_ref[...]
-    three_ref[1] = near_ref[...]
-    three_ref[2] = second_ref[...]
-    relay_ref[...] = second_ref[...]
-
-
 def put(out_ref, blocks, router):
     groups, height, width = out_ref.shape
     spare = height - CAP - router.shape[0]
@@ -411,24 +407,21 @@
         [shape((groups, ROWS, width), BF16)],
         "stack",
     )
-    if relative:
-        near, second = swap(stacked, "z", 1), swap(stacked, "z", 2)
-        three, relay = call(
-            relay_kernel,
-            (stacked, near, second, up_mark, down_mark, picked[0]),
-            [shape((3, *stacked.shape), BF16), shape(stacked.shape, BF16)],
-            "relay",
-        )
-        blocks = [three, swap(relay, "z", 1)[None]]
-    else:
-        blocks = gather(stacked)
-    blocks = blocks + [swap(block, "core", 1) for block in blocks]
+    blocks_x = [stacked] + [swap(stacked, "z", k) for k in range(1, hops)] if relative else gather(stacked)
     blocks_d = [picked[0]] + [swap(picked[q], "expert", q) for q in range(1, groups)]
+    own_x, own_d = call(
+        functools.partial(join_kernel, groups),
+        (up_mark, down_mark, *blocks_d, *blocks_x),
+        [shape((hops, *stacked.shape), BF16), shape((groups, *picked[0].shape), BF16)],
+        "join",
+    )
+    far_x = swap(own_x, "core", 1)
+    far_d = swap(own_d, "core", 1)
 
     cost = 2 * rows * model * units
     rows_x, hidden, active, slope, gates, rival, others, keep, give = call(
         functools.partial(forward_kernel, relative, groups, hops),
-        (*blocks, gate_w, up_w, down_w, picked[0]),
+        (own_x, far_x, gate_w, up_w, down_w),
         [
             shape((rows, model), BF16),
             shape((rows, units), BF16),
@@ -446,13 +439,6 @@
         limit=16 * MIB,
     )
     got = swap(give, "core", 1)
-    (own_d,) = call(
-        functools.partial(stack_kernel, groups),
-        (*blocks_d, gates),
-        [shape((groups, hops, CAP, width), BF16)],
-        "stack_d",
-    )
-    far_d = swap(own_d, "core", 1)
     rows_d, d_gate, d_up, router_keep, router_give = call(
         functools.partial(backward_kernel, relative, groups, hops),
         (own_d, far_d, rows_x, active, slope, hidden, gates, rival, others, down_w),
@@ -476,7 +462,7 @@
         "merge",
     )
     if relative:
-        outs = [merged[0]] + [swap(merged[k], "z", k) for k in range(1, hops)]
+        outs = [merged[0]] + [swap(merged[k], "z", k) for k in range(hops - 1, 0, -1)]
     else:
         outs = lax.all_to_all(jnp.stack(merged), "z", split_axis=0, concat_axis=0, tiled=True)
         outs = [outs[k] for k in range(hops)]

time: 69.9 us -> 68.5 us (0.980)
  waiting for transfers between devices: 16.7 us -> 12.9 us
  starting transfers between devices: 24.3 us -> 26.9 us
    ppermute x23 -> x22, waiting for transfers between devices: 16.7 us -> 12.9 us  [swap(): return lax.ppermute(block, axis, [(i, i ^ bits) for i in range(size)])]
    ppermute x23 -> x22, starting transfers between devices: 24.3 us -> 26.9 us  [swap(): return lax.ppermute(block, axis, [(i, i ^ bits) for i in range(size)])]
    pallas_call x13 -> x12, Pallas kernels: 19 us -> 18.8 us  [call(): pl.pallas_call(kernel, out_shape=tuple(outs), in_specs=[fixed if i in loo...]
  transfers between devices with their start and end apart: 23 -> 22, of which waited for: 10 -> 9; matrix products, arithmetic and copies ran while one was open for 0% -> 0% of each run, Pallas kernels for 36% -> 37%
where the time goes in v4:
time: 68.5 us; the launch traced here: 68.3 us
  Pallas kernels  27.7 us (40%)
  starting transfers between devices  26.9 us (39%)
  waiting for transfers between devices  12.9 us (19%)
  between operations  0.79 us (1%)
    ppermute x22, starting transfers between devices, swap(): return lax.ppermute(block, axis, [(i, i ^ bits) for i in range(size)])  26.9 us
    pallas_call x12, Pallas kernels, call(): pl.pallas_call(kernel, out_shape=tuple(outs), in_specs=[fixed if i in loo...  18.8 us
    ppermute x22, waiting for transfers between devices, swap(): return lax.ppermute(block, axis, [(i, i ^ bits) for i in range(size)])  12.9 us
    pallas_call x1, Pallas kernels, shards(): pl.pallas_call(grads_kernel, grid=(parts,), out_shape=(shape(w_gate.shape...  8.84 us
  transfers between devices with their start and end apart: 22, of which 9 were waited for; matrix products, arithmetic and copies ran while one was open for 0% of the time, Pallas kernels for 37%

profile of v4, /device:TPU:0, one launch (start us, length us, event | category | flops | bytes accessed | tf_op | source)
XLA Modules:
  0.0 68.3 jit_solution(10271950072789445510)
XLA Ops:
  0.6 1.6 %pack.1 = (s32[1,256]{1,0:T(1,128)S(1)}, bf16[128,384]{1,0:T(8,128)(2,1)S(1)}, bf16[48,384]{1,0:T(8,128)(2,1)S(1)}, bf16[48,384]{1,0:T(8,128)(2,1)S(1)}, bf16[48...) custom-call(s32[4]{0:T(128)} %refs_0_.1, s32[4]{0:T(128)} %refs_1_.1, s32[2,128]{1,0:T(2,128)} %bitcast.4, ...), custom_call_target="tpu_custom_call" | custom-call | tf_op jit(solution)/shard_map/pack/pallas_call | solution.py:349
  2.2 4.1 %collective-permute-start.1 = (bf16[128,384]{1,0:T(8,128)(2,1)S(1)}, bf16[128,384]{1,0:T(8,128)(2,1)S(1)}, u32[]{:S(2)}, u32[]{:S(2)}) collective-permute-start(bf16[128,384]{1,0:T(8,128)(2,1)S(1)} %get-tuple-element.54.refs_0_), channel_id=1, source_target_pairs={{0,4},{2,6},{4,0},{6,2},{1,5},{3,7},{5,1},{7,3},{8,12},{10,14},{12... | collective-permute-start | bytes 294920 | tf_op jit(solution)/shard_map/ppermute | solution.py:330
  6.3 1.6 %collective-permute-start = (bf16[128,384]{1,0:T(8,128)(2,1)S(1)}, bf16[128,384]{1,0:T(8,128)(2,1)S(1)}, u32[]{:S(2)}, u32[]{:S(2)}) collective-permute-start(bf16[128,384]{1,0:T(8,128)(2,1)S(1)} %get-tuple-element.54.refs_0_), channel_id=1, source_target_pairs={{0,2},{2,0},{4,6},{6,4},{1,3},{3,1},{5,7},{7,5},{8,10},{10,8},{12,... | collective-permute-start | bytes 294920 | tf_op jit(solution)/shard_map/ppermute | solution.py:330
  7.9 1.5 %collective-permute-start.6 = (bf16[48,384]{1,0:T(8,128)(2,1)S(1)}, bf16[48,384]{1,0:T(8,128)(2,1)S(1)}, u32[]{:S(2)}, u32[]{:S(2)}) collective-permute-start(bf16[48,384]{1,0:T(8,128)(2,1)S(1)} %get-tuple-element.60), channel_id=1, source_target_pairs={{0,8},{8,0},{16,24},{24,16},{1,9},{9,1},{17,25},{25,17},{2,10},{10... | collective-permute-start | bytes 110600 | tf_op jit(solution)/shard_map/ppermute | solution.py:330
  9.4 1.5 %collective-permute-start.7 = (bf16[48,384]{1,0:T(8,128)(2,1)S(1)}, bf16[48,384]{1,0:T(8,128)(2,1)S(1)}, u32[]{:S(2)}, u32[]{:S(2)}) collective-permute-start(bf16[48,384]{1,0:T(8,128)(2,1)S(1)} %get-tuple-element.61), channel_id=1, source_target_pairs={{0,16},{8,24},{16,0},{24,8},{1,17},{9,25},{17,1},{25,9},{2,18},{10... | collective-permute-start | bytes 110600 | tf_op jit(solution)/shard_map/ppermute | solution.py:330
  10.9 0.5 collective-permute-start.8
  11.4 2.8 %load_gate.1 = (bf16[1,3072,1024]{2,1,0:T(8,128)(2,1)S(1)}, f32[8,128]{1,0:T(8,128)S(1)}) custom-call(bf16[1,3072,1024]{2,1,0:T(8,128)(2,1)} %source.5), custom_call_target="tpu_custom_call" | custom-call | bytes 12582912 | tf_op jit(solution)/shard_map/load_gate/pallas_call | solution.py:349
  14.2 0.0 collective-permute-done.6.refs_1_
  14.2 0.0 collective-permute-done.7.refs_2_
  14.2 1.6 %collective-permute-done.8.refs_3_ = bf16[48,384]{1,0:T(8,128)(2,1)S(1)} collective-permute-done((bf16[48,384]{1,0:T(8,128)(2,1)S(1)}, bf16[48,384]{1,0:T(8,128)(2,1)S(1)}, u32[]{:S(2)}, u32[]{:S(2)}) %collective-permute-start.8) | collective-permute-done | bytes 36896 | tf_op jit(solution)/shard_map/ppermute | solution.py:330
  15.8 0.0 collective-permute-done.1.refs_2_.refs_6_
  15.8 0.0 collective-permute-done.refs_1_.refs_5_
  15.8 0.4 collective-permute-start.10
  16.2 0.5 collective-permute-start.2
  16.6 3.6 %collective-permute-start.11 = (bf16[4,48,384]{2,1,0:T(8,128)(2,1)S(1)}, bf16[4,48,384]{2,1,0:T(8,128)(2,1)S(1)}, u32[]{:S(2)}, u32[]{:S(2)}) collective-permute-start(bf16[4,48,384]{2,1,0:T(8,128)(2,1)S(1)} %stack.1.refs_4_), channel_id=1, source_target_pairs={{0,6},{2,4},{4,2},{6,0},{1,7},{3,5},{5,3},{7,1},{8,14},{10,12},{12... | collective-permute-start | bytes 442376 | tf_op jit(solution)/shard_map/ppermute | solution.py:330
  20.2 0.0 collective-permute-start.9
  20.2 4.4 %collective-permute-done.2.refs_3_ = bf16[128,384]{1,0:T(8,128)(2,1)S(1)} collective-permute-done((bf16[128,384]{1,0:T(8,128)(2,1)S(1)}, bf16[128,384]{1,0:T(8,128)(2,1)S(1)}, u32[]{:S(2)}, u32[]{:S(2)}) %collective-permute-start.2) | collective-permute-done | bytes 98336 | tf_op jit(solution)/shard_map/ppermute | solution.py:330
  24.6 0.3 pick.1
  24.9 0.3 collective-permute-start.3
  25.3 2.2 %collective-permute-start.4 = (bf16[4,40,384]{2,1,0:T(8,128)(2,1)S(1)}, bf16[4,40,384]{2,1,0:T(8,128)(2,1)S(1)}, u32[]{:S(2)}, u32[]{:S(2)}) collective-permute-start(bf16[4,40,384]{2,1,0:T(8,128)(2,1)S(1)} %get-tuple-element.57), channel_id=1, source_target_pairs={{0,16},{8,24},{16,0},{24,8},{1,17},{9,25},{17,1},{25,9},{2,18},{10... | collective-permute-start | bytes 368648 | tf_op jit(solution)/shard_map/ppermute | solution.py:330
  27.4 0.2 collective-permute-done.10.refs_6_
  27.6 1.6 %collective-permute-start.5 = (bf16[4,40,384]{2,1,0:T(8,128)(2,1)S(1)}, bf16[4,40,384]{2,1,0:T(8,128)(2,1)S(1)}, u32[]{:S(2)}, u32[]{:S(2)}) collective-permute-start(bf16[4,40,384]{2,1,0:T(8,128)(2,1)S(1)} %get-tuple-element.58), channel_id=1, source_target_pairs={{0,24},{8,16},{16,8},{24,0},{1,25},{9,17},{17,9},{25,1},{2,26},{10... | collective-permute-start | bytes 368648 | tf_op jit(solution)/shard_map/ppermute | solution.py:330
  29.2 2.8 %load_up.1 = (bf16[1,3072,1024]{2,1,0:T(8,128)(2,1)S(1)}, f32[8,128]{1,0:T(8,128)S(1)}) custom-call(bf16[1,3072,1024]{2,1,0:T(8,128)(2,1)} %source.3), custom_call_target="tpu_custom_call" | custom-call | bytes 12582912 | tf_op jit(solution)/shard_map/load_up/pallas_call | solution.py:349
  32.0 2.8 %load_down.1 = (bf16[1,1024,3072]{2,1,0:T(8,128)(2,1)S(1)}, f32[8,128]{1,0:T(8,128)S(1)}) custom-call(bf16[1,1024,3072]{2,1,0:T(8,128)(2,1)} %source.4), custom_call_target="tpu_custom_call" | custom-call | bytes 12582912 | tf_op jit(solution)/shard_map/load_down/pallas_call | solution.py:349
  34.8 0.0 collective-permute-done.11.refs_7_
  34.8 0.0 collective-permute-done.9.refs_5_
  34.8 0.0 collective-permute-done.3.refs_1_
  34.8 0.0 collective-permute-done.4.refs_2_
  34.8 0.0 collective-permute-done.5.refs_3_
  34.8 0.1 join.1
  34.9 0.1 collective-permute-start.12
  35.0 0.5 collective-permute-start.14
  35.5 1.5 %collective-permute-done.12.refs_1_ = bf16[4,4,48,384]{3,2,1,0:T(8,128)(2,1)S(1)} collective-permute-done((bf16[4,4,48,384]{3,2,1,0:T(8,128)(2,1)S(1)}, bf16[4,4,48,384]{3,2,1,0:T(8,128)(2,1)S(1)}, u32[]{:S(2)}, u32[]{:S(2)}) %collective-permute-start.12) | collective-permute-done | bytes 589856 | tf_op jit(solution)/shard_map/ppermute | solution.py:330
  37.0 4.2 %forward.1 = (bf16[192,3072]{1,0:T(8,128)(2,1)S(1)}, bf16[192,1024]{1,0:T(8,128)(2,1)S(1)}, f32[192,1024]{1,0:T(8,128)S(1)}, f32[192,1024]{1,0:T(8,128)S(1)}, f3...) custom-call(bf16[4,4,48,384]{3,2,1,0:T(8,128)(2,1)S(1)} %get-tuple-e, ...), custom_call_target="tpu_custom_call" | custom-call | flops 3623878656 | bytes 18874368 | tf_op jit(solution)/shard_map/forward/pallas_call | solution.py:349
  41.2 0.2 collective-permute-start.13
  41.4 0.0 collective-permute-done.14.refs_1_
  41.4 3.2 %backward.1 = (bf16[192,3072]{1,0:T(8,128)(2,1)S(1)}, bf16[192,1024]{1,0:T(8,128)(2,1)S(1)}, bf16[192,1024]{1,0:T(8,128)(2,1)S(1)}, f32[4,4,384]{2,1,0:T(4,128)S(1)}, bf16[4,8,384]{2,1,0:T(8,128)(2,1)S(1)}) custom-call(bf16[4,4,40,384]{3,2,1,0:T(8,128)(2,1)S(1)} %get-tuple-element.70.refs_0_, bf16[4,4,40,384]{3,2,1,0:T(8,128)(2,1)S(1)} %collective-permute-done.14.refs_1_, ...), custom_call_target="tpu_custom_call" | custom-call | flops 1207959552 | bytes 6291456 | tf_op jit(solution)/shard_map/backward/pallas_call | solution.py:349
  44.7 0.5 collective-permute-start.15
  45.1 0.8 %collective-permute-done.15.rgot_ref = bf16[4,8,384]{2,1,0:T(8,128)(2,1)S(1)} collective-permute-done((bf16[4,8,384]{2,1,0:T(8,128)(2,1)S(1)}, bf16[4,8,384]{2,1,0:T(8,128)(2,1)S(1)}, u32[]{:S(2)}, u32[]{:S(2)}) %collective-permute-start.15) | collective-permute-done | bytes 24608 | tf_op jit(solution)/shard_map/ppermute | solution.py:330
  46.0 0.0 collective-permute-done.13.got_ref
  46.0 0.1 merge.1
  46.1 2.3 %collective-permute-start.16 = (bf16[4,48,384]{2,1,0:T(8,128)(2,1)S(1)}, bf16[4,48,384]{2,1,0:T(8,128)(2,1)S(1)}, u32[]{:S(2)}, u32[]{:S(2)}) collective-permute-start(bf16[4,48,384]{2,1,0:T(8,128)(2,1)S(1)} %get-tuple-element.81), channel_id=1, source_target_pairs={{0,6},{2,4},{4,2},{6,0},{1,7},{3,5},{5,3},{7,1},{8,14},{10,12},{12... | collective-permute-start | bytes 442376 | tf_op jit(solution)/shard_map/ppermute | solution.py:330
  48.4 0.0 collective-permute-start.17
  48.4 2.2 %collective-permute-start.18 = (bf16[4,48,384]{2,1,0:T(8,128)(2,1)S(1)}, bf16[4,48,384]{2,1,0:T(8,128)(2,1)S(1)}, u32[]{:S(2)}, u32[]{:S(2)}) collective-permute-start(bf16[4,48,384]{2,1,0:T(8,128)(2,1)S(1)} %get-tuple-element.83), channel_id=1, source_target_pairs={{0,2},{2,0},{4,6},{6,4},{1,3},{3,1},{5,7},{7,5},{8,10},{10,8},{12,... | collective-permute-start | bytes 442376 | tf_op jit(solution)/shard_map/ppermute | solution.py:330
  50.5 8.8 %grads.1 = (bf16[1,3072,1024]{2,1,0:T(8,128)(2,1)}, bf16[1,3072,1024]{2,1,0:T(8,128)(2,1)}, bf16[1,1024,3072]{2,1,0:T(8,128)(2,1)}, f32[8,128]{1,0:T(8,128)S(1)}) custom-call(bf16[192,3072]{1,0:T(8,128)(2,1)S(1)} %get-tuple-element.71.refs_2_.x_ref, bf16[192,3072]{1,0:T(8,128)(2,1)S(1)} %get-tuple-element.84.d_ref, ...), custom_call_target="tpu_custom_call" | custom-call | flops 3623878656 | bytes 18874368 | tf_op jit(solution)/shard_map/grads/pallas_call | solution.py:474
  59.4 0.0 collective-permute-done.16.refs_1_
  59.4 1.3 %collective-permute-done.17.refs_2_ = bf16[4,48,384]{2,1,0:T(8,128)(2,1)S(1)} collective-permute-done((bf16[4,48,384]{2,1,0:T(8,128)(2,1)S(1)}, bf16[4,48,384]{2,1,0:T(8,128)(2,1)S(1)}, u32[]{:S(2)}, u32[]{:S(2)}) %collective-permute-start.17) | collective-permute-done | bytes 147488 | tf_op jit(solution)/shard_map/ppermute | solution.py:330
  60.7 0.0 collective-permute-done.18.refs_3_
  60.7 0.1 total.1
  60.8 0.8 %collective-permute-start.19 = (bf16[48,384]{1,0:T(8,128)(2,1)S(1)}, bf16[48,384]{1,0:T(8,128)(2,1)S(1)}, u32[]{:S(2)}, u32[]{:S(2)}) collective-permute-start(bf16[48,384]{1,0:T(8,128)(2,1)S(1)} %get-tuple-element.89), channel_id=1, source_target_pairs={{0,8},{8,0},{16,24},{24,16},{1,9},{9,1},{17,25},{25,17},{2,10},{10... | collective-permute-start | bytes 110600 | tf_op jit(solution)/shard_map/ppermute | solution.py:330
  61.6 1.0 %collective-permute-start.20 = (bf16[48,384]{1,0:T(8,128)(2,1)S(1)}, bf16[48,384]{1,0:T(8,128)(2,1)S(1)}, u32[]{:S(2)}, u32[]{:S(2)}) collective-permute-start(bf16[48,384]{1,0:T(8,128)(2,1)S(1)} %get-tuple-element.90), channel_id=1, source_target_pairs={{0,16},{8,24},{16,0},{24,8},{1,17},{9,25},{17,1},{25,9},{2,18},{10... | collective-permute-start | bytes 110600 | tf_op jit(solution)/shard_map/ppermute | solution.py:330
  62.6 1.8 %collective-permute-start.21 = (bf16[48,384]{1,0:T(8,128)(2,1)S(1)}, bf16[48,384]{1,0:T(8,128)(2,1)S(1)}, u32[]{:S(2)}, u32[]{:S(2)}) collective-permute-start(bf16[48,384]{1,0:T(8,128)(2,1)S(1)} %get-tuple-element.91), channel_id=1, source_target_pairs={{0,24},{8,16},{16,8},{24,0},{1,25},{9,17},{17,9},{25,1},{2,26},{10... | collective-permute-start | bytes 110600 | tf_op jit(solution)/shard_map/ppermute | solution.py:330
  64.3 0.5 collective-permute-done.19.refs_1_
  64.8 0.7 %collective-permute-done.20.refs_2_ = bf16[48,384]{1,0:T(8,128)(2,1)S(1)} collective-permute-done((bf16[48,384]{1,0:T(8,128)(2,1)S(1)}, bf16[48,384]{1,0:T(8,128)(2,1)S(1)}, u32[]{:S(2)}, u32[]{:S(2)}) %collective-permute-start.20) | collective-permute-done | bytes 36896 | tf_op jit(solution)/shard_map/ppermute | solution.py:330
  65.5 1.9 %collective-permute-done.21.refs_3_ = bf16[48,384]{1,0:T(8,128)(2,1)S(1)} collective-permute-done((bf16[48,384]{1,0:T(8,128)(2,1)S(1)}, bf16[48,384]{1,0:T(8,128)(2,1)S(1)}, u32[]{:S(2)}, u32[]{:S(2)}) %collective-permute-start.21) | collective-permute-done | bytes 36896 | tf_op jit(solution)/shard_map/ppermute | solution.py:330
  67.4 0.9 %combine.1 = (bf16[128,384]{1,0:T(8,128)(2,1)}, bf16[4,384]{1,0:T(4,128)(2,1)}) custom-call(s32[1,256]{1,0:T(1,128)S(1)} %get-tuple-element.51.pos_ref, bf16[48,384]{1,0:T(8,128)(2,1)S(1)} %get-tuple-element.88.refs_0_, bf16[48,384]{1,0:T(8,128)(2,1)S(1)} %collective-permute-done.19.refs_1_, bf16[48,384]{1,0:T(8,128)(2,1)S(1)} %collective-permute-done.20.refs_2_, ...), custom_call_target="tpu_custom_call" | custom-call | tf_op jit(solution)/shard_map/combine/pallas_call | solution.py:349
  (1 shorter events, 0.0 us)
Async XLA Ops:
  2.2 13.6 %collective-permute-start.1 = (bf16[128,384]{1,0:T(8,128)(2,1)S(1)}, bf16[128,384]{1,0:T(8,128)(2,1)S(1)}, u32[]{:S(2)}, u32[]{:S(2)}) collective-permute-start(bf16[128,384]{1,0:T(8,128)(2,1)S(1)} %get-tuple-element.54.refs_0_), channel_id=1, source_target_pairs={{0,4},{2,6},{4,0},{6,2},{1,5},{3,7},{5,1},{7,3},{8,12},{10,14},{12... | collective-permute-start | bytes 294920 | tf_op jit(solution)/shard_map/ppermute | solution.py:330
  6.3 9.5 %collective-permute-start = (bf16[128,384]{1,0:T(8,128)(2,1)S(1)}, bf16[128,384]{1,0:T(8,128)(2,1)S(1)}, u32[]{:S(2)}, u32[]{:S(2)}) collective-permute-start(bf16[128,384]{1,0:T(8,128)(2,1)S(1)} %get-tuple-element.54.refs_0_), channel_id=1, source_target_pairs={{0,2},{2,0},{4,6},{6,4},{1,3},{3,1},{5,7},{7,5},{8,10},{10,8},{12,... | collective-permute-start | bytes 294920 | tf_op jit(solution)/shard_map/ppermute | solution.py:330
  7.9 6.3 %collective-permute-start.6 = (bf16[48,384]{1,0:T(8,128)(2,1)S(1)}, bf16[48,384]{1,0:T(8,128)(2,1)S(1)}, u32[]{:S(2)}, u32[]{:S(2)}) collective-permute-start(bf16[48,384]{1,0:T(8,128)(2,1)S(1)} %get-tuple-element.60), channel_id=1, source_target_pairs={{0,8},{8,0},{16,24},{24,16},{1,9},{9,1},{17,25},{25,17},{2,10},{10... | collective-permute-start | bytes 110600 | tf_op jit(solution)/shard_map/ppermute | solution.py:330
  9.4 4.8 %collective-permute-start.7 = (bf16[48,384]{1,0:T(8,128)(2,1)S(1)}, bf16[48,384]{1,0:T(8,128)(2,1)S(1)}, u32[]{:S(2)}, u32[]{:S(2)}) collective-permute-start(bf16[48,384]{1,0:T(8,128)(2,1)S(1)} %get-tuple-element.61), channel_id=1, source_target_pairs={{0,16},{8,24},{16,0},{24,8},{1,17},{9,25},{17,1},{25,9},{2,18},{10... | collective-permute-start | bytes 110600 | tf_op jit(solution)/shard_map/ppermute | solution.py:330
  10.9 4.9 %collective-permute-start.8 = (bf16[48,384]{1,0:T(8,128)(2,1)S(1)}, bf16[48,384]{1,0:T(8,128)(2,1)S(1)}, u32[]{:S(2)}, u32[]{:S(2)}) collective-permute-start(bf16[48,384]{1,0:T(8,128)(2,1)S(1)} %get-tuple-element.62), channel_id=1, source_target_pairs={{0,24},{8,16},{16,8},{24,0},{1,25},{9,17},{17,9},{25,1},{2,26},{10... | collective-permute-start | bytes 110600 | tf_op jit(solution)/shard_map/ppermute | solution.py:330
  15.8 11.8 %collective-permute-start.10 = (bf16[4,48,384]{2,1,0:T(8,128)(2,1)S(1)}, bf16[4,48,384]{2,1,0:T(8,128)(2,1)S(1)}, u32[]{:S(2)}, u32[]{:S(2)}) collective-permute-start(bf16[4,48,384]{2,1,0:T(8,128)(2,1)S(1)} %stack.1.refs_4_), channel_id=1, source_target_pairs={{0,4},{2,6},{4,0},{6,2},{1,5},{3,7},{5,1},{7,3},{8,12},{10,14},{12... | collective-permute-start | bytes 442376 | tf_op jit(solution)/shard_map/ppermute | solution.py:330
  16.2 8.4 %collective-permute-start.2 = (bf16[128,384]{1,0:T(8,128)(2,1)S(1)}, bf16[128,384]{1,0:T(8,128)(2,1)S(1)}, u32[]{:S(2)}, u32[]{:S(2)}) collective-permute-start(bf16[128,384]{1,0:T(8,128)(2,1)S(1)} %collective-permute-done.1.refs_2_.refs_6_), channel_id=1, source_target_pairs={{0,2},{2,0},{4,6},{6,4},{1,3},{3,1},{5,7},{7,5},{8,10},{10,8},{12,... | collective-permute-start | bytes 294920 | tf_op jit(solution)/shard_map/ppermute | solution.py:330
  16.6 18.1 %collective-permute-start.11 = (bf16[4,48,384]{2,1,0:T(8,128)(2,1)S(1)}, bf16[4,48,384]{2,1,0:T(8,128)(2,1)S(1)}, u32[]{:S(2)}, u32[]{:S(2)}) collective-permute-start(bf16[4,48,384]{2,1,0:T(8,128)(2,1)S(1)} %stack.1.refs_4_), channel_id=1, source_target_pairs={{0,6},{2,4},{4,2},{6,0},{1,7},{3,5},{5,3},{7,1},{8,14},{10,12},{12... | collective-permute-start | bytes 442376 | tf_op jit(solution)/shard_map/ppermute | solution.py:330
  20.2 14.6 %collective-permute-start.9 = (bf16[4,48,384]{2,1,0:T(8,128)(2,1)S(1)}, bf16[4,48,384]{2,1,0:T(8,128)(2,1)S(1)}, u32[]{:S(2)}, u32[]{:S(2)}) collective-permute-start(bf16[4,48,384]{2,1,0:T(8,128)(2,1)S(1)} %stack.1.refs_4_), channel_id=1, source_target_pairs={{0,2},{2,0},{4,6},{6,4},{1,3},{3,1},{5,7},{7,5},{8,10},{10,8},{12,... | collective-permute-start | bytes 442376 | tf_op jit(solution)/shard_map/ppermute | solution.py:330
  24.9 9.9 %collective-permute-start.3 = (bf16[4,40,384]{2,1,0:T(8,128)(2,1)S(1)}, bf16[4,40,384]{2,1,0:T(8,128)(2,1)S(1)}, u32[]{:S(2)}, u32[]{:S(2)}) collective-permute-start(bf16[4,40,384]{2,1,0:T(8,128)(2,1)S(1)} %get-tuple-element.56), channel_id=1, source_target_pairs={{0,8},{8,0},{16,24},{24,16},{1,9},{9,1},{17,25},{25,17},{2,10},{10... | collective-permute-start | bytes 368648 | tf_op jit(solution)/shard_map/ppermute | solution.py:330
  25.3 9.6 %collective-permute-start.4 = (bf16[4,40,384]{2,1,0:T(8,128)(2,1)S(1)}, bf16[4,40,384]{2,1,0:T(8,128)(2,1)S(1)}, u32[]{:S(2)}, u32[]{:S(2)}) collective-permute-start(bf16[4,40,384]{2,1,0:T(8,128)(2,1)S(1)} %get-tuple-element.57), channel_id=1, source_target_pairs={{0,16},{8,24},{16,0},{24,8},{1,17},{9,25},{17,1},{25,9},{2,18},{10... | collective-permute-start | bytes 368648 | tf_op jit(solution)/shard_map/ppermute | solution.py:330
  27.6 7.2 %collective-permute-start.5 = (bf16[4,40,384]{2,1,0:T(8,128)(2,1)S(1)}, bf16[4,40,384]{2,1,0:T(8,128)(2,1)S(1)}, u32[]{:S(2)}, u32[]{:S(2)}) collective-permute-start(bf16[4,40,384]{2,1,0:T(8,128)(2,1)S(1)} %get-tuple-element.58), channel_id=1, source_target_pairs={{0,24},{8,16},{16,8},{24,0},{1,25},{9,17},{17,9},{25,1},{2,26},{10... | collective-permute-start | bytes 368648 | tf_op jit(solution)/shard_map/ppermute | solution.py:330
  34.9 2.1 %collective-permute-start.12 = (bf16[4,4,48,384]{3,2,1,0:T(8,128)(2,1)S(1)}, bf16[4,4,48,384]{3,2,1,0:T(8,128)(2,1)S(1)}, u32[]{:S(2)}, u32[]{:S(2)}) collective-permute-start(bf16[4,4,48,384]{3,2,1,0:T(8,128)(2,1)S(1)} %get-tuple-element.64.refs_0_), channel_id=1, source_target_pairs={{0,1},{1,0},{2,3},{3,2},{4,5},{5,4},{6,7},{7,6},{8,9},{9,8},{10,11... | collective-permute-start | bytes 1769480 | tf_op jit(solution)/shard_map/ppermute | solution.py:330
  35.0 6.4 %collective-permute-start.14 = (bf16[4,4,40,384]{3,2,1,0:T(8,128)(2,1)S(1)}, bf16[4,4,40,384]{3,2,1,0:T(8,128)(2,1)S(1)}, u32[]{:S(2)}, u32[]{:S(2)}) collective-permute-start(bf16[4,4,40,384]{3,2,1,0:T(8,128)(2,1)S(1)} %get-tuple-element.70.refs_0_), channel_id=1, source_target_pairs={{0,1},{1,0},{2,3},{3,2},{4,5},{5,4},{6,7},{7,6},{8,9},{9,8},{10,11... | collective-permute-start | bytes 1474568 | tf_op jit(solution)/shard_map/ppermute | solution.py:330
  41.2 4.7 %collective-permute-start.13 = (bf16[4,4,48,384]{3,2,1,0:T(8,128)(2,1)S(1)}, bf16[4,4,48,384]{3,2,1,0:T(8,128)(2,1)S(1)}, u32[]{:S(2)}, u32[]{:S(2)}) collective-permute-start(bf16[4,4,48,384]{3,2,1,0:T(8,128)(2,1)S(1)} %get-tuple-element.69), channel_id=1, source_target_pairs={{0,1},{1,0},{2,3},{3,2},{4,5},{5,4},{6,7},{7,6},{8,9},{9,8},{10,11... | collective-permute-start | bytes 1769480 | tf_op jit(solution)/shard_map/ppermute | solution.py:330
  44.7 1.3 %collective-permute-start.15 = (bf16[4,8,384]{2,1,0:T(8,128)(2,1)S(1)}, bf16[4,8,384]{2,1,0:T(8,128)(2,1)S(1)}, u32[]{:S(2)}, u32[]{:S(2)}) collective-permute-start(bf16[4,8,384]{2,1,0:T(8,128)(2,1)S(1)} %get-tuple-element.79), channel_id=1, source_target_pairs={{0,1},{1,0},{2,3},{3,2},{4,5},{5,4},{6,7},{7,6},{8,9},{9,8},{10,11... | collective-permute-start | bytes 73736 | tf_op jit(solution)/shard_map/ppermute | solution.py:330
  46.1 13.3 %collective-permute-start.16 = (bf16[4,48,384]{2,1,0:T(8,128)(2,1)S(1)}, bf16[4,48,384]{2,1,0:T(8,128)(2,1)S(1)}, u32[]{:S(2)}, u32[]{:S(2)}) collective-permute-start(bf16[4,48,384]{2,1,0:T(8,128)(2,1)S(1)} %get-tuple-element.81), channel_id=1, source_target_pairs={{0,6},{2,4},{4,2},{6,0},{1,7},{3,5},{5,3},{7,1},{8,14},{10,12},{12... | collective-permute-start | bytes 442376 | tf_op jit(solution)/shard_map/ppermute | solution.py:330
  48.4 12.3 %collective-permute-start.17 = (bf16[4,48,384]{2,1,0:T(8,128)(2,1)S(1)}, bf16[4,48,384]{2,1,0:T(8,128)(2,1)S(1)}, u32[]{:S(2)}, u32[]{:S(2)}) collective-permute-start(bf16[4,48,384]{2,1,0:T(8,128)(2,1)S(1)} %get-tuple-element.82), channel_id=1, source_target_pairs={{0,4},{2,6},{4,0},{6,2},{1,5},{3,7},{5,1},{7,3},{8,12},{10,14},{12... | collective-permute-start | bytes 442376 | tf_op jit(solution)/shard_map/ppermute | solution.py:330
  48.4 12.3 %collective-permute-start.18 = (bf16[4,48,384]{2,1,0:T(8,128)(2,1)S(1)}, bf16[4,48,384]{2,1,0:T(8,128)(2,1)S(1)}, u32[]{:S(2)}, u32[]{:S(2)}) collective-permute-start(bf16[4,48,384]{2,1,0:T(8,128)(2,1)S(1)} %get-tuple-element.83), channel_id=1, source_target_pairs={{0,2},{2,0},{4,6},{6,4},{1,3},{3,1},{5,7},{7,5},{8,10},{10,8},{12,... | collective-permute-start | bytes 442376 | tf_op jit(solution)/shard_map/ppermute | solution.py:330
  60.8 4.0 %collective-permute-start.19 = (bf16[48,384]{1,0:T(8,128)(2,1)S(1)}, bf16[48,384]{1,0:T(8,128)(2,1)S(1)}, u32[]{:S(2)}, u32[]{:S(2)}) collective-permute-start(bf16[48,384]{1,0:T(8,128)(2,1)S(1)} %get-tuple-element.89), channel_id=1, source_target_pairs={{0,8},{8,0},{16,24},{24,16},{1,9},{9,1},{17,25},{25,17},{2,10},{10... | collective-permute-start | bytes 110600 | tf_op jit(solution)/shard_map/ppermute | solution.py:330
  61.6 4.0 %collective-permute-start.20 = (bf16[48,384]{1,0:T(8,128)(2,1)S(1)}, bf16[48,384]{1,0:T(8,128)(2,1)S(1)}, u32[]{:S(2)}, u32[]{:S(2)}) collective-permute-start(bf16[48,384]{1,0:T(8,128)(2,1)S(1)} %get-tuple-element.90), channel_id=1, source_target_pairs={{0,16},{8,24},{16,0},{24,8},{1,17},{9,25},{17,1},{25,9},{2,18},{10... | collective-permute-start | bytes 110600 | tf_op jit(solution)/shard_map/ppermute | solution.py:330
  62.6 4.9 %collective-permute-start.21 = (bf16[48,384]{1,0:T(8,128)(2,1)S(1)}, bf16[48,384]{1,0:T(8,128)(2,1)S(1)}, u32[]{:S(2)}, u32[]{:S(2)}) collective-permute-start(bf16[48,384]{1,0:T(8,128)(2,1)S(1)} %get-tuple-element.91), channel_id=1, source_target_pairs={{0,24},{8,16},{16,8},{24,0},{1,25},{9,17},{17,9},{25,1},{2,26},{10... | collective-permute-start | bytes 110600 | tf_op jit(solution)/shard_map/ppermute | solution.py:330

commit v5 on v4

--- a/solution.py
+++ b/solution.py
@@ -14,6 +14,7 @@
 ROWS = CAP + META
 MIB = 1024 * 1024
 LANES = 128
+PARTS = 4
 
 F32 = jnp.float32
 BF16 = jnp.bfloat16
@@ -108,19 +109,17 @@
         refs[-1][q] = refs[q][...]
 
 
-def join_kernel(groups, _, __, *refs):
-    blocks_d, blocks_x, own_x, own_d = refs[:groups], refs[groups:-2], refs[-2], refs[-1]
-    for q in range(groups):
-        own_d[q] = blocks_d[q][...]
-    if len(blocks_x) == 1:
-        own_x[...] = blocks_x[0][...]
+def join_kernel(*refs):
+    blocks, out_ref = refs[:-2], refs[-1]
+    if len(blocks) == 1:
+        out_ref[...] = blocks[0][...]
     else:
-        for k in range(len(blocks_x)):
-            own_x[k] = blocks_x[k][...]
+        for k, block in enumerate(blocks):
+            out_ref[k] = block[...]
 
 
 def pick_kernel(relative, experts, hops, pos_ref, *refs):
-    sources, sends = refs[: len(refs) - experts], refs[len(refs) - experts :]
+    sources, sends = refs[: len(refs) - experts - 2], refs[len(refs) - experts :]
     merged = chosen(pos_ref[...], experts)
     for k in range(hops):
         rows = dot(merged, sources[k][...] if relative else sources[0][k], ((1,), (0,)))
@@ -154,17 +153,22 @@
                     body(side, k, pl.ds(at, width))
 
 
-def load_kernel(source, out, mark, sem):
+def load_kernel(start, source, out, mark, sems):
     mark[...] = jnp.zeros(mark.shape, F32)
-    copy = pltpu.make_async_copy(source, out, sem)
-    copy.start()
-    copy.wait()
+    copies = []
+    part = out.shape[0] // PARTS
+    for n in range(PARTS):
+        there = source.at[0, pl.ds(start + n * part, part)]
+        copies.append(pltpu.make_async_copy(there, out.at[pl.ds(n * part, part)], sems.at[n]))
+        copies[-1].start()
+    for copy in copies:
+        copy.wait()
 
 
 def forward_kernel(relative, groups, hops, *refs):
-    sides, (gate_ref, up_ref, down_ref) = refs[:2], refs[2:5]
+    sides, (gate_ref, up_a_ref, up_b_ref, down_ref) = refs[:2], refs[2:6]
     x_ref, hid_ref, active_ref, slope_ref, gates_ref, rival_ref, other_ref, keep_ref, give_ref, total = refs[
-        5:
+        7:
     ]
     width = keep_ref.shape[-1]
     model = x_ref.shape[1]
@@ -189,10 +193,12 @@
         other_ref[here, :] = column(meta[3:4])
 
     rows_x = x_ref[...]
+    half = up_a_ref.shape[0]
     for f in range(0, units, tile):
         now = slice(f, f + tile)
-        gate_pre = dot(rows_x, gate_ref[0, :, now], ((1,), (0,)))
-        up_pre = dot(rows_x, up_ref[0, :, now], ((1,), (0,)))
+        gate_pre = dot(rows_x, gate_ref[:, now], ((1,), (0,)))
+        up_pre = dot(rows_x[:, :half], up_a_ref[:, now], ((1,), (0,)))
+        up_pre = up_pre + dot(rows_x[:, half:], up_b_ref[:, now], ((1,), (0,)))
         sigma = jax.nn.sigmoid(gate_pre)
         active = gate_pre * sigma
         active_ref[:, now] = active
@@ -201,7 +207,7 @@
     hidden = hid_ref[...]
     for f in range(0, model, 512):
         now = slice(f, f + 512)
-        total[:, now] = gates_ref[...] * dot(hidden, down_ref[0, :, now], ((1,), (0,)))
+        total[:, now] = gates_ref[...] * dot(hidden, down_ref[:, now], ((1,), (0,)))
 
     def emit(side, k, features):
         for q in range(groups):
@@ -233,7 +239,7 @@
     dots = jnp.zeros((rows_d.shape[0], 1), F32)
     for f in range(0, units, tile):
         now = slice(f, f + tile)
-        d_hidden = dot(rows_d, down_ref[0, now, :], ((1,), (1,)))
+        d_hidden = dot(rows_d, down_ref[now, :], ((1,), (1,)))
         dgate_ref[:, now] = (d_hidden * slope_ref[:, now]).astype(BF16)
         dup_ref[:, now] = (d_hidden * active_ref[:, now]).astype(BF16)
         dots += jnp.sum(hid_ref[:, now].astype(F32) * d_hidden, axis=1, keepdims=True)
@@ -372,56 +378,60 @@
         ],
         loose=range(6),
     )
-    def load(weight, name):
+    def load(weight, name, start=0, size=None):
+        height, length = size or weight.shape[1], weight.shape[2]
         return call(
-            load_kernel,
+            functools.partial(load_kernel, start),
             (weight,),
-            [pltpu.VMEM(weight.shape, BF16), shape((8, LANES), F32)],
+            [pltpu.VMEM((height, length), BF16), shape((8, LANES), F32)],
             name,
-            scratch=[pltpu.SemaphoreType.DMA],
+            scratch=[pltpu.SemaphoreType.DMA((PARTS,))],
             loose=(0,),
-            cost=pl.CostEstimate(flops=0, bytes_accessed=2 * 2 * model * units, transcendentals=0),
+            cost=pl.CostEstimate(flops=0, bytes_accessed=4 * height * length, transcendentals=0),
             limit=8 * MIB,
         )
 
+    half = model // 2
     gate_w, gate_mark = load(w_gate, "load_gate")
-    up_w, up_mark = load(w_up, "load_up")
+    up_a, up_mark = load(w_up, "load_up_a", 0, half)
+    up_b, late_mark = load(w_up, "load_up_b", half, half)
     down_w, down_mark = load(w_down, "load_down")
-    def gather(block):
-        if relative:
+    def gather(block, relayed=False):
+        if relative and relayed:
             second = swap(block, "z", 2)
             return [block, swap(block, "z", 1), second, swap(second, "z", 1)]
+        if relative:
+            return [block] + [swap(block, "z", k) for k in range(1, hops)]
         return [lax.all_gather(block, "z", axis=0, tiled=False)]
 
     arrived = [sends[0]] + [swap(sends[q], "expert", q) for q in range(1, groups)]
-    slices = gather(handed)
+    slices = gather(handed, True)
     picked = call(
         functools.partial(pick_kernel, relative, experts, hops),
-        (position, *slices),
+        (position, *slices, late_mark, down_mark),
         [shape((hops, CAP, width), BF16)] * experts,
         "pick",
     )
     (stacked,) = call(
         functools.partial(stack_kernel, groups),
-        (*arrived, gate_mark, *slices[1:3]),
+        (*arrived, gate_mark, up_mark, *slices[1:3]),
         [shape((groups, ROWS, width), BF16)],
         "stack",
     )
-    blocks_x = [stacked] + [swap(stacked, "z", k) for k in range(1, hops)] if relative else gather(stacked)
+    blocks_x = gather(stacked)
     blocks_d = [picked[0]] + [swap(picked[q], "expert", q) for q in range(1, groups)]
-    own_x, own_d = call(
-        functools.partial(join_kernel, groups),
-        (up_mark, down_mark, *blocks_d, *blocks_x),
-        [shape((hops, *stacked.shape), BF16), shape((groups, *picked[0].shape), BF16)],
+    (own_x,) = call(
+        join_kernel,
+        (*blocks_x, picked[0]),
+        [shape((hops, *stacked.shape), BF16)],
         "join",
     )
     far_x = swap(own_x, "core", 1)
-    far_d = swap(own_d, "core", 1)
 
     cost = 2 * rows * model * units
     rows_x, hidden, active, slope, gates, rival, others, keep, give = call(
         functools.partial(forward_kernel, relative, groups, hops),
-        (own_x, far_x, gate_w, up_w, down_w),
+        (own_x, far_x, gate_w, up_a, up_b, down_w, picked[0]),
         [
             shape((rows, model), BF16),
             shape((rows, units), BF16),
@@ -439,6 +449,13 @@
         limit=16 * MIB,
     )
     got = swap(give, "core", 1)
+    (own_d,) = call(
+        functools.partial(stack_kernel, groups),
+        (*blocks_d, gates),
+        [shape((groups, hops, CAP, width), BF16)],
+        "stack_d",
+    )
+    far_d = swap(own_d, "core", 1)
     rows_d, d_gate, d_up, router_keep, router_give = call(
         functools.partial(backward_kernel, relative, groups, hops),
         (own_d, far_d, rows_x, active, slope, hidden, gates, rival, others, down_w),

time: 68.5 us -> 69.9 us (1.020)
  Pallas kernels: 27.7 us -> 28.9 us
  waiting for transfers between devices: 12.9 us -> 13.9 us
  starting transfers between devices: 26.9 us -> 26.1 us
    pallas_call x12 -> x14, Pallas kernels: 18.8 us -> 20.1 us  [call(): pl.pallas_call(kernel, out_shape=tuple(outs), in_specs=[fixed if i in loo...]
    ppermute x22, waiting for transfers between devices: 12.9 us -> 13.9 us  [swap(): return lax.ppermute(block, axis, [(i, i ^ bits) for i in range(size)])]
    ppermute x22, starting transfers between devices: 26.9 us -> 26.1 us  [swap(): return lax.ppermute(block, axis, [(i, i ^ bits) for i in range(size)])]
  transfers between devices with their start and end apart: 22 -> 22, of which waited for: 9 -> 8; matrix products, arithmetic and copies ran while one was open for 0% -> 0% of each run, Pallas kernels for 37% -> 38%
where the time goes in v5:
time: 69.9 us; the launch traced here: 69.7 us
  Pallas kernels  28.9 us (41%)
  starting transfers between devices  26.1 us (37%)
  waiting for transfers between devices  13.9 us (20%)
  between operations  0.84 us (1%)
    ppermute x22, starting transfers between devices, swap(): return lax.ppermute(block, axis, [(i, i ^ bits) for i in range(size)])  26.1 us
    pallas_call x14, Pallas kernels, call(): pl.pallas_call(kernel, out_shape=tuple(outs), in_specs=[fixed if i in loo...  20.1 us
    ppermute x22, waiting for transfers between devices, swap(): return lax.ppermute(block, axis, [(i, i ^ bits) for i in range(size)])  13.9 us
    pallas_call x1, Pallas kernels, shards(): pl.pallas_call(grads_kernel, grid=(parts,), out_shape=(shape(w_gate.shape...  8.84 us
  transfers between devices with their start and end apart: 22, of which 8 were waited for; matrix products, arithmetic and copies ran while one was open for 0% of the time, Pallas kernels for 38%

profile of v5, /device:TPU:0, one launch (start us, length us, event | category | flops | bytes accessed | tf_op | source)
XLA Modules:
  0.0 69.7 jit_solution(10573210965542591779)
XLA Ops:
  0.6 1.6 %pack.1 = (s32[1,256]{1,0:T(1,128)S(1)}, bf16[128,384]{1,0:T(8,128)(2,1)S(1)}, bf16[48,384]{1,0:T(8,128)(2,1)S(1)}, bf16[48,384]{1,0:T(8,128)(2,1)S(1)}, bf16[48...) custom-call(s32[4]{0:T(128)} %refs_0_.1, s32[4]{0:T(128)} %refs_1_.1, s32[2,128]{1,0:T(2,128)} %bitcast.4, ...), custom_call_target="tpu_custom_call" | custom-call | tf_op jit(solution)/shard_map/pack/pallas_call | solution.py:355
  2.2 4.1 %collective-permute-start.4 = (bf16[128,384]{1,0:T(8,128)(2,1)S(1)}, bf16[128,384]{1,0:T(8,128)(2,1)S(1)}, u32[]{:S(2)}, u32[]{:S(2)}) collective-permute-start(bf16[128,384]{1,0:T(8,128)(2,1)S(1)} %get-tuple-element.58.refs_0_), channel_id=1, source_target_pairs={{0,4},{2,6},{4,0},{6,2},{1,5},{3,7},{5,1},{7,3},{8,12},{10,14},{12... | collective-permute-start | bytes 294920 | tf_op jit(solution)/shard_map/ppermute | solution.py:336
  6.3 1.6 %collective-permute-start.3 = (bf16[128,384]{1,0:T(8,128)(2,1)S(1)}, bf16[128,384]{1,0:T(8,128)(2,1)S(1)}, u32[]{:S(2)}, u32[]{:S(2)}) collective-permute-start(bf16[128,384]{1,0:T(8,128)(2,1)S(1)} %get-tuple-element.58.refs_0_), channel_id=1, source_target_pairs={{0,2},{2,0},{4,6},{6,4},{1,3},{3,1},{5,7},{7,5},{8,10},{10,8},{12,... | collective-permute-start | bytes 294920 | tf_op jit(solution)/shard_map/ppermute | solution.py:336
  7.9 1.5 %collective-permute-start = (bf16[48,384]{1,0:T(8,128)(2,1)S(1)}, bf16[48,384]{1,0:T(8,128)(2,1)S(1)}, u32[]{:S(2)}, u32[]{:S(2)}) collective-permute-start(bf16[48,384]{1,0:T(8,128)(2,1)S(1)} %get-tuple-element.53), channel_id=1, source_target_pairs={{0,8},{8,0},{16,24},{24,16},{1,9},{9,1},{17,25},{25,17},{2,10},{10... | collective-permute-start | bytes 110600 | tf_op jit(solution)/shard_map/ppermute | solution.py:336
  9.4 1.5 %collective-permute-start.1 = (bf16[48,384]{1,0:T(8,128)(2,1)S(1)}, bf16[48,384]{1,0:T(8,128)(2,1)S(1)}, u32[]{:S(2)}, u32[]{:S(2)}) collective-permute-start(bf16[48,384]{1,0:T(8,128)(2,1)S(1)} %get-tuple-element.54), channel_id=1, source_target_pairs={{0,16},{8,24},{16,0},{24,8},{1,17},{9,25},{17,1},{25,9},{2,18},{10... | collective-permute-start | bytes 110600 | tf_op jit(solution)/shard_map/ppermute | solution.py:336
  10.9 0.5 collective-permute-start.2
  11.4 1.9 %load_up_a.1 = (bf16[1536,1024]{1,0:T(8,128)(2,1)S(1)}, f32[8,128]{1,0:T(8,128)S(1)}) custom-call(bf16[1,3072,1024]{2,1,0:T(8,128)(2,1)} %source.6), custom_call_target="tpu_custom_call" | custom-call | bytes 6291456 | tf_op jit(solution)/shard_map/load_up_a/pallas_call | solution.py:355
  13.3 2.9 %load_gate.1 = (bf16[3072,1024]{1,0:T(8,128)(2,1)S(1)}, f32[8,128]{1,0:T(8,128)S(1)}) custom-call(bf16[1,3072,1024]{2,1,0:T(8,128)(2,1)} %source.4), custom_call_target="tpu_custom_call" | custom-call | bytes 12582912 | tf_op jit(solution)/shard_map/load_gate/pallas_call | solution.py:355
  16.1 0.0 collective-permute-done.refs_1_
  16.2 0.0 collective-permute-done.1.refs_2_
  16.2 0.0 collective-permute-done.2.refs_3_
  16.2 0.0 collective-permute-done.4.refs_7_.refs_2_
  16.2 0.0 collective-permute-done.3.refs_6_.refs_1_
  16.2 0.1 collective-permute-start.7
  16.3 1.9 %collective-permute-start.6 = (bf16[4,48,384]{2,1,0:T(8,128)(2,1)S(1)}, bf16[4,48,384]{2,1,0:T(8,128)(2,1)S(1)}, u32[]{:S(2)}, u32[]{:S(2)}) collective-permute-start(bf16[4,48,384]{2,1,0:T(8,128)(2,1)S(1)} %stack.1.refs_0_), channel_id=1, source_target_pairs={{0,4},{2,6},{4,0},{6,2},{1,5},{3,7},{5,1},{7,3},{8,12},{10,14},{12... | collective-permute-start | bytes 442376 | tf_op jit(solution)/shard_map/ppermute | solution.py:336
  18.2 2.5 %collective-permute-start.5 = (bf16[4,48,384]{2,1,0:T(8,128)(2,1)S(1)}, bf16[4,48,384]{2,1,0:T(8,128)(2,1)S(1)}, u32[]{:S(2)}, u32[]{:S(2)}) collective-permute-start(bf16[4,48,384]{2,1,0:T(8,128)(2,1)S(1)} %stack.1.refs_0_), channel_id=1, source_target_pairs={{0,2},{2,0},{4,6},{6,4},{1,3},{3,1},{5,7},{7,5},{8,10},{10,8},{12,... | collective-permute-start | bytes 442376 | tf_op jit(solution)/shard_map/ppermute | solution.py:336
  20.7 0.0 collective-permute-start.8
  20.7 1.9 %load_up_b.1 = (bf16[1536,1024]{1,0:T(8,128)(2,1)S(1)}, f32[8,128]{1,0:T(8,128)S(1)}) custom-call(bf16[1,3072,1024]{2,1,0:T(8,128)(2,1)} %source.6), custom_call_target="tpu_custom_call" | custom-call | bytes 6291456 | tf_op jit(solution)/shard_map/load_up_b/pallas_call | solution.py:355
  22.6 2.9 %load_down.1 = (bf16[1024,3072]{1,0:T(8,128)(2,1)S(1)}, f32[8,128]{1,0:T(8,128)S(1)}) custom-call(bf16[1,1024,3072]{2,1,0:T(8,128)(2,1)} %source.7), custom_call_target="tpu_custom_call" | custom-call | bytes 12582912 | tf_op jit(solution)/shard_map/load_down/pallas_call | solution.py:355
  25.5 4.9 %collective-permute-done.8.refs_3_ = bf16[128,384]{1,0:T(8,128)(2,1)S(1)} collective-permute-done((bf16[128,384]{1,0:T(8,128)(2,1)S(1)}, bf16[128,384]{1,0:T(8,128)(2,1)S(1)}, u32[]{:S(2)}, u32[]{:S(2)}) %collective-permute-start.8) | collective-permute-done | bytes 98336 | tf_op jit(solution)/shard_map/ppermute | solution.py:336
  30.4 0.3 pick.1
  30.7 0.0 collective-permute-done.7.refs_3_
  30.7 0.0 collective-permute-done.6.refs_2_
  30.7 0.0 collective-permute-done.5.refs_1_
  30.7 0.1 join.1.refs_0_
  30.8 0.1 collective-permute-start.9
  30.9 1.6 %collective-permute-start.11 = (bf16[4,40,384]{2,1,0:T(8,128)(2,1)S(1)}, bf16[4,40,384]{2,1,0:T(8,128)(2,1)S(1)}, u32[]{:S(2)}, u32[]{:S(2)}) collective-permute-start(bf16[4,40,384]{2,1,0:T(8,128)(2,1)S(1)} %get-tuple-element.68), channel_id=1, source_target_pairs={{0,8},{8,0},{16,24},{24,16},{1,9},{9,1},{17,25},{25,17},{2,10},{10... | collective-permute-start | bytes 368648 | tf_op jit(solution)/shard_map/ppermute | solution.py:336
  32.4 1.5 %collective-permute-start.12 = (bf16[4,40,384]{2,1,0:T(8,128)(2,1)S(1)}, bf16[4,40,384]{2,1,0:T(8,128)(2,1)S(1)}, u32[]{:S(2)}, u32[]{:S(2)}) collective-permute-start(bf16[4,40,384]{2,1,0:T(8,128)(2,1)S(1)} %get-tuple-element.69), channel_id=1, source_target_pairs={{0,16},{8,24},{16,0},{24,8},{1,17},{9,25},{17,1},{25,9},{2,18},{10... | collective-permute-start | bytes 368648 | tf_op jit(solution)/shard_map/ppermute | solution.py:336
  33.9 0.5 collective-permute-start.13
  34.4 0.0 collective-permute-done.9.refs_1_
  34.4 4.2 %forward.1 = (bf16[192,3072]{1,0:T(8,128)(2,1)S(1)}, bf16[192,1024]{1,0:T(8,128)(2,1)S(1)}, f32[192,1024]{1,0:T(8,128)S(1)}, f32[192,1024]{1,0:T(8,128)S(1)}, f3...) custom-call(bf16[4,4,48,384]{3,2,1,0:T(8,128)(2,1)S(1)} %join.1.refs, ...), custom_call_target="tpu_custom_call" | custom-call | flops 3623878656 | bytes 18874368 | tf_op jit(solution)/shard_map/forward/pallas_call | solution.py:355
  38.7 0.0 collective-permute-done.11.refs_1_
  38.7 1.8 %collective-permute-done.12.refs_2_ = bf16[4,40,384]{2,1,0:T(8,128)(2,1)S(1)} collective-permute-done((bf16[4,40,384]{2,1,0:T(8,128)(2,1)S(1)}, bf16[4,40,384]{2,1,0:T(8,128)(2,1)S(1)}, u32[]{:S(2)}, u32[]{:S(2)}) %collective-permute-start.12) | collective-permute-done | bytes 122912 | tf_op jit(solution)/shard_map/ppermute | solution.py:336
  40.4 0.0 collective-permute-done.13.refs_3_
  40.5 0.1 collective-permute-start.14
  40.6 0.5 collective-permute-start.10
  41.1 1.4 %collective-permute-done.14.refs_1_ = bf16[4,4,40,384]{3,2,1,0:T(8,128)(2,1)S(1)} collective-permute-done((bf16[4,4,40,384]{3,2,1,0:T(8,128)(2,1)S(1)}, bf16[4,4,40,384]{3,2,1,0:T(8,128)(2,1)S(1)}, u32[]{:S(2)}, u32[]{:S(2)}) %collective-permute-start.14) | collective-permute-done | bytes 491552 | tf_op jit(solution)/shard_map/ppermute | solution.py:336
  42.4 3.3 %backward.1 = (bf16[192,3072]{1,0:T(8,128)(2,1)S(1)}, bf16[192,1024]{1,0:T(8,128)(2,1)S(1)}, bf16[192,1024]{1,0:T(8,128)(2,1)S(1)}, f32[4,4,384]{2,1,0:T(4,128)S(1)}, bf16[4,8,384]{2,1,0:T(8,128)(2,1)S(1)}) custom-call(bf16[4,4,40,384]{3,2,1,0:T(8,128)(2,1)S(1)} %stack_d.1.refs_0_, bf16[4,4,40,384]{3,2,1,0:T(8,128)(2,1)S(1)} %collective-permute-done.14.refs_1_, ...), custom_call_target="tpu_custom_call" | custom-call | flops 1207959552 | bytes 6291456 | tf_op jit(solution)/shard_map/backward/pallas_call | solution.py:355
  45.7 0.2 collective-permute-start.15
  45.9 1.1 %collective-permute-done.15.rgot_ref = bf16[4,8,384]{2,1,0:T(8,128)(2,1)S(1)} collective-permute-done((bf16[4,8,384]{2,1,0:T(8,128)(2,1)S(1)}, bf16[4,8,384]{2,1,0:T(8,128)(2,1)S(1)}, u32[]{:S(2)}, u32[]{:S(2)}) %collective-permute-start.15) | collective-permute-done | bytes 24608 | tf_op jit(solution)/shard_map/ppermute | solution.py:336
  47.0 0.0 collective-permute-done.10.got_ref
  47.0 0.1 merge.1
  47.1 0.6 collective-permute-start.16
  47.7 0.5 collective-permute-start.17
  48.2 3.3 %collective-permute-start.18 = (bf16[4,48,384]{2,1,0:T(8,128)(2,1)S(1)}, bf16[4,48,384]{2,1,0:T(8,128)(2,1)S(1)}, u32[]{:S(2)}, u32[]{:S(2)}) collective-permute-start(bf16[4,48,384]{2,1,0:T(8,128)(2,1)S(1)} %get-tuple-element.83), channel_id=1, source_target_pairs={{0,2},{2,0},{4,6},{6,4},{1,3},{3,1},{5,7},{7,5},{8,10},{10,8},{12,... | collective-permute-start | bytes 442376 | tf_op jit(solution)/shard_map/ppermute | solution.py:336
  51.5 8.8 %grads.1 = (bf16[1,3072,1024]{2,1,0:T(8,128)(2,1)}, bf16[1,3072,1024]{2,1,0:T(8,128)(2,1)}, bf16[1,1024,3072]{2,1,0:T(8,128)(2,1)}, f32[8,128]{1,0:T(8,128)S(1)}) custom-call(bf16[192,3072]{1,0:T(8,128)(2,1)S(1)} %get-tuple-element.72.refs_2_.x_ref, bf16[192,3072]{1,0:T(8,128)(2,1)S(1)} %get-tuple-element.84.d_ref, ...), custom_call_target="tpu_custom_call" | custom-call | flops 3623878656 | bytes 18874368 | tf_op jit(solution)/shard_map/grads/pallas_call | solution.py:491
  60.4 0.0 collective-permute-done.16.refs_1_
  60.4 1.4 %collective-permute-done.17.refs_2_ = bf16[4,48,384]{2,1,0:T(8,128)(2,1)S(1)} collective-permute-done((bf16[4,48,384]{2,1,0:T(8,128)(2,1)S(1)}, bf16[4,48,384]{2,1,0:T(8,128)(2,1)S(1)}, u32[]{:S(2)}, u32[]{:S(2)}) %collective-permute-start.17) | collective-permute-done | bytes 147488 | tf_op jit(solution)/shard_map/ppermute | solution.py:336
  61.8 0.0 collective-permute-done.18.refs_3_
  61.8 0.1 total.1
  61.9 1.3 %collective-permute-start.19 = (bf16[48,384]{1,0:T(8,128)(2,1)S(1)}, bf16[48,384]{1,0:T(8,128)(2,1)S(1)}, u32[]{:S(2)}, u32[]{:S(2)}) collective-permute-start(bf16[48,384]{1,0:T(8,128)(2,1)S(1)} %get-tuple-element.89), channel_id=1, source_target_pairs={{0,8},{8,0},{16,24},{24,16},{1,9},{9,1},{17,25},{25,17},{2,10},{10... | collective-permute-start | bytes 110600 | tf_op jit(solution)/shard_map/ppermute | solution.py:336
  63.2 0.8 %collective-permute-start.20 = (bf16[48,384]{1,0:T(8,128)(2,1)S(1)}, bf16[48,384]{1,0:T(8,128)(2,1)S(1)}, u32[]{:S(2)}, u32[]{:S(2)}) collective-permute-start(bf16[48,384]{1,0:T(8,128)(2,1)S(1)} %get-tuple-element.90), channel_id=1, source_target_pairs={{0,16},{8,24},{16,0},{24,8},{1,17},{9,25},{17,1},{25,9},{2,18},{10... | collective-permute-start | bytes 110600 | tf_op jit(solution)/shard_map/ppermute | solution.py:336
  64.0 1.4 %collective-permute-start.21 = (bf16[48,384]{1,0:T(8,128)(2,1)S(1)}, bf16[48,384]{1,0:T(8,128)(2,1)S(1)}, u32[]{:S(2)}, u32[]{:S(2)}) collective-permute-start(bf16[48,384]{1,0:T(8,128)(2,1)S(1)} %get-tuple-element.91), channel_id=1, source_target_pairs={{0,24},{8,16},{16,8},{24,0},{1,25},{9,17},{17,9},{25,1},{2,26},{10... | collective-permute-start | bytes 110600 | tf_op jit(solution)/shard_map/ppermute | solution.py:336
  65.4 0.5 collective-permute-done.19.refs_1_
  65.9 1.5 %collective-permute-done.20.refs_2_ = bf16[48,384]{1,0:T(8,128)(2,1)S(1)} collective-permute-done((bf16[48,384]{1,0:T(8,128)(2,1)S(1)}, bf16[48,384]{1,0:T(8,128)(2,1)S(1)}, u32[]{:S(2)}, u32[]{:S(2)}) %collective-permute-start.20) | collective-permute-done | bytes 36896 | tf_op jit(solution)/shard_map/ppermute | solution.py:336
  67.4 1.5 %collective-permute-done.21.refs_3_ = bf16[48,384]{1,0:T(8,128)(2,1)S(1)} collective-permute-done((bf16[48,384]{1,0:T(8,128)(2,1)S(1)}, bf16[48,384]{1,0:T(8,128)(2,1)S(1)}, u32[]{:S(2)}, u32[]{:S(2)}) %collective-permute-start.21) | collective-permute-done | bytes 36896 | tf_op jit(solution)/shard_map/ppermute | solution.py:336
  68.9 0.9 %combine.1 = (bf16[128,384]{1,0:T(8,128)(2,1)}, bf16[4,384]{1,0:T(4,128)(2,1)}) custom-call(s32[1,256]{1,0:T(1,128)S(1)} %get-tuple-element.51.pos_ref, bf16[48,384]{1,0:T(8,128)(2,1)S(1)} %get-tuple-element.88.refs_0_, bf16[48,384]{1,0:T(8,128)(2,1)S(1)} %collective-permute-done.19.refs_1_, bf16[48,384]{1,0:T(8,128)(2,1)S(1)} %collective-permute-done.20.refs_2_, ...), custom_call_target="tpu_custom_call" | custom-call | tf_op jit(solution)/shard_map/combine/pallas_call | solution.py:355
  (2 shorter events, 0.1 us)
Async XLA Ops:
  2.2 14.0 %collective-permute-start.4 = (bf16[128,384]{1,0:T(8,128)(2,1)S(1)}, bf16[128,384]{1,0:T(8,128)(2,1)S(1)}, u32[]{:S(2)}, u32[]{:S(2)}) collective-permute-start(bf16[128,384]{1,0:T(8,128)(2,1)S(1)} %get-tuple-element.58.refs_0_), channel_id=1, source_target_pairs={{0,4},{2,6},{4,0},{6,2},{1,5},{3,7},{5,1},{7,3},{8,12},{10,14},{12... | collective-permute-start | bytes 294920 | tf_op jit(solution)/shard_map/ppermute | solution.py:336
  6.3 9.9 %collective-permute-start.3 = (bf16[128,384]{1,0:T(8,128)(2,1)S(1)}, bf16[128,384]{1,0:T(8,128)(2,1)S(1)}, u32[]{:S(2)}, u32[]{:S(2)}) collective-permute-start(bf16[128,384]{1,0:T(8,128)(2,1)S(1)} %get-tuple-element.58.refs_0_), channel_id=1, source_target_pairs={{0,2},{2,0},{4,6},{6,4},{1,3},{3,1},{5,7},{7,5},{8,10},{10,8},{12,... | collective-permute-start | bytes 294920 | tf_op jit(solution)/shard_map/ppermute | solution.py:336
  7.9 8.3 %collective-permute-start = (bf16[48,384]{1,0:T(8,128)(2,1)S(1)}, bf16[48,384]{1,0:T(8,128)(2,1)S(1)}, u32[]{:S(2)}, u32[]{:S(2)}) collective-permute-start(bf16[48,384]{1,0:T(8,128)(2,1)S(1)} %get-tuple-element.53), channel_id=1, source_target_pairs={{0,8},{8,0},{16,24},{24,16},{1,9},{9,1},{17,25},{25,17},{2,10},{10... | collective-permute-start | bytes 110600 | tf_op jit(solution)/shard_map/ppermute | solution.py:336
  9.4 6.8 %collective-permute-start.1 = (bf16[48,384]{1,0:T(8,128)(2,1)S(1)}, bf16[48,384]{1,0:T(8,128)(2,1)S(1)}, u32[]{:S(2)}, u32[]{:S(2)}) collective-permute-start(bf16[48,384]{1,0:T(8,128)(2,1)S(1)} %get-tuple-element.54), channel_id=1, source_target_pairs={{0,16},{8,24},{16,0},{24,8},{1,17},{9,25},{17,1},{25,9},{2,18},{10... | collective-permute-start | bytes 110600 | tf_op jit(solution)/shard_map/ppermute | solution.py:336
  10.9 5.3 %collective-permute-start.2 = (bf16[48,384]{1,0:T(8,128)(2,1)S(1)}, bf16[48,384]{1,0:T(8,128)(2,1)S(1)}, u32[]{:S(2)}, u32[]{:S(2)}) collective-permute-start(bf16[48,384]{1,0:T(8,128)(2,1)S(1)} %get-tuple-element.55), channel_id=1, source_target_pairs={{0,24},{8,16},{16,8},{24,0},{1,25},{9,17},{17,9},{25,1},{2,26},{10... | collective-permute-start | bytes 110600 | tf_op jit(solution)/shard_map/ppermute | solution.py:336
  16.2 14.5 %collective-permute-start.7 = (bf16[4,48,384]{2,1,0:T(8,128)(2,1)S(1)}, bf16[4,48,384]{2,1,0:T(8,128)(2,1)S(1)}, u32[]{:S(2)}, u32[]{:S(2)}) collective-permute-start(bf16[4,48,384]{2,1,0:T(8,128)(2,1)S(1)} %stack.1.refs_0_), channel_id=1, source_target_pairs={{0,6},{2,4},{4,2},{6,0},{1,7},{3,5},{5,3},{7,1},{8,14},{10,12},{12... | collective-permute-start | bytes 442376 | tf_op jit(solution)/shard_map/ppermute | solution.py:336
  16.3 14.4 %collective-permute-start.6 = (bf16[4,48,384]{2,1,0:T(8,128)(2,1)S(1)}, bf16[4,48,384]{2,1,0:T(8,128)(2,1)S(1)}, u32[]{:S(2)}, u32[]{:S(2)}) collective-permute-start(bf16[4,48,384]{2,1,0:T(8,128)(2,1)S(1)} %stack.1.refs_0_), channel_id=1, source_target_pairs={{0,4},{2,6},{4,0},{6,2},{1,5},{3,7},{5,1},{7,3},{8,12},{10,14},{12... | collective-permute-start | bytes 442376 | tf_op jit(solution)/shard_map/ppermute | solution.py:336
  18.2 12.5 %collective-permute-start.5 = (bf16[4,48,384]{2,1,0:T(8,128)(2,1)S(1)}, bf16[4,48,384]{2,1,0:T(8,128)(2,1)S(1)}, u32[]{:S(2)}, u32[]{:S(2)}) collective-permute-start(bf16[4,48,384]{2,1,0:T(8,128)(2,1)S(1)} %stack.1.refs_0_), channel_id=1, source_target_pairs={{0,2},{2,0},{4,6},{6,4},{1,3},{3,1},{5,7},{7,5},{8,10},{10,8},{12,... | collective-permute-start | bytes 442376 | tf_op jit(solution)/shard_map/ppermute | solution.py:336
  20.7 9.7 %collective-permute-start.8 = (bf16[128,384]{1,0:T(8,128)(2,1)S(1)}, bf16[128,384]{1,0:T(8,128)(2,1)S(1)}, u32[]{:S(2)}, u32[]{:S(2)}) collective-permute-start(bf16[128,384]{1,0:T(8,128)(2,1)S(1)} %collective-permute-done.4.refs_7_.refs_2_), channel_id=1, source_target_pairs={{0,2},{2,0},{4,6},{6,4},{1,3},{3,1},{5,7},{7,5},{8,10},{10,8},{12,... | collective-permute-start | bytes 294920 | tf_op jit(solution)/shard_map/ppermute | solution.py:336
  30.8 3.6 %collective-permute-start.9 = (bf16[4,4,48,384]{3,2,1,0:T(8,128)(2,1)S(1)}, bf16[4,4,48,384]{3,2,1,0:T(8,128)(2,1)S(1)}, u32[]{:S(2)}, u32[]{:S(2)}) collective-permute-start(bf16[4,4,48,384]{3,2,1,0:T(8,128)(2,1)S(1)} %join.1.refs_0_), channel_id=1, source_target_pairs={{0,1},{1,0},{2,3},{3,2},{4,5},{5,4},{6,7},{7,6},{8,9},{9,8},{10,11... | collective-permute-start | bytes 1769480 | tf_op jit(solution)/shard_map/ppermute | solution.py:336
  30.9 7.8 %collective-permute-start.11 = (bf16[4,40,384]{2,1,0:T(8,128)(2,1)S(1)}, bf16[4,40,384]{2,1,0:T(8,128)(2,1)S(1)}, u32[]{:S(2)}, u32[]{:S(2)}) collective-permute-start(bf16[4,40,384]{2,1,0:T(8,128)(2,1)S(1)} %get-tuple-element.68), channel_id=1, source_target_pairs={{0,8},{8,0},{16,24},{24,16},{1,9},{9,1},{17,25},{25,17},{2,10},{10... | collective-permute-start | bytes 368648 | tf_op jit(solution)/shard_map/ppermute | solution.py:336
  32.4 8.0 %collective-permute-start.12 = (bf16[4,40,384]{2,1,0:T(8,128)(2,1)S(1)}, bf16[4,40,384]{2,1,0:T(8,128)(2,1)S(1)}, u32[]{:S(2)}, u32[]{:S(2)}) collective-permute-start(bf16[4,40,384]{2,1,0:T(8,128)(2,1)S(1)} %get-tuple-element.69), channel_id=1, source_target_pairs={{0,16},{8,24},{16,0},{24,8},{1,17},{9,25},{17,1},{25,9},{2,18},{10... | collective-permute-start | bytes 368648 | tf_op jit(solution)/shard_map/ppermute | solution.py:336
  33.9 6.5 %collective-permute-start.13 = (bf16[4,40,384]{2,1,0:T(8,128)(2,1)S(1)}, bf16[4,40,384]{2,1,0:T(8,128)(2,1)S(1)}, u32[]{:S(2)}, u32[]{:S(2)}) collective-permute-start(bf16[4,40,384]{2,1,0:T(8,128)(2,1)S(1)} %get-tuple-element.70), channel_id=1, source_target_pairs={{0,24},{8,16},{16,8},{24,0},{1,25},{9,17},{17,9},{25,1},{2,26},{10... | collective-permute-start | bytes 368648 | tf_op jit(solution)/shard_map/ppermute | solution.py:336
  40.5 1.9 %collective-permute-start.14 = (bf16[4,4,40,384]{3,2,1,0:T(8,128)(2,1)S(1)}, bf16[4,4,40,384]{3,2,1,0:T(8,128)(2,1)S(1)}, u32[]{:S(2)}, u32[]{:S(2)}) collective-permute-start(bf16[4,4,40,384]{3,2,1,0:T(8,128)(2,1)S(1)} %stack_d.1.refs_0_), channel_id=1, source_target_pairs={{0,1},{1,0},{2,3},{3,2},{4,5},{5,4},{6,7},{7,6},{8,9},{9,8},{10,11... | collective-permute-start | bytes 1474568 | tf_op jit(solution)/shard_map/ppermute | solution.py:336
  40.6 6.4 %collective-permute-start.10 = (bf16[4,4,48,384]{3,2,1,0:T(8,128)(2,1)S(1)}, bf16[4,4,48,384]{3,2,1,0:T(8,128)(2,1)S(1)}, u32[]{:S(2)}, u32[]{:S(2)}) collective-permute-start(bf16[4,4,48,384]{3,2,1,0:T(8,128)(2,1)S(1)} %get-tuple-element.67), channel_id=1, source_target_pairs={{0,1},{1,0},{2,3},{3,2},{4,5},{5,4},{6,7},{7,6},{8,9},{9,8},{10,11... | collective-permute-start | bytes 1769480 | tf_op jit(solution)/shard_map/ppermute | solution.py:336
  45.7 1.3 %collective-permute-start.15 = (bf16[4,8,384]{2,1,0:T(8,128)(2,1)S(1)}, bf16[4,8,384]{2,1,0:T(8,128)(2,1)S(1)}, u32[]{:S(2)}, u32[]{:S(2)}) collective-permute-start(bf16[4,8,384]{2,1,0:T(8,128)(2,1)S(1)} %get-tuple-element.79), channel_id=1, source_target_pairs={{0,1},{1,0},{2,3},{3,2},{4,5},{5,4},{6,7},{7,6},{8,9},{9,8},{10,11... | collective-permute-start | bytes 73736 | tf_op jit(solution)/shard_map/ppermute | solution.py:336
  47.1 13.3 %collective-permute-start.16 = (bf16[4,48,384]{2,1,0:T(8,128)(2,1)S(1)}, bf16[4,48,384]{2,1,0:T(8,128)(2,1)S(1)}, u32[]{:S(2)}, u32[]{:S(2)}) collective-permute-start(bf16[4,48,384]{2,1,0:T(8,128)(2,1)S(1)} %get-tuple-element.81), channel_id=1, source_target_pairs={{0,6},{2,4},{4,2},{6,0},{1,7},{3,5},{5,3},{7,1},{8,14},{10,12},{12... | collective-permute-start | bytes 442376 | tf_op jit(solution)/shard_map/ppermute | solution.py:336
  47.7 14.1 %collective-permute-start.17 = (bf16[4,48,384]{2,1,0:T(8,128)(2,1)S(1)}, bf16[4,48,384]{2,1,0:T(8,128)(2,1)S(1)}, u32[]{:S(2)}, u32[]{:S(2)}) collective-permute-start(bf16[4,48,384]{2,1,0:T(8,128)(2,1)S(1)} %get-tuple-element.82), channel_id=1, source_target_pairs={{0,4},{2,6},{4,0},{6,2},{1,5},{3,7},{5,1},{7,3},{8,12},{10,14},{12... | collective-permute-start | bytes 442376 | tf_op jit(solution)/shard_map/ppermute | solution.py:336
  48.2 13.6 %collective-permute-start.18 = (bf16[4,48,384]{2,1,0:T(8,128)(2,1)S(1)}, bf16[4,48,384]{2,1,0:T(8,128)(2,1)S(1)}, u32[]{:S(2)}, u32[]{:S(2)}) collective-permute-start(bf16[4,48,384]{2,1,0:T(8,128)(2,1)S(1)} %get-tuple-element.83), channel_id=1, source_target_pairs={{0,2},{2,0},{4,6},{6,4},{1,3},{3,1},{5,7},{7,5},{8,10},{10,8},{12,... | collective-permute-start | bytes 442376 | tf_op jit(solution)/shard_map/ppermute | solution.py:336
  61.9 4.0 %collective-permute-start.19 = (bf16[48,384]{1,0:T(8,128)(2,1)S(1)}, bf16[48,384]{1,0:T(8,128)(2,1)S(1)}, u32[]{:S(2)}, u32[]{:S(2)}) collective-permute-start(bf16[48,384]{1,0:T(8,128)(2,1)S(1)} %get-tuple-element.89), channel_id=1, source_target_pairs={{0,8},{8,0},{16,24},{24,16},{1,9},{9,1},{17,25},{25,17},{2,10},{10... | collective-permute-start | bytes 110600 | tf_op jit(solution)/shard_map/ppermute | solution.py:336
  63.2 4.2 %collective-permute-start.20 = (bf16[48,384]{1,0:T(8,128)(2,1)S(1)}, bf16[48,384]{1,0:T(8,128)(2,1)S(1)}, u32[]{:S(2)}, u32[]{:S(2)}) collective-permute-start(bf16[48,384]{1,0:T(8,128)(2,1)S(1)} %get-tuple-element.90), channel_id=1, source_target_pairs={{0,16},{8,24},{16,0},{24,8},{1,17},{9,25},{17,1},{25,9},{2,18},{10... | collective-permute-start | bytes 110600 | tf_op jit(solution)/shard_map/ppermute | solution.py:336
  64.0 4.9 %collective-permute-start.21 = (bf16[48,384]{1,0:T(8,128)(2,1)S(1)}, bf16[48,384]{1,0:T(8,128)(2,1)S(1)}, u32[]{:S(2)}, u32[]{:S(2)}) collective-permute-start(bf16[48,384]{1,0:T(8,128)(2,1)S(1)} %get-tuple-element.91), channel_id=1, source_target_pairs={{0,24},{8,16},{16,8},{24,0},{1,25},{9,17},{17,9},{25,1},{2,26},{10... | collective-permute-start | bytes 110600 | tf_op jit(solution)/shard_map/ppermute | solution.py:336

commit v6 on v4

--- a/solution.py
+++ b/solution.py
@@ -120,7 +120,7 @@
 
 
 def pick_kernel(relative, experts, hops, pos_ref, *refs):
-    sources, sends = refs[: len(refs) - experts], refs[len(refs) - experts :]
+    sources, sends = refs[: len(refs) - experts - 1], refs[len(refs) - experts :]
     merged = chosen(pos_ref[...], experts)
     for k in range(hops):
         rows = dot(merged, sources[k][...] if relative else sources[0][k], ((1,), (0,)))
@@ -154,17 +154,17 @@
                     body(side, k, pl.ds(at, width))
 
 
-def load_kernel(source, out, mark, sem):
+def load_kernel(start, source, out, mark, sem):
     mark[...] = jnp.zeros(mark.shape, F32)
-    copy = pltpu.make_async_copy(source, out, sem)
+    copy = pltpu.make_async_copy(source.at[0, pl.ds(start, out.shape[0])], out, sem)
     copy.start()
     copy.wait()
 
 
 def forward_kernel(relative, groups, hops, *refs):
-    sides, (gate_ref, up_ref, down_ref) = refs[:2], refs[2:5]
+    sides, (gate_ref, up_a_ref, up_b_ref, down_ref) = refs[:2], refs[2:6]
     x_ref, hid_ref, active_ref, slope_ref, gates_ref, rival_ref, other_ref, keep_ref, give_ref, total = refs[
-        5:
+        6:
     ]
     width = keep_ref.shape[-1]
     model = x_ref.shape[1]
@@ -189,10 +189,12 @@
         other_ref[here, :] = column(meta[3:4])
 
     rows_x = x_ref[...]
+    half = up_a_ref.shape[0]
     for f in range(0, units, tile):
         now = slice(f, f + tile)
-        gate_pre = dot(rows_x, gate_ref[0, :, now], ((1,), (0,)))
-        up_pre = dot(rows_x, up_ref[0, :, now], ((1,), (0,)))
+        gate_pre = dot(rows_x, gate_ref[:, now], ((1,), (0,)))
+        up_pre = dot(rows_x[:, :half], up_a_ref[:, now], ((1,), (0,)))
+        up_pre = up_pre + dot(rows_x[:, half:], up_b_ref[:, now], ((1,), (0,)))
         sigma = jax.nn.sigmoid(gate_pre)
         active = gate_pre * sigma
         active_ref[:, now] = active
@@ -201,7 +203,7 @@
     hidden = hid_ref[...]
     for f in range(0, model, 512):
         now = slice(f, f + 512)
-        total[:, now] = gates_ref[...] * dot(hidden, down_ref[0, :, now], ((1,), (0,)))
+        total[:, now] = gates_ref[...] * dot(hidden, down_ref[:, now], ((1,), (0,)))
 
     def emit(side, k, features):
         for q in range(groups):
@@ -233,7 +235,7 @@
     dots = jnp.zeros((rows_d.shape[0], 1), F32)
     for f in range(0, units, tile):
         now = slice(f, f + tile)
-        d_hidden = dot(rows_d, down_ref[0, now, :], ((1,), (1,)))
+        d_hidden = dot(rows_d, down_ref[now, :], ((1,), (1,)))
         dgate_ref[:, now] = (d_hidden * slope_ref[:, now]).astype(BF16)
         dup_ref[:, now] = (d_hidden * active_ref[:, now]).astype(BF16)
         dots += jnp.sum(hid_ref[:, now].astype(F32) * d_hidden, axis=1, keepdims=True)
@@ -269,6 +271,10 @@
         got = rgot_ref[k].astype(F32)
         router = halves(rkeep_ref[k] + got[:experts] + got[experts:])
         put(out_refs[k], keep_ref[k] + got_ref[k].astype(F32), router)
+
+
+def pass_kernel(block_ref, _, out_ref):
+    out_ref[...] = block_ref[...]
 
 
 def put(out_ref, blocks, router):
@@ -372,46 +378,50 @@
         ],
         loose=range(6),
     )
-    def load(weight, name):
+    def load(weight, name, start=0, size=None):
+        height, length = size or weight.shape[1], weight.shape[2]
         return call(
-            load_kernel,
+            functools.partial(load_kernel, start),
             (weight,),
-            [pltpu.VMEM(weight.shape, BF16), shape((8, LANES), F32)],
+            [pltpu.VMEM((height, length), BF16), shape((8, LANES), F32)],
             name,
             scratch=[pltpu.SemaphoreType.DMA],
             loose=(0,),
-            cost=pl.CostEstimate(flops=0, bytes_accessed=2 * 2 * model * units, transcendentals=0),
+            cost=pl.CostEstimate(flops=0, bytes_accessed=4 * height * length, transcendentals=0),
             limit=8 * MIB,
         )
 
+    half = model // 2
     gate_w, gate_mark = load(w_gate, "load_gate")
-    up_w, up_mark = load(w_up, "load_up")
+    up_a, up_mark = load(w_up, "load_up_a", 0, half)
+    up_b, late_mark = load(w_up, "load_up_b", half, half)
     down_w, down_mark = load(w_down, "load_down")
     def gather(block):
         if relative:
             second = swap(block, "z", 2)
-            return [block, swap(block, "z", 1), second, swap(second, "z", 1)]
+            (held,) = call(pass_kernel, (second, gate_mark), [shape(block.shape, BF16)], "relay")
+            return [block, swap(block, "z", 1), second, swap(held, "z", 1)]
         return [lax.all_gather(block, "z", axis=0, tiled=False)]
 
     arrived = [sends[0]] + [swap(sends[q], "expert", q) for q in range(1, groups)]
     slices = gather(handed)
+    (stacked,) = call(
+        functools.partial(stack_kernel, groups),
+        (*arrived, gate_mark, up_mark, *slices[1:]),
+        [shape((groups, ROWS, width), BF16)],
+        "stack",
+    )
     picked = call(
         functools.partial(pick_kernel, relative, experts, hops),
-        (position, *slices),
+        (position, *slices, stacked),
         [shape((hops, CAP, width), BF16)] * experts,
         "pick",
-    )
-    (stacked,) = call(
-        functools.partial(stack_kernel, groups),
-        (*arrived, gate_mark, *slices[1:3]),
-        [shape((groups, ROWS, width), BF16)],
-        "stack",
     )
     blocks_x = [stacked] + [swap(stacked, "z", k) for k in range(1, hops)] if relative else gather(stacked)
     blocks_d = [picked[0]] + [swap(picked[q], "expert", q) for q in range(1, groups)]
     own_x, own_d = call(
         functools.partial(join_kernel, groups),
-        (up_mark, down_mark, *blocks_d, *blocks_x),
+        (late_mark, down_mark, *blocks_d, *blocks_x),
         [shape((hops, *stacked.shape), BF16), shape((groups, *picked[0].shape), BF16)],
         "join",
     )
@@ -421,7 +431,7 @@
     cost = 2 * rows * model * units
     rows_x, hidden, active, slope, gates, rival, others, keep, give = call(
         functools.partial(forward_kernel, relative, groups, hops),
-        (own_x, far_x, gate_w, up_w, down_w),
+        (own_x, far_x, gate_w, up_a, up_b, down_w),
         [
             shape((rows, model), BF16),
             shape((rows, units), BF16),

time: 68.5 us -> 70.3 us (1.026)
  Pallas kernels: 27.7 us -> 28.7 us
  waiting for transfers between devices: 12.9 us -> 13.8 us
    pallas_call x12 -> x14, Pallas kernels: 18.8 us -> 19.9 us  [call(): pl.pallas_call(kernel, out_shape=tuple(outs), in_specs=[fixed if i in loo...]
    ppermute x22, waiting for transfers between devices: 12.9 us -> 13.8 us  [swap(): return lax.ppermute(block, axis, [(i, i ^ bits) for i in range(size)])]
where the time goes in v6:
time: 70.3 us; the launch traced here: 70.1 us
  Pallas kernels  28.7 us (41%)
  starting transfers between devices  26.8 us (38%)
  waiting for transfers between devices  13.8 us (20%)
  between operations  0.77 us (1%)
    ppermute x22, starting transfers between devices, swap(): return lax.ppermute(block, axis, [(i, i ^ bits) for i in range(size)])  26.8 us
    pallas_call x14, Pallas kernels, call(): pl.pallas_call(kernel, out_shape=tuple(outs), in_specs=[fixed if i in loo...  19.9 us
    ppermute x22, waiting for transfers between devices, swap(): return lax.ppermute(block, axis, [(i, i ^ bits) for i in range(size)])  13.8 us
    pallas_call x1, Pallas kernels, shards(): pl.pallas_call(grads_kernel, grid=(parts,), out_shape=(shape(w_gate.shape...  8.84 us
  transfers between devices with their start and end apart: 22, of which 9 were waited for; matrix products, arithmetic and copies ran while one was open for 0% of the time, Pallas kernels for 37%

profile of v6, /device:TPU:0, one launch (start us, length us, event | category | flops | bytes accessed | tf_op | source)
XLA Modules:
  0.0 70.1 jit_solution(42524809554559262)
XLA Ops:
  0.6 1.6 %pack.1 = (s32[1,256]{1,0:T(1,128)S(1)}, bf16[128,384]{1,0:T(8,128)(2,1)S(1)}, bf16[48,384]{1,0:T(8,128)(2,1)S(1)}, bf16[48,384]{1,0:T(8,128)(2,1)S(1)}, bf16[48...) custom-call(s32[4]{0:T(128)} %refs_0_.1, s32[4]{0:T(128)} %refs_1_.1, s32[2,128]{1,0:T(2,128)} %bitcast.4, ...), custom_call_target="tpu_custom_call" | custom-call | tf_op jit(solution)/shard_map/pack/pallas_call | solution.py:355
  2.2 4.1 %collective-permute-start.1 = (bf16[128,384]{1,0:T(8,128)(2,1)S(1)}, bf16[128,384]{1,0:T(8,128)(2,1)S(1)}, u32[]{:S(2)}, u32[]{:S(2)}) collective-permute-start(bf16[128,384]{1,0:T(8,128)(2,1)S(1)} %get-tuple-element.56.refs_0_), channel_id=1, source_target_pairs={{0,4},{2,6},{4,0},{6,2},{1,5},{3,7},{5,1},{7,3},{8,12},{10,14},{12... | collective-permute-start | bytes 294920 | tf_op jit(solution)/shard_map/ppermute | solution.py:336
  6.3 1.6 %collective-permute-start = (bf16[128,384]{1,0:T(8,128)(2,1)S(1)}, bf16[128,384]{1,0:T(8,128)(2,1)S(1)}, u32[]{:S(2)}, u32[]{:S(2)}) collective-permute-start(bf16[128,384]{1,0:T(8,128)(2,1)S(1)} %get-tuple-element.56.refs_0_), channel_id=1, source_target_pairs={{0,2},{2,0},{4,6},{6,4},{1,3},{3,1},{5,7},{7,5},{8,10},{10,8},{12,... | collective-permute-start | bytes 294920 | tf_op jit(solution)/shard_map/ppermute | solution.py:336
  7.9 2.8 %load_gate.1 = (bf16[3072,1024]{1,0:T(8,128)(2,1)S(1)}, f32[8,128]{1,0:T(8,128)S(1)}) custom-call(bf16[1,3072,1024]{2,1,0:T(8,128)(2,1)} %source.6), custom_call_target="tpu_custom_call" | custom-call | bytes 12582912 | tf_op jit(solution)/shard_map/load_gate/pallas_call | solution.py:355
  10.7 0.4 collective-permute-done.1.block_ref.refs_7_.refs_2_
  11.1 0.9 %collective-permute-start.2 = (bf16[128,384]{1,0:T(8,128)(2,1)S(1)}, bf16[128,384]{1,0:T(8,128)(2,1)S(1)}, u32[]{:S(2)}, u32[]{:S(2)}) collective-permute-start(bf16[128,384]{1,0:T(8,128)(2,1)S(1)} %relay.1), channel_id=1, source_target_pairs={{0,2},{2,0},{4,6},{6,4},{1,3},{3,1},{5,7},{7,5},{8,10},{10,8},{12,... | collective-permute-start | bytes 294920 | tf_op jit(solution)/shard_map/ppermute | solution.py:336
  12.0 1.5 %collective-permute-start.3 = (bf16[48,384]{1,0:T(8,128)(2,1)S(1)}, bf16[48,384]{1,0:T(8,128)(2,1)S(1)}, u32[]{:S(2)}, u32[]{:S(2)}) collective-permute-start(bf16[48,384]{1,0:T(8,128)(2,1)S(1)} %get-tuple-element.59), channel_id=1, source_target_pairs={{0,8},{8,0},{16,24},{24,16},{1,9},{9,1},{17,25},{25,17},{2,10},{10... | collective-permute-start | bytes 110600 | tf_op jit(solution)/shard_map/ppermute | solution.py:336
  13.5 1.5 %collective-permute-start.4 = (bf16[48,384]{1,0:T(8,128)(2,1)S(1)}, bf16[48,384]{1,0:T(8,128)(2,1)S(1)}, u32[]{:S(2)}, u32[]{:S(2)}) collective-permute-start(bf16[48,384]{1,0:T(8,128)(2,1)S(1)} %get-tuple-element.60), channel_id=1, source_target_pairs={{0,16},{8,24},{16,0},{24,8},{1,17},{9,25},{17,1},{25,9},{2,18},{10... | collective-permute-start | bytes 110600 | tf_op jit(solution)/shard_map/ppermute | solution.py:336
  15.0 0.5 collective-permute-start.5
  15.5 1.9 %load_up_a.1 = (bf16[1536,1024]{1,0:T(8,128)(2,1)S(1)}, f32[8,128]{1,0:T(8,128)S(1)}) custom-call(bf16[1,3072,1024]{2,1,0:T(8,128)(2,1)} %source.7), custom_call_target="tpu_custom_call" | custom-call | bytes 6291456 | tf_op jit(solution)/shard_map/load_up_a/pallas_call | solution.py:355
  17.4 0.0 collective-permute-done.3.refs_1_
  17.4 0.0 collective-permute-done.4.refs_2_
  17.5 2.4 %collective-permute-done.5.refs_3_ = bf16[48,384]{1,0:T(8,128)(2,1)S(1)} collective-permute-done((bf16[48,384]{1,0:T(8,128)(2,1)S(1)}, bf16[48,384]{1,0:T(8,128)(2,1)S(1)}, u32[]{:S(2)}, u32[]{:S(2)}) %collective-permute-start.5) | collective-permute-done | bytes 36896 | tf_op jit(solution)/shard_map/ppermute | solution.py:336
  19.9 0.0 collective-permute-done.refs_6_.refs_1_
  19.9 0.0 collective-permute-done.2.refs_8_.refs_3_
  19.9 0.3 pick.1
  20.2 0.6 collective-permute-start.6
  20.8 3.4 %collective-permute-start.10 = (bf16[4,48,384]{2,1,0:T(8,128)(2,1)S(1)}, bf16[4,48,384]{2,1,0:T(8,128)(2,1)S(1)}, u32[]{:S(2)}, u32[]{:S(2)}) collective-permute-start(bf16[4,48,384]{2,1,0:T(8,128)(2,1)S(1)} %stack.1.refs_4_), channel_id=1, source_target_pairs={{0,4},{2,6},{4,0},{6,2},{1,5},{3,7},{5,1},{7,3},{8,12},{10,14},{12... | collective-permute-start | bytes 442376 | tf_op jit(solution)/shard_map/ppermute | solution.py:336
  24.2 0.4 collective-permute-start.11
  24.6 0.1 collective-permute-start.9
  24.8 0.5 collective-permute-start.7
  25.3 0.0 collective-permute-done.6.refs_1_
  25.3 2.4 %collective-permute-start.8 = (bf16[4,40,384]{2,1,0:T(8,128)(2,1)S(1)}, bf16[4,40,384]{2,1,0:T(8,128)(2,1)S(1)}, u32[]{:S(2)}, u32[]{:S(2)}) collective-permute-start(bf16[4,40,384]{2,1,0:T(8,128)(2,1)S(1)} %get-tuple-element.66), channel_id=1, source_target_pairs={{0,24},{8,16},{16,8},{24,0},{1,25},{9,17},{17,9},{25,1},{2,26},{10... | collective-permute-start | bytes 368648 | tf_op jit(solution)/shard_map/ppermute | solution.py:336
  27.7 1.9 %load_up_b.1 = (bf16[1536,1024]{1,0:T(8,128)(2,1)S(1)}, f32[8,128]{1,0:T(8,128)S(1)}) custom-call(bf16[1,3072,1024]{2,1,0:T(8,128)(2,1)} %source.7), custom_call_target="tpu_custom_call" | custom-call | bytes 6291456 | tf_op jit(solution)/shard_map/load_up_b/pallas_call | solution.py:355
  29.6 2.8 %load_down.1 = (bf16[1024,3072]{1,0:T(8,128)(2,1)S(1)}, f32[8,128]{1,0:T(8,128)S(1)}) custom-call(bf16[1,1024,3072]{2,1,0:T(8,128)(2,1)} %source.5), custom_call_target="tpu_custom_call" | custom-call | bytes 12582912 | tf_op jit(solution)/shard_map/load_down/pallas_call | solution.py:355
  32.4 0.0 collective-permute-done.7.refs_2_
  32.5 0.0 collective-permute-done.8.refs_3_
  32.5 1.2 %collective-permute-done.10.refs_6_ = bf16[4,48,384]{2,1,0:T(8,128)(2,1)S(1)} collective-permute-done((bf16[4,48,384]{2,1,0:T(8,128)(2,1)S(1)}, bf16[4,48,384]{2,1,0:T(8,128)(2,1)S(1)}, u32[]{:S(2)}, u32[]{:S(2)}) %collective-permute-start.10) | collective-permute-done | bytes 147488 | tf_op jit(solution)/shard_map/ppermute | solution.py:336
  33.7 0.0 collective-permute-done.11.refs_7_
  33.7 0.0 collective-permute-done.9.refs_5_
  33.7 0.1 join.1
  33.8 0.1 collective-permute-start.12
  33.8 0.5 collective-permute-start.14
  34.3 1.5 %collective-permute-done.12.refs_1_ = bf16[4,4,48,384]{3,2,1,0:T(8,128)(2,1)S(1)} collective-permute-done((bf16[4,4,48,384]{3,2,1,0:T(8,128)(2,1)S(1)}, bf16[4,4,48,384]{3,2,1,0:T(8,128)(2,1)S(1)}, u32[]{:S(2)}, u32[]{:S(2)}) %collective-permute-start.12) | collective-permute-done | bytes 589856 | tf_op jit(solution)/shard_map/ppermute | solution.py:336
  35.8 4.2 %forward.1 = (bf16[192,3072]{1,0:T(8,128)(2,1)S(1)}, bf16[192,1024]{1,0:T(8,128)(2,1)S(1)}, f32[192,1024]{1,0:T(8,128)S(1)}, f32[192,1024]{1,0:T(8,128)S(1)}, f3...) custom-call(bf16[4,4,48,384]{3,2,1,0:T(8,128)(2,1)S(1)} %get-tuple-e, ...), custom_call_target="tpu_custom_call" | custom-call | flops 3623878656 | bytes 18874368 | tf_op jit(solution)/shard_map/forward/pallas_call | solution.py:355
  40.0 0.2 collective-permute-start.13
  40.2 0.0 collective-permute-done.14.refs_1_
  40.2 3.2 %backward.1 = (bf16[192,3072]{1,0:T(8,128)(2,1)S(1)}, bf16[192,1024]{1,0:T(8,128)(2,1)S(1)}, bf16[192,1024]{1,0:T(8,128)(2,1)S(1)}, f32[4,4,384]{2,1,0:T(4,128)S(1)}, bf16[4,8,384]{2,1,0:T(8,128)(2,1)S(1)}) custom-call(bf16[4,4,40,384]{3,2,1,0:T(8,128)(2,1)S(1)} %get-tuple-element.74.refs_0_, bf16[4,4,40,384]{3,2,1,0:T(8,128)(2,1)S(1)} %collective-permute-done.14.refs_1_, ...), custom_call_target="tpu_custom_call" | custom-call | flops 1207959552 | bytes 6291456 | tf_op jit(solution)/shard_map/backward/pallas_call | solution.py:355
  43.5 0.4 collective-permute-start.15
  43.9 0.8 %collective-permute-done.15.rgot_ref = bf16[4,8,384]{2,1,0:T(8,128)(2,1)S(1)} collective-permute-done((bf16[4,8,384]{2,1,0:T(8,128)(2,1)S(1)}, bf16[4,8,384]{2,1,0:T(8,128)(2,1)S(1)}, u32[]{:S(2)}, u32[]{:S(2)}) %collective-permute-start.15) | collective-permute-done | bytes 24608 | tf_op jit(solution)/shard_map/ppermute | solution.py:336
  44.8 0.0 collective-permute-done.13.got_ref
  44.8 0.1 merge.1
  44.9 2.6 %collective-permute-start.16 = (bf16[4,48,384]{2,1,0:T(8,128)(2,1)S(1)}, bf16[4,48,384]{2,1,0:T(8,128)(2,1)S(1)}, u32[]{:S(2)}, u32[]{:S(2)}) collective-permute-start(bf16[4,48,384]{2,1,0:T(8,128)(2,1)S(1)} %get-tuple-element.85), channel_id=1, source_target_pairs={{0,6},{2,4},{4,2},{6,0},{1,7},{3,5},{5,3},{7,1},{8,14},{10,12},{12... | collective-permute-start | bytes 442376 | tf_op jit(solution)/shard_map/ppermute | solution.py:336
  47.5 1.0 %collective-permute-start.17 = (bf16[4,48,384]{2,1,0:T(8,128)(2,1)S(1)}, bf16[4,48,384]{2,1,0:T(8,128)(2,1)S(1)}, u32[]{:S(2)}, u32[]{:S(2)}) collective-permute-start(bf16[4,48,384]{2,1,0:T(8,128)(2,1)S(1)} %get-tuple-element.86), channel_id=1, source_target_pairs={{0,4},{2,6},{4,0},{6,2},{1,5},{3,7},{5,1},{7,3},{8,12},{10,14},{12... | collective-permute-start | bytes 442376 | tf_op jit(solution)/shard_map/ppermute | solution.py:336
  48.6 0.8 %collective-permute-start.18 = (bf16[4,48,384]{2,1,0:T(8,128)(2,1)S(1)}, bf16[4,48,384]{2,1,0:T(8,128)(2,1)S(1)}, u32[]{:S(2)}, u32[]{:S(2)}) collective-permute-start(bf16[4,48,384]{2,1,0:T(8,128)(2,1)S(1)} %get-tuple-element.87), channel_id=1, source_target_pairs={{0,2},{2,0},{4,6},{6,4},{1,3},{3,1},{5,7},{7,5},{8,10},{10,8},{12,... | collective-permute-start | bytes 442376 | tf_op jit(solution)/shard_map/ppermute | solution.py:336
  49.3 8.8 %grads.1 = (bf16[1,3072,1024]{2,1,0:T(8,128)(2,1)}, bf16[1,3072,1024]{2,1,0:T(8,128)(2,1)}, bf16[1,1024,3072]{2,1,0:T(8,128)(2,1)}, f32[8,128]{1,0:T(8,128)S(1)}) custom-call(bf16[192,3072]{1,0:T(8,128)(2,1)S(1)} %get-tuple-element.75.refs_2_.x_ref, bf16[192,3072]{1,0:T(8,128)(2,1)S(1)} %get-tuple-element.88.d_ref, ...), custom_call_target="tpu_custom_call" | custom-call | flops 3623878656 | bytes 18874368 | tf_op jit(solution)/shard_map/grads/pallas_call | solution.py:484
  58.2 0.0 collective-permute-done.16.refs_1_
  58.2 4.0 %collective-permute-done.17.refs_2_ = bf16[4,48,384]{2,1,0:T(8,128)(2,1)S(1)} collective-permute-done((bf16[4,48,384]{2,1,0:T(8,128)(2,1)S(1)}, bf16[4,48,384]{2,1,0:T(8,128)(2,1)S(1)}, u32[]{:S(2)}, u32[]{:S(2)}) %collective-permute-start.17) | collective-permute-done | bytes 147488 | tf_op jit(solution)/shard_map/ppermute | solution.py:336
  62.2 0.0 collective-permute-done.18.refs_3_
  62.2 0.1 total.1
  62.2 1.6 %collective-permute-start.19 = (bf16[48,384]{1,0:T(8,128)(2,1)S(1)}, bf16[48,384]{1,0:T(8,128)(2,1)S(1)}, u32[]{:S(2)}, u32[]{:S(2)}) collective-permute-start(bf16[48,384]{1,0:T(8,128)(2,1)S(1)} %get-tuple-element.93), channel_id=1, source_target_pairs={{0,8},{8,0},{16,24},{24,16},{1,9},{9,1},{17,25},{25,17},{2,10},{10... | collective-permute-start | bytes 110600 | tf_op jit(solution)/shard_map/ppermute | solution.py:336
  63.8 0.5 collective-permute-start.20
  64.3 1.5 %collective-permute-start.21 = (bf16[48,384]{1,0:T(8,128)(2,1)S(1)}, bf16[48,384]{1,0:T(8,128)(2,1)S(1)}, u32[]{:S(2)}, u32[]{:S(2)}) collective-permute-start(bf16[48,384]{1,0:T(8,128)(2,1)S(1)} %get-tuple-element.95), channel_id=1, source_target_pairs={{0,24},{8,16},{16,8},{24,0},{1,25},{9,17},{17,9},{25,1},{2,26},{10... | collective-permute-start | bytes 110600 | tf_op jit(solution)/shard_map/ppermute | solution.py:336
  65.8 0.5 collective-permute-done.19.refs_1_
  66.3 1.6 %collective-permute-done.20.refs_2_ = bf16[48,384]{1,0:T(8,128)(2,1)S(1)} collective-permute-done((bf16[48,384]{1,0:T(8,128)(2,1)S(1)}, bf16[48,384]{1,0:T(8,128)(2,1)S(1)}, u32[]{:S(2)}, u32[]{:S(2)}) %collective-permute-start.20) | collective-permute-done | bytes 36896 | tf_op jit(solution)/shard_map/ppermute | solution.py:336
  67.9 1.3 %collective-permute-done.21.refs_3_ = bf16[48,384]{1,0:T(8,128)(2,1)S(1)} collective-permute-done((bf16[48,384]{1,0:T(8,128)(2,1)S(1)}, bf16[48,384]{1,0:T(8,128)(2,1)S(1)}, u32[]{:S(2)}, u32[]{:S(2)}) %collective-permute-start.21) | collective-permute-done | bytes 36896 | tf_op jit(solution)/shard_map/ppermute | solution.py:336
  69.2 0.9 %combine.1 = (bf16[128,384]{1,0:T(8,128)(2,1)}, bf16[4,384]{1,0:T(4,128)(2,1)}) custom-call(s32[1,256]{1,0:T(1,128)S(1)} %get-tuple-element.53.pos_ref, bf16[48,384]{1,0:T(8,128)(2,1)S(1)} %get-tuple-element.92.refs_0_, bf16[48,384]{1,0:T(8,128)(2,1)S(1)} %collective-permute-done.19.refs_1_, bf16[48,384]{1,0:T(8,128)(2,1)S(1)} %collective-permute-done.20.refs_2_, ...), custom_call_target="tpu_custom_call" | custom-call | tf_op jit(solution)/shard_map/combine/pallas_call | solution.py:355
  (2 shorter events, 0.0 us)
Async XLA Ops:
  2.2 8.9 %collective-permute-start.1 = (bf16[128,384]{1,0:T(8,128)(2,1)S(1)}, bf16[128,384]{1,0:T(8,128)(2,1)S(1)}, u32[]{:S(2)}, u32[]{:S(2)}) collective-permute-start(bf16[128,384]{1,0:T(8,128)(2,1)S(1)} %get-tuple-element.56.refs_0_), channel_id=1, source_target_pairs={{0,4},{2,6},{4,0},{6,2},{1,5},{3,7},{5,1},{7,3},{8,12},{10,14},{12... | collective-permute-start | bytes 294920 | tf_op jit(solution)/shard_map/ppermute | solution.py:336
  6.3 13.6 %collective-permute-start = (bf16[128,384]{1,0:T(8,128)(2,1)S(1)}, bf16[128,384]{1,0:T(8,128)(2,1)S(1)}, u32[]{:S(2)}, u32[]{:S(2)}) collective-permute-start(bf16[128,384]{1,0:T(8,128)(2,1)S(1)} %get-tuple-element.56.refs_0_), channel_id=1, source_target_pairs={{0,2},{2,0},{4,6},{6,4},{1,3},{3,1},{5,7},{7,5},{8,10},{10,8},{12,... | collective-permute-start | bytes 294920 | tf_op jit(solution)/shard_map/ppermute | solution.py:336
  11.1 8.8 %collective-permute-start.2 = (bf16[128,384]{1,0:T(8,128)(2,1)S(1)}, bf16[128,384]{1,0:T(8,128)(2,1)S(1)}, u32[]{:S(2)}, u32[]{:S(2)}) collective-permute-start(bf16[128,384]{1,0:T(8,128)(2,1)S(1)} %relay.1), channel_id=1, source_target_pairs={{0,2},{2,0},{4,6},{6,4},{1,3},{3,1},{5,7},{7,5},{8,10},{10,8},{12,... | collective-permute-start | bytes 294920 | tf_op jit(solution)/shard_map/ppermute | solution.py:336
  12.0 5.4 %collective-permute-start.3 = (bf16[48,384]{1,0:T(8,128)(2,1)S(1)}, bf16[48,384]{1,0:T(8,128)(2,1)S(1)}, u32[]{:S(2)}, u32[]{:S(2)}) collective-permute-start(bf16[48,384]{1,0:T(8,128)(2,1)S(1)} %get-tuple-element.59), channel_id=1, source_target_pairs={{0,8},{8,0},{16,24},{24,16},{1,9},{9,1},{17,25},{25,17},{2,10},{10... | collective-permute-start | bytes 110600 | tf_op jit(solution)/shard_map/ppermute | solution.py:336
  13.5 4.0 %collective-permute-start.4 = (bf16[48,384]{1,0:T(8,128)(2,1)S(1)}, bf16[48,384]{1,0:T(8,128)(2,1)S(1)}, u32[]{:S(2)}, u32[]{:S(2)}) collective-permute-start(bf16[48,384]{1,0:T(8,128)(2,1)S(1)} %get-tuple-element.60), channel_id=1, source_target_pairs={{0,16},{8,24},{16,0},{24,8},{1,17},{9,25},{17,1},{25,9},{2,18},{10... | collective-permute-start | bytes 110600 | tf_op jit(solution)/shard_map/ppermute | solution.py:336
  15.0 4.9 %collective-permute-start.5 = (bf16[48,384]{1,0:T(8,128)(2,1)S(1)}, bf16[48,384]{1,0:T(8,128)(2,1)S(1)}, u32[]{:S(2)}, u32[]{:S(2)}) collective-permute-start(bf16[48,384]{1,0:T(8,128)(2,1)S(1)} %get-tuple-element.61), channel_id=1, source_target_pairs={{0,24},{8,16},{16,8},{24,0},{1,25},{9,17},{17,9},{25,1},{2,26},{10... | collective-permute-start | bytes 110600 | tf_op jit(solution)/shard_map/ppermute | solution.py:336
  20.2 5.1 %collective-permute-start.6 = (bf16[4,40,384]{2,1,0:T(8,128)(2,1)S(1)}, bf16[4,40,384]{2,1,0:T(8,128)(2,1)S(1)}, u32[]{:S(2)}, u32[]{:S(2)}) collective-permute-start(bf16[4,40,384]{2,1,0:T(8,128)(2,1)S(1)} %get-tuple-element.64), channel_id=1, source_target_pairs={{0,8},{8,0},{16,24},{24,16},{1,9},{9,1},{17,25},{25,17},{2,10},{10... | collective-permute-start | bytes 368648 | tf_op jit(solution)/shard_map/ppermute | solution.py:336
  20.8 12.8 %collective-permute-start.10 = (bf16[4,48,384]{2,1,0:T(8,128)(2,1)S(1)}, bf16[4,48,384]{2,1,0:T(8,128)(2,1)S(1)}, u32[]{:S(2)}, u32[]{:S(2)}) collective-permute-start(bf16[4,48,384]{2,1,0:T(8,128)(2,1)S(1)} %stack.1.refs_4_), channel_id=1, source_target_pairs={{0,4},{2,6},{4,0},{6,2},{1,5},{3,7},{5,1},{7,3},{8,12},{10,14},{12... | collective-permute-start | bytes 442376 | tf_op jit(solution)/shard_map/ppermute | solution.py:336
  24.2 9.5 %collective-permute-start.11 = (bf16[4,48,384]{2,1,0:T(8,128)(2,1)S(1)}, bf16[4,48,384]{2,1,0:T(8,128)(2,1)S(1)}, u32[]{:S(2)}, u32[]{:S(2)}) collective-permute-start(bf16[4,48,384]{2,1,0:T(8,128)(2,1)S(1)} %stack.1.refs_4_), channel_id=1, source_target_pairs={{0,6},{2,4},{4,2},{6,0},{1,7},{3,5},{5,3},{7,1},{8,14},{10,12},{12... | collective-permute-start | bytes 442376 | tf_op jit(solution)/shard_map/ppermute | solution.py:336
  24.6 9.0 %collective-permute-start.9 = (bf16[4,48,384]{2,1,0:T(8,128)(2,1)S(1)}, bf16[4,48,384]{2,1,0:T(8,128)(2,1)S(1)}, u32[]{:S(2)}, u32[]{:S(2)}) collective-permute-start(bf16[4,48,384]{2,1,0:T(8,128)(2,1)S(1)} %stack.1.refs_4_), channel_id=1, source_target_pairs={{0,2},{2,0},{4,6},{6,4},{1,3},{3,1},{5,7},{7,5},{8,10},{10,8},{12,... | collective-permute-start | bytes 442376 | tf_op jit(solution)/shard_map/ppermute | solution.py:336
  24.8 7.7 %collective-permute-start.7 = (bf16[4,40,384]{2,1,0:T(8,128)(2,1)S(1)}, bf16[4,40,384]{2,1,0:T(8,128)(2,1)S(1)}, u32[]{:S(2)}, u32[]{:S(2)}) collective-permute-start(bf16[4,40,384]{2,1,0:T(8,128)(2,1)S(1)} %get-tuple-element.65), channel_id=1, source_target_pairs={{0,16},{8,24},{16,0},{24,8},{1,17},{9,25},{17,1},{25,9},{2,18},{10... | collective-permute-start | bytes 368648 | tf_op jit(solution)/shard_map/ppermute | solution.py:336
  25.3 7.2 %collective-permute-start.8 = (bf16[4,40,384]{2,1,0:T(8,128)(2,1)S(1)}, bf16[4,40,384]{2,1,0:T(8,128)(2,1)S(1)}, u32[]{:S(2)}, u32[]{:S(2)}) collective-permute-start(bf16[4,40,384]{2,1,0:T(8,128)(2,1)S(1)} %get-tuple-element.66), channel_id=1, source_target_pairs={{0,24},{8,16},{16,8},{24,0},{1,25},{9,17},{17,9},{25,1},{2,26},{10... | collective-permute-start | bytes 368648 | tf_op jit(solution)/shard_map/ppermute | solution.py:336
  33.8 2.1 %collective-permute-start.12 = (bf16[4,4,48,384]{3,2,1,0:T(8,128)(2,1)S(1)}, bf16[4,4,48,384]{3,2,1,0:T(8,128)(2,1)S(1)}, u32[]{:S(2)}, u32[]{:S(2)}) collective-permute-start(bf16[4,4,48,384]{3,2,1,0:T(8,128)(2,1)S(1)} %get-tuple-element.67.refs_0_), channel_id=1, source_target_pairs={{0,1},{1,0},{2,3},{3,2},{4,5},{5,4},{6,7},{7,6},{8,9},{9,8},{10,11... | collective-permute-start | bytes 1769480 | tf_op jit(solution)/shard_map/ppermute | solution.py:336
  33.8 6.4 %collective-permute-start.14 = (bf16[4,4,40,384]{3,2,1,0:T(8,128)(2,1)S(1)}, bf16[4,4,40,384]{3,2,1,0:T(8,128)(2,1)S(1)}, u32[]{:S(2)}, u32[]{:S(2)}) collective-permute-start(bf16[4,4,40,384]{3,2,1,0:T(8,128)(2,1)S(1)} %get-tuple-element.74.refs_0_), channel_id=1, source_target_pairs={{0,1},{1,0},{2,3},{3,2},{4,5},{5,4},{6,7},{7,6},{8,9},{9,8},{10,11... | collective-permute-start | bytes 1474568 | tf_op jit(solution)/shard_map/ppermute | solution.py:336
  40.0 4.7 %collective-permute-start.13 = (bf16[4,4,48,384]{3,2,1,0:T(8,128)(2,1)S(1)}, bf16[4,4,48,384]{3,2,1,0:T(8,128)(2,1)S(1)}, u32[]{:S(2)}, u32[]{:S(2)}) collective-permute-start(bf16[4,4,48,384]{3,2,1,0:T(8,128)(2,1)S(1)} %get-tuple-element.73), channel_id=1, source_target_pairs={{0,1},{1,0},{2,3},{3,2},{4,5},{5,4},{6,7},{7,6},{8,9},{9,8},{10,11... | collective-permute-start | bytes 1769480 | tf_op jit(solution)/shard_map/ppermute | solution.py:336
  43.5 1.3 %collective-permute-start.15 = (bf16[4,8,384]{2,1,0:T(8,128)(2,1)S(1)}, bf16[4,8,384]{2,1,0:T(8,128)(2,1)S(1)}, u32[]{:S(2)}, u32[]{:S(2)}) collective-permute-start(bf16[4,8,384]{2,1,0:T(8,128)(2,1)S(1)} %get-tuple-element.83), channel_id=1, source_target_pairs={{0,1},{1,0},{2,3},{3,2},{4,5},{5,4},{6,7},{7,6},{8,9},{9,8},{10,11... | collective-permute-start | bytes 73736 | tf_op jit(solution)/shard_map/ppermute | solution.py:336
  44.9 13.3 %collective-permute-start.16 = (bf16[4,48,384]{2,1,0:T(8,128)(2,1)S(1)}, bf16[4,48,384]{2,1,0:T(8,128)(2,1)S(1)}, u32[]{:S(2)}, u32[]{:S(2)}) collective-permute-start(bf16[4,48,384]{2,1,0:T(8,128)(2,1)S(1)} %get-tuple-element.85), channel_id=1, source_target_pairs={{0,6},{2,4},{4,2},{6,0},{1,7},{3,5},{5,3},{7,1},{8,14},{10,12},{12... | collective-permute-start | bytes 442376 | tf_op jit(solution)/shard_map/ppermute | solution.py:336
  47.5 14.6 %collective-permute-start.17 = (bf16[4,48,384]{2,1,0:T(8,128)(2,1)S(1)}, bf16[4,48,384]{2,1,0:T(8,128)(2,1)S(1)}, u32[]{:S(2)}, u32[]{:S(2)}) collective-permute-start(bf16[4,48,384]{2,1,0:T(8,128)(2,1)S(1)} %get-tuple-element.86), channel_id=1, source_target_pairs={{0,4},{2,6},{4,0},{6,2},{1,5},{3,7},{5,1},{7,3},{8,12},{10,14},{12... | collective-permute-start | bytes 442376 | tf_op jit(solution)/shard_map/ppermute | solution.py:336
  48.6 13.6 %collective-permute-start.18 = (bf16[4,48,384]{2,1,0:T(8,128)(2,1)S(1)}, bf16[4,48,384]{2,1,0:T(8,128)(2,1)S(1)}, u32[]{:S(2)}, u32[]{:S(2)}) collective-permute-start(bf16[4,48,384]{2,1,0:T(8,128)(2,1)S(1)} %get-tuple-element.87), channel_id=1, source_target_pairs={{0,2},{2,0},{4,6},{6,4},{1,3},{3,1},{5,7},{7,5},{8,10},{10,8},{12,... | collective-permute-start | bytes 442376 | tf_op jit(solution)/shard_map/ppermute | solution.py:336
  62.2 4.0 %collective-permute-start.19 = (bf16[48,384]{1,0:T(8,128)(2,1)S(1)}, bf16[48,384]{1,0:T(8,128)(2,1)S(1)}, u32[]{:S(2)}, u32[]{:S(2)}) collective-permute-start(bf16[48,384]{1,0:T(8,128)(2,1)S(1)} %get-tuple-element.93), channel_id=1, source_target_pairs={{0,8},{8,0},{16,24},{24,16},{1,9},{9,1},{17,25},{25,17},{2,10},{10... | collective-permute-start | bytes 110600 | tf_op jit(solution)/shard_map/ppermute | solution.py:336
  63.8 4.1 %collective-permute-start.20 = (bf16[48,384]{1,0:T(8,128)(2,1)S(1)}, bf16[48,384]{1,0:T(8,128)(2,1)S(1)}, u32[]{:S(2)}, u32[]{:S(2)}) collective-permute-start(bf16[48,384]{1,0:T(8,128)(2,1)S(1)} %get-tuple-element.94), channel_id=1, source_target_pairs={{0,16},{8,24},{16,0},{24,8},{1,17},{9,25},{17,1},{25,9},{2,18},{10... | collective-permute-start | bytes 110600 | tf_op jit(solution)/shard_map/ppermute | solution.py:336
  64.3 4.9 %collective-permute-start.21 = (bf16[48,384]{1,0:T(8,128)(2,1)S(1)}, bf16[48,384]{1,0:T(8,128)(2,1)S(1)}, u32[]{:S(2)}, u32[]{:S(2)}) collective-permute-start(bf16[48,384]{1,0:T(8,128)(2,1)S(1)} %get-tuple-element.95), channel_id=1, source_target_pairs={{0,24},{8,16},{16,8},{24,0},{1,25},{9,17},{17,9},{25,1},{2,26},{10... | collective-permute-start | bytes 110600 | tf_op jit(solution)/shard_map/ppermute | solution.py:336

commit v7 on v1

--- a/solution.py
+++ b/solution.py
@@ -257,18 +257,13 @@
         put(out_refs[k], keep_ref[k] + got_ref[k].astype(F32), router)
 
 
-def pass_kernel(block_ref, _, out_ref):
+def pass_kernel(block_ref, _, __, out_ref):
     out_ref[...] = block_ref[...]
 
 
 def put(out_ref, blocks, router):
-    groups, height, width = out_ref.shape
-    spare = height - CAP - router.shape[0]
-    for q in range(groups):
-        rows = [blocks[q][:CAP], router]
-        if spare:
-            rows.append(jnp.zeros((spare, width), F32))
-        out_ref[q] = jnp.concatenate(rows, axis=0).astype(BF16)
+    rows = [blocks[q, :CAP] for q in range(blocks.shape[0])]
+    out_ref[...] = jnp.concatenate([*rows, router], axis=0).astype(BF16)
 
 
 def grads_kernel(x_ref, d_ref, dgate_ref, dup_ref, hid_ref, _, gate_ref, up_ref, down_ref, mark_ref):
@@ -280,23 +275,19 @@
     mark_ref[...] = jnp.zeros(mark_ref.shape, F32)
 
 
-def add_blocks(experts, parts, sends):
-    router = None
+def sum_kernel(experts, groups, *refs):
+    parts, sends = refs[: len(refs) - groups - 1], refs[len(refs) - groups :]
+    total = parts[0][...].astype(F32)
+    for ref in parts[1:]:
+        total = total + ref[...].astype(F32)
+    router = total[groups * CAP :]
+    router = halves(router[:experts] + router[experts:])
+    height, width = sends[0].shape
     for q, send in enumerate(sends):
-        block = parts[0][q].astype(F32)
-        for ref in parts[1:]:
-            block = block + ref[q].astype(F32)
-        if router is None:
-            router = halves(block[CAP : CAP + experts] + block[CAP + experts : CAP + 2 * experts])
-        height, width = send.shape
-        rows = [block[:CAP], router]
+        rows = [total[q * CAP : (q + 1) * CAP], router]
         if height > CAP + 2 * experts:
             rows.append(jnp.zeros((height - CAP - 2 * experts, width), F32))
         send[...] = jnp.concatenate(rows, axis=0).astype(BF16)
-
-
-def sum_kernel(experts, groups, *refs):
-    add_blocks(experts, refs[: len(refs) - groups - 1], refs[len(refs) - groups :])
 
 
 def combine_kernel(groups, pos_ref, *refs):
@@ -395,7 +386,7 @@
         if hops > 1:
             blocks.append(swap(stacked, "z", 1))
         if hops > 2:
-            (relay,) = call(pass_kernel, (second, down_mark), [shape(second.shape, BF16)], "relay")
+            (relay,) = call(pass_kernel, (second, blocks[1], down_mark), [shape(second.shape, BF16)], "relay")
             blocks += [second, swap(relay, "z", 1)]
     else:
         blocks = [lax.all_gather(stacked, "z", axis=0, tiled=False)]
@@ -441,11 +432,11 @@
     merged = call(
         merge_kernel,
         (keep, got, router_keep, router_got),
-        [shape((groups, height, width), BF16)] * hops,
+        [shape((groups * CAP + 2 * experts, width), BF16)] * hops,
         "merge",
     )
     if relative:
-        outs = [merged[0]] + [swap(merged[k], "z", k) for k in range(1, hops)]
+        outs = [merged[0]] + [swap(merged[k], "z", k) for k in range(hops - 1, 0, -1)]
     else:
         outs = lax.all_to_all(jnp.stack(merged), "z", split_axis=0, concat_axis=0, tiled=True)
         outs = [outs[k] for k in range(hops)]

time: 70.6 us -> 70 us (level)
  waiting for transfers between devices: 22.9 us -> 20.8 us
  starting transfers between devices: 19.2 us -> 20.8 us
    ppermute x18, waiting for transfers between devices: 22.9 us -> 20.8 us  [swap(): return lax.ppermute(block, axis, [(i, i ^ bits) for i in range(size)])]
    ppermute x18, starting transfers between devices: 19.2 us -> 20.8 us  [swap(): return lax.ppermute(block, axis, [(i, i ^ bits) for i in range(size)])]
where the time goes in v7:
time: 70 us; the launch traced here: 69.7 us
  Pallas kernels  27.4 us (39%)
  starting transfers between devices  20.8 us (30%)
  waiting for transfers between devices  20.8 us (30%)
  between operations  0.75 us (1%)
    ppermute x18, waiting for transfers between devices, swap(): return lax.ppermute(block, axis, [(i, i ^ bits) for i in range(size)])  20.8 us
    ppermute x18, starting transfers between devices, swap(): return lax.ppermute(block, axis, [(i, i ^ bits) for i in range(size)])  20.8 us
    pallas_call x11, Pallas kernels, call(): pl.pallas_call(kernel, out_shape=tuple(outs), in_specs=[fixed if i in loo...  18.5 us
    pallas_call x1, Pallas kernels, shards(): pl.pallas_call(grads_kernel, grid=(parts,), out_shape=(shape(w_gate.shape...  8.84 us
  transfers between devices with their start and end apart: 18, of which 9 were waited for; matrix products, arithmetic and copies ran while one was open for 0% of the time, Pallas kernels for 29%

profile of v7, /device:TPU:0, one launch (start us, length us, event | category | flops | bytes accessed | tf_op | source)
XLA Modules:
  0.0 69.7 jit_solution(1554798249757704139)
XLA Ops:
  0.6 1.6 %pack.1 = (s32[1,256]{1,0:T(1,128)S(1)}, bf16[88,384]{1,0:T(8,128)(2,1)S(1)}, bf16[88,384]{1,0:T(8,128)(2,1)S(1)}, bf16[88,384]{1,0:T(8,128)(2,1)S(1)}, bf16[88,384]{1,0:T(8,128)(2,1)S(1)}) custom-call(s32[4]{0:T(128)} %refs_0_.1, s32[4]{0:T(128)} %refs_1_.1, s32[2,128]{1,0:T(2,128)} %bitcast.4, bf16[4,384]{1,0:T(4,128)(2,1)} %bitcast.3, ...), custom_call_target="tpu_custom_call" | custom-call | tf_op jit(solution)/shard_map/pack/pallas_call | solution.py:333
  2.2 3.0 %collective-permute-start = (bf16[88,384]{1,0:T(8,128)(2,1)S(1)}, bf16[88,384]{1,0:T(8,128)(2,1)S(1)}, u32[]{:S(2)}, u32[]{:S(2)}) collective-permute-start(bf16[88,384]{1,0:T(8,128)(2,1)S(1)} %get-tuple-element.46), channel_id=1, source_target_pairs={{0,8},{8,0},{16,24},{24,16},{1,9},{9,1},{17,25},{25,17},{2,10},{10... | collective-permute-start | bytes 202760 | tf_op jit(solution)/shard_map/ppermute | solution.py:314
  5.2 1.5 %collective-permute-start.1 = (bf16[88,384]{1,0:T(8,128)(2,1)S(1)}, bf16[88,384]{1,0:T(8,128)(2,1)S(1)}, u32[]{:S(2)}, u32[]{:S(2)}) collective-permute-start(bf16[88,384]{1,0:T(8,128)(2,1)S(1)} %get-tuple-element.47), channel_id=1, source_target_pairs={{0,16},{8,24},{16,0},{24,8},{1,17},{9,25},{17,1},{25,9},{2,18},{10... | collective-permute-start | bytes 202760 | tf_op jit(solution)/shard_map/ppermute | solution.py:314
  6.7 0.0 collective-permute-start.2
  6.8 2.8 %load_gate.1 = (bf16[1,3072,1024]{2,1,0:T(8,128)(2,1)S(1)}, f32[8,128]{1,0:T(8,128)S(1)}) custom-call(bf16[1,3072,1024]{2,1,0:T(8,128)(2,1)} %source.3), custom_call_target="tpu_custom_call" | custom-call | bytes 12582912 | tf_op jit(solution)/shard_map/load_gate/pallas_call | solution.py:333
  9.6 2.8 %load_up.1 = (bf16[1,3072,1024]{2,1,0:T(8,128)(2,1)S(1)}, f32[8,128]{1,0:T(8,128)S(1)}) custom-call(bf16[1,3072,1024]{2,1,0:T(8,128)(2,1)} %source.4), custom_call_target="tpu_custom_call" | custom-call | bytes 12582912 | tf_op jit(solution)/shard_map/load_up/pallas_call | solution.py:333
  12.4 0.0 collective-permute-done.refs_1_
  12.4 0.0 collective-permute-done.1.refs_2_
  12.4 0.0 collective-permute-done.2.refs_3_
  12.4 3.1 %collective-permute-start.4 = (bf16[4,88,384]{2,1,0:T(8,128)(2,1)S(1)}, bf16[4,88,384]{2,1,0:T(8,128)(2,1)S(1)}, u32[]{:S(2)}, u32[]{:S(2)}) collective-permute-start(bf16[4,88,384]{2,1,0:T(8,128)(2,1)S(1)} %stack.1.refs_0_), channel_id=1, source_target_pairs={{0,4},{2,6},{4,0},{6,2},{1,5},{3,7},{5,1},{7,3},{8,12},{10,14},{12... | collective-permute-start | bytes 811016 | tf_op jit(solution)/shard_map/ppermute | solution.py:314
  15.6 1.6 %collective-permute-start.3 = (bf16[4,88,384]{2,1,0:T(8,128)(2,1)S(1)}, bf16[4,88,384]{2,1,0:T(8,128)(2,1)S(1)}, u32[]{:S(2)}, u32[]{:S(2)}) collective-permute-start(bf16[4,88,384]{2,1,0:T(8,128)(2,1)S(1)} %stack.1.refs_0_), channel_id=1, source_target_pairs={{0,2},{2,0},{4,6},{6,4},{1,3},{3,1},{5,7},{7,5},{8,10},{10,8},{12,... | collective-permute-start | bytes 811016 | tf_op jit(solution)/shard_map/ppermute | solution.py:314
  17.1 2.8 %load_down.1 = (bf16[1,1024,3072]{2,1,0:T(8,128)(2,1)S(1)}, f32[8,128]{1,0:T(8,128)S(1)}) custom-call(bf16[1,1024,3072]{2,1,0:T(8,128)(2,1)} %source.5), custom_call_target="tpu_custom_call" | custom-call | bytes 12582912 | tf_op jit(solution)/shard_map/load_down/pallas_call | solution.py:333
  19.9 7.2 %collective-permute-done.4.block_ref.refs_2_ = bf16[4,88,384]{2,1,0:T(8,128)(2,1)S(1)} collective-permute-done((bf16[4,88,384]{2,1,0:T(8,128)(2,1)S(1)}, bf16[4,88,384]{2,1,0:T(8,128)(2,1)S(1)}, u32[]{:S(2)}, u32[]{:S(2)}) %collective-permute-start.4) | collective-permute-done | bytes 270368 | tf_op jit(solution)/shard_map/ppermute | solution.py:314
  27.1 0.2 collective-permute-done.3._.refs_1_
  27.3 1.6 %collective-permute-start.5 = (bf16[4,88,384]{2,1,0:T(8,128)(2,1)S(1)}, bf16[4,88,384]{2,1,0:T(8,128)(2,1)S(1)}, u32[]{:S(2)}, u32[]{:S(2)}) collective-permute-start(bf16[4,88,384]{2,1,0:T(8,128)(2,1)S(1)} %relay.1), channel_id=1, source_target_pairs={{0,2},{2,0},{4,6},{6,4},{1,3},{3,1},{5,7},{7,5},{8,10},{10,8},{12,... | collective-permute-start | bytes 811016 | tf_op jit(solution)/shard_map/ppermute | solution.py:314
  28.9 0.0 collective-permute-start.6
  28.9 0.5 collective-permute-start.8
  29.4 0.0 collective-permute-start.7
  29.4 5.1 %collective-permute-done.5.refs_3_ = bf16[4,88,384]{2,1,0:T(8,128)(2,1)S(1)} collective-permute-done((bf16[4,88,384]{2,1,0:T(8,128)(2,1)S(1)}, bf16[4,88,384]{2,1,0:T(8,128)(2,1)S(1)}, u32[]{:S(2)}, u32[]{:S(2)}) %collective-permute-start.5) | collective-permute-done | bytes 270368 | tf_op jit(solution)/shard_map/ppermute | solution.py:314
  34.5 0.0 collective-permute-start.9
  34.5 0.0 collective-permute-done.6.refs_4_
  34.5 0.0 collective-permute-done.8.refs_6_
  34.5 0.0 collective-permute-done.7.refs_5_
  34.5 1.5 %collective-permute-done.9.refs_7_ = bf16[4,88,384]{2,1,0:T(8,128)(2,1)S(1)} collective-permute-done((bf16[4,88,384]{2,1,0:T(8,128)(2,1)S(1)}, bf16[4,88,384]{2,1,0:T(8,128)(2,1)S(1)}, u32[]{:S(2)}, u32[]{:S(2)}) %collective-permute-start.9) | collective-permute-done | bytes 270368 | tf_op jit(solution)/shard_map/ppermute | solution.py:314
  36.0 4.2 %forward.1 = (bf16[192,3072]{1,0:T(8,128)(2,1)S(1)}, bf16[192,1024]{1,0:T(8,128)(2,1)S(1)}, f32[192,1024]{1,0:T(8,128)S(1)}, f32[192,1024]{1,0:T(8,128)S(1)}, f3...) custom-call(bf16[4,88,384]{2,1,0:T(8,128)(2,1)S(1)} %stack.1.refs_0_, ...), custom_call_target="tpu_custom_call" | custom-call | flops 3623878656 | bytes 18874368 | tf_op jit(solution)/shard_map/forward/pallas_call | solution.py:333
  40.3 0.2 collective-permute-start.10
  40.4 3.3 %backward.1 = (bf16[192,3072]{1,0:T(8,128)(2,1)S(1)}, bf16[192,1024]{1,0:T(8,128)(2,1)S(1)}, bf16[192,1024]{1,0:T(8,128)(2,1)S(1)}, f32[4,4,384]{2,1,0:T(4,128)S(1)}, bf16[4,8,384]{2,1,0:T(8,128)(2,1)S(1)}) custom-call(bf16[4,88,384]{2,1,0:T(8,128)(2,1)S(1)} %stack.1.refs_0_, bf16[4,88,384]{2,1,0:T(8,128)(2,1)S(1)} %collective-permute-done.3._.refs_1_, ...), custom_call_target="tpu_custom_call" | custom-call | flops 1207959552 | bytes 6291456 | tf_op jit(solution)/shard_map/backward/pallas_call | solution.py:333
  43.7 0.4 collective-permute-start.11
  44.2 0.8 %collective-permute-done.11.rgot_ref = bf16[4,8,384]{2,1,0:T(8,128)(2,1)S(1)} collective-permute-done((bf16[4,8,384]{2,1,0:T(8,128)(2,1)S(1)}, bf16[4,8,384]{2,1,0:T(8,128)(2,1)S(1)}, u32[]{:S(2)}, u32[]{:S(2)}) %collective-permute-start.11) | collective-permute-done | bytes 24608 | tf_op jit(solution)/shard_map/ppermute | solution.py:314
  45.0 0.0 collective-permute-done.10.got_ref
  45.0 0.1 merge.1
  45.1 4.6 %collective-permute-start.12 = (bf16[168,384]{1,0:T(8,128)(2,1)S(1)}, bf16[168,384]{1,0:T(8,128)(2,1)S(1)}, u32[]{:S(2)}, u32[]{:S(2)}) collective-permute-start(bf16[168,384]{1,0:T(8,128)(2,1)S(1)} %get-tuple-element.67), channel_id=1, source_target_pairs={{0,6},{2,4},{4,2},{6,0},{1,7},{3,5},{5,3},{7,1},{8,14},{10,12},{12... | collective-permute-start | bytes 387080 | tf_op jit(solution)/shard_map/ppermute | solution.py:314
  49.7 0.0 collective-permute-start.13
  49.7 0.6 collective-permute-start.14
  50.4 8.8 %grads.1 = (bf16[1,3072,1024]{2,1,0:T(8,128)(2,1)}, bf16[1,3072,1024]{2,1,0:T(8,128)(2,1)}, bf16[1,1024,3072]{2,1,0:T(8,128)(2,1)}, f32[8,128]{1,0:T(8,128)S(1)}) custom-call(bf16[192,3072]{1,0:T(8,128)(2,1)S(1)} %get-tuple-element.57.refs_8_.x_ref, bf16[192,3072]{1,0:T(8,128)(2,1)S(1)} %get-tuple-element.70.d_ref, ...), custom_call_target="tpu_custom_call" | custom-call | flops 3623878656 | bytes 18874368 | tf_op jit(solution)/shard_map/grads/pallas_call | solution.py:448
  59.2 0.0 collective-permute-done.12.refs_1_
  59.2 1.6 %collective-permute-done.13.refs_2_ = bf16[168,384]{1,0:T(8,128)(2,1)S(1)} collective-permute-done((bf16[168,384]{1,0:T(8,128)(2,1)S(1)}, bf16[168,384]{1,0:T(8,128)(2,1)S(1)}, u32[]{:S(2)}, u32[]{:S(2)}) %collective-permute-start.13) | collective-permute-done | bytes 129056 | tf_op jit(solution)/shard_map/ppermute | solution.py:314
  60.8 0.0 collective-permute-done.14.refs_3_
  60.8 0.1 total.1
  60.9 1.6 %collective-permute-start.15 = (bf16[48,384]{1,0:T(8,128)(2,1)S(1)}, bf16[48,384]{1,0:T(8,128)(2,1)S(1)}, u32[]{:S(2)}, u32[]{:S(2)}) collective-permute-start(bf16[48,384]{1,0:T(8,128)(2,1)S(1)} %get-tuple-element.75), channel_id=1, source_target_pairs={{0,8},{8,0},{16,24},{24,16},{1,9},{9,1},{17,25},{25,17},{2,10},{10... | collective-permute-start | bytes 110600 | tf_op jit(solution)/shard_map/ppermute | solution.py:314
  62.5 1.5 %collective-permute-start.16 = (bf16[48,384]{1,0:T(8,128)(2,1)S(1)}, bf16[48,384]{1,0:T(8,128)(2,1)S(1)}, u32[]{:S(2)}, u32[]{:S(2)}) collective-permute-start(bf16[48,384]{1,0:T(8,128)(2,1)S(1)} %get-tuple-element.76), channel_id=1, source_target_pairs={{0,16},{8,24},{16,0},{24,8},{1,17},{9,25},{17,1},{25,9},{2,18},{10... | collective-permute-start | bytes 110600 | tf_op jit(solution)/shard_map/ppermute | solution.py:314
  64.0 0.5 collective-permute-start.17
  64.5 0.5 collective-permute-done.15.refs_1_
  64.9 1.5 %collective-permute-done.16.refs_2_ = bf16[48,384]{1,0:T(8,128)(2,1)S(1)} collective-permute-done((bf16[48,384]{1,0:T(8,128)(2,1)S(1)}, bf16[48,384]{1,0:T(8,128)(2,1)S(1)}, u32[]{:S(2)}, u32[]{:S(2)}) %collective-permute-start.16) | collective-permute-done | bytes 36896 | tf_op jit(solution)/shard_map/ppermute | solution.py:314
  66.4 2.4 %collective-permute-done.17.refs_3_ = bf16[48,384]{1,0:T(8,128)(2,1)S(1)} collective-permute-done((bf16[48,384]{1,0:T(8,128)(2,1)S(1)}, bf16[48,384]{1,0:T(8,128)(2,1)S(1)}, u32[]{:S(2)}, u32[]{:S(2)}) %collective-permute-start.17) | collective-permute-done | bytes 36896 | tf_op jit(solution)/shard_map/ppermute | solution.py:314
  68.8 0.9 %combine.1 = (bf16[128,384]{1,0:T(8,128)(2,1)}, bf16[4,384]{1,0:T(4,128)(2,1)}) custom-call(s32[1,256]{1,0:T(1,128)S(1)} %get-tuple-element.44.pos_ref, bf16[48,384]{1,0:T(8,128)(2,1)S(1)} %get-tuple-element.74.refs_0_, bf16[48,384]{1,0:T(8,128)(2,1)S(1)} %collective-permute-done.15.refs_1_, bf16[48,384]{1,0:T(8,128)(2,1)S(1)} %collective-permute-done.16.refs_2_, ...), custom_call_target="tpu_custom_call" | custom-call | tf_op jit(solution)/shard_map/combine/pallas_call | solution.py:333
  (2 shorter events, 0.1 us)
Async XLA Ops:
  2.2 10.2 %collective-permute-start = (bf16[88,384]{1,0:T(8,128)(2,1)S(1)}, bf16[88,384]{1,0:T(8,128)(2,1)S(1)}, u32[]{:S(2)}, u32[]{:S(2)}) collective-permute-start(bf16[88,384]{1,0:T(8,128)(2,1)S(1)} %get-tuple-element.46), channel_id=1, source_target_pairs={{0,8},{8,0},{16,24},{24,16},{1,9},{9,1},{17,25},{25,17},{2,10},{10... | collective-permute-start | bytes 202760 | tf_op jit(solution)/shard_map/ppermute | solution.py:314
  5.2 7.2 %collective-permute-start.1 = (bf16[88,384]{1,0:T(8,128)(2,1)S(1)}, bf16[88,384]{1,0:T(8,128)(2,1)S(1)}, u32[]{:S(2)}, u32[]{:S(2)}) collective-permute-start(bf16[88,384]{1,0:T(8,128)(2,1)S(1)} %get-tuple-element.47), channel_id=1, source_target_pairs={{0,16},{8,24},{16,0},{24,8},{1,17},{9,25},{17,1},{25,9},{2,18},{10... | collective-permute-start | bytes 202760 | tf_op jit(solution)/shard_map/ppermute | solution.py:314
  6.7 5.6 %collective-permute-start.2 = (bf16[88,384]{1,0:T(8,128)(2,1)S(1)}, bf16[88,384]{1,0:T(8,128)(2,1)S(1)}, u32[]{:S(2)}, u32[]{:S(2)}) collective-permute-start(bf16[88,384]{1,0:T(8,128)(2,1)S(1)} %get-tuple-element.48), channel_id=1, source_target_pairs={{0,24},{8,16},{16,8},{24,0},{1,25},{9,17},{17,9},{25,1},{2,26},{10... | collective-permute-start | bytes 202760 | tf_op jit(solution)/shard_map/ppermute | solution.py:314
  12.4 14.7 %collective-permute-start.4 = (bf16[4,88,384]{2,1,0:T(8,128)(2,1)S(1)}, bf16[4,88,384]{2,1,0:T(8,128)(2,1)S(1)}, u32[]{:S(2)}, u32[]{:S(2)}) collective-permute-start(bf16[4,88,384]{2,1,0:T(8,128)(2,1)S(1)} %stack.1.refs_0_), channel_id=1, source_target_pairs={{0,4},{2,6},{4,0},{6,2},{1,5},{3,7},{5,1},{7,3},{8,12},{10,14},{12... | collective-permute-start | bytes 811016 | tf_op jit(solution)/shard_map/ppermute | solution.py:314
  15.6 11.7 %collective-permute-start.3 = (bf16[4,88,384]{2,1,0:T(8,128)(2,1)S(1)}, bf16[4,88,384]{2,1,0:T(8,128)(2,1)S(1)}, u32[]{:S(2)}, u32[]{:S(2)}) collective-permute-start(bf16[4,88,384]{2,1,0:T(8,128)(2,1)S(1)} %stack.1.refs_0_), channel_id=1, source_target_pairs={{0,2},{2,0},{4,6},{6,4},{1,3},{3,1},{5,7},{7,5},{8,10},{10,8},{12,... | collective-permute-start | bytes 811016 | tf_op jit(solution)/shard_map/ppermute | solution.py:314
  27.3 7.2 %collective-permute-start.5 = (bf16[4,88,384]{2,1,0:T(8,128)(2,1)S(1)}, bf16[4,88,384]{2,1,0:T(8,128)(2,1)S(1)}, u32[]{:S(2)}, u32[]{:S(2)}) collective-permute-start(bf16[4,88,384]{2,1,0:T(8,128)(2,1)S(1)} %relay.1), channel_id=1, source_target_pairs={{0,2},{2,0},{4,6},{6,4},{1,3},{3,1},{5,7},{7,5},{8,10},{10,8},{12,... | collective-permute-start | bytes 811016 | tf_op jit(solution)/shard_map/ppermute | solution.py:314
  28.9 5.6 %collective-permute-start.6 = (bf16[4,88,384]{2,1,0:T(8,128)(2,1)S(1)}, bf16[4,88,384]{2,1,0:T(8,128)(2,1)S(1)}, u32[]{:S(2)}, u32[]{:S(2)}) collective-permute-start(bf16[4,88,384]{2,1,0:T(8,128)(2,1)S(1)} %stack.1.refs_0_), channel_id=1, source_target_pairs={{0,1},{1,0},{2,3},{3,2},{4,5},{5,4},{6,7},{7,6},{8,9},{9,8},{10,11... | collective-permute-start | bytes 811016 | tf_op jit(solution)/shard_map/ppermute | solution.py:314
  28.9 5.6 %collective-permute-start.8 = (bf16[4,88,384]{2,1,0:T(8,128)(2,1)S(1)}, bf16[4,88,384]{2,1,0:T(8,128)(2,1)S(1)}, u32[]{:S(2)}, u32[]{:S(2)}) collective-permute-start(bf16[4,88,384]{2,1,0:T(8,128)(2,1)S(1)} %collective-permute-done.4.block_ref.refs_2_), channel_id=1, source_target_pairs={{0,1},{1,0},{2,3},{3,2},{4,5},{5,4},{6,7},{7,6},{8,9},{9,8},{10,11... | collective-permute-start | bytes 811016 | tf_op jit(solution)/shard_map/ppermute | solution.py:314
  29.4 5.1 %collective-permute-start.7 = (bf16[4,88,384]{2,1,0:T(8,128)(2,1)S(1)}, bf16[4,88,384]{2,1,0:T(8,128)(2,1)S(1)}, u32[]{:S(2)}, u32[]{:S(2)}) collective-permute-start(bf16[4,88,384]{2,1,0:T(8,128)(2,1)S(1)} %collective-permute-done.3._.refs_1_), channel_id=1, source_target_pairs={{0,1},{1,0},{2,3},{3,2},{4,5},{5,4},{6,7},{7,6},{8,9},{9,8},{10,11... | collective-permute-start | bytes 811016 | tf_op jit(solution)/shard_map/ppermute | solution.py:314
  34.5 1.5 %collective-permute-start.9 = (bf16[4,88,384]{2,1,0:T(8,128)(2,1)S(1)}, bf16[4,88,384]{2,1,0:T(8,128)(2,1)S(1)}, u32[]{:S(2)}, u32[]{:S(2)}) collective-permute-start(bf16[4,88,384]{2,1,0:T(8,128)(2,1)S(1)} %collective-permute-done.5.refs_3_), channel_id=1, source_target_pairs={{0,1},{1,0},{2,3},{3,2},{4,5},{5,4},{6,7},{7,6},{8,9},{9,8},{10,11... | collective-permute-start | bytes 811016 | tf_op jit(solution)/shard_map/ppermute | solution.py:314
  40.3 4.8 %collective-permute-start.10 = (bf16[4,4,48,384]{3,2,1,0:T(8,128)(2,1)S(1)}, bf16[4,4,48,384]{3,2,1,0:T(8,128)(2,1)S(1)}, u32[]{:S(2)}, u32[]{:S(2)}) collective-permute-start(bf16[4,4,48,384]{3,2,1,0:T(8,128)(2,1)S(1)} %get-tuple-element.56), channel_id=1, source_target_pairs={{0,1},{1,0},{2,3},{3,2},{4,5},{5,4},{6,7},{7,6},{8,9},{9,8},{10,11... | collective-permute-start | bytes 1769480 | tf_op jit(solution)/shard_map/ppermute | solution.py:314
  43.7 1.3 %collective-permute-start.11 = (bf16[4,8,384]{2,1,0:T(8,128)(2,1)S(1)}, bf16[4,8,384]{2,1,0:T(8,128)(2,1)S(1)}, u32[]{:S(2)}, u32[]{:S(2)}) collective-permute-start(bf16[4,8,384]{2,1,0:T(8,128)(2,1)S(1)} %get-tuple-element.65), channel_id=1, source_target_pairs={{0,1},{1,0},{2,3},{3,2},{4,5},{5,4},{6,7},{7,6},{8,9},{9,8},{10,11... | collective-permute-start | bytes 73736 | tf_op jit(solution)/shard_map/ppermute | solution.py:314
  45.1 14.1 %collective-permute-start.12 = (bf16[168,384]{1,0:T(8,128)(2,1)S(1)}, bf16[168,384]{1,0:T(8,128)(2,1)S(1)}, u32[]{:S(2)}, u32[]{:S(2)}) collective-permute-start(bf16[168,384]{1,0:T(8,128)(2,1)S(1)} %get-tuple-element.67), channel_id=1, source_target_pairs={{0,6},{2,4},{4,2},{6,0},{1,7},{3,5},{5,3},{7,1},{8,14},{10,12},{12... | collective-permute-start | bytes 387080 | tf_op jit(solution)/shard_map/ppermute | solution.py:314
  49.7 11.1 %collective-permute-start.13 = (bf16[168,384]{1,0:T(8,128)(2,1)S(1)}, bf16[168,384]{1,0:T(8,128)(2,1)S(1)}, u32[]{:S(2)}, u32[]{:S(2)}) collective-permute-start(bf16[168,384]{1,0:T(8,128)(2,1)S(1)} %get-tuple-element.68), channel_id=1, source_target_pairs={{0,4},{2,6},{4,0},{6,2},{1,5},{3,7},{5,1},{7,3},{8,12},{10,14},{12... | collective-permute-start | bytes 387080 | tf_op jit(solution)/shard_map/ppermute | solution.py:314
  49.7 11.1 %collective-permute-start.14 = (bf16[168,384]{1,0:T(8,128)(2,1)S(1)}, bf16[168,384]{1,0:T(8,128)(2,1)S(1)}, u32[]{:S(2)}, u32[]{:S(2)}) collective-permute-start(bf16[168,384]{1,0:T(8,128)(2,1)S(1)} %get-tuple-element.69), channel_id=1, source_target_pairs={{0,2},{2,0},{4,6},{6,4},{1,3},{3,1},{5,7},{7,5},{8,10},{10,8},{12,... | collective-permute-start | bytes 387080 | tf_op jit(solution)/shard_map/ppermute | solution.py:314
  60.9 4.0 %collective-permute-start.15 = (bf16[48,384]{1,0:T(8,128)(2,1)S(1)}, bf16[48,384]{1,0:T(8,128)(2,1)S(1)}, u32[]{:S(2)}, u32[]{:S(2)}) collective-permute-start(bf16[48,384]{1,0:T(8,128)(2,1)S(1)} %get-tuple-element.75), channel_id=1, source_target_pairs={{0,8},{8,0},{16,24},{24,16},{1,9},{9,1},{17,25},{25,17},{2,10},{10... | collective-permute-start | bytes 110600 | tf_op jit(solution)/shard_map/ppermute | solution.py:314
  62.5 4.0 %collective-permute-start.16 = (bf16[48,384]{1,0:T(8,128)(2,1)S(1)}, bf16[48,384]{1,0:T(8,128)(2,1)S(1)}, u32[]{:S(2)}, u32[]{:S(2)}) collective-permute-start(bf16[48,384]{1,0:T(8,128)(2,1)S(1)} %get-tuple-element.76), channel_id=1, source_target_pairs={{0,16},{8,24},{16,0},{24,8},{1,17},{9,25},{17,1},{25,9},{2,18},{10... | collective-permute-start | bytes 110600 | tf_op jit(solution)/shard_map/ppermute | solution.py:314
  64.0 4.9 %collective-permute-start.17 = (bf16[48,384]{1,0:T(8,128)(2,1)S(1)}, bf16[48,384]{1,0:T(8,128)(2,1)S(1)}, u32[]{:S(2)}, u32[]{:S(2)}) collective-permute-start(bf16[48,384]{1,0:T(8,128)(2,1)S(1)} %get-tuple-element.77), channel_id=1, source_target_pairs={{0,24},{8,16},{16,8},{24,0},{1,25},{9,17},{17,9},{25,1},{2,26},{10... | collective-permute-start | bytes 110600 | tf_op jit(solution)/shard_map/ppermute | solution.py:314

commit v8 on v4

--- a/solution.py
+++ b/solution.py
@@ -108,7 +108,7 @@
         refs[-1][q] = refs[q][...]
 
 
-def join_kernel(groups, _, __, *refs):
+def join_kernel(groups, _, *refs):
     blocks_d, blocks_x, own_x, own_d = refs[:groups], refs[groups:-2], refs[-2], refs[-1]
     for q in range(groups):
         own_d[q] = blocks_d[q][...]
@@ -120,7 +120,7 @@
 
 
 def pick_kernel(relative, experts, hops, pos_ref, *refs):
-    sources, sends = refs[: len(refs) - experts], refs[len(refs) - experts :]
+    sources, sends = refs[: len(refs) - experts - 1], refs[len(refs) - experts :]
     merged = chosen(pos_ref[...], experts)
     for k in range(hops):
         rows = dot(merged, sources[k][...] if relative else sources[0][k], ((1,), (0,)))
@@ -272,45 +272,40 @@
 
 
 def put(out_ref, blocks, router):
-    groups, height, width = out_ref.shape
-    spare = height - CAP - router.shape[0]
-    for q in range(groups):
-        rows = [blocks[q][:CAP], router]
-        if spare:
-            rows.append(jnp.zeros((spare, width), F32))
-        out_ref[q] = jnp.concatenate(rows, axis=0).astype(BF16)
-
-
-def grads_kernel(x_ref, d_ref, dgate_ref, dup_ref, hid_ref, _, gate_ref, up_ref, down_ref, mark_ref):
+    rows = [blocks[q, :CAP] for q in range(blocks.shape[0])]
+    out_ref[...] = jnp.concatenate([*rows, router], axis=0).astype(BF16)
+
+
+def grads_kernel(x_ref, dgate_ref, dup_ref, _, gate_ref, up_ref, mark_ref):
     rows_x = x_ref[...]
     first = ((0,), (0,))
     gate_ref[0] = dot(rows_x, dgate_ref[...], first).astype(BF16)
     up_ref[0] = dot(rows_x, dup_ref[...], first).astype(BF16)
-    down_ref[0] = dot(hid_ref[...], d_ref[...], first).astype(BF16)
     mark_ref[...] = jnp.zeros(mark_ref.shape, F32)
 
 
-def add_blocks(experts, parts, sends):
-    router = None
+def grad_down_kernel(d_ref, hid_ref, _, down_ref, mark_ref):
+    down_ref[0] = dot(hid_ref[...], d_ref[...], ((0,), (0,))).astype(BF16)
+    mark_ref[...] = jnp.zeros(mark_ref.shape, F32)
+
+
+def sum_kernel(experts, groups, *refs):
+    parts, sends = refs[: len(refs) - groups - 1], refs[len(refs) - groups :]
+    total = parts[0][...].astype(F32)
+    for ref in parts[1:]:
+        total = total + ref[...].astype(F32)
+    router = total[groups * CAP :]
+    router = halves(router[:experts] + router[experts:])
+    height, width = sends[0].shape
     for q, send in enumerate(sends):
-        block = parts[0][q].astype(F32)
-        for ref in parts[1:]:
-            block = block + ref[q].astype(F32)
-        if router is None:
-            router = halves(block[CAP : CAP + experts] + block[CAP + experts : CAP + 2 * experts])
-        height, width = send.shape
-        rows = [block[:CAP], router]
+        rows = [total[q * CAP : (q + 1) * CAP], router]
         if height > CAP + 2 * experts:
             rows.append(jnp.zeros((height - CAP - 2 * experts, width), F32))
         send[...] = jnp.concatenate(rows, axis=0).astype(BF16)
 
 
-def sum_kernel(experts, groups, *refs):
-    add_blocks(experts, refs[: len(refs) - groups - 1], refs[len(refs) - groups :])
-
-
 def combine_kernel(groups, pos_ref, *refs):
-    backs, mixed_ref, router_ref = refs[:groups], refs[groups], refs[groups + 1]
+    backs, mixed_ref, router_ref = refs[:groups], refs[groups + 1], refs[groups + 2]
     experts, width = router_ref.shape
     blocks = []
     router = jnp.zeros((2 * experts, width), F32)
@@ -397,7 +392,7 @@
     slices = gather(handed)
     picked = call(
         functools.partial(pick_kernel, relative, experts, hops),
-        (position, *slices),
+        (position, *slices, up_mark),
         [shape((hops, CAP, width), BF16)] * experts,
         "pick",
     )
@@ -411,7 +406,7 @@
     blocks_d = [picked[0]] + [swap(picked[q], "expert", q) for q in range(1, groups)]
     own_x, own_d = call(
         functools.partial(join_kernel, groups),
-        (up_mark, down_mark, *blocks_d, *blocks_x),
+        (down_mark, *blocks_d, *blocks_x),
         [shape((hops, *stacked.shape), BF16), shape((groups, *picked[0].shape), BF16)],
         "join",
     )
@@ -458,7 +453,7 @@
     merged = call(
         merge_kernel,
         (keep, got, router_keep, router_got),
-        [shape((groups, height, width), BF16)] * hops,
+        [shape((groups * CAP + 2 * experts, width), BF16)] * hops,
         "merge",
     )
     if relative:
@@ -470,34 +465,26 @@
     parts = 8
     once = lambda *shape: pl.BlockSpec(shape, lambda i: (0,) * len(shape))
     strip = max(units // parts, LANES)
-    at = lambda i: i if units >= LANES * parts else 0
-    grad_gate, grad_up, grad_down, mark = pl.pallas_call(
+    marked = shape((8, LANES), F32)
+    grad_gate, grad_up, mark = pl.pallas_call(
         grads_kernel,
         grid=(parts,),
-        out_shape=(
-            shape(w_gate.shape, BF16),
-            shape(w_up.shape, BF16),
-            shape(w_down.shape, BF16),
-            shape((8, LANES), F32),
-        ),
+        out_shape=(shape(w_gate.shape, BF16), shape(w_up.shape, BF16), marked),
         in_specs=[
             pl.BlockSpec((rows, model // parts), lambda i: (0, i)),
-            once(rows, model),
             once(rows, units),
             once(rows, units),
-            pl.BlockSpec((rows, strip), lambda i: (0, at(i))),
             anywhere,
         ],
         out_specs=(
             pl.BlockSpec((1, model // parts, units), lambda i: (0, i, 0)),
             pl.BlockSpec((1, model // parts, units), lambda i: (0, i, 0)),
-            pl.BlockSpec((1, strip, model), lambda i: (0, at(i), 0)),
             once(8, LANES),
         ),
-        compiler_params=pltpu.CompilerParams(vmem_limit_bytes=24 * MIB),
-        cost_estimate=pl.CostEstimate(flops=3 * cost, bytes_accessed=6 * model * units, transcendentals=0),
+        compiler_params=pltpu.CompilerParams(vmem_limit_bytes=20 * MIB),
+        cost_estimate=pl.CostEstimate(flops=2 * cost, bytes_accessed=4 * model * units, transcendentals=0),
         name="grads",
-    )(rows_x, rows_d, d_gate, d_up, hidden, merged[0])
+    )(rows_x, d_gate, d_up, merged[0])
 
     backs = call(
         functools.partial(sum_kernel, experts, groups),
@@ -505,10 +492,20 @@
         [shape((height, width), BF16)] * groups,
         "total",
     )
+    grad_down, last = pl.pallas_call(
+        grad_down_kernel,
+        grid=(units // strip,),
+        out_shape=(shape(w_down.shape, BF16), marked),
+        in_specs=[once(rows, model), pl.BlockSpec((rows, strip), lambda i: (0, i)), anywhere],
+        out_specs=(pl.BlockSpec((1, strip, model), lambda i: (0, i, 0)), once(8, LANES)),
+        compiler_params=pltpu.CompilerParams(vmem_limit_bytes=20 * MIB),
+        cost_estimate=pl.CostEstimate(flops=cost, bytes_accessed=2 * model * units, transcendentals=0),
+        name="grad_down",
+    )(rows_d, hidden, backs[0])
     backs = [backs[0]] + [swap(backs[q], "expert", q) for q in range(1, groups)]
     mixed, grad_router = call(
         functools.partial(combine_kernel, groups),
-        (position, *backs),
+        (position, *backs, last),
         [shape((count, width), BF16), shape((experts, width), BF16)],
         "combine",
     )

time: 68.5 us -> 68.1 us (level)
  waiting for transfers between devices: 12.9 us -> 8.9 us
  Pallas kernels: 27.7 us -> 31.2 us
    pallas_call x0 -> x1, Pallas kernels: none -> 5.58 us  [shards(): pl.pallas_call(grad_down_kernel, grid=(units // strip,), out_shape=(shape...]
    ppermute x22, waiting for transfers between devices: 12.9 us -> 8.9 us  [swap(): return lax.ppermute(block, axis, [(i, i ^ bits) for i in range(size)])]
    pallas_call x1, Pallas kernels: 8.84 us -> 6.8 us  [shards(): pl.pallas_call(grads_kernel, grid=(parts,), out_shape=(shape(w_gate.shape...]
  transfers between devices with their start and end apart: 22 -> 22, of which waited for: 9 -> 7; matrix products, arithmetic and copies ran while one was open for 0% -> 0% of each run, Pallas kernels for 37% -> 42%
where the time goes in v8:
time: 68.1 us; the launch traced here: 67.8 us
  Pallas kernels  31.2 us (46%)
  starting transfers between devices  26.9 us (40%)
  waiting for transfers between devices  8.9 us (13%)
  between operations  0.78 us (1%)
    ppermute x22, starting transfers between devices, swap(): return lax.ppermute(block, axis, [(i, i ^ bits) for i in range(size)])  26.9 us
    pallas_call x12, Pallas kernels, call(): pl.pallas_call(kernel, out_shape=tuple(outs), in_specs=[fixed if i in loo...  18.9 us
    ppermute x22, waiting for transfers between devices, swap(): return lax.ppermute(block, axis, [(i, i ^ bits) for i in range(size)])  8.9 us
    pallas_call x1, Pallas kernels, shards(): pl.pallas_call(grads_kernel, grid=(parts,), out_shape=(shape(w_gate.shape...  6.8 us
    pallas_call x1, Pallas kernels, shards(): pl.pallas_call(grad_down_kernel, grid=(units // strip,), out_shape=(shape...  5.58 us
  transfers between devices with their start and end apart: 22, of which 7 were waited for; matrix products, arithmetic and copies ran while one was open for 0% of the time, Pallas kernels for 42%

profile of v8, /device:TPU:0, one launch (start us, length us, event | category | flops | bytes accessed | tf_op | source)
XLA Modules:
  0.0 67.8 jit_solution(10344522856237908801)
XLA Ops:
  0.6 1.6 %pack.1 = (s32[1,256]{1,0:T(1,128)S(1)}, bf16[128,384]{1,0:T(8,128)(2,1)S(1)}, bf16[48,384]{1,0:T(8,128)(2,1)S(1)}, bf16[48,384]{1,0:T(8,128)(2,1)S(1)}, bf16[48...) custom-call(s32[4]{0:T(128)} %refs_0_.1, s32[4]{0:T(128)} %refs_1_.1, s32[2,128]{1,0:T(2,128)} %bitcast.4, ...), custom_call_target="tpu_custom_call" | custom-call | tf_op jit(solution)/shard_map/pack/pallas_call | solution.py:344
  2.2 4.1 %collective-permute-start.1 = (bf16[128,384]{1,0:T(8,128)(2,1)S(1)}, bf16[128,384]{1,0:T(8,128)(2,1)S(1)}, u32[]{:S(2)}, u32[]{:S(2)}) collective-permute-start(bf16[128,384]{1,0:T(8,128)(2,1)S(1)} %get-tuple-element.54.refs_0_), channel_id=1, source_target_pairs={{0,4},{2,6},{4,0},{6,2},{1,5},{3,7},{5,1},{7,3},{8,12},{10,14},{12... | collective-permute-start | bytes 294920 | tf_op jit(solution)/shard_map/ppermute | solution.py:325
  6.3 1.6 %collective-permute-start = (bf16[128,384]{1,0:T(8,128)(2,1)S(1)}, bf16[128,384]{1,0:T(8,128)(2,1)S(1)}, u32[]{:S(2)}, u32[]{:S(2)}) collective-permute-start(bf16[128,384]{1,0:T(8,128)(2,1)S(1)} %get-tuple-element.54.refs_0_), channel_id=1, source_target_pairs={{0,2},{2,0},{4,6},{6,4},{1,3},{3,1},{5,7},{7,5},{8,10},{10,8},{12,... | collective-permute-start | bytes 294920 | tf_op jit(solution)/shard_map/ppermute | solution.py:325
  7.9 1.5 %collective-permute-start.6 = (bf16[48,384]{1,0:T(8,128)(2,1)S(1)}, bf16[48,384]{1,0:T(8,128)(2,1)S(1)}, u32[]{:S(2)}, u32[]{:S(2)}) collective-permute-start(bf16[48,384]{1,0:T(8,128)(2,1)S(1)} %get-tuple-element.61), channel_id=1, source_target_pairs={{0,8},{8,0},{16,24},{24,16},{1,9},{9,1},{17,25},{25,17},{2,10},{10... | collective-permute-start | bytes 110600 | tf_op jit(solution)/shard_map/ppermute | solution.py:325
  9.4 1.5 %collective-permute-start.7 = (bf16[48,384]{1,0:T(8,128)(2,1)S(1)}, bf16[48,384]{1,0:T(8,128)(2,1)S(1)}, u32[]{:S(2)}, u32[]{:S(2)}) collective-permute-start(bf16[48,384]{1,0:T(8,128)(2,1)S(1)} %get-tuple-element.62), channel_id=1, source_target_pairs={{0,16},{8,24},{16,0},{24,8},{1,17},{9,25},{17,1},{25,9},{2,18},{10... | collective-permute-start | bytes 110600 | tf_op jit(solution)/shard_map/ppermute | solution.py:325
  10.9 0.5 collective-permute-start.8
  11.4 2.8 %load_gate.1 = (bf16[1,3072,1024]{2,1,0:T(8,128)(2,1)S(1)}, f32[8,128]{1,0:T(8,128)S(1)}) custom-call(bf16[1,3072,1024]{2,1,0:T(8,128)(2,1)} %source.5), custom_call_target="tpu_custom_call" | custom-call | bytes 12582912 | tf_op jit(solution)/shard_map/load_gate/pallas_call | solution.py:344
  14.2 0.0 collective-permute-done.6.refs_1_
  14.2 0.0 collective-permute-done.7.refs_2_
  14.2 1.6 %collective-permute-done.8.refs_3_ = bf16[48,384]{1,0:T(8,128)(2,1)S(1)} collective-permute-done((bf16[48,384]{1,0:T(8,128)(2,1)S(1)}, bf16[48,384]{1,0:T(8,128)(2,1)S(1)}, u32[]{:S(2)}, u32[]{:S(2)}) %collective-permute-start.8) | collective-permute-done | bytes 36896 | tf_op jit(solution)/shard_map/ppermute | solution.py:325
  15.8 0.0 collective-permute-done.1.refs_2_.refs_6_
  15.8 0.0 collective-permute-done.refs_1_.refs_5_
  15.8 0.4 collective-permute-start.10
  16.2 0.5 collective-permute-start.2
  16.6 3.6 %collective-permute-start.11 = (bf16[4,48,384]{2,1,0:T(8,128)(2,1)S(1)}, bf16[4,48,384]{2,1,0:T(8,128)(2,1)S(1)}, u32[]{:S(2)}, u32[]{:S(2)}) collective-permute-start(bf16[4,48,384]{2,1,0:T(8,128)(2,1)S(1)} %stack.1.refs_4_), channel_id=1, source_target_pairs={{0,6},{2,4},{4,2},{6,0},{1,7},{3,5},{5,3},{7,1},{8,14},{10,12},{12... | collective-permute-start | bytes 442376 | tf_op jit(solution)/shard_map/ppermute | solution.py:325
  20.2 0.0 collective-permute-start.9
  20.2 2.8 %load_up.1 = (bf16[1,3072,1024]{2,1,0:T(8,128)(2,1)S(1)}, f32[8,128]{1,0:T(8,128)S(1)}) custom-call(bf16[1,3072,1024]{2,1,0:T(8,128)(2,1)} %source.4), custom_call_target="tpu_custom_call" | custom-call | bytes 12582912 | tf_op jit(solution)/shard_map/load_up/pallas_call | solution.py:344
  23.0 1.6 %collective-permute-done.2.refs_3_ = bf16[128,384]{1,0:T(8,128)(2,1)S(1)} collective-permute-done((bf16[128,384]{1,0:T(8,128)(2,1)S(1)}, bf16[128,384]{1,0:T(8,128)(2,1)S(1)}, u32[]{:S(2)}, u32[]{:S(2)}) %collective-permute-start.2) | collective-permute-done | bytes 98336 | tf_op jit(solution)/shard_map/ppermute | solution.py:325
  24.6 0.3 pick.1
  25.0 0.3 collective-permute-start.3
  25.3 2.2 %collective-permute-start.4 = (bf16[4,40,384]{2,1,0:T(8,128)(2,1)S(1)}, bf16[4,40,384]{2,1,0:T(8,128)(2,1)S(1)}, u32[]{:S(2)}, u32[]{:S(2)}) collective-permute-start(bf16[4,40,384]{2,1,0:T(8,128)(2,1)S(1)} %get-tuple-element.58), channel_id=1, source_target_pairs={{0,16},{8,24},{16,0},{24,8},{1,17},{9,25},{17,1},{25,9},{2,18},{10... | collective-permute-start | bytes 368648 | tf_op jit(solution)/shard_map/ppermute | solution.py:325
  27.4 0.2 collective-permute-done.10.refs_6_
  27.6 1.6 %collective-permute-start.5 = (bf16[4,40,384]{2,1,0:T(8,128)(2,1)S(1)}, bf16[4,40,384]{2,1,0:T(8,128)(2,1)S(1)}, u32[]{:S(2)}, u32[]{:S(2)}) collective-permute-start(bf16[4,40,384]{2,1,0:T(8,128)(2,1)S(1)} %get-tuple-element.59), channel_id=1, source_target_pairs={{0,24},{8,16},{16,8},{24,0},{1,25},{9,17},{17,9},{25,1},{2,26},{10... | collective-permute-start | bytes 368648 | tf_op jit(solution)/shard_map/ppermute | solution.py:325
  29.2 2.8 %load_down.1 = (bf16[1,1024,3072]{2,1,0:T(8,128)(2,1)S(1)}, f32[8,128]{1,0:T(8,128)S(1)}) custom-call(bf16[1,1024,3072]{2,1,0:T(8,128)(2,1)} %source.3), custom_call_target="tpu_custom_call" | custom-call | bytes 12582912 | tf_op jit(solution)/shard_map/load_down/pallas_call | solution.py:344
  32.0 0.0 collective-permute-done.11.refs_7_
  32.0 0.0 collective-permute-done.9.refs_5_
  32.0 0.0 collective-permute-done.3.refs_1_
  32.0 0.0 collective-permute-done.4.refs_2_
  32.0 1.4 %collective-permute-done.5.refs_3_ = bf16[4,40,384]{2,1,0:T(8,128)(2,1)S(1)} collective-permute-done((bf16[4,40,384]{2,1,0:T(8,128)(2,1)S(1)}, bf16[4,40,384]{2,1,0:T(8,128)(2,1)S(1)}, u32[]{:S(2)}, u32[]{:S(2)}) %collective-permute-start.5) | collective-permute-done | bytes 122912 | tf_op jit(solution)/shard_map/ppermute | solution.py:325
  33.4 0.1 join.1
  33.5 0.1 collective-permute-start.12
  33.6 0.5 collective-permute-start.14
  34.1 1.5 %collective-permute-done.12.refs_1_ = bf16[4,4,48,384]{3,2,1,0:T(8,128)(2,1)S(1)} collective-permute-done((bf16[4,4,48,384]{3,2,1,0:T(8,128)(2,1)S(1)}, bf16[4,4,48,384]{3,2,1,0:T(8,128)(2,1)S(1)}, u32[]{:S(2)}, u32[]{:S(2)}) %collective-permute-start.12) | collective-permute-done | bytes 589856 | tf_op jit(solution)/shard_map/ppermute | solution.py:325
  35.5 4.2 %forward.1 = (bf16[192,3072]{1,0:T(8,128)(2,1)S(1)}, bf16[192,1024]{1,0:T(8,128)(2,1)S(1)}, f32[192,1024]{1,0:T(8,128)S(1)}, f32[192,1024]{1,0:T(8,128)S(1)}, f3...) custom-call(bf16[4,4,48,384]{3,2,1,0:T(8,128)(2,1)S(1)} %get-tuple-e, ...), custom_call_target="tpu_custom_call" | custom-call | flops 3623878656 | bytes 18874368 | tf_op jit(solution)/shard_map/forward/pallas_call | solution.py:344
  39.8 0.2 collective-permute-start.13
  39.9 0.0 collective-permute-done.14.refs_1_
  39.9 3.2 %backward.1 = (bf16[192,3072]{1,0:T(8,128)(2,1)S(1)}, bf16[192,1024]{1,0:T(8,128)(2,1)S(1)}, bf16[192,1024]{1,0:T(8,128)(2,1)S(1)}, f32[4,4,384]{2,1,0:T(4,128)S(1)}, bf16[4,8,384]{2,1,0:T(8,128)(2,1)S(1)}) custom-call(bf16[4,4,40,384]{3,2,1,0:T(8,128)(2,1)S(1)} %get-tuple-element.71.refs_0_, bf16[4,4,40,384]{3,2,1,0:T(8,128)(2,1)S(1)} %collective-permute-done.14.refs_1_, ...), custom_call_target="tpu_custom_call" | custom-call | flops 1207959552 | bytes 6291456 | tf_op jit(solution)/shard_map/backward/pallas_call | solution.py:344
  43.2 0.5 collective-permute-start.15
  43.6 0.8 %collective-permute-done.15.rgot_ref = bf16[4,8,384]{2,1,0:T(8,128)(2,1)S(1)} collective-permute-done((bf16[4,8,384]{2,1,0:T(8,128)(2,1)S(1)}, bf16[4,8,384]{2,1,0:T(8,128)(2,1)S(1)}, u32[]{:S(2)}, u32[]{:S(2)}) %collective-permute-start.15) | collective-permute-done | bytes 24608 | tf_op jit(solution)/shard_map/ppermute | solution.py:325
  44.5 0.0 collective-permute-done.13.got_ref
  44.5 0.1 merge.1
  44.6 2.9 %collective-permute-start.16 = (bf16[168,384]{1,0:T(8,128)(2,1)S(1)}, bf16[168,384]{1,0:T(8,128)(2,1)S(1)}, u32[]{:S(2)}, u32[]{:S(2)}) collective-permute-start(bf16[168,384]{1,0:T(8,128)(2,1)S(1)} %get-tuple-element.82), channel_id=1, source_target_pairs={{0,6},{2,4},{4,2},{6,0},{1,7},{3,5},{5,3},{7,1},{8,14},{10,12},{12... | collective-permute-start | bytes 387080 | tf_op jit(solution)/shard_map/ppermute | solution.py:325
  47.6 0.0 collective-permute-start.17
  47.6 1.5 %collective-permute-start.18 = (bf16[168,384]{1,0:T(8,128)(2,1)S(1)}, bf16[168,384]{1,0:T(8,128)(2,1)S(1)}, u32[]{:S(2)}, u32[]{:S(2)}) collective-permute-start(bf16[168,384]{1,0:T(8,128)(2,1)S(1)} %get-tuple-element.84), channel_id=1, source_target_pairs={{0,2},{2,0},{4,6},{6,4},{1,3},{3,1},{5,7},{7,5},{8,10},{10,8},{12,... | collective-permute-start | bytes 387080 | tf_op jit(solution)/shard_map/ppermute | solution.py:325
  49.1 6.8 %grads.1 = (bf16[1,3072,1024]{2,1,0:T(8,128)(2,1)}, bf16[1,3072,1024]{2,1,0:T(8,128)(2,1)}, f32[8,128]{1,0:T(8,128)S(1)}) custom-call(bf16[192,3072]{1,0:T(8,128)(2,1)S(1)} %get-tuple-element.72.refs_2_.x_ref, bf16[192,1024]{1,0:T(8,128)(2,1)S(1)} %get-tuple-element.85.dgate_ref, bf16[192,1024]{1,0:T(8,128)(2,1)S(1)} %get-tuple-element.86.dup_ref, ...), custom_call_target="tpu_custom_call" | custom-call | flops 2415919104 | bytes 12582912 | tf_op jit(solution)/shard_map/grads/pallas_call | solution.py:469
  55.9 0.0 collective-permute-done.16.refs_1_
  55.9 1.8 %collective-permute-done.17.refs_2_ = bf16[168,384]{1,0:T(8,128)(2,1)S(1)} collective-permute-done((bf16[168,384]{1,0:T(8,128)(2,1)S(1)}, bf16[168,384]{1,0:T(8,128)(2,1)S(1)}, u32[]{:S(2)}, u32[]{:S(2)}) %collective-permute-start.17) | collective-permute-done | bytes 129056 | tf_op jit(solution)/shard_map/ppermute | solution.py:325
  57.7 0.0 collective-permute-done.18.refs_3_
  57.7 0.1 total.1
  57.8 1.2 %collective-permute-start.19 = (bf16[48,384]{1,0:T(8,128)(2,1)S(1)}, bf16[48,384]{1,0:T(8,128)(2,1)S(1)}, u32[]{:S(2)}, u32[]{:S(2)}) collective-permute-start(bf16[48,384]{1,0:T(8,128)(2,1)S(1)} %get-tuple-element.89), channel_id=1, source_target_pairs={{0,8},{8,0},{16,24},{24,16},{1,9},{9,1},{17,25},{25,17},{2,10},{10... | collective-permute-start | bytes 110600 | tf_op jit(solution)/shard_map/ppermute | solution.py:325
  59.0 1.2 %collective-permute-start.20 = (bf16[48,384]{1,0:T(8,128)(2,1)S(1)}, bf16[48,384]{1,0:T(8,128)(2,1)S(1)}, u32[]{:S(2)}, u32[]{:S(2)}) collective-permute-start(bf16[48,384]{1,0:T(8,128)(2,1)S(1)} %get-tuple-element.90), channel_id=1, source_target_pairs={{0,16},{8,24},{16,0},{24,8},{1,17},{9,25},{17,1},{25,9},{2,18},{10... | collective-permute-start | bytes 110600 | tf_op jit(solution)/shard_map/ppermute | solution.py:325
  60.2 1.2 %collective-permute-start.21 = (bf16[48,384]{1,0:T(8,128)(2,1)S(1)}, bf16[48,384]{1,0:T(8,128)(2,1)S(1)}, u32[]{:S(2)}, u32[]{:S(2)}) collective-permute-start(bf16[48,384]{1,0:T(8,128)(2,1)S(1)} %get-tuple-element.91), channel_id=1, source_target_pairs={{0,24},{8,16},{16,8},{24,0},{1,25},{9,17},{17,9},{25,1},{2,26},{10... | collective-permute-start | bytes 110600 | tf_op jit(solution)/shard_map/ppermute | solution.py:325
  61.3 5.6 %grad_down.1 = (bf16[1,1024,3072]{2,1,0:T(8,128)(2,1)}, f32[8,128]{1,0:T(8,128)S(1)}) custom-call(bf16[192,3072]{1,0:T(8,128)(2,1)S(1)} %get-tuple-element.92.d_ref, bf16[192,1024]{1,0:T(8,128)(2,1)S(1)} %get-tuple-element.75.refs_5_.hid_ref, bf16[48,384]{1,0:T(8,128)(2,1)S(1)} %get-tuple-element.88._.refs_0_), custom_call_target="tpu_custom_call" | custom-call | flops 1207959552 | bytes 6291456 | tf_op jit(solution)/shard_map/grad_down/pallas_call | solution.py:495
  66.9 0.0 collective-permute-done.19.refs_1_
  66.9 0.0 collective-permute-done.20.refs_2_
  66.9 0.0 collective-permute-done.21.refs_3_
  66.9 0.9 %combine.1 = (bf16[128,384]{1,0:T(8,128)(2,1)}, bf16[4,384]{1,0:T(4,128)(2,1)}) custom-call(s32[1,256]{1,0:T(1,128)S(1)} %get-tuple-element.52.pos_ref, bf16[48,384]{1,0:T(8,128)(2,1)S(1)} %get-tuple-element.88._.refs_0_, bf16[48,384]{1,0:T(8,128)(2,1)S(1)} %collective-permute-done.19.refs_1_, bf16[48,384]{1,0:T(8,128)(2,1)S(1)} %collective-permute-done.20.refs_2_, ...), custom_call_target="tpu_custom_call" | custom-call | tf_op jit(solution)/shard_map/combine/pallas_call | solution.py:344
  (1 shorter events, 0.0 us)
Async XLA Ops:
  2.2 13.6 %collective-permute-start.1 = (bf16[128,384]{1,0:T(8,128)(2,1)S(1)}, bf16[128,384]{1,0:T(8,128)(2,1)S(1)}, u32[]{:S(2)}, u32[]{:S(2)}) collective-permute-start(bf16[128,384]{1,0:T(8,128)(2,1)S(1)} %get-tuple-element.54.refs_0_), channel_id=1, source_target_pairs={{0,4},{2,6},{4,0},{6,2},{1,5},{3,7},{5,1},{7,3},{8,12},{10,14},{12... | collective-permute-start | bytes 294920 | tf_op jit(solution)/shard_map/ppermute | solution.py:325
  6.3 9.5 %collective-permute-start = (bf16[128,384]{1,0:T(8,128)(2,1)S(1)}, bf16[128,384]{1,0:T(8,128)(2,1)S(1)}, u32[]{:S(2)}, u32[]{:S(2)}) collective-permute-start(bf16[128,384]{1,0:T(8,128)(2,1)S(1)} %get-tuple-element.54.refs_0_), channel_id=1, source_target_pairs={{0,2},{2,0},{4,6},{6,4},{1,3},{3,1},{5,7},{7,5},{8,10},{10,8},{12,... | collective-permute-start | bytes 294920 | tf_op jit(solution)/shard_map/ppermute | solution.py:325
  7.9 6.3 %collective-permute-start.6 = (bf16[48,384]{1,0:T(8,128)(2,1)S(1)}, bf16[48,384]{1,0:T(8,128)(2,1)S(1)}, u32[]{:S(2)}, u32[]{:S(2)}) collective-permute-start(bf16[48,384]{1,0:T(8,128)(2,1)S(1)} %get-tuple-element.61), channel_id=1, source_target_pairs={{0,8},{8,0},{16,24},{24,16},{1,9},{9,1},{17,25},{25,17},{2,10},{10... | collective-permute-start | bytes 110600 | tf_op jit(solution)/shard_map/ppermute | solution.py:325
  9.4 4.8 %collective-permute-start.7 = (bf16[48,384]{1,0:T(8,128)(2,1)S(1)}, bf16[48,384]{1,0:T(8,128)(2,1)S(1)}, u32[]{:S(2)}, u32[]{:S(2)}) collective-permute-start(bf16[48,384]{1,0:T(8,128)(2,1)S(1)} %get-tuple-element.62), channel_id=1, source_target_pairs={{0,16},{8,24},{16,0},{24,8},{1,17},{9,25},{17,1},{25,9},{2,18},{10... | collective-permute-start | bytes 110600 | tf_op jit(solution)/shard_map/ppermute | solution.py:325
  10.9 4.9 %collective-permute-start.8 = (bf16[48,384]{1,0:T(8,128)(2,1)S(1)}, bf16[48,384]{1,0:T(8,128)(2,1)S(1)}, u32[]{:S(2)}, u32[]{:S(2)}) collective-permute-start(bf16[48,384]{1,0:T(8,128)(2,1)S(1)} %get-tuple-element.63), channel_id=1, source_target_pairs={{0,24},{8,16},{16,8},{24,0},{1,25},{9,17},{17,9},{25,1},{2,26},{10... | collective-permute-start | bytes 110600 | tf_op jit(solution)/shard_map/ppermute | solution.py:325
  15.8 11.8 %collective-permute-start.10 = (bf16[4,48,384]{2,1,0:T(8,128)(2,1)S(1)}, bf16[4,48,384]{2,1,0:T(8,128)(2,1)S(1)}, u32[]{:S(2)}, u32[]{:S(2)}) collective-permute-start(bf16[4,48,384]{2,1,0:T(8,128)(2,1)S(1)} %stack.1.refs_4_), channel_id=1, source_target_pairs={{0,4},{2,6},{4,0},{6,2},{1,5},{3,7},{5,1},{7,3},{8,12},{10,14},{12... | collective-permute-start | bytes 442376 | tf_op jit(solution)/shard_map/ppermute | solution.py:325
  16.2 8.4 %collective-permute-start.2 = (bf16[128,384]{1,0:T(8,128)(2,1)S(1)}, bf16[128,384]{1,0:T(8,128)(2,1)S(1)}, u32[]{:S(2)}, u32[]{:S(2)}) collective-permute-start(bf16[128,384]{1,0:T(8,128)(2,1)S(1)} %collective-permute-done.1.refs_2_.refs_6_), channel_id=1, source_target_pairs={{0,2},{2,0},{4,6},{6,4},{1,3},{3,1},{5,7},{7,5},{8,10},{10,8},{12,... | collective-permute-start | bytes 294920 | tf_op jit(solution)/shard_map/ppermute | solution.py:325
  16.6 15.3 %collective-permute-start.11 = (bf16[4,48,384]{2,1,0:T(8,128)(2,1)S(1)}, bf16[4,48,384]{2,1,0:T(8,128)(2,1)S(1)}, u32[]{:S(2)}, u32[]{:S(2)}) collective-permute-start(bf16[4,48,384]{2,1,0:T(8,128)(2,1)S(1)} %stack.1.refs_4_), channel_id=1, source_target_pairs={{0,6},{2,4},{4,2},{6,0},{1,7},{3,5},{5,3},{7,1},{8,14},{10,12},{12... | collective-permute-start | bytes 442376 | tf_op jit(solution)/shard_map/ppermute | solution.py:325
  20.2 11.7 %collective-permute-start.9 = (bf16[4,48,384]{2,1,0:T(8,128)(2,1)S(1)}, bf16[4,48,384]{2,1,0:T(8,128)(2,1)S(1)}, u32[]{:S(2)}, u32[]{:S(2)}) collective-permute-start(bf16[4,48,384]{2,1,0:T(8,128)(2,1)S(1)} %stack.1.refs_4_), channel_id=1, source_target_pairs={{0,2},{2,0},{4,6},{6,4},{1,3},{3,1},{5,7},{7,5},{8,10},{10,8},{12,... | collective-permute-start | bytes 442376 | tf_op jit(solution)/shard_map/ppermute | solution.py:325
  25.0 7.0 %collective-permute-start.3 = (bf16[4,40,384]{2,1,0:T(8,128)(2,1)S(1)}, bf16[4,40,384]{2,1,0:T(8,128)(2,1)S(1)}, u32[]{:S(2)}, u32[]{:S(2)}) collective-permute-start(bf16[4,40,384]{2,1,0:T(8,128)(2,1)S(1)} %get-tuple-element.57), channel_id=1, source_target_pairs={{0,8},{8,0},{16,24},{24,16},{1,9},{9,1},{17,25},{25,17},{2,10},{10... | collective-permute-start | bytes 368648 | tf_op jit(solution)/shard_map/ppermute | solution.py:325
  25.3 6.8 %collective-permute-start.4 = (bf16[4,40,384]{2,1,0:T(8,128)(2,1)S(1)}, bf16[4,40,384]{2,1,0:T(8,128)(2,1)S(1)}, u32[]{:S(2)}, u32[]{:S(2)}) collective-permute-start(bf16[4,40,384]{2,1,0:T(8,128)(2,1)S(1)} %get-tuple-element.58), channel_id=1, source_target_pairs={{0,16},{8,24},{16,0},{24,8},{1,17},{9,25},{17,1},{25,9},{2,18},{10... | collective-permute-start | bytes 368648 | tf_op jit(solution)/shard_map/ppermute | solution.py:325
  27.6 5.8 %collective-permute-start.5 = (bf16[4,40,384]{2,1,0:T(8,128)(2,1)S(1)}, bf16[4,40,384]{2,1,0:T(8,128)(2,1)S(1)}, u32[]{:S(2)}, u32[]{:S(2)}) collective-permute-start(bf16[4,40,384]{2,1,0:T(8,128)(2,1)S(1)} %get-tuple-element.59), channel_id=1, source_target_pairs={{0,24},{8,16},{16,8},{24,0},{1,25},{9,17},{17,9},{25,1},{2,26},{10... | collective-permute-start | bytes 368648 | tf_op jit(solution)/shard_map/ppermute | solution.py:325
  33.5 2.1 %collective-permute-start.12 = (bf16[4,4,48,384]{3,2,1,0:T(8,128)(2,1)S(1)}, bf16[4,4,48,384]{3,2,1,0:T(8,128)(2,1)S(1)}, u32[]{:S(2)}, u32[]{:S(2)}) collective-permute-start(bf16[4,4,48,384]{3,2,1,0:T(8,128)(2,1)S(1)} %get-tuple-element.65.refs_0_), channel_id=1, source_target_pairs={{0,1},{1,0},{2,3},{3,2},{4,5},{5,4},{6,7},{7,6},{8,9},{9,8},{10,11... | collective-permute-start | bytes 1769480 | tf_op jit(solution)/shard_map/ppermute | solution.py:325
  33.6 6.4 %collective-permute-start.14 = (bf16[4,4,40,384]{3,2,1,0:T(8,128)(2,1)S(1)}, bf16[4,4,40,384]{3,2,1,0:T(8,128)(2,1)S(1)}, u32[]{:S(2)}, u32[]{:S(2)}) collective-permute-start(bf16[4,4,40,384]{3,2,1,0:T(8,128)(2,1)S(1)} %get-tuple-element.71.refs_0_), channel_id=1, source_target_pairs={{0,1},{1,0},{2,3},{3,2},{4,5},{5,4},{6,7},{7,6},{8,9},{9,8},{10,11... | collective-permute-start | bytes 1474568 | tf_op jit(solution)/shard_map/ppermute | solution.py:325
  39.8 4.8 %collective-permute-start.13 = (bf16[4,4,48,384]{3,2,1,0:T(8,128)(2,1)S(1)}, bf16[4,4,48,384]{3,2,1,0:T(8,128)(2,1)S(1)}, u32[]{:S(2)}, u32[]{:S(2)}) collective-permute-start(bf16[4,4,48,384]{3,2,1,0:T(8,128)(2,1)S(1)} %get-tuple-element.70), channel_id=1, source_target_pairs={{0,1},{1,0},{2,3},{3,2},{4,5},{5,4},{6,7},{7,6},{8,9},{9,8},{10,11... | collective-permute-start | bytes 1769480 | tf_op jit(solution)/shard_map/ppermute | solution.py:325
  43.2 1.3 %collective-permute-start.15 = (bf16[4,8,384]{2,1,0:T(8,128)(2,1)S(1)}, bf16[4,8,384]{2,1,0:T(8,128)(2,1)S(1)}, u32[]{:S(2)}, u32[]{:S(2)}) collective-permute-start(bf16[4,8,384]{2,1,0:T(8,128)(2,1)S(1)} %get-tuple-element.80), channel_id=1, source_target_pairs={{0,1},{1,0},{2,3},{3,2},{4,5},{5,4},{6,7},{7,6},{8,9},{9,8},{10,11... | collective-permute-start | bytes 73736 | tf_op jit(solution)/shard_map/ppermute | solution.py:325
  44.6 11.3 %collective-permute-start.16 = (bf16[168,384]{1,0:T(8,128)(2,1)S(1)}, bf16[168,384]{1,0:T(8,128)(2,1)S(1)}, u32[]{:S(2)}, u32[]{:S(2)}) collective-permute-start(bf16[168,384]{1,0:T(8,128)(2,1)S(1)} %get-tuple-element.82), channel_id=1, source_target_pairs={{0,6},{2,4},{4,2},{6,0},{1,7},{3,5},{5,3},{7,1},{8,14},{10,12},{12... | collective-permute-start | bytes 387080 | tf_op jit(solution)/shard_map/ppermute | solution.py:325
  47.6 10.2 %collective-permute-start.17 = (bf16[168,384]{1,0:T(8,128)(2,1)S(1)}, bf16[168,384]{1,0:T(8,128)(2,1)S(1)}, u32[]{:S(2)}, u32[]{:S(2)}) collective-permute-start(bf16[168,384]{1,0:T(8,128)(2,1)S(1)} %get-tuple-element.83), channel_id=1, source_target_pairs={{0,4},{2,6},{4,0},{6,2},{1,5},{3,7},{5,1},{7,3},{8,12},{10,14},{12... | collective-permute-start | bytes 387080 | tf_op jit(solution)/shard_map/ppermute | solution.py:325
  47.6 10.2 %collective-permute-start.18 = (bf16[168,384]{1,0:T(8,128)(2,1)S(1)}, bf16[168,384]{1,0:T(8,128)(2,1)S(1)}, u32[]{:S(2)}, u32[]{:S(2)}) collective-permute-start(bf16[168,384]{1,0:T(8,128)(2,1)S(1)} %get-tuple-element.84), channel_id=1, source_target_pairs={{0,2},{2,0},{4,6},{6,4},{1,3},{3,1},{5,7},{7,5},{8,10},{10,8},{12,... | collective-permute-start | bytes 387080 | tf_op jit(solution)/shard_map/ppermute | solution.py:325
  57.8 9.1 %collective-permute-start.19 = (bf16[48,384]{1,0:T(8,128)(2,1)S(1)}, bf16[48,384]{1,0:T(8,128)(2,1)S(1)}, u32[]{:S(2)}, u32[]{:S(2)}) collective-permute-start(bf16[48,384]{1,0:T(8,128)(2,1)S(1)} %get-tuple-element.89), channel_id=1, source_target_pairs={{0,8},{8,0},{16,24},{24,16},{1,9},{9,1},{17,25},{25,17},{2,10},{10... | collective-permute-start | bytes 110600 | tf_op jit(solution)/shard_map/ppermute | solution.py:325
  59.0 7.9 %collective-permute-start.20 = (bf16[48,384]{1,0:T(8,128)(2,1)S(1)}, bf16[48,384]{1,0:T(8,128)(2,1)S(1)}, u32[]{:S(2)}, u32[]{:S(2)}) collective-permute-start(bf16[48,384]{1,0:T(8,128)(2,1)S(1)} %get-tuple-element.90), channel_id=1, source_target_pairs={{0,16},{8,24},{16,0},{24,8},{1,17},{9,25},{17,1},{25,9},{2,18},{10... | collective-permute-start | bytes 110600 | tf_op jit(solution)/shard_map/ppermute | solution.py:325
  60.2 6.8 %collective-permute-start.21 = (bf16[48,384]{1,0:T(8,128)(2,1)S(1)}, bf16[48,384]{1,0:T(8,128)(2,1)S(1)}, u32[]{:S(2)}, u32[]{:S(2)}) collective-permute-start(bf16[48,384]{1,0:T(8,128)(2,1)S(1)} %get-tuple-element.91), channel_id=1, source_target_pairs={{0,24},{8,16},{16,8},{24,0},{1,25},{9,17},{17,9},{25,1},{2,26},{10... | collective-permute-start | bytes 110600 | tf_op jit(solution)/shard_map/ppermute | solution.py:325

commit v9 on v4

--- a/solution.py
+++ b/solution.py
@@ -108,7 +108,7 @@
         refs[-1][q] = refs[q][...]
 
 
-def join_kernel(groups, _, __, *refs):
+def join_kernel(groups, _, *refs):
     blocks_d, blocks_x, own_x, own_d = refs[:groups], refs[groups:-2], refs[-2], refs[-1]
     for q in range(groups):
         own_d[q] = blocks_d[q][...]
@@ -120,7 +120,7 @@
 
 
 def pick_kernel(relative, experts, hops, pos_ref, *refs):
-    sources, sends = refs[: len(refs) - experts], refs[len(refs) - experts :]
+    sources, sends = refs[: len(refs) - experts - 1], refs[len(refs) - experts :]
     merged = chosen(pos_ref[...], experts)
     for k in range(hops):
         rows = dot(merged, sources[k][...] if relative else sources[0][k], ((1,), (0,)))
@@ -272,13 +272,8 @@
 
 
 def put(out_ref, blocks, router):
-    groups, height, width = out_ref.shape
-    spare = height - CAP - router.shape[0]
-    for q in range(groups):
-        rows = [blocks[q][:CAP], router]
-        if spare:
-            rows.append(jnp.zeros((spare, width), F32))
-        out_ref[q] = jnp.concatenate(rows, axis=0).astype(BF16)
+    rows = [blocks[q, :CAP] for q in range(blocks.shape[0])]
+    out_ref[...] = jnp.concatenate([*rows, router], axis=0).astype(BF16)
 
 
 def grads_kernel(x_ref, d_ref, dgate_ref, dup_ref, hid_ref, _, gate_ref, up_ref, down_ref, mark_ref):
@@ -290,23 +285,19 @@
     mark_ref[...] = jnp.zeros(mark_ref.shape, F32)
 
 
-def add_blocks(experts, parts, sends):
-    router = None
+def sum_kernel(experts, groups, *refs):
+    parts, sends = refs[: len(refs) - groups - 1], refs[len(refs) - groups :]
+    total = parts[0][...].astype(F32)
+    for ref in parts[1:]:
+        total = total + ref[...].astype(F32)
+    router = total[groups * CAP :]
+    router = halves(router[:experts] + router[experts:])
+    height, width = sends[0].shape
     for q, send in enumerate(sends):
-        block = parts[0][q].astype(F32)
-        for ref in parts[1:]:
-            block = block + ref[q].astype(F32)
-        if router is None:
-            router = halves(block[CAP : CAP + experts] + block[CAP + experts : CAP + 2 * experts])
-        height, width = send.shape
-        rows = [block[:CAP], router]
+        rows = [total[q * CAP : (q + 1) * CAP], router]
         if height > CAP + 2 * experts:
             rows.append(jnp.zeros((height - CAP - 2 * experts, width), F32))
         send[...] = jnp.concatenate(rows, axis=0).astype(BF16)
-
-
-def sum_kernel(experts, groups, *refs):
-    add_blocks(experts, refs[: len(refs) - groups - 1], refs[len(refs) - groups :])
 
 
 def combine_kernel(groups, pos_ref, *refs):
@@ -397,7 +388,7 @@
     slices = gather(handed)
     picked = call(
         functools.partial(pick_kernel, relative, experts, hops),
-        (position, *slices),
+        (position, *slices, up_mark),
         [shape((hops, CAP, width), BF16)] * experts,
         "pick",
     )
@@ -411,7 +402,7 @@
     blocks_d = [picked[0]] + [swap(picked[q], "expert", q) for q in range(1, groups)]
     own_x, own_d = call(
         functools.partial(join_kernel, groups),
-        (up_mark, down_mark, *blocks_d, *blocks_x),
+        (down_mark, *blocks_d, *blocks_x),
         [shape((hops, *stacked.shape), BF16), shape((groups, *picked[0].shape), BF16)],
         "join",
     )
@@ -458,7 +449,7 @@
     merged = call(
         merge_kernel,
         (keep, got, router_keep, router_got),
-        [shape((groups, height, width), BF16)] * hops,
+        [shape((groups * CAP + 2 * experts, width), BF16)] * hops,
         "merge",
     )
     if relative:

time: 68.5 us -> 66.2 us (0.966)
  waiting for transfers between devices: 12.9 us -> 10.6 us
    ppermute x22, waiting for transfers between devices: 12.9 us -> 10.6 us  [swap(): return lax.ppermute(block, axis, [(i, i ^ bits) for i in range(size)])]
  transfers between devices with their start and end apart: 22 -> 22, of which waited for: 9 -> 9; matrix products, arithmetic and copies ran while one was open for 0% -> 0% of each run, Pallas kernels for 37% -> 38%
where the time goes in v9:
time: 66.2 us; the launch traced here: 65.9 us
  Pallas kernels  27.7 us (42%)
  starting transfers between devices  26.9 us (41%)
  waiting for transfers between devices  10.6 us (16%)
  between operations  0.79 us (1%)
    ppermute x22, starting transfers between devices, swap(): return lax.ppermute(block, axis, [(i, i ^ bits) for i in range(size)])  26.9 us
    pallas_call x12, Pallas kernels, call(): pl.pallas_call(kernel, out_shape=tuple(outs), in_specs=[fixed if i in loo...  18.9 us
    ppermute x22, waiting for transfers between devices, swap(): return lax.ppermute(block, axis, [(i, i ^ bits) for i in range(size)])  10.6 us
    pallas_call x1, Pallas kernels, shards(): pl.pallas_call(grads_kernel, grid=(parts,), out_shape=(shape(w_gate.shape...  8.84 us
  transfers between devices with their start and end apart: 22, of which 9 were waited for; matrix products, arithmetic and copies ran while one was open for 0% of the time, Pallas kernels for 38%

profile of v9, /device:TPU:0, one launch (start us, length us, event | category | flops | bytes accessed | tf_op | source)
XLA Modules:
  0.0 65.9 jit_solution(1624498068823243978)
XLA Ops:
  0.6 1.6 %pack.1 = (s32[1,256]{1,0:T(1,128)S(1)}, bf16[128,384]{1,0:T(8,128)(2,1)S(1)}, bf16[48,384]{1,0:T(8,128)(2,1)S(1)}, bf16[48,384]{1,0:T(8,128)(2,1)S(1)}, bf16[48...) custom-call(s32[4]{0:T(128)} %refs_0_.1, s32[4]{0:T(128)} %refs_1_.1, s32[2,128]{1,0:T(2,128)} %bitcast.4, ...), custom_call_target="tpu_custom_call" | custom-call | tf_op jit(solution)/shard_map/pack/pallas_call | solution.py:340
  2.2 4.1 %collective-permute-start.1 = (bf16[128,384]{1,0:T(8,128)(2,1)S(1)}, bf16[128,384]{1,0:T(8,128)(2,1)S(1)}, u32[]{:S(2)}, u32[]{:S(2)}) collective-permute-start(bf16[128,384]{1,0:T(8,128)(2,1)S(1)} %get-tuple-element.53.refs_0_), channel_id=1, source_target_pairs={{0,4},{2,6},{4,0},{6,2},{1,5},{3,7},{5,1},{7,3},{8,12},{10,14},{12... | collective-permute-start | bytes 294920 | tf_op jit(solution)/shard_map/ppermute | solution.py:321
  6.3 1.6 %collective-permute-start = (bf16[128,384]{1,0:T(8,128)(2,1)S(1)}, bf16[128,384]{1,0:T(8,128)(2,1)S(1)}, u32[]{:S(2)}, u32[]{:S(2)}) collective-permute-start(bf16[128,384]{1,0:T(8,128)(2,1)S(1)} %get-tuple-element.53.refs_0_), channel_id=1, source_target_pairs={{0,2},{2,0},{4,6},{6,4},{1,3},{3,1},{5,7},{7,5},{8,10},{10,8},{12,... | collective-permute-start | bytes 294920 | tf_op jit(solution)/shard_map/ppermute | solution.py:321
  7.9 1.5 %collective-permute-start.6 = (bf16[48,384]{1,0:T(8,128)(2,1)S(1)}, bf16[48,384]{1,0:T(8,128)(2,1)S(1)}, u32[]{:S(2)}, u32[]{:S(2)}) collective-permute-start(bf16[48,384]{1,0:T(8,128)(2,1)S(1)} %get-tuple-element.60), channel_id=1, source_target_pairs={{0,8},{8,0},{16,24},{24,16},{1,9},{9,1},{17,25},{25,17},{2,10},{10... | collective-permute-start | bytes 110600 | tf_op jit(solution)/shard_map/ppermute | solution.py:321
  9.4 1.5 %collective-permute-start.7 = (bf16[48,384]{1,0:T(8,128)(2,1)S(1)}, bf16[48,384]{1,0:T(8,128)(2,1)S(1)}, u32[]{:S(2)}, u32[]{:S(2)}) collective-permute-start(bf16[48,384]{1,0:T(8,128)(2,1)S(1)} %get-tuple-element.61), channel_id=1, source_target_pairs={{0,16},{8,24},{16,0},{24,8},{1,17},{9,25},{17,1},{25,9},{2,18},{10... | collective-permute-start | bytes 110600 | tf_op jit(solution)/shard_map/ppermute | solution.py:321
  10.9 0.5 collective-permute-start.8
  11.4 2.8 %load_gate.1 = (bf16[1,3072,1024]{2,1,0:T(8,128)(2,1)S(1)}, f32[8,128]{1,0:T(8,128)S(1)}) custom-call(bf16[1,3072,1024]{2,1,0:T(8,128)(2,1)} %source.5), custom_call_target="tpu_custom_call" | custom-call | bytes 12582912 | tf_op jit(solution)/shard_map/load_gate/pallas_call | solution.py:340
  14.2 0.0 collective-permute-done.6.refs_1_
  14.2 0.0 collective-permute-done.7.refs_2_
  14.2 1.6 %collective-permute-done.8.refs_3_ = bf16[48,384]{1,0:T(8,128)(2,1)S(1)} collective-permute-done((bf16[48,384]{1,0:T(8,128)(2,1)S(1)}, bf16[48,384]{1,0:T(8,128)(2,1)S(1)}, u32[]{:S(2)}, u32[]{:S(2)}) %collective-permute-start.8) | collective-permute-done | bytes 36896 | tf_op jit(solution)/shard_map/ppermute | solution.py:321
  15.8 0.0 collective-permute-done.1.refs_2_.refs_6_
  15.8 0.0 collective-permute-done.refs_1_.refs_5_
  15.8 0.4 collective-permute-start.10
  16.2 0.5 collective-permute-start.2
  16.6 3.6 %collective-permute-start.11 = (bf16[4,48,384]{2,1,0:T(8,128)(2,1)S(1)}, bf16[4,48,384]{2,1,0:T(8,128)(2,1)S(1)}, u32[]{:S(2)}, u32[]{:S(2)}) collective-permute-start(bf16[4,48,384]{2,1,0:T(8,128)(2,1)S(1)} %stack.1.refs_4_), channel_id=1, source_target_pairs={{0,6},{2,4},{4,2},{6,0},{1,7},{3,5},{5,3},{7,1},{8,14},{10,12},{12... | collective-permute-start | bytes 442376 | tf_op jit(solution)/shard_map/ppermute | solution.py:321
  20.2 0.0 collective-permute-start.9
  20.2 2.8 %load_up.1 = (bf16[1,3072,1024]{2,1,0:T(8,128)(2,1)S(1)}, f32[8,128]{1,0:T(8,128)S(1)}) custom-call(bf16[1,3072,1024]{2,1,0:T(8,128)(2,1)} %source.4), custom_call_target="tpu_custom_call" | custom-call | bytes 12582912 | tf_op jit(solution)/shard_map/load_up/pallas_call | solution.py:340
  23.0 1.6 %collective-permute-done.2.refs_3_ = bf16[128,384]{1,0:T(8,128)(2,1)S(1)} collective-permute-done((bf16[128,384]{1,0:T(8,128)(2,1)S(1)}, bf16[128,384]{1,0:T(8,128)(2,1)S(1)}, u32[]{:S(2)}, u32[]{:S(2)}) %collective-permute-start.2) | collective-permute-done | bytes 98336 | tf_op jit(solution)/shard_map/ppermute | solution.py:321
  24.6 0.3 pick.1
  25.0 0.3 collective-permute-start.3
  25.3 2.2 %collective-permute-start.4 = (bf16[4,40,384]{2,1,0:T(8,128)(2,1)S(1)}, bf16[4,40,384]{2,1,0:T(8,128)(2,1)S(1)}, u32[]{:S(2)}, u32[]{:S(2)}) collective-permute-start(bf16[4,40,384]{2,1,0:T(8,128)(2,1)S(1)} %get-tuple-element.57), channel_id=1, source_target_pairs={{0,16},{8,24},{16,0},{24,8},{1,17},{9,25},{17,1},{25,9},{2,18},{10... | collective-permute-start | bytes 368648 | tf_op jit(solution)/shard_map/ppermute | solution.py:321
  27.4 0.2 collective-permute-done.10.refs_6_
  27.6 1.6 %collective-permute-start.5 = (bf16[4,40,384]{2,1,0:T(8,128)(2,1)S(1)}, bf16[4,40,384]{2,1,0:T(8,128)(2,1)S(1)}, u32[]{:S(2)}, u32[]{:S(2)}) collective-permute-start(bf16[4,40,384]{2,1,0:T(8,128)(2,1)S(1)} %get-tuple-element.58), channel_id=1, source_target_pairs={{0,24},{8,16},{16,8},{24,0},{1,25},{9,17},{17,9},{25,1},{2,26},{10... | collective-permute-start | bytes 368648 | tf_op jit(solution)/shard_map/ppermute | solution.py:321
  29.2 2.8 %load_down.1 = (bf16[1,1024,3072]{2,1,0:T(8,128)(2,1)S(1)}, f32[8,128]{1,0:T(8,128)S(1)}) custom-call(bf16[1,1024,3072]{2,1,0:T(8,128)(2,1)} %source.3), custom_call_target="tpu_custom_call" | custom-call | bytes 12582912 | tf_op jit(solution)/shard_map/load_down/pallas_call | solution.py:340
  32.0 0.0 collective-permute-done.11.refs_7_
  32.0 0.0 collective-permute-done.9.refs_5_
  32.0 0.0 collective-permute-done.3.refs_1_
  32.0 0.0 collective-permute-done.4.refs_2_
  32.0 1.4 %collective-permute-done.5.refs_3_ = bf16[4,40,384]{2,1,0:T(8,128)(2,1)S(1)} collective-permute-done((bf16[4,40,384]{2,1,0:T(8,128)(2,1)S(1)}, bf16[4,40,384]{2,1,0:T(8,128)(2,1)S(1)}, u32[]{:S(2)}, u32[]{:S(2)}) %collective-permute-start.5) | collective-permute-done | bytes 122912 | tf_op jit(solution)/shard_map/ppermute | solution.py:321
  33.4 0.1 join.1
  33.5 0.1 collective-permute-start.12
  33.6 0.5 collective-permute-start.14
  34.1 1.5 %collective-permute-done.12.refs_1_ = bf16[4,4,48,384]{3,2,1,0:T(8,128)(2,1)S(1)} collective-permute-done((bf16[4,4,48,384]{3,2,1,0:T(8,128)(2,1)S(1)}, bf16[4,4,48,384]{3,2,1,0:T(8,128)(2,1)S(1)}, u32[]{:S(2)}, u32[]{:S(2)}) %collective-permute-start.12) | collective-permute-done | bytes 589856 | tf_op jit(solution)/shard_map/ppermute | solution.py:321
  35.5 4.2 %forward.1 = (bf16[192,3072]{1,0:T(8,128)(2,1)S(1)}, bf16[192,1024]{1,0:T(8,128)(2,1)S(1)}, f32[192,1024]{1,0:T(8,128)S(1)}, f32[192,1024]{1,0:T(8,128)S(1)}, f3...) custom-call(bf16[4,4,48,384]{3,2,1,0:T(8,128)(2,1)S(1)} %get-tuple-e, ...), custom_call_target="tpu_custom_call" | custom-call | flops 3623878656 | bytes 18874368 | tf_op jit(solution)/shard_map/forward/pallas_call | solution.py:340
  39.7 0.2 collective-permute-start.13
  39.9 0.0 collective-permute-done.14.refs_1_
  39.9 3.2 %backward.1 = (bf16[192,3072]{1,0:T(8,128)(2,1)S(1)}, bf16[192,1024]{1,0:T(8,128)(2,1)S(1)}, bf16[192,1024]{1,0:T(8,128)(2,1)S(1)}, f32[4,4,384]{2,1,0:T(4,128)S(1)}, bf16[4,8,384]{2,1,0:T(8,128)(2,1)S(1)}) custom-call(bf16[4,4,40,384]{3,2,1,0:T(8,128)(2,1)S(1)} %get-tuple-element.70.refs_0_, bf16[4,4,40,384]{3,2,1,0:T(8,128)(2,1)S(1)} %collective-permute-done.14.refs_1_, ...), custom_call_target="tpu_custom_call" | custom-call | flops 1207959552 | bytes 6291456 | tf_op jit(solution)/shard_map/backward/pallas_call | solution.py:340
  43.2 0.5 collective-permute-start.15
  43.6 0.8 %collective-permute-done.15.rgot_ref = bf16[4,8,384]{2,1,0:T(8,128)(2,1)S(1)} collective-permute-done((bf16[4,8,384]{2,1,0:T(8,128)(2,1)S(1)}, bf16[4,8,384]{2,1,0:T(8,128)(2,1)S(1)}, u32[]{:S(2)}, u32[]{:S(2)}) %collective-permute-start.15) | collective-permute-done | bytes 24608 | tf_op jit(solution)/shard_map/ppermute | solution.py:321
  44.5 0.0 collective-permute-done.13.got_ref
  44.5 0.1 merge.1
  44.6 2.9 %collective-permute-start.16 = (bf16[168,384]{1,0:T(8,128)(2,1)S(1)}, bf16[168,384]{1,0:T(8,128)(2,1)S(1)}, u32[]{:S(2)}, u32[]{:S(2)}) collective-permute-start(bf16[168,384]{1,0:T(8,128)(2,1)S(1)} %get-tuple-element.81), channel_id=1, source_target_pairs={{0,6},{2,4},{4,2},{6,0},{1,7},{3,5},{5,3},{7,1},{8,14},{10,12},{12... | collective-permute-start | bytes 387080 | tf_op jit(solution)/shard_map/ppermute | solution.py:321
  47.6 0.0 collective-permute-start.17
  47.6 1.5 %collective-permute-start.18 = (bf16[168,384]{1,0:T(8,128)(2,1)S(1)}, bf16[168,384]{1,0:T(8,128)(2,1)S(1)}, u32[]{:S(2)}, u32[]{:S(2)}) collective-permute-start(bf16[168,384]{1,0:T(8,128)(2,1)S(1)} %get-tuple-element.83), channel_id=1, source_target_pairs={{0,2},{2,0},{4,6},{6,4},{1,3},{3,1},{5,7},{7,5},{8,10},{10,8},{12,... | collective-permute-start | bytes 387080 | tf_op jit(solution)/shard_map/ppermute | solution.py:321
  49.1 8.8 %grads.1 = (bf16[1,3072,1024]{2,1,0:T(8,128)(2,1)}, bf16[1,3072,1024]{2,1,0:T(8,128)(2,1)}, bf16[1,1024,3072]{2,1,0:T(8,128)(2,1)}, f32[8,128]{1,0:T(8,128)S(1)}) custom-call(bf16[192,3072]{1,0:T(8,128)(2,1)S(1)} %get-tuple-element.71.refs_2_.x_ref, bf16[192,3072]{1,0:T(8,128)(2,1)S(1)} %get-tuple-element.84.d_ref, ...), custom_call_target="tpu_custom_call" | custom-call | flops 3623878656 | bytes 18874368 | tf_op jit(solution)/shard_map/grads/pallas_call | solution.py:465
  57.9 0.0 collective-permute-done.16.refs_1_
  57.9 0.0 collective-permute-done.17.refs_2_
  57.9 0.0 collective-permute-done.18.refs_3_
  57.9 0.1 total.1
  58.0 1.2 %collective-permute-start.19 = (bf16[48,384]{1,0:T(8,128)(2,1)S(1)}, bf16[48,384]{1,0:T(8,128)(2,1)S(1)}, u32[]{:S(2)}, u32[]{:S(2)}) collective-permute-start(bf16[48,384]{1,0:T(8,128)(2,1)S(1)} %get-tuple-element.89), channel_id=1, source_target_pairs={{0,8},{8,0},{16,24},{24,16},{1,9},{9,1},{17,25},{25,17},{2,10},{10... | collective-permute-start | bytes 110600 | tf_op jit(solution)/shard_map/ppermute | solution.py:321
  59.2 1.0 %collective-permute-start.20 = (bf16[48,384]{1,0:T(8,128)(2,1)S(1)}, bf16[48,384]{1,0:T(8,128)(2,1)S(1)}, u32[]{:S(2)}, u32[]{:S(2)}) collective-permute-start(bf16[48,384]{1,0:T(8,128)(2,1)S(1)} %get-tuple-element.90), channel_id=1, source_target_pairs={{0,16},{8,24},{16,0},{24,8},{1,17},{9,25},{17,1},{25,9},{2,18},{10... | collective-permute-start | bytes 110600 | tf_op jit(solution)/shard_map/ppermute | solution.py:321
  60.2 1.4 %collective-permute-start.21 = (bf16[48,384]{1,0:T(8,128)(2,1)S(1)}, bf16[48,384]{1,0:T(8,128)(2,1)S(1)}, u32[]{:S(2)}, u32[]{:S(2)}) collective-permute-start(bf16[48,384]{1,0:T(8,128)(2,1)S(1)} %get-tuple-element.91), channel_id=1, source_target_pairs={{0,24},{8,16},{16,8},{24,0},{1,25},{9,17},{17,9},{25,1},{2,26},{10... | collective-permute-start | bytes 110600 | tf_op jit(solution)/shard_map/ppermute | solution.py:321
  61.5 0.5 collective-permute-done.19.refs_1_
  62.0 1.1 %collective-permute-done.20.refs_2_ = bf16[48,384]{1,0:T(8,128)(2,1)S(1)} collective-permute-done((bf16[48,384]{1,0:T(8,128)(2,1)S(1)}, bf16[48,384]{1,0:T(8,128)(2,1)S(1)}, u32[]{:S(2)}, u32[]{:S(2)}) %collective-permute-start.20) | collective-permute-done | bytes 36896 | tf_op jit(solution)/shard_map/ppermute | solution.py:321
  63.1 1.9 %collective-permute-done.21.refs_3_ = bf16[48,384]{1,0:T(8,128)(2,1)S(1)} collective-permute-done((bf16[48,384]{1,0:T(8,128)(2,1)S(1)}, bf16[48,384]{1,0:T(8,128)(2,1)S(1)}, u32[]{:S(2)}, u32[]{:S(2)}) %collective-permute-start.21) | collective-permute-done | bytes 36896 | tf_op jit(solution)/shard_map/ppermute | solution.py:321
  65.1 0.9 %combine.1 = (bf16[128,384]{1,0:T(8,128)(2,1)}, bf16[4,384]{1,0:T(4,128)(2,1)}) custom-call(s32[1,256]{1,0:T(1,128)S(1)} %get-tuple-element.51.pos_ref, bf16[48,384]{1,0:T(8,128)(2,1)S(1)} %get-tuple-element.88.refs_0_, bf16[48,384]{1,0:T(8,128)(2,1)S(1)} %collective-permute-done.19.refs_1_, bf16[48,384]{1,0:T(8,128)(2,1)S(1)} %collective-permute-done.20.refs_2_, ...), custom_call_target="tpu_custom_call" | custom-call | tf_op jit(solution)/shard_map/combine/pallas_call | solution.py:340
  (1 shorter events, 0.0 us)
Async XLA Ops:
  2.2 13.6 %collective-permute-start.1 = (bf16[128,384]{1,0:T(8,128)(2,1)S(1)}, bf16[128,384]{1,0:T(8,128)(2,1)S(1)}, u32[]{:S(2)}, u32[]{:S(2)}) collective-permute-start(bf16[128,384]{1,0:T(8,128)(2,1)S(1)} %get-tuple-element.53.refs_0_), channel_id=1, source_target_pairs={{0,4},{2,6},{4,0},{6,2},{1,5},{3,7},{5,1},{7,3},{8,12},{10,14},{12... | collective-permute-start | bytes 294920 | tf_op jit(solution)/shard_map/ppermute | solution.py:321
  6.3 9.5 %collective-permute-start = (bf16[128,384]{1,0:T(8,128)(2,1)S(1)}, bf16[128,384]{1,0:T(8,128)(2,1)S(1)}, u32[]{:S(2)}, u32[]{:S(2)}) collective-permute-start(bf16[128,384]{1,0:T(8,128)(2,1)S(1)} %get-tuple-element.53.refs_0_), channel_id=1, source_target_pairs={{0,2},{2,0},{4,6},{6,4},{1,3},{3,1},{5,7},{7,5},{8,10},{10,8},{12,... | collective-permute-start | bytes 294920 | tf_op jit(solution)/shard_map/ppermute | solution.py:321
  7.9 6.3 %collective-permute-start.6 = (bf16[48,384]{1,0:T(8,128)(2,1)S(1)}, bf16[48,384]{1,0:T(8,128)(2,1)S(1)}, u32[]{:S(2)}, u32[]{:S(2)}) collective-permute-start(bf16[48,384]{1,0:T(8,128)(2,1)S(1)} %get-tuple-element.60), channel_id=1, source_target_pairs={{0,8},{8,0},{16,24},{24,16},{1,9},{9,1},{17,25},{25,17},{2,10},{10... | collective-permute-start | bytes 110600 | tf_op jit(solution)/shard_map/ppermute | solution.py:321
  9.4 4.8 %collective-permute-start.7 = (bf16[48,384]{1,0:T(8,128)(2,1)S(1)}, bf16[48,384]{1,0:T(8,128)(2,1)S(1)}, u32[]{:S(2)}, u32[]{:S(2)}) collective-permute-start(bf16[48,384]{1,0:T(8,128)(2,1)S(1)} %get-tuple-element.61), channel_id=1, source_target_pairs={{0,16},{8,24},{16,0},{24,8},{1,17},{9,25},{17,1},{25,9},{2,18},{10... | collective-permute-start | bytes 110600 | tf_op jit(solution)/shard_map/ppermute | solution.py:321
  10.9 4.9 %collective-permute-start.8 = (bf16[48,384]{1,0:T(8,128)(2,1)S(1)}, bf16[48,384]{1,0:T(8,128)(2,1)S(1)}, u32[]{:S(2)}, u32[]{:S(2)}) collective-permute-start(bf16[48,384]{1,0:T(8,128)(2,1)S(1)} %get-tuple-element.62), channel_id=1, source_target_pairs={{0,24},{8,16},{16,8},{24,0},{1,25},{9,17},{17,9},{25,1},{2,26},{10... | collective-permute-start | bytes 110600 | tf_op jit(solution)/shard_map/ppermute | solution.py:321
  15.8 11.8 %collective-permute-start.10 = (bf16[4,48,384]{2,1,0:T(8,128)(2,1)S(1)}, bf16[4,48,384]{2,1,0:T(8,128)(2,1)S(1)}, u32[]{:S(2)}, u32[]{:S(2)}) collective-permute-start(bf16[4,48,384]{2,1,0:T(8,128)(2,1)S(1)} %stack.1.refs_4_), channel_id=1, source_target_pairs={{0,4},{2,6},{4,0},{6,2},{1,5},{3,7},{5,1},{7,3},{8,12},{10,14},{12... | collective-permute-start | bytes 442376 | tf_op jit(solution)/shard_map/ppermute | solution.py:321
  16.2 8.4 %collective-permute-start.2 = (bf16[128,384]{1,0:T(8,128)(2,1)S(1)}, bf16[128,384]{1,0:T(8,128)(2,1)S(1)}, u32[]{:S(2)}, u32[]{:S(2)}) collective-permute-start(bf16[128,384]{1,0:T(8,128)(2,1)S(1)} %collective-permute-done.1.refs_2_.refs_6_), channel_id=1, source_target_pairs={{0,2},{2,0},{4,6},{6,4},{1,3},{3,1},{5,7},{7,5},{8,10},{10,8},{12,... | collective-permute-start | bytes 294920 | tf_op jit(solution)/shard_map/ppermute | solution.py:321
  16.6 15.3 %collective-permute-start.11 = (bf16[4,48,384]{2,1,0:T(8,128)(2,1)S(1)}, bf16[4,48,384]{2,1,0:T(8,128)(2,1)S(1)}, u32[]{:S(2)}, u32[]{:S(2)}) collective-permute-start(bf16[4,48,384]{2,1,0:T(8,128)(2,1)S(1)} %stack.1.refs_4_), channel_id=1, source_target_pairs={{0,6},{2,4},{4,2},{6,0},{1,7},{3,5},{5,3},{7,1},{8,14},{10,12},{12... | collective-permute-start | bytes 442376 | tf_op jit(solution)/shard_map/ppermute | solution.py:321
  20.2 11.7 %collective-permute-start.9 = (bf16[4,48,384]{2,1,0:T(8,128)(2,1)S(1)}, bf16[4,48,384]{2,1,0:T(8,128)(2,1)S(1)}, u32[]{:S(2)}, u32[]{:S(2)}) collective-permute-start(bf16[4,48,384]{2,1,0:T(8,128)(2,1)S(1)} %stack.1.refs_4_), channel_id=1, source_target_pairs={{0,2},{2,0},{4,6},{6,4},{1,3},{3,1},{5,7},{7,5},{8,10},{10,8},{12,... | collective-permute-start | bytes 442376 | tf_op jit(solution)/shard_map/ppermute | solution.py:321
  25.0 7.1 %collective-permute-start.3 = (bf16[4,40,384]{2,1,0:T(8,128)(2,1)S(1)}, bf16[4,40,384]{2,1,0:T(8,128)(2,1)S(1)}, u32[]{:S(2)}, u32[]{:S(2)}) collective-permute-start(bf16[4,40,384]{2,1,0:T(8,128)(2,1)S(1)} %get-tuple-element.56), channel_id=1, source_target_pairs={{0,8},{8,0},{16,24},{24,16},{1,9},{9,1},{17,25},{25,17},{2,10},{10... | collective-permute-start | bytes 368648 | tf_op jit(solution)/shard_map/ppermute | solution.py:321
  25.3 6.8 %collective-permute-start.4 = (bf16[4,40,384]{2,1,0:T(8,128)(2,1)S(1)}, bf16[4,40,384]{2,1,0:T(8,128)(2,1)S(1)}, u32[]{:S(2)}, u32[]{:S(2)}) collective-permute-start(bf16[4,40,384]{2,1,0:T(8,128)(2,1)S(1)} %get-tuple-element.57), channel_id=1, source_target_pairs={{0,16},{8,24},{16,0},{24,8},{1,17},{9,25},{17,1},{25,9},{2,18},{10... | collective-permute-start | bytes 368648 | tf_op jit(solution)/shard_map/ppermute | solution.py:321
  27.6 5.8 %collective-permute-start.5 = (bf16[4,40,384]{2,1,0:T(8,128)(2,1)S(1)}, bf16[4,40,384]{2,1,0:T(8,128)(2,1)S(1)}, u32[]{:S(2)}, u32[]{:S(2)}) collective-permute-start(bf16[4,40,384]{2,1,0:T(8,128)(2,1)S(1)} %get-tuple-element.58), channel_id=1, source_target_pairs={{0,24},{8,16},{16,8},{24,0},{1,25},{9,17},{17,9},{25,1},{2,26},{10... | collective-permute-start | bytes 368648 | tf_op jit(solution)/shard_map/ppermute | solution.py:321
  33.5 2.1 %collective-permute-start.12 = (bf16[4,4,48,384]{3,2,1,0:T(8,128)(2,1)S(1)}, bf16[4,4,48,384]{3,2,1,0:T(8,128)(2,1)S(1)}, u32[]{:S(2)}, u32[]{:S(2)}) collective-permute-start(bf16[4,4,48,384]{3,2,1,0:T(8,128)(2,1)S(1)} %get-tuple-element.64.refs_0_), channel_id=1, source_target_pairs={{0,1},{1,0},{2,3},{3,2},{4,5},{5,4},{6,7},{7,6},{8,9},{9,8},{10,11... | collective-permute-start | bytes 1769480 | tf_op jit(solution)/shard_map/ppermute | solution.py:321
  33.6 6.4 %collective-permute-start.14 = (bf16[4,4,40,384]{3,2,1,0:T(8,128)(2,1)S(1)}, bf16[4,4,40,384]{3,2,1,0:T(8,128)(2,1)S(1)}, u32[]{:S(2)}, u32[]{:S(2)}) collective-permute-start(bf16[4,4,40,384]{3,2,1,0:T(8,128)(2,1)S(1)} %get-tuple-element.70.refs_0_), channel_id=1, source_target_pairs={{0,1},{1,0},{2,3},{3,2},{4,5},{5,4},{6,7},{7,6},{8,9},{9,8},{10,11... | collective-permute-start | bytes 1474568 | tf_op jit(solution)/shard_map/ppermute | solution.py:321
  39.7 4.7 %collective-permute-start.13 = (bf16[4,4,48,384]{3,2,1,0:T(8,128)(2,1)S(1)}, bf16[4,4,48,384]{3,2,1,0:T(8,128)(2,1)S(1)}, u32[]{:S(2)}, u32[]{:S(2)}) collective-permute-start(bf16[4,4,48,384]{3,2,1,0:T(8,128)(2,1)S(1)} %get-tuple-element.69), channel_id=1, source_target_pairs={{0,1},{1,0},{2,3},{3,2},{4,5},{5,4},{6,7},{7,6},{8,9},{9,8},{10,11... | collective-permute-start | bytes 1769480 | tf_op jit(solution)/shard_map/ppermute | solution.py:321
  43.2 1.3 %collective-permute-start.15 = (bf16[4,8,384]{2,1,0:T(8,128)(2,1)S(1)}, bf16[4,8,384]{2,1,0:T(8,128)(2,1)S(1)}, u32[]{:S(2)}, u32[]{:S(2)}) collective-permute-start(bf16[4,8,384]{2,1,0:T(8,128)(2,1)S(1)} %get-tuple-element.79), channel_id=1, source_target_pairs={{0,1},{1,0},{2,3},{3,2},{4,5},{5,4},{6,7},{7,6},{8,9},{9,8},{10,11... | collective-permute-start | bytes 73736 | tf_op jit(solution)/shard_map/ppermute | solution.py:321
  44.6 13.3 %collective-permute-start.16 = (bf16[168,384]{1,0:T(8,128)(2,1)S(1)}, bf16[168,384]{1,0:T(8,128)(2,1)S(1)}, u32[]{:S(2)}, u32[]{:S(2)}) collective-permute-start(bf16[168,384]{1,0:T(8,128)(2,1)S(1)} %get-tuple-element.81), channel_id=1, source_target_pairs={{0,6},{2,4},{4,2},{6,0},{1,7},{3,5},{5,3},{7,1},{8,14},{10,12},{12... | collective-permute-start | bytes 387080 | tf_op jit(solution)/shard_map/ppermute | solution.py:321
  47.6 10.3 %collective-permute-start.17 = (bf16[168,384]{1,0:T(8,128)(2,1)S(1)}, bf16[168,384]{1,0:T(8,128)(2,1)S(1)}, u32[]{:S(2)}, u32[]{:S(2)}) collective-permute-start(bf16[168,384]{1,0:T(8,128)(2,1)S(1)} %get-tuple-element.82), channel_id=1, source_target_pairs={{0,4},{2,6},{4,0},{6,2},{1,5},{3,7},{5,1},{7,3},{8,12},{10,14},{12... | collective-permute-start | bytes 387080 | tf_op jit(solution)/shard_map/ppermute | solution.py:321
  47.6 10.3 %collective-permute-start.18 = (bf16[168,384]{1,0:T(8,128)(2,1)S(1)}, bf16[168,384]{1,0:T(8,128)(2,1)S(1)}, u32[]{:S(2)}, u32[]{:S(2)}) collective-permute-start(bf16[168,384]{1,0:T(8,128)(2,1)S(1)} %get-tuple-element.83), channel_id=1, source_target_pairs={{0,2},{2,0},{4,6},{6,4},{1,3},{3,1},{5,7},{7,5},{8,10},{10,8},{12,... | collective-permute-start | bytes 387080 | tf_op jit(solution)/shard_map/ppermute | solution.py:321
  58.0 4.0 %collective-permute-start.19 = (bf16[48,384]{1,0:T(8,128)(2,1)S(1)}, bf16[48,384]{1,0:T(8,128)(2,1)S(1)}, u32[]{:S(2)}, u32[]{:S(2)}) collective-permute-start(bf16[48,384]{1,0:T(8,128)(2,1)S(1)} %get-tuple-element.89), channel_id=1, source_target_pairs={{0,8},{8,0},{16,24},{24,16},{1,9},{9,1},{17,25},{25,17},{2,10},{10... | collective-permute-start | bytes 110600 | tf_op jit(solution)/shard_map/ppermute | solution.py:321
  59.2 4.0 %collective-permute-start.20 = (bf16[48,384]{1,0:T(8,128)(2,1)S(1)}, bf16[48,384]{1,0:T(8,128)(2,1)S(1)}, u32[]{:S(2)}, u32[]{:S(2)}) collective-permute-start(bf16[48,384]{1,0:T(8,128)(2,1)S(1)} %get-tuple-element.90), channel_id=1, source_target_pairs={{0,16},{8,24},{16,0},{24,8},{1,17},{9,25},{17,1},{25,9},{2,18},{10... | collective-permute-start | bytes 110600 | tf_op jit(solution)/shard_map/ppermute | solution.py:321
  60.2 4.9 %collective-permute-start.21 = (bf16[48,384]{1,0:T(8,128)(2,1)S(1)}, bf16[48,384]{1,0:T(8,128)(2,1)S(1)}, u32[]{:S(2)}, u32[]{:S(2)}) collective-permute-start(bf16[48,384]{1,0:T(8,128)(2,1)S(1)} %get-tuple-element.91), channel_id=1, source_target_pairs={{0,24},{8,16},{16,8},{24,0},{1,25},{9,17},{17,9},{25,1},{2,26},{10... | collective-permute-start | bytes 110600 | tf_op jit(solution)/shard_map/ppermute | solution.py:321

commit v10 on v9

--- a/solution.py
+++ b/solution.py
@@ -105,13 +105,13 @@
 
 def stack_kernel(count, *refs):
     for q in range(count):
-        refs[-1][q] = refs[q][...]
+        refs[-1][q] = refs[count - 1 - q][...]
 
 
 def join_kernel(groups, _, *refs):
     blocks_d, blocks_x, own_x, own_d = refs[:groups], refs[groups:-2], refs[-2], refs[-1]
     for q in range(groups):
-        own_d[q] = blocks_d[q][...]
+        own_d[q] = blocks_d[groups - 1 - q][...]
     if len(blocks_x) == 1:
         own_x[...] = blocks_x[0][...]
     else:
@@ -305,7 +305,7 @@
     experts, width = router_ref.shape
     blocks = []
     router = jnp.zeros((2 * experts, width), F32)
-    for ref in backs:
+    for ref in reversed(backs):
         block = ref[...].astype(F32)
         router = router + block[CAP : CAP + 2 * experts]
         blocks.append(block[:CAP])
@@ -384,7 +384,10 @@
             return [block, swap(block, "z", 1), second, swap(second, "z", 1)]
         return [lax.all_gather(block, "z", axis=0, tiled=False)]
 
-    arrived = [sends[0]] + [swap(sends[q], "expert", q) for q in range(1, groups)]
+    def exchange(blocks):
+        return [swap(blocks[q], "expert", q) for q in range(groups - 1, 0, -1)] + [blocks[0]]
+
+    arrived = exchange(sends)
     slices = gather(handed)
     picked = call(
         functools.partial(pick_kernel, relative, experts, hops),
@@ -399,7 +402,7 @@
         "stack",
     )
     blocks_x = [stacked] + [swap(stacked, "z", k) for k in range(1, hops)] if relative else gather(stacked)
-    blocks_d = [picked[0]] + [swap(picked[q], "expert", q) for q in range(1, groups)]
+    blocks_d = exchange(picked)
     own_x, own_d = call(
         functools.partial(join_kernel, groups),
         (down_mark, *blocks_d, *blocks_x),
@@ -496,7 +499,7 @@
         [shape((height, width), BF16)] * groups,
         "total",
     )
-    backs = [backs[0]] + [swap(backs[q], "expert", q) for q in range(1, groups)]
+    backs = exchange(backs)
     mixed, grad_router = call(
         functools.partial(combine_kernel, groups),
         (position, *backs),

time: 66.2 us -> 64.5 us (0.974)
  waiting for transfers between devices: 10.6 us -> 8.65 us
    ppermute x22, waiting for transfers between devices: 10.6 us -> 8.65 us  [swap(): return lax.ppermute(block, axis, [(i, i ^ bits) for i in range(size)])]
  transfers between devices with their start and end apart: 22 -> 22, of which waited for: 9 -> 10; matrix products, arithmetic and copies ran while one was open for 0% -> 0% of each run, Pallas kernels for 38% -> 39%
where the time goes in v10:
time: 64.5 us; the launch traced here: 64.2 us
  Pallas kernels  27.7 us (43%)
  starting transfers between devices  27.1 us (42%)
  waiting for transfers between devices  8.65 us (13%)
  between operations  0.77 us (1%)
    ppermute x22, starting transfers between devices, swap(): return lax.ppermute(block, axis, [(i, i ^ bits) for i in range(size)])  27.1 us
    pallas_call x12, Pallas kernels, call(): pl.pallas_call(kernel, out_shape=tuple(outs), in_specs=[fixed if i in loo...  18.8 us
    pallas_call x1, Pallas kernels, shards(): pl.pallas_call(grads_kernel, grid=(parts,), out_shape=(shape(w_gate.shape...  8.84 us
    ppermute x22, waiting for transfers between devices, swap(): return lax.ppermute(block, axis, [(i, i ^ bits) for i in range(size)])  8.65 us
  transfers between devices with their start and end apart: 22, of which 10 were waited for; matrix products, arithmetic and copies ran while one was open for 0% of the time, Pallas kernels for 39%

profile of v10, /device:TPU:0, one launch (start us, length us, event | category | flops | bytes accessed | tf_op | source)
XLA Modules:
  0.0 64.2 jit_solution(2315401154678182540)
XLA Ops:
  0.6 1.6 %pack.1 = (s32[1,256]{1,0:T(1,128)S(1)}, bf16[128,384]{1,0:T(8,128)(2,1)S(1)}, bf16[48,384]{1,0:T(8,128)(2,1)S(1)}, bf16[48,384]{1,0:T(8,128)(2,1)S(1)}, bf16[48...) custom-call(s32[4]{0:T(128)} %refs_0_.1, s32[4]{0:T(128)} %refs_1_.1, s32[2,128]{1,0:T(2,128)} %bitcast.4, ...), custom_call_target="tpu_custom_call" | custom-call | tf_op jit(solution)/shard_map/pack/pallas_call | solution.py:340
  2.2 4.1 %collective-permute-start.1 = (bf16[128,384]{1,0:T(8,128)(2,1)S(1)}, bf16[128,384]{1,0:T(8,128)(2,1)S(1)}, u32[]{:S(2)}, u32[]{:S(2)}) collective-permute-start(bf16[128,384]{1,0:T(8,128)(2,1)S(1)} %get-tuple-element.53.refs_0_), channel_id=1, source_target_pairs={{0,4},{2,6},{4,0},{6,2},{1,5},{3,7},{5,1},{7,3},{8,12},{10,14},{12... | collective-permute-start | bytes 294920 | tf_op jit(solution)/shard_map/ppermute | solution.py:321
  6.3 1.6 %collective-permute-start = (bf16[128,384]{1,0:T(8,128)(2,1)S(1)}, bf16[128,384]{1,0:T(8,128)(2,1)S(1)}, u32[]{:S(2)}, u32[]{:S(2)}) collective-permute-start(bf16[128,384]{1,0:T(8,128)(2,1)S(1)} %get-tuple-element.53.refs_0_), channel_id=1, source_target_pairs={{0,2},{2,0},{4,6},{6,4},{1,3},{3,1},{5,7},{7,5},{8,10},{10,8},{12,... | collective-permute-start | bytes 294920 | tf_op jit(solution)/shard_map/ppermute | solution.py:321
  7.9 2.4 %collective-permute-start.6 = (bf16[48,384]{1,0:T(8,128)(2,1)S(1)}, bf16[48,384]{1,0:T(8,128)(2,1)S(1)}, u32[]{:S(2)}, u32[]{:S(2)}) collective-permute-start(bf16[48,384]{1,0:T(8,128)(2,1)S(1)} %get-tuple-element.59), channel_id=1, source_target_pairs={{0,24},{8,16},{16,8},{24,0},{1,25},{9,17},{17,9},{25,1},{2,26},{10... | collective-permute-start | bytes 110600 | tf_op jit(solution)/shard_map/ppermute | solution.py:321
  10.3 0.5 collective-permute-start.7
  10.8 0.5 collective-permute-start.8
  11.4 2.8 %load_gate.1 = (bf16[1,3072,1024]{2,1,0:T(8,128)(2,1)S(1)}, f32[8,128]{1,0:T(8,128)S(1)}) custom-call(bf16[1,3072,1024]{2,1,0:T(8,128)(2,1)} %source.5), custom_call_target="tpu_custom_call" | custom-call | bytes 12582912 | tf_op jit(solution)/shard_map/load_gate/pallas_call | solution.py:340
  14.2 0.0 collective-permute-done.6.refs_0_
  14.2 0.1 collective-permute-done.7.refs_1_
  14.3 0.5 collective-permute-done.8.refs_2_
  14.8 0.0 collective-permute-done.1.refs_2_.refs_6_
  14.8 0.0 collective-permute-done.refs_1_.refs_5_
  14.8 0.4 collective-permute-start.10
  15.2 0.4 collective-permute-start.2
  15.7 3.6 %collective-permute-start.11 = (bf16[4,48,384]{2,1,0:T(8,128)(2,1)S(1)}, bf16[4,48,384]{2,1,0:T(8,128)(2,1)S(1)}, u32[]{:S(2)}, u32[]{:S(2)}) collective-permute-start(bf16[4,48,384]{2,1,0:T(8,128)(2,1)S(1)} %stack.1.refs_4_), channel_id=1, source_target_pairs={{0,6},{2,4},{4,2},{6,0},{1,7},{3,5},{5,3},{7,1},{8,14},{10,12},{12... | collective-permute-start | bytes 442376 | tf_op jit(solution)/shard_map/ppermute | solution.py:321
  19.3 0.0 collective-permute-start.9
  19.3 2.8 %load_up.1 = (bf16[1,3072,1024]{2,1,0:T(8,128)(2,1)S(1)}, f32[8,128]{1,0:T(8,128)S(1)}) custom-call(bf16[1,3072,1024]{2,1,0:T(8,128)(2,1)} %source.4), custom_call_target="tpu_custom_call" | custom-call | bytes 12582912 | tf_op jit(solution)/shard_map/load_up/pallas_call | solution.py:340
  22.1 1.5 %collective-permute-done.2.refs_3_ = bf16[128,384]{1,0:T(8,128)(2,1)S(1)} collective-permute-done((bf16[128,384]{1,0:T(8,128)(2,1)S(1)}, bf16[128,384]{1,0:T(8,128)(2,1)S(1)}, u32[]{:S(2)}, u32[]{:S(2)}) %collective-permute-start.2) | collective-permute-done | bytes 98336 | tf_op jit(solution)/shard_map/ppermute | solution.py:321
  23.6 0.3 pick.1
  23.9 2.9 %collective-permute-start.3 = (bf16[4,40,384]{2,1,0:T(8,128)(2,1)S(1)}, bf16[4,40,384]{2,1,0:T(8,128)(2,1)S(1)}, u32[]{:S(2)}, u32[]{:S(2)}) collective-permute-start(bf16[4,40,384]{2,1,0:T(8,128)(2,1)S(1)} %get-tuple-element.55), channel_id=1, source_target_pairs={{0,24},{8,16},{16,8},{24,0},{1,25},{9,17},{17,9},{25,1},{2,26},{10... | collective-permute-start | bytes 368648 | tf_op jit(solution)/shard_map/ppermute | solution.py:321
  26.9 0.5 collective-permute-start.4
  27.4 0.0 collective-permute-done.10.refs_6_
  27.4 0.9 %collective-permute-start.5 = (bf16[4,40,384]{2,1,0:T(8,128)(2,1)S(1)}, bf16[4,40,384]{2,1,0:T(8,128)(2,1)S(1)}, u32[]{:S(2)}, u32[]{:S(2)}) collective-permute-start(bf16[4,40,384]{2,1,0:T(8,128)(2,1)S(1)} %get-tuple-element.57), channel_id=1, source_target_pairs={{0,8},{8,0},{16,24},{24,16},{1,9},{9,1},{17,25},{25,17},{2,10},{10... | collective-permute-start | bytes 368648 | tf_op jit(solution)/shard_map/ppermute | solution.py:321
  28.2 2.8 %load_down.1 = (bf16[1,1024,3072]{2,1,0:T(8,128)(2,1)S(1)}, f32[8,128]{1,0:T(8,128)S(1)}) custom-call(bf16[1,1024,3072]{2,1,0:T(8,128)(2,1)} %source.3), custom_call_target="tpu_custom_call" | custom-call | bytes 12582912 | tf_op jit(solution)/shard_map/load_down/pallas_call | solution.py:340
  31.0 0.0 collective-permute-done.11.refs_7_
  31.0 0.0 collective-permute-done.9.refs_5_
  31.0 0.0 collective-permute-done.3.refs_0_
  31.1 0.7 %collective-permute-done.4.refs_1_ = bf16[4,40,384]{2,1,0:T(8,128)(2,1)S(1)} collective-permute-done((bf16[4,40,384]{2,1,0:T(8,128)(2,1)S(1)}, bf16[4,40,384]{2,1,0:T(8,128)(2,1)S(1)}, u32[]{:S(2)}, u32[]{:S(2)}) %collective-permute-start.4) | collective-permute-done | bytes 122912 | tf_op jit(solution)/shard_map/ppermute | solution.py:321
  31.7 0.5 collective-permute-done.5.refs_2_
  32.2 0.1 join.1
  32.3 0.1 collective-permute-start.12
  32.4 0.5 collective-permute-start.14
  32.9 1.5 %collective-permute-done.12.refs_1_ = bf16[4,4,48,384]{3,2,1,0:T(8,128)(2,1)S(1)} collective-permute-done((bf16[4,4,48,384]{3,2,1,0:T(8,128)(2,1)S(1)}, bf16[4,4,48,384]{3,2,1,0:T(8,128)(2,1)S(1)}, u32[]{:S(2)}, u32[]{:S(2)}) %collective-permute-start.12) | collective-permute-done | bytes 589856 | tf_op jit(solution)/shard_map/ppermute | solution.py:321
  34.4 4.2 %forward.1 = (bf16[192,3072]{1,0:T(8,128)(2,1)S(1)}, bf16[192,1024]{1,0:T(8,128)(2,1)S(1)}, f32[192,1024]{1,0:T(8,128)S(1)}, f32[192,1024]{1,0:T(8,128)S(1)}, f3...) custom-call(bf16[4,4,48,384]{3,2,1,0:T(8,128)(2,1)S(1)} %get-tuple-e, ...), custom_call_target="tpu_custom_call" | custom-call | flops 3623878656 | bytes 18874368 | tf_op jit(solution)/shard_map/forward/pallas_call | solution.py:340
  38.6 0.2 collective-permute-start.13
  38.8 0.0 collective-permute-done.14.refs_1_
  38.8 3.2 %backward.1 = (bf16[192,3072]{1,0:T(8,128)(2,1)S(1)}, bf16[192,1024]{1,0:T(8,128)(2,1)S(1)}, bf16[192,1024]{1,0:T(8,128)(2,1)S(1)}, f32[4,4,384]{2,1,0:T(4,128)S(1)}, bf16[4,8,384]{2,1,0:T(8,128)(2,1)S(1)}) custom-call(bf16[4,4,40,384]{3,2,1,0:T(8,128)(2,1)S(1)} %get-tuple-element.70.refs_0_, bf16[4,4,40,384]{3,2,1,0:T(8,128)(2,1)S(1)} %collective-permute-done.14.refs_1_, ...), custom_call_target="tpu_custom_call" | custom-call | flops 1207959552 | bytes 6291456 | tf_op jit(solution)/shard_map/backward/pallas_call | solution.py:340
  42.1 0.4 collective-permute-start.15
  42.5 0.8 %collective-permute-done.15.rgot_ref = bf16[4,8,384]{2,1,0:T(8,128)(2,1)S(1)} collective-permute-done((bf16[4,8,384]{2,1,0:T(8,128)(2,1)S(1)}, bf16[4,8,384]{2,1,0:T(8,128)(2,1)S(1)}, u32[]{:S(2)}, u32[]{:S(2)}) %collective-permute-start.15) | collective-permute-done | bytes 24608 | tf_op jit(solution)/shard_map/ppermute | solution.py:321
  43.3 0.0 collective-permute-done.13.got_ref
  43.3 0.1 merge.1
  43.5 3.6 %collective-permute-start.16 = (bf16[168,384]{1,0:T(8,128)(2,1)S(1)}, bf16[168,384]{1,0:T(8,128)(2,1)S(1)}, u32[]{:S(2)}, u32[]{:S(2)}) collective-permute-start(bf16[168,384]{1,0:T(8,128)(2,1)S(1)} %get-tuple-element.81), channel_id=1, source_target_pairs={{0,6},{2,4},{4,2},{6,0},{1,7},{3,5},{5,3},{7,1},{8,14},{10,12},{12... | collective-permute-start | bytes 387080 | tf_op jit(solution)/shard_map/ppermute | solution.py:321
  47.0 0.0 collective-permute-start.17
  47.0 0.9 %collective-permute-start.18 = (bf16[168,384]{1,0:T(8,128)(2,1)S(1)}, bf16[168,384]{1,0:T(8,128)(2,1)S(1)}, u32[]{:S(2)}, u32[]{:S(2)}) collective-permute-start(bf16[168,384]{1,0:T(8,128)(2,1)S(1)} %get-tuple-element.83), channel_id=1, source_target_pairs={{0,2},{2,0},{4,6},{6,4},{1,3},{3,1},{5,7},{7,5},{8,10},{10,8},{12,... | collective-permute-start | bytes 387080 | tf_op jit(solution)/shard_map/ppermute | solution.py:321
  47.9 8.8 %grads.1 = (bf16[1,3072,1024]{2,1,0:T(8,128)(2,1)}, bf16[1,3072,1024]{2,1,0:T(8,128)(2,1)}, bf16[1,1024,3072]{2,1,0:T(8,128)(2,1)}, f32[8,128]{1,0:T(8,128)S(1)}) custom-call(bf16[192,3072]{1,0:T(8,128)(2,1)S(1)} %get-tuple-element.71.refs_2_.x_ref, bf16[192,3072]{1,0:T(8,128)(2,1)S(1)} %get-tuple-element.84.d_ref, ...), custom_call_target="tpu_custom_call" | custom-call | flops 3623878656 | bytes 18874368 | tf_op jit(solution)/shard_map/grads/pallas_call | solution.py:468
  56.8 0.0 collective-permute-done.16.refs_1_
  56.8 0.0 collective-permute-done.17.refs_2_
  56.8 0.0 collective-permute-done.18.refs_3_
  56.8 0.1 total.1
  56.8 1.9 %collective-permute-start.19 = (bf16[48,384]{1,0:T(8,128)(2,1)S(1)}, bf16[48,384]{1,0:T(8,128)(2,1)S(1)}, u32[]{:S(2)}, u32[]{:S(2)}) collective-permute-start(bf16[48,384]{1,0:T(8,128)(2,1)S(1)} %get-tuple-element.88), channel_id=1, source_target_pairs={{0,24},{8,16},{16,8},{24,0},{1,25},{9,17},{17,9},{25,1},{2,26},{10... | collective-permute-start | bytes 110600 | tf_op jit(solution)/shard_map/ppermute | solution.py:321
  58.7 0.6 %collective-permute-start.20 = (bf16[48,384]{1,0:T(8,128)(2,1)S(1)}, bf16[48,384]{1,0:T(8,128)(2,1)S(1)}, u32[]{:S(2)}, u32[]{:S(2)}) collective-permute-start(bf16[48,384]{1,0:T(8,128)(2,1)S(1)} %get-tuple-element.89), channel_id=1, source_target_pairs={{0,16},{8,24},{16,0},{24,8},{1,17},{9,25},{17,1},{25,9},{2,18},{10... | collective-permute-start | bytes 110600 | tf_op jit(solution)/shard_map/ppermute | solution.py:321
  59.4 1.0 %collective-permute-start.21 = (bf16[48,384]{1,0:T(8,128)(2,1)S(1)}, bf16[48,384]{1,0:T(8,128)(2,1)S(1)}, u32[]{:S(2)}, u32[]{:S(2)}) collective-permute-start(bf16[48,384]{1,0:T(8,128)(2,1)S(1)} %get-tuple-element.90), channel_id=1, source_target_pairs={{0,8},{8,0},{16,24},{24,16},{1,9},{9,1},{17,25},{25,17},{2,10},{10... | collective-permute-start | bytes 110600 | tf_op jit(solution)/shard_map/ppermute | solution.py:321
  60.4 1.5 %collective-permute-done.19.refs_0_ = bf16[48,384]{1,0:T(8,128)(2,1)S(1)} collective-permute-done((bf16[48,384]{1,0:T(8,128)(2,1)S(1)}, bf16[48,384]{1,0:T(8,128)(2,1)S(1)}, u32[]{:S(2)}, u32[]{:S(2)}) %collective-permute-start.19) | collective-permute-done | bytes 36896 | tf_op jit(solution)/shard_map/ppermute | solution.py:321
  61.9 0.8 %collective-permute-done.20.refs_1_ = bf16[48,384]{1,0:T(8,128)(2,1)S(1)} collective-permute-done((bf16[48,384]{1,0:T(8,128)(2,1)S(1)}, bf16[48,384]{1,0:T(8,128)(2,1)S(1)}, u32[]{:S(2)}, u32[]{:S(2)}) %collective-permute-start.20) | collective-permute-done | bytes 36896 | tf_op jit(solution)/shard_map/ppermute | solution.py:321
  62.7 0.6 %collective-permute-done.21.refs_2_ = bf16[48,384]{1,0:T(8,128)(2,1)S(1)} collective-permute-done((bf16[48,384]{1,0:T(8,128)(2,1)S(1)}, bf16[48,384]{1,0:T(8,128)(2,1)S(1)}, u32[]{:S(2)}, u32[]{:S(2)}) %collective-permute-start.21) | collective-permute-done | bytes 36896 | tf_op jit(solution)/shard_map/ppermute | solution.py:321
  63.3 0.9 %combine.1 = (bf16[128,384]{1,0:T(8,128)(2,1)}, bf16[4,384]{1,0:T(4,128)(2,1)}) custom-call(s32[1,256]{1,0:T(1,128)S(1)} %get-tuple-element.51.pos_ref, bf16[48,384]{1,0:T(8,128)(2,1)S(1)} %collective-permute-done.19.refs_0_, bf16[48,384]{1,0:T(8,128)(2,1)S(1)} %collective-permute-done.20.refs_1_, bf16[48,384]{1,0:T(8,128)(2,1)S(1)} %collective-permute-done.21.refs_2_, ...), custom_call_target="tpu_custom_call" | custom-call | tf_op jit(solution)/shard_map/combine/pallas_call | solution.py:340
  (1 shorter events, 0.0 us)
Async XLA Ops:
  2.2 12.6 %collective-permute-start.1 = (bf16[128,384]{1,0:T(8,128)(2,1)S(1)}, bf16[128,384]{1,0:T(8,128)(2,1)S(1)}, u32[]{:S(2)}, u32[]{:S(2)}) collective-permute-start(bf16[128,384]{1,0:T(8,128)(2,1)S(1)} %get-tuple-element.53.refs_0_), channel_id=1, source_target_pairs={{0,4},{2,6},{4,0},{6,2},{1,5},{3,7},{5,1},{7,3},{8,12},{10,14},{12... | collective-permute-start | bytes 294920 | tf_op jit(solution)/shard_map/ppermute | solution.py:321
  6.3 8.5 %collective-permute-start = (bf16[128,384]{1,0:T(8,128)(2,1)S(1)}, bf16[128,384]{1,0:T(8,128)(2,1)S(1)}, u32[]{:S(2)}, u32[]{:S(2)}) collective-permute-start(bf16[128,384]{1,0:T(8,128)(2,1)S(1)} %get-tuple-element.53.refs_0_), channel_id=1, source_target_pairs={{0,2},{2,0},{4,6},{6,4},{1,3},{3,1},{5,7},{7,5},{8,10},{10,8},{12,... | collective-permute-start | bytes 294920 | tf_op jit(solution)/shard_map/ppermute | solution.py:321
  7.9 6.3 %collective-permute-start.6 = (bf16[48,384]{1,0:T(8,128)(2,1)S(1)}, bf16[48,384]{1,0:T(8,128)(2,1)S(1)}, u32[]{:S(2)}, u32[]{:S(2)}) collective-permute-start(bf16[48,384]{1,0:T(8,128)(2,1)S(1)} %get-tuple-element.59), channel_id=1, source_target_pairs={{0,24},{8,16},{16,8},{24,0},{1,25},{9,17},{17,9},{25,1},{2,26},{10... | collective-permute-start | bytes 110600 | tf_op jit(solution)/shard_map/ppermute | solution.py:321
  10.3 4.0 %collective-permute-start.7 = (bf16[48,384]{1,0:T(8,128)(2,1)S(1)}, bf16[48,384]{1,0:T(8,128)(2,1)S(1)}, u32[]{:S(2)}, u32[]{:S(2)}) collective-permute-start(bf16[48,384]{1,0:T(8,128)(2,1)S(1)} %get-tuple-element.60), channel_id=1, source_target_pairs={{0,16},{8,24},{16,0},{24,8},{1,17},{9,25},{17,1},{25,9},{2,18},{10... | collective-permute-start | bytes 110600 | tf_op jit(solution)/shard_map/ppermute | solution.py:321
  10.8 4.0 %collective-permute-start.8 = (bf16[48,384]{1,0:T(8,128)(2,1)S(1)}, bf16[48,384]{1,0:T(8,128)(2,1)S(1)}, u32[]{:S(2)}, u32[]{:S(2)}) collective-permute-start(bf16[48,384]{1,0:T(8,128)(2,1)S(1)} %get-tuple-element.61), channel_id=1, source_target_pairs={{0,8},{8,0},{16,24},{24,16},{1,9},{9,1},{17,25},{25,17},{2,10},{10... | collective-permute-start | bytes 110600 | tf_op jit(solution)/shard_map/ppermute | solution.py:321
  14.8 12.5 %collective-permute-start.10 = (bf16[4,48,384]{2,1,0:T(8,128)(2,1)S(1)}, bf16[4,48,384]{2,1,0:T(8,128)(2,1)S(1)}, u32[]{:S(2)}, u32[]{:S(2)}) collective-permute-start(bf16[4,48,384]{2,1,0:T(8,128)(2,1)S(1)} %stack.1.refs_4_), channel_id=1, source_target_pairs={{0,4},{2,6},{4,0},{6,2},{1,5},{3,7},{5,1},{7,3},{8,12},{10,14},{12... | collective-permute-start | bytes 442376 | tf_op jit(solution)/shard_map/ppermute | solution.py:321
  15.2 8.4 %collective-permute-start.2 = (bf16[128,384]{1,0:T(8,128)(2,1)S(1)}, bf16[128,384]{1,0:T(8,128)(2,1)S(1)}, u32[]{:S(2)}, u32[]{:S(2)}) collective-permute-start(bf16[128,384]{1,0:T(8,128)(2,1)S(1)} %collective-permute-done.1.refs_2_.refs_6_), channel_id=1, source_target_pairs={{0,2},{2,0},{4,6},{6,4},{1,3},{3,1},{5,7},{7,5},{8,10},{10,8},{12,... | collective-permute-start | bytes 294920 | tf_op jit(solution)/shard_map/ppermute | solution.py:321
  15.7 15.3 %collective-permute-start.11 = (bf16[4,48,384]{2,1,0:T(8,128)(2,1)S(1)}, bf16[4,48,384]{2,1,0:T(8,128)(2,1)S(1)}, u32[]{:S(2)}, u32[]{:S(2)}) collective-permute-start(bf16[4,48,384]{2,1,0:T(8,128)(2,1)S(1)} %stack.1.refs_4_), channel_id=1, source_target_pairs={{0,6},{2,4},{4,2},{6,0},{1,7},{3,5},{5,3},{7,1},{8,14},{10,12},{12... | collective-permute-start | bytes 442376 | tf_op jit(solution)/shard_map/ppermute | solution.py:321
  19.3 11.7 %collective-permute-start.9 = (bf16[4,48,384]{2,1,0:T(8,128)(2,1)S(1)}, bf16[4,48,384]{2,1,0:T(8,128)(2,1)S(1)}, u32[]{:S(2)}, u32[]{:S(2)}) collective-permute-start(bf16[4,48,384]{2,1,0:T(8,128)(2,1)S(1)} %stack.1.refs_4_), channel_id=1, source_target_pairs={{0,2},{2,0},{4,6},{6,4},{1,3},{3,1},{5,7},{7,5},{8,10},{10,8},{12,... | collective-permute-start | bytes 442376 | tf_op jit(solution)/shard_map/ppermute | solution.py:321
  23.9 7.1 %collective-permute-start.3 = (bf16[4,40,384]{2,1,0:T(8,128)(2,1)S(1)}, bf16[4,40,384]{2,1,0:T(8,128)(2,1)S(1)}, u32[]{:S(2)}, u32[]{:S(2)}) collective-permute-start(bf16[4,40,384]{2,1,0:T(8,128)(2,1)S(1)} %get-tuple-element.55), channel_id=1, source_target_pairs={{0,24},{8,16},{16,8},{24,0},{1,25},{9,17},{17,9},{25,1},{2,26},{10... | collective-permute-start | bytes 368648 | tf_op jit(solution)/shard_map/ppermute | solution.py:321
  26.9 4.9 %collective-permute-start.4 = (bf16[4,40,384]{2,1,0:T(8,128)(2,1)S(1)}, bf16[4,40,384]{2,1,0:T(8,128)(2,1)S(1)}, u32[]{:S(2)}, u32[]{:S(2)}) collective-permute-start(bf16[4,40,384]{2,1,0:T(8,128)(2,1)S(1)} %get-tuple-element.56), channel_id=1, source_target_pairs={{0,16},{8,24},{16,0},{24,8},{1,17},{9,25},{17,1},{25,9},{2,18},{10... | collective-permute-start | bytes 368648 | tf_op jit(solution)/shard_map/ppermute | solution.py:321
  27.4 4.9 %collective-permute-start.5 = (bf16[4,40,384]{2,1,0:T(8,128)(2,1)S(1)}, bf16[4,40,384]{2,1,0:T(8,128)(2,1)S(1)}, u32[]{:S(2)}, u32[]{:S(2)}) collective-permute-start(bf16[4,40,384]{2,1,0:T(8,128)(2,1)S(1)} %get-tuple-element.57), channel_id=1, source_target_pairs={{0,8},{8,0},{16,24},{24,16},{1,9},{9,1},{17,25},{25,17},{2,10},{10... | collective-permute-start | bytes 368648 | tf_op jit(solution)/shard_map/ppermute | solution.py:321
  32.3 2.1 %collective-permute-start.12 = (bf16[4,4,48,384]{3,2,1,0:T(8,128)(2,1)S(1)}, bf16[4,4,48,384]{3,2,1,0:T(8,128)(2,1)S(1)}, u32[]{:S(2)}, u32[]{:S(2)}) collective-permute-start(bf16[4,4,48,384]{3,2,1,0:T(8,128)(2,1)S(1)} %get-tuple-element.64.refs_0_), channel_id=1, source_target_pairs={{0,1},{1,0},{2,3},{3,2},{4,5},{5,4},{6,7},{7,6},{8,9},{9,8},{10,11... | collective-permute-start | bytes 1769480 | tf_op jit(solution)/shard_map/ppermute | solution.py:321
  32.4 6.4 %collective-permute-start.14 = (bf16[4,4,40,384]{3,2,1,0:T(8,128)(2,1)S(1)}, bf16[4,4,40,384]{3,2,1,0:T(8,128)(2,1)S(1)}, u32[]{:S(2)}, u32[]{:S(2)}) collective-permute-start(bf16[4,4,40,384]{3,2,1,0:T(8,128)(2,1)S(1)} %get-tuple-element.70.refs_0_), channel_id=1, source_target_pairs={{0,1},{1,0},{2,3},{3,2},{4,5},{5,4},{6,7},{7,6},{8,9},{9,8},{10,11... | collective-permute-start | bytes 1474568 | tf_op jit(solution)/shard_map/ppermute | solution.py:321
  38.6 4.7 %collective-permute-start.13 = (bf16[4,4,48,384]{3,2,1,0:T(8,128)(2,1)S(1)}, bf16[4,4,48,384]{3,2,1,0:T(8,128)(2,1)S(1)}, u32[]{:S(2)}, u32[]{:S(2)}) collective-permute-start(bf16[4,4,48,384]{3,2,1,0:T(8,128)(2,1)S(1)} %get-tuple-element.69), channel_id=1, source_target_pairs={{0,1},{1,0},{2,3},{3,2},{4,5},{5,4},{6,7},{7,6},{8,9},{9,8},{10,11... | collective-permute-start | bytes 1769480 | tf_op jit(solution)/shard_map/ppermute | solution.py:321
  42.1 1.3 %collective-permute-start.15 = (bf16[4,8,384]{2,1,0:T(8,128)(2,1)S(1)}, bf16[4,8,384]{2,1,0:T(8,128)(2,1)S(1)}, u32[]{:S(2)}, u32[]{:S(2)}) collective-permute-start(bf16[4,8,384]{2,1,0:T(8,128)(2,1)S(1)} %get-tuple-element.79), channel_id=1, source_target_pairs={{0,1},{1,0},{2,3},{3,2},{4,5},{5,4},{6,7},{7,6},{8,9},{9,8},{10,11... | collective-permute-start | bytes 73736 | tf_op jit(solution)/shard_map/ppermute | solution.py:321
  43.5 13.3 %collective-permute-start.16 = (bf16[168,384]{1,0:T(8,128)(2,1)S(1)}, bf16[168,384]{1,0:T(8,128)(2,1)S(1)}, u32[]{:S(2)}, u32[]{:S(2)}) collective-permute-start(bf16[168,384]{1,0:T(8,128)(2,1)S(1)} %get-tuple-element.81), channel_id=1, source_target_pairs={{0,6},{2,4},{4,2},{6,0},{1,7},{3,5},{5,3},{7,1},{8,14},{10,12},{12... | collective-permute-start | bytes 387080 | tf_op jit(solution)/shard_map/ppermute | solution.py:321
  47.0 9.7 %collective-permute-start.17 = (bf16[168,384]{1,0:T(8,128)(2,1)S(1)}, bf16[168,384]{1,0:T(8,128)(2,1)S(1)}, u32[]{:S(2)}, u32[]{:S(2)}) collective-permute-start(bf16[168,384]{1,0:T(8,128)(2,1)S(1)} %get-tuple-element.82), channel_id=1, source_target_pairs={{0,4},{2,6},{4,0},{6,2},{1,5},{3,7},{5,1},{7,3},{8,12},{10,14},{12... | collective-permute-start | bytes 387080 | tf_op jit(solution)/shard_map/ppermute | solution.py:321
  47.0 9.7 %collective-permute-start.18 = (bf16[168,384]{1,0:T(8,128)(2,1)S(1)}, bf16[168,384]{1,0:T(8,128)(2,1)S(1)}, u32[]{:S(2)}, u32[]{:S(2)}) collective-permute-start(bf16[168,384]{1,0:T(8,128)(2,1)S(1)} %get-tuple-element.83), channel_id=1, source_target_pairs={{0,2},{2,0},{4,6},{6,4},{1,3},{3,1},{5,7},{7,5},{8,10},{10,8},{12,... | collective-permute-start | bytes 387080 | tf_op jit(solution)/shard_map/ppermute | solution.py:321
  56.8 5.0 %collective-permute-start.19 = (bf16[48,384]{1,0:T(8,128)(2,1)S(1)}, bf16[48,384]{1,0:T(8,128)(2,1)S(1)}, u32[]{:S(2)}, u32[]{:S(2)}) collective-permute-start(bf16[48,384]{1,0:T(8,128)(2,1)S(1)} %get-tuple-element.88), channel_id=1, source_target_pairs={{0,24},{8,16},{16,8},{24,0},{1,25},{9,17},{17,9},{25,1},{2,26},{10... | collective-permute-start | bytes 110600 | tf_op jit(solution)/shard_map/ppermute | solution.py:321
  58.7 4.0 %collective-permute-start.20 = (bf16[48,384]{1,0:T(8,128)(2,1)S(1)}, bf16[48,384]{1,0:T(8,128)(2,1)S(1)}, u32[]{:S(2)}, u32[]{:S(2)}) collective-permute-start(bf16[48,384]{1,0:T(8,128)(2,1)S(1)} %get-tuple-element.89), channel_id=1, source_target_pairs={{0,16},{8,24},{16,0},{24,8},{1,17},{9,25},{17,1},{25,9},{2,18},{10... | collective-permute-start | bytes 110600 | tf_op jit(solution)/shard_map/ppermute | solution.py:321
  59.4 4.0 %collective-permute-start.21 = (bf16[48,384]{1,0:T(8,128)(2,1)S(1)}, bf16[48,384]{1,0:T(8,128)(2,1)S(1)}, u32[]{:S(2)}, u32[]{:S(2)}) collective-permute-start(bf16[48,384]{1,0:T(8,128)(2,1)S(1)} %get-tuple-element.90), channel_id=1, source_target_pairs={{0,8},{8,0},{16,24},{24,16},{1,9},{9,1},{17,25},{25,17},{2,10},{10... | collective-permute-start | bytes 110600 | tf_op jit(solution)/shard_map/ppermute | solution.py:321

commit v11 on v10

--- a/solution.py
+++ b/solution.py
@@ -116,7 +116,7 @@
         own_x[...] = blocks_x[0][...]
     else:
         for k in range(len(blocks_x)):
-            own_x[k] = blocks_x[k][...]
+            own_x[k] = blocks_x[len(blocks_x) - 1 - k][...]
 
 
 def pick_kernel(relative, experts, hops, pos_ref, *refs):
@@ -401,7 +401,7 @@
         [shape((groups, ROWS, width), BF16)],
         "stack",
     )
-    blocks_x = [stacked] + [swap(stacked, "z", k) for k in range(1, hops)] if relative else gather(stacked)
+    blocks_x = [swap(stacked, "z", k) for k in range(hops - 1, 0, -1)] + [stacked] if relative else gather(stacked)
     blocks_d = exchange(picked)
     own_x, own_d = call(
         functools.partial(join_kernel, groups),

time: 64.5 us -> 64.3 us (level)
  no operation moved by 1% of the time
where the time goes in v11:
time: 64.3 us; the launch traced here: 64 us
  Pallas kernels  27.7 us (43%)
  starting transfers between devices  27.1 us (42%)
  waiting for transfers between devices  8.49 us (13%)
  between operations  0.76 us (1%)
    ppermute x22, starting transfers between devices, swap(): return lax.ppermute(block, axis, [(i, i ^ bits) for i in range(size)])  27.1 us
    pallas_call x12, Pallas kernels, call(): pl.pallas_call(kernel, out_shape=tuple(outs), in_specs=[fixed if i in loo...  18.9 us
    pallas_call x1, Pallas kernels, shards(): pl.pallas_call(grads_kernel, grid=(parts,), out_shape=(shape(w_gate.shape...  8.84 us
    ppermute x22, waiting for transfers between devices, swap(): return lax.ppermute(block, axis, [(i, i ^ bits) for i in range(size)])  8.49 us
  transfers between devices with their start and end apart: 22, of which 10 were waited for; matrix products, arithmetic and copies ran while one was open for 0% of the time, Pallas kernels for 39%

profile of v11, /device:TPU:0, one launch (start us, length us, event | category | flops | bytes accessed | tf_op | source)
XLA Modules:
  0.0 64.0 jit_solution(374183715211186448)
XLA Ops:
  0.6 1.6 %pack.1 = (s32[1,256]{1,0:T(1,128)S(1)}, bf16[128,384]{1,0:T(8,128)(2,1)S(1)}, bf16[48,384]{1,0:T(8,128)(2,1)S(1)}, bf16[48,384]{1,0:T(8,128)(2,1)S(1)}, bf16[48...) custom-call(s32[4]{0:T(128)} %refs_0_.1, s32[4]{0:T(128)} %refs_1_.1, s32[2,128]{1,0:T(2,128)} %bitcast.4, ...), custom_call_target="tpu_custom_call" | custom-call | tf_op jit(solution)/shard_map/pack/pallas_call | solution.py:340
  2.2 4.1 %collective-permute-start.1 = (bf16[128,384]{1,0:T(8,128)(2,1)S(1)}, bf16[128,384]{1,0:T(8,128)(2,1)S(1)}, u32[]{:S(2)}, u32[]{:S(2)}) collective-permute-start(bf16[128,384]{1,0:T(8,128)(2,1)S(1)} %get-tuple-element.53.refs_0_), channel_id=1, source_target_pairs={{0,4},{2,6},{4,0},{6,2},{1,5},{3,7},{5,1},{7,3},{8,12},{10,14},{12... | collective-permute-start | bytes 294920 | tf_op jit(solution)/shard_map/ppermute | solution.py:321
  6.3 1.6 %collective-permute-start = (bf16[128,384]{1,0:T(8,128)(2,1)S(1)}, bf16[128,384]{1,0:T(8,128)(2,1)S(1)}, u32[]{:S(2)}, u32[]{:S(2)}) collective-permute-start(bf16[128,384]{1,0:T(8,128)(2,1)S(1)} %get-tuple-element.53.refs_0_), channel_id=1, source_target_pairs={{0,2},{2,0},{4,6},{6,4},{1,3},{3,1},{5,7},{7,5},{8,10},{10,8},{12,... | collective-permute-start | bytes 294920 | tf_op jit(solution)/shard_map/ppermute | solution.py:321
  7.9 2.4 %collective-permute-start.6 = (bf16[48,384]{1,0:T(8,128)(2,1)S(1)}, bf16[48,384]{1,0:T(8,128)(2,1)S(1)}, u32[]{:S(2)}, u32[]{:S(2)}) collective-permute-start(bf16[48,384]{1,0:T(8,128)(2,1)S(1)} %get-tuple-element.59), channel_id=1, source_target_pairs={{0,24},{8,16},{16,8},{24,0},{1,25},{9,17},{17,9},{25,1},{2,26},{10... | collective-permute-start | bytes 110600 | tf_op jit(solution)/shard_map/ppermute | solution.py:321
  10.3 0.5 collective-permute-start.7
  10.8 0.5 collective-permute-start.8
  11.4 2.8 %load_gate.1 = (bf16[1,3072,1024]{2,1,0:T(8,128)(2,1)S(1)}, f32[8,128]{1,0:T(8,128)S(1)}) custom-call(bf16[1,3072,1024]{2,1,0:T(8,128)(2,1)} %source.5), custom_call_target="tpu_custom_call" | custom-call | bytes 12582912 | tf_op jit(solution)/shard_map/load_gate/pallas_call | solution.py:340
  14.2 0.0 collective-permute-done.6.refs_0_
  14.2 0.1 collective-permute-done.7.refs_1_
  14.3 0.5 collective-permute-done.8.refs_2_
  14.8 0.0 collective-permute-done.1.refs_2_.refs_6_
  14.8 0.0 collective-permute-done.refs_1_.refs_5_
  14.8 0.4 collective-permute-start.10
  15.2 0.4 collective-permute-start.2
  15.7 1.6 %collective-permute-start.11 = (bf16[4,48,384]{2,1,0:T(8,128)(2,1)S(1)}, bf16[4,48,384]{2,1,0:T(8,128)(2,1)S(1)}, u32[]{:S(2)}, u32[]{:S(2)}) collective-permute-start(bf16[4,48,384]{2,1,0:T(8,128)(2,1)S(1)} %stack.1.refs_7_), channel_id=1, source_target_pairs={{0,2},{2,0},{4,6},{6,4},{1,3},{3,1},{5,7},{7,5},{8,10},{10,8},{12,... | collective-permute-start | bytes 442376 | tf_op jit(solution)/shard_map/ppermute | solution.py:321
  17.3 2.5 %collective-permute-start.9 = (bf16[4,48,384]{2,1,0:T(8,128)(2,1)S(1)}, bf16[4,48,384]{2,1,0:T(8,128)(2,1)S(1)}, u32[]{:S(2)}, u32[]{:S(2)}) collective-permute-start(bf16[4,48,384]{2,1,0:T(8,128)(2,1)S(1)} %stack.1.refs_7_), channel_id=1, source_target_pairs={{0,6},{2,4},{4,2},{6,0},{1,7},{3,5},{5,3},{7,1},{8,14},{10,12},{12... | collective-permute-start | bytes 442376 | tf_op jit(solution)/shard_map/ppermute | solution.py:321
  19.7 2.8 %load_up.1 = (bf16[1,3072,1024]{2,1,0:T(8,128)(2,1)S(1)}, f32[8,128]{1,0:T(8,128)S(1)}) custom-call(bf16[1,3072,1024]{2,1,0:T(8,128)(2,1)} %source.4), custom_call_target="tpu_custom_call" | custom-call | bytes 12582912 | tf_op jit(solution)/shard_map/load_up/pallas_call | solution.py:340
  22.5 0.0 collective-permute-done.2.refs_3_
  22.6 0.3 pick.1
  22.9 3.0 %collective-permute-start.3 = (bf16[4,40,384]{2,1,0:T(8,128)(2,1)S(1)}, bf16[4,40,384]{2,1,0:T(8,128)(2,1)S(1)}, u32[]{:S(2)}, u32[]{:S(2)}) collective-permute-start(bf16[4,40,384]{2,1,0:T(8,128)(2,1)S(1)} %get-tuple-element.55), channel_id=1, source_target_pairs={{0,24},{8,16},{16,8},{24,0},{1,25},{9,17},{17,9},{25,1},{2,26},{10... | collective-permute-start | bytes 368648 | tf_op jit(solution)/shard_map/ppermute | solution.py:321
  25.9 0.5 collective-permute-start.4
  26.4 0.0 collective-permute-done.10.refs_5_
  26.4 0.2 collective-permute-start.5
  26.6 2.8 %load_down.1 = (bf16[1,1024,3072]{2,1,0:T(8,128)(2,1)S(1)}, f32[8,128]{1,0:T(8,128)S(1)}) custom-call(bf16[1,1024,3072]{2,1,0:T(8,128)(2,1)} %source.3), custom_call_target="tpu_custom_call" | custom-call | bytes 12582912 | tf_op jit(solution)/shard_map/load_down/pallas_call | solution.py:340
  29.4 0.0 collective-permute-done.11.refs_6_
  29.5 0.0 collective-permute-done.9.refs_4_
  29.5 0.0 collective-permute-done.3.refs_0_
  29.5 1.3 %collective-permute-done.4.refs_1_ = bf16[4,40,384]{2,1,0:T(8,128)(2,1)S(1)} collective-permute-done((bf16[4,40,384]{2,1,0:T(8,128)(2,1)S(1)}, bf16[4,40,384]{2,1,0:T(8,128)(2,1)S(1)}, u32[]{:S(2)}, u32[]{:S(2)}) %collective-permute-start.4) | collective-permute-done | bytes 122912 | tf_op jit(solution)/shard_map/ppermute | solution.py:321
  30.8 0.5 collective-permute-done.5.refs_2_
  31.3 0.1 join.1
  31.4 0.1 collective-permute-start.12
  31.5 0.5 collective-permute-start.14
  32.0 1.5 %collective-permute-done.12.refs_1_ = bf16[4,4,48,384]{3,2,1,0:T(8,128)(2,1)S(1)} collective-permute-done((bf16[4,4,48,384]{3,2,1,0:T(8,128)(2,1)S(1)}, bf16[4,4,48,384]{3,2,1,0:T(8,128)(2,1)S(1)}, u32[]{:S(2)}, u32[]{:S(2)}) %collective-permute-start.12) | collective-permute-done | bytes 589856 | tf_op jit(solution)/shard_map/ppermute | solution.py:321
  33.5 4.2 %forward.1 = (bf16[192,3072]{1,0:T(8,128)(2,1)S(1)}, bf16[192,1024]{1,0:T(8,128)(2,1)S(1)}, f32[192,1024]{1,0:T(8,128)S(1)}, f32[192,1024]{1,0:T(8,128)S(1)}, f3...) custom-call(bf16[4,4,48,384]{3,2,1,0:T(8,128)(2,1)S(1)} %get-tuple-e, ...), custom_call_target="tpu_custom_call" | custom-call | flops 3623878656 | bytes 18874368 | tf_op jit(solution)/shard_map/forward/pallas_call | solution.py:340
  37.7 0.2 collective-permute-start.13
  37.9 0.0 collective-permute-done.14.refs_1_
  37.9 3.2 %backward.1 = (bf16[192,3072]{1,0:T(8,128)(2,1)S(1)}, bf16[192,1024]{1,0:T(8,128)(2,1)S(1)}, bf16[192,1024]{1,0:T(8,128)(2,1)S(1)}, f32[4,4,384]{2,1,0:T(4,128)S(1)}, bf16[4,8,384]{2,1,0:T(8,128)(2,1)S(1)}) custom-call(bf16[4,4,40,384]{3,2,1,0:T(8,128)(2,1)S(1)} %get-tuple-element.70.refs_0_, bf16[4,4,40,384]{3,2,1,0:T(8,128)(2,1)S(1)} %collective-permute-done.14.refs_1_, ...), custom_call_target="tpu_custom_call" | custom-call | flops 1207959552 | bytes 6291456 | tf_op jit(solution)/shard_map/backward/pallas_call | solution.py:340
  41.1 0.5 collective-permute-start.15
  41.6 0.8 %collective-permute-done.15.rgot_ref = bf16[4,8,384]{2,1,0:T(8,128)(2,1)S(1)} collective-permute-done((bf16[4,8,384]{2,1,0:T(8,128)(2,1)S(1)}, bf16[4,8,384]{2,1,0:T(8,128)(2,1)S(1)}, u32[]{:S(2)}, u32[]{:S(2)}) %collective-permute-start.15) | collective-permute-done | bytes 24608 | tf_op jit(solution)/shard_map/ppermute | solution.py:321
  42.4 0.0 collective-permute-done.13.got_ref
  42.4 0.1 merge.1
  42.5 2.4 %collective-permute-start.16 = (bf16[168,384]{1,0:T(8,128)(2,1)S(1)}, bf16[168,384]{1,0:T(8,128)(2,1)S(1)}, u32[]{:S(2)}, u32[]{:S(2)}) collective-permute-start(bf16[168,384]{1,0:T(8,128)(2,1)S(1)} %get-tuple-element.81), channel_id=1, source_target_pairs={{0,6},{2,4},{4,2},{6,0},{1,7},{3,5},{5,3},{7,1},{8,14},{10,12},{12... | collective-permute-start | bytes 387080 | tf_op jit(solution)/shard_map/ppermute | solution.py:321
  44.9 0.0 collective-permute-start.17
  44.9 2.0 %collective-permute-start.18 = (bf16[168,384]{1,0:T(8,128)(2,1)S(1)}, bf16[168,384]{1,0:T(8,128)(2,1)S(1)}, u32[]{:S(2)}, u32[]{:S(2)}) collective-permute-start(bf16[168,384]{1,0:T(8,128)(2,1)S(1)} %get-tuple-element.83), channel_id=1, source_target_pairs={{0,2},{2,0},{4,6},{6,4},{1,3},{3,1},{5,7},{7,5},{8,10},{10,8},{12,... | collective-permute-start | bytes 387080 | tf_op jit(solution)/shard_map/ppermute | solution.py:321
  47.0 8.8 %grads.1 = (bf16[1,3072,1024]{2,1,0:T(8,128)(2,1)}, bf16[1,3072,1024]{2,1,0:T(8,128)(2,1)}, bf16[1,1024,3072]{2,1,0:T(8,128)(2,1)}, f32[8,128]{1,0:T(8,128)S(1)}) custom-call(bf16[192,3072]{1,0:T(8,128)(2,1)S(1)} %get-tuple-element.71.refs_2_.x_ref, bf16[192,3072]{1,0:T(8,128)(2,1)S(1)} %get-tuple-element.84.d_ref, ...), custom_call_target="tpu_custom_call" | custom-call | flops 3623878656 | bytes 18874368 | tf_op jit(solution)/shard_map/grads/pallas_call | solution.py:468
  55.8 0.0 collective-permute-done.16.refs_1_
  55.8 0.6 collective-permute-done.17.refs_2_
  56.4 0.0 collective-permute-done.18.refs_3_
  56.4 0.1 total.1
  56.5 2.2 %collective-permute-start.19 = (bf16[48,384]{1,0:T(8,128)(2,1)S(1)}, bf16[48,384]{1,0:T(8,128)(2,1)S(1)}, u32[]{:S(2)}, u32[]{:S(2)}) collective-permute-start(bf16[48,384]{1,0:T(8,128)(2,1)S(1)} %get-tuple-element.88), channel_id=1, source_target_pairs={{0,24},{8,16},{16,8},{24,0},{1,25},{9,17},{17,9},{25,1},{2,26},{10... | collective-permute-start | bytes 110600 | tf_op jit(solution)/shard_map/ppermute | solution.py:321
  58.7 0.5 collective-permute-start.20
  59.2 0.8 %collective-permute-start.21 = (bf16[48,384]{1,0:T(8,128)(2,1)S(1)}, bf16[48,384]{1,0:T(8,128)(2,1)S(1)}, u32[]{:S(2)}, u32[]{:S(2)}) collective-permute-start(bf16[48,384]{1,0:T(8,128)(2,1)S(1)} %get-tuple-element.90), channel_id=1, source_target_pairs={{0,8},{8,0},{16,24},{24,16},{1,9},{9,1},{17,25},{25,17},{2,10},{10... | collective-permute-start | bytes 110600 | tf_op jit(solution)/shard_map/ppermute | solution.py:321
  60.0 1.4 %collective-permute-done.19.refs_0_ = bf16[48,384]{1,0:T(8,128)(2,1)S(1)} collective-permute-done((bf16[48,384]{1,0:T(8,128)(2,1)S(1)}, bf16[48,384]{1,0:T(8,128)(2,1)S(1)}, u32[]{:S(2)}, u32[]{:S(2)}) %collective-permute-start.19) | collective-permute-done | bytes 36896 | tf_op jit(solution)/shard_map/ppermute | solution.py:321
  61.4 1.2 %collective-permute-done.20.refs_1_ = bf16[48,384]{1,0:T(8,128)(2,1)S(1)} collective-permute-done((bf16[48,384]{1,0:T(8,128)(2,1)S(1)}, bf16[48,384]{1,0:T(8,128)(2,1)S(1)}, u32[]{:S(2)}, u32[]{:S(2)}) %collective-permute-start.20) | collective-permute-done | bytes 36896 | tf_op jit(solution)/shard_map/ppermute | solution.py:321
  62.6 0.5 collective-permute-done.21.refs_2_
  63.1 0.9 %combine.1 = (bf16[128,384]{1,0:T(8,128)(2,1)}, bf16[4,384]{1,0:T(4,128)(2,1)}) custom-call(s32[1,256]{1,0:T(1,128)S(1)} %get-tuple-element.51.pos_ref, bf16[48,384]{1,0:T(8,128)(2,1)S(1)} %collective-permute-done.19.refs_0_, bf16[48,384]{1,0:T(8,128)(2,1)S(1)} %collective-permute-done.20.refs_1_, bf16[48,384]{1,0:T(8,128)(2,1)S(1)} %collective-permute-done.21.refs_2_, ...), custom_call_target="tpu_custom_call" | custom-call | tf_op jit(solution)/shard_map/combine/pallas_call | solution.py:340
  (1 shorter events, 0.0 us)
Async XLA Ops:
  2.2 12.6 %collective-permute-start.1 = (bf16[128,384]{1,0:T(8,128)(2,1)S(1)}, bf16[128,384]{1,0:T(8,128)(2,1)S(1)}, u32[]{:S(2)}, u32[]{:S(2)}) collective-permute-start(bf16[128,384]{1,0:T(8,128)(2,1)S(1)} %get-tuple-element.53.refs_0_), channel_id=1, source_target_pairs={{0,4},{2,6},{4,0},{6,2},{1,5},{3,7},{5,1},{7,3},{8,12},{10,14},{12... | collective-permute-start | bytes 294920 | tf_op jit(solution)/shard_map/ppermute | solution.py:321
  6.3 8.5 %collective-permute-start = (bf16[128,384]{1,0:T(8,128)(2,1)S(1)}, bf16[128,384]{1,0:T(8,128)(2,1)S(1)}, u32[]{:S(2)}, u32[]{:S(2)}) collective-permute-start(bf16[128,384]{1,0:T(8,128)(2,1)S(1)} %get-tuple-element.53.refs_0_), channel_id=1, source_target_pairs={{0,2},{2,0},{4,6},{6,4},{1,3},{3,1},{5,7},{7,5},{8,10},{10,8},{12,... | collective-permute-start | bytes 294920 | tf_op jit(solution)/shard_map/ppermute | solution.py:321
  7.9 6.3 %collective-permute-start.6 = (bf16[48,384]{1,0:T(8,128)(2,1)S(1)}, bf16[48,384]{1,0:T(8,128)(2,1)S(1)}, u32[]{:S(2)}, u32[]{:S(2)}) collective-permute-start(bf16[48,384]{1,0:T(8,128)(2,1)S(1)} %get-tuple-element.59), channel_id=1, source_target_pairs={{0,24},{8,16},{16,8},{24,0},{1,25},{9,17},{17,9},{25,1},{2,26},{10... | collective-permute-start | bytes 110600 | tf_op jit(solution)/shard_map/ppermute | solution.py:321
  10.3 4.0 %collective-permute-start.7 = (bf16[48,384]{1,0:T(8,128)(2,1)S(1)}, bf16[48,384]{1,0:T(8,128)(2,1)S(1)}, u32[]{:S(2)}, u32[]{:S(2)}) collective-permute-start(bf16[48,384]{1,0:T(8,128)(2,1)S(1)} %get-tuple-element.60), channel_id=1, source_target_pairs={{0,16},{8,24},{16,0},{24,8},{1,17},{9,25},{17,1},{25,9},{2,18},{10... | collective-permute-start | bytes 110600 | tf_op jit(solution)/shard_map/ppermute | solution.py:321
  10.8 4.0 %collective-permute-start.8 = (bf16[48,384]{1,0:T(8,128)(2,1)S(1)}, bf16[48,384]{1,0:T(8,128)(2,1)S(1)}, u32[]{:S(2)}, u32[]{:S(2)}) collective-permute-start(bf16[48,384]{1,0:T(8,128)(2,1)S(1)} %get-tuple-element.61), channel_id=1, source_target_pairs={{0,8},{8,0},{16,24},{24,16},{1,9},{9,1},{17,25},{25,17},{2,10},{10... | collective-permute-start | bytes 110600 | tf_op jit(solution)/shard_map/ppermute | solution.py:321
  14.8 11.6 %collective-permute-start.10 = (bf16[4,48,384]{2,1,0:T(8,128)(2,1)S(1)}, bf16[4,48,384]{2,1,0:T(8,128)(2,1)S(1)}, u32[]{:S(2)}, u32[]{:S(2)}) collective-permute-start(bf16[4,48,384]{2,1,0:T(8,128)(2,1)S(1)} %stack.1.refs_7_), channel_id=1, source_target_pairs={{0,4},{2,6},{4,0},{6,2},{1,5},{3,7},{5,1},{7,3},{8,12},{10,14},{12... | collective-permute-start | bytes 442376 | tf_op jit(solution)/shard_map/ppermute | solution.py:321
  15.2 7.3 %collective-permute-start.2 = (bf16[128,384]{1,0:T(8,128)(2,1)S(1)}, bf16[128,384]{1,0:T(8,128)(2,1)S(1)}, u32[]{:S(2)}, u32[]{:S(2)}) collective-permute-start(bf16[128,384]{1,0:T(8,128)(2,1)S(1)} %collective-permute-done.1.refs_2_.refs_6_), channel_id=1, source_target_pairs={{0,2},{2,0},{4,6},{6,4},{1,3},{3,1},{5,7},{7,5},{8,10},{10,8},{12,... | collective-permute-start | bytes 294920 | tf_op jit(solution)/shard_map/ppermute | solution.py:321
  15.7 13.8 %collective-permute-start.11 = (bf16[4,48,384]{2,1,0:T(8,128)(2,1)S(1)}, bf16[4,48,384]{2,1,0:T(8,128)(2,1)S(1)}, u32[]{:S(2)}, u32[]{:S(2)}) collective-permute-start(bf16[4,48,384]{2,1,0:T(8,128)(2,1)S(1)} %stack.1.refs_7_), channel_id=1, source_target_pairs={{0,2},{2,0},{4,6},{6,4},{1,3},{3,1},{5,7},{7,5},{8,10},{10,8},{12,... | collective-permute-start | bytes 442376 | tf_op jit(solution)/shard_map/ppermute | solution.py:321
  17.3 12.2 %collective-permute-start.9 = (bf16[4,48,384]{2,1,0:T(8,128)(2,1)S(1)}, bf16[4,48,384]{2,1,0:T(8,128)(2,1)S(1)}, u32[]{:S(2)}, u32[]{:S(2)}) collective-permute-start(bf16[4,48,384]{2,1,0:T(8,128)(2,1)S(1)} %stack.1.refs_7_), channel_id=1, source_target_pairs={{0,6},{2,4},{4,2},{6,0},{1,7},{3,5},{5,3},{7,1},{8,14},{10,12},{12... | collective-permute-start | bytes 442376 | tf_op jit(solution)/shard_map/ppermute | solution.py:321
  22.9 6.6 %collective-permute-start.3 = (bf16[4,40,384]{2,1,0:T(8,128)(2,1)S(1)}, bf16[4,40,384]{2,1,0:T(8,128)(2,1)S(1)}, u32[]{:S(2)}, u32[]{:S(2)}) collective-permute-start(bf16[4,40,384]{2,1,0:T(8,128)(2,1)S(1)} %get-tuple-element.55), channel_id=1, source_target_pairs={{0,24},{8,16},{16,8},{24,0},{1,25},{9,17},{17,9},{25,1},{2,26},{10... | collective-permute-start | bytes 368648 | tf_op jit(solution)/shard_map/ppermute | solution.py:321
  25.9 4.9 %collective-permute-start.4 = (bf16[4,40,384]{2,1,0:T(8,128)(2,1)S(1)}, bf16[4,40,384]{2,1,0:T(8,128)(2,1)S(1)}, u32[]{:S(2)}, u32[]{:S(2)}) collective-permute-start(bf16[4,40,384]{2,1,0:T(8,128)(2,1)S(1)} %get-tuple-element.56), channel_id=1, source_target_pairs={{0,16},{8,24},{16,0},{24,8},{1,17},{9,25},{17,1},{25,9},{2,18},{10... | collective-permute-start | bytes 368648 | tf_op jit(solution)/shard_map/ppermute | solution.py:321
  26.4 4.9 %collective-permute-start.5 = (bf16[4,40,384]{2,1,0:T(8,128)(2,1)S(1)}, bf16[4,40,384]{2,1,0:T(8,128)(2,1)S(1)}, u32[]{:S(2)}, u32[]{:S(2)}) collective-permute-start(bf16[4,40,384]{2,1,0:T(8,128)(2,1)S(1)} %get-tuple-element.57), channel_id=1, source_target_pairs={{0,8},{8,0},{16,24},{24,16},{1,9},{9,1},{17,25},{25,17},{2,10},{10... | collective-permute-start | bytes 368648 | tf_op jit(solution)/shard_map/ppermute | solution.py:321
  31.4 2.1 %collective-permute-start.12 = (bf16[4,4,48,384]{3,2,1,0:T(8,128)(2,1)S(1)}, bf16[4,4,48,384]{3,2,1,0:T(8,128)(2,1)S(1)}, u32[]{:S(2)}, u32[]{:S(2)}) collective-permute-start(bf16[4,4,48,384]{3,2,1,0:T(8,128)(2,1)S(1)} %get-tuple-element.64.refs_0_), channel_id=1, source_target_pairs={{0,1},{1,0},{2,3},{3,2},{4,5},{5,4},{6,7},{7,6},{8,9},{9,8},{10,11... | collective-permute-start | bytes 1769480 | tf_op jit(solution)/shard_map/ppermute | solution.py:321
  31.5 6.4 %collective-permute-start.14 = (bf16[4,4,40,384]{3,2,1,0:T(8,128)(2,1)S(1)}, bf16[4,4,40,384]{3,2,1,0:T(8,128)(2,1)S(1)}, u32[]{:S(2)}, u32[]{:S(2)}) collective-permute-start(bf16[4,4,40,384]{3,2,1,0:T(8,128)(2,1)S(1)} %get-tuple-element.70.refs_0_), channel_id=1, source_target_pairs={{0,1},{1,0},{2,3},{3,2},{4,5},{5,4},{6,7},{7,6},{8,9},{9,8},{10,11... | collective-permute-start | bytes 1474568 | tf_op jit(solution)/shard_map/ppermute | solution.py:321
  37.7 4.7 %collective-permute-start.13 = (bf16[4,4,48,384]{3,2,1,0:T(8,128)(2,1)S(1)}, bf16[4,4,48,384]{3,2,1,0:T(8,128)(2,1)S(1)}, u32[]{:S(2)}, u32[]{:S(2)}) collective-permute-start(bf16[4,4,48,384]{3,2,1,0:T(8,128)(2,1)S(1)} %get-tuple-element.69), channel_id=1, source_target_pairs={{0,1},{1,0},{2,3},{3,2},{4,5},{5,4},{6,7},{7,6},{8,9},{9,8},{10,11... | collective-permute-start | bytes 1769480 | tf_op jit(solution)/shard_map/ppermute | solution.py:321
  41.1 1.3 %collective-permute-start.15 = (bf16[4,8,384]{2,1,0:T(8,128)(2,1)S(1)}, bf16[4,8,384]{2,1,0:T(8,128)(2,1)S(1)}, u32[]{:S(2)}, u32[]{:S(2)}) collective-permute-start(bf16[4,8,384]{2,1,0:T(8,128)(2,1)S(1)} %get-tuple-element.79), channel_id=1, source_target_pairs={{0,1},{1,0},{2,3},{3,2},{4,5},{5,4},{6,7},{7,6},{8,9},{9,8},{10,11... | collective-permute-start | bytes 73736 | tf_op jit(solution)/shard_map/ppermute | solution.py:321
  42.5 13.3 %collective-permute-start.16 = (bf16[168,384]{1,0:T(8,128)(2,1)S(1)}, bf16[168,384]{1,0:T(8,128)(2,1)S(1)}, u32[]{:S(2)}, u32[]{:S(2)}) collective-permute-start(bf16[168,384]{1,0:T(8,128)(2,1)S(1)} %get-tuple-element.81), channel_id=1, source_target_pairs={{0,6},{2,4},{4,2},{6,0},{1,7},{3,5},{5,3},{7,1},{8,14},{10,12},{12... | collective-permute-start | bytes 387080 | tf_op jit(solution)/shard_map/ppermute | solution.py:321
  44.9 11.4 %collective-permute-start.17 = (bf16[168,384]{1,0:T(8,128)(2,1)S(1)}, bf16[168,384]{1,0:T(8,128)(2,1)S(1)}, u32[]{:S(2)}, u32[]{:S(2)}) collective-permute-start(bf16[168,384]{1,0:T(8,128)(2,1)S(1)} %get-tuple-element.82), channel_id=1, source_target_pairs={{0,4},{2,6},{4,0},{6,2},{1,5},{3,7},{5,1},{7,3},{8,12},{10,14},{12... | collective-permute-start | bytes 387080 | tf_op jit(solution)/shard_map/ppermute | solution.py:321
  44.9 11.4 %collective-permute-start.18 = (bf16[168,384]{1,0:T(8,128)(2,1)S(1)}, bf16[168,384]{1,0:T(8,128)(2,1)S(1)}, u32[]{:S(2)}, u32[]{:S(2)}) collective-permute-start(bf16[168,384]{1,0:T(8,128)(2,1)S(1)} %get-tuple-element.83), channel_id=1, source_target_pairs={{0,2},{2,0},{4,6},{6,4},{1,3},{3,1},{5,7},{7,5},{8,10},{10,8},{12,... | collective-permute-start | bytes 387080 | tf_op jit(solution)/shard_map/ppermute | solution.py:321
  56.5 4.9 %collective-permute-start.19 = (bf16[48,384]{1,0:T(8,128)(2,1)S(1)}, bf16[48,384]{1,0:T(8,128)(2,1)S(1)}, u32[]{:S(2)}, u32[]{:S(2)}) collective-permute-start(bf16[48,384]{1,0:T(8,128)(2,1)S(1)} %get-tuple-element.88), channel_id=1, source_target_pairs={{0,24},{8,16},{16,8},{24,0},{1,25},{9,17},{17,9},{25,1},{2,26},{10... | collective-permute-start | bytes 110600 | tf_op jit(solution)/shard_map/ppermute | solution.py:321
  58.7 4.0 %collective-permute-start.20 = (bf16[48,384]{1,0:T(8,128)(2,1)S(1)}, bf16[48,384]{1,0:T(8,128)(2,1)S(1)}, u32[]{:S(2)}, u32[]{:S(2)}) collective-permute-start(bf16[48,384]{1,0:T(8,128)(2,1)S(1)} %get-tuple-element.89), channel_id=1, source_target_pairs={{0,16},{8,24},{16,0},{24,8},{1,17},{9,25},{17,1},{25,9},{2,18},{10... | collective-permute-start | bytes 110600 | tf_op jit(solution)/shard_map/ppermute | solution.py:321
  59.2 4.0 %collective-permute-start.21 = (bf16[48,384]{1,0:T(8,128)(2,1)S(1)}, bf16[48,384]{1,0:T(8,128)(2,1)S(1)}, u32[]{:S(2)}, u32[]{:S(2)}) collective-permute-start(bf16[48,384]{1,0:T(8,128)(2,1)S(1)} %get-tuple-element.90), channel_id=1, source_target_pairs={{0,8},{8,0},{16,24},{24,16},{1,9},{9,1},{17,25},{25,17},{2,10},{10... | collective-permute-start | bytes 110600 | tf_op jit(solution)/shard_map/ppermute | solution.py:321
